TPU v7x, 32 devices: a whole 2x2x4 slice. The times are simulated.
32 devices in a mesh: sect: 2 (over core), grp: 4 (over y, x), dev: 4 (over z).
Axes of the slice: x: 2, y: 2, z: 4, core: 2. Of those that a mesh axis runs over, the one named last changes fastest.
Arguments:
- tokens: bfloat16 [128, 7168], P(('sect', 'grp', 'dev')), may hold values from -6 to 6
- expert_ids: int32 [128, 8], P(('sect', 'grp', 'dev')), may hold values from 0 to 15, all different within a row; in each aligned block of 4 rows (0 to 3, 4 to 7, ...) at most 2 rows name the same one
- gate_weights: float32 [128, 8], P(('sect', 'grp', 'dev')), may hold values from 0.1 to 0.6
- w_gate: bfloat16 [16, 7168, 2048], P(('sect', 'grp'), None, 'dev'), may hold values from -0.0625 to 0.0625
- w_up: bfloat16 [16, 7168, 2048], P(('sect', 'grp'), None, 'dev'), may hold values from -0.0625 to 0.0625
- w_down: bfloat16 [16, 2048, 7168], P(('sect', 'grp'), 'dev'), may hold values from -0.125 to 0.125
Outputs:
- mixed: bfloat16 [128, 7168], P(('sect', 'grp', 'dev'))
Inputs may be any that keep to these rules, and one draw needn't show every extreme that they name: `expert_ids`: each row names 8 different experts. Within the 4 rows of one device no expert is named by more than 2 rows, and on some device some expert is named by exactly 2.
All inputs are finite; a program needn't handle non-finite values.
Results may differ from a plain program's by a relative error of at most 0.015.
Values may be sent and summed in bfloat16 or wider, within the bound.
No kernel may reach another device: no remote copies, remote signals or barrier semaphores. Data moves between devices by JAX's collectives and lax.ppermute only.
A program may use at most 128 MiB of HBM per device.

v0:
```python
import jax
import jax.numpy as jnp
from jax import lax
from jax.sharding import PartitionSpec as P

TOP = 8
CAP = 2


def body(tokens, expert_ids, gate_weights, w_gate, w_up, w_down):
    groups = lax.axis_size(("sect", "grp"))
    lane_count = lax.axis_size("dev")
    row_count, model_width = tokens.shape
    local_experts = w_gate.shape[0]
    expert_count = groups * local_experts
    slot_count = expert_count * CAP
    catalog = jnp.arange(expert_count, dtype=jnp.int32)
    per_row = jnp.sum((expert_ids[:, :, None] == catalog[None, None, :]).astype(jnp.int32), axis=1)
    earlier = jnp.cumsum(per_row, axis=0) - per_row
    slot_of = expert_ids * CAP + jnp.take_along_axis(earlier, expert_ids, axis=1)
    positions = jnp.arange(slot_count, dtype=jnp.int32)
    placing = jnp.sum(
        (slot_of[:, :, None] == positions[None, None, :]).astype(jnp.bfloat16), axis=1
    )
    outbound = jnp.dot(placing.T, tokens, preferred_element_type=jnp.float32).astype(jnp.bfloat16)
    outbound = outbound.reshape(groups, 1, local_experts, CAP, model_width)
    copies = jnp.broadcast_to(outbound, (groups, lane_count, local_experts, CAP, model_width))
    copies = copies.reshape(groups * lane_count, local_experts, CAP, model_width)
    arrived = lax.all_to_all(
        copies, ("sect", "grp", "dev"), split_axis=0, concat_axis=0, tiled=True
    )
    arrived = arrived.reshape(groups, lane_count, local_experts, CAP, model_width)
    gate_proj = jnp.einsum("abjcd,jdf->jabcf", arrived, w_gate, preferred_element_type=jnp.float32)
    up_proj = jnp.einsum("abjcd,jdf->jabcf", arrived, w_up, preferred_element_type=jnp.float32)
    hidden = (jax.nn.silu(gate_proj) * up_proj).astype(jnp.bfloat16)
    partial_value = jnp.einsum(
        "jabcf,jfd->abjcd", hidden, w_down, preferred_element_type=jnp.float32
    ).astype(jnp.bfloat16)
    flattened = partial_value.reshape(groups * lane_count, local_experts, CAP, model_width)
    returned = lax.all_to_all(
        flattened, ("sect", "grp", "dev"), split_axis=0, concat_axis=0, tiled=True
    )
    returned = returned.reshape(groups, lane_count, local_experts, CAP, model_width)
    expert_out = jnp.sum(returned.astype(jnp.float32), axis=1).astype(jnp.bfloat16)
    slot_rows = expert_out.reshape(slot_count, model_width)
    picked = jnp.take(slot_rows, slot_of.reshape(-1), axis=0).reshape(row_count, TOP, model_width)
    mixed = jnp.sum(gate_weights[:, :, None] * picked.astype(jnp.float32), axis=1)
    return mixed.astype(jnp.bfloat16)


def solution(mesh):
    in_specs = (
        P(("sect", "grp", "dev"), None),
        P(("sect", "grp", "dev"), None),
        P(("sect", "grp", "dev"), None),
        P(("sect", "grp"), None, "dev"),
        P(("sect", "grp"), None, "dev"),
        P(("sect", "grp"), "dev", None),
    )
    out_specs = P(("sect", "grp", "dev"), None)
    return jax.shard_map(body, mesh=mesh, in_specs=in_specs, out_specs=out_specs, check_vma=False)
```

profile of v0, /device:TPU:0, one launch (start us, length us, event | category | flops | bytes accessed | tf_op | source)
XLA Modules:
  0.0 132.8 jit_solution(4225002961187281044)
XLA Ops:
  0.0 0.0 copy-start
  0.0 0.0 copy-start.1
  0.0 0.8 convert_reduce_fusion
  0.8 0.7 bitcast_or_fusion
  1.6 0.1 reshape.87
  1.7 0.8 gather_fusion.1
  2.4 0.1 reshape.90
  2.5 0.0 copy-done.1
  2.5 0.1 fusion.35
  2.6 0.0 copy-done
  2.6 0.3 convolution_convert_fusion
  2.9 0.2 broadcast_in_dim.28
  3.1 1.1 broadcast_in_dim.29
  4.2 50.9 %all_to_all.10 = bf16[32,2,2,7168]{3,2,1,0:T(2,128)(2,1)S(1)} all-to-all(bf16[32,2,2,7168]{3,2,1,0:T(2,128)(2,1)S(1)} %bitcast.46), channel_id=1, replica_groups=mesh['sect'=2,'grp'=4,'dev'=4] {'sect','grp','dev'}, dimensions={0} | all-to-all | bytes 3670016 | tf_op jit(solution)/shard_map/all_to_all | solution.py:29
  55.1 7.5 %fusion.4 = f32[2,8,4,2,512]{4,1,3,2,0:T(8,128)S(1)} fusion(bf16[2,7168,512]{2,1,0:T(8,128)(2,1)} %param.9, bf16[8,4,2,2,7168]{4,3,2,1,0:T(2,128)(2,1)S(1)} %bitcast.44), kind=kOutput, calls=%fused_computation.6 | convolution fusion | flops 939524096 | bytes 16777216 | tf_op jit(solution)/shard_map/abjcd,jdf->jabcf/dot_general | solution.py:33
  62.6 15.7 %fusion.9 = bf16[8,4,2,2,7168]{4,0,3,1,2:T(8,128)(2,1)} fusion(bf16[2,512,7168]{2,1,0:T(8,128)(2,1)} %param.11, bf16[2,7168,512]{2,1,0:T(8,128)(2,1)} %param.10, bf16[8,4,2,2,7168]{4,3,2,1,0:T(2,128)(2,1)S(1)} %bitcast.45, f32[2,8,4,2,512]{4,1,3,2,0:T(8,128)S(1)} %fusion.4), kind=kOutput, calls=%fused_computation.9 | convolution fusion | flops 1880358912 | bytes 33292288 | tf_op jit(solution)/shard_map/jabcf,jfd->abjcd/dot_general | solution.py:36
  78.2 4.6 %copy.11 = bf16[8,4,2,2,7168]{4,3,2,1,0:T(2,128)(2,1)} copy(bf16[8,4,2,2,7168]{4,0,3,1,2:T(8,128)(2,1)} %fusion.9) | data formatting | bytes 3670016 | tf_op jit(solution)/shard_map/convert_element_type | solution.py:38
  82.9 2.9 %all-to-all-start.1 = ((bf16[32,2,2,7168]{3,2,1,0:T(2,128)(2,1)}), bf16[32,2,2,7168]{3,2,1,0:T(2,128)(2,1)S(1)}, u32[]{:S(2)}, u32[]{:S(2)}) async-start(bf16[32,2,2,7168]{3,2,1,0:T(2,128)(2,1)} %bitcast.10), calls=%async_computation.1 | async-start | bytes 3670016 | tf_op jit(solution)/shard_map/all_to_all | solution.py:40
  85.8 0.1 reshape.78
  85.9 42.9 %all-to-all-done.1 = bf16[32,2,2,7168]{3,2,1,0:T(2,128)(2,1)S(1)} async-done(((bf16[32,2,2,7168]{3,2,1,0:T(2,128)(2,1)}), bf16[32,2,2,7168]{3,2,1,0:T(2,128)(2,1)S(1)}, u32[]{:S(2)}, u32[]{:S(2)}) %all-to-all-start.1) | async-done | bytes 1835040 | tf_op jit(solution)/shard_map/all_to_all | solution.py:40
  128.8 1.9 %bitcast_reduce_fusion = bf16[8,2,2,7168]{3,2,1,0:T(2,128)(2,1)S(1)} fusion(bf16[32,2,2,7168]{3,2,1,0:T(2,128)(2,1)S(1)} %all-to-all-done.1), kind=kLoop, calls=%fused_computation.11 | loop fusion | flops 688128 | bytes 2293760 | tf_op jit(solution)/shard_map/reduce_sum | solution.py:44
  130.7 0.2 reshape.77
  130.9 0.0 copy-start.2
  130.9 0.8 gather_fusion
  131.7 0.0 copy-done.2
  131.7 1.0 multiply_reduce_fusion
  (5 shorter events, 0.1 us)
Async XLA Ops:
  0.0 2.6 %copy-start = (bf16[4,7168]{1,0:T(4,128)(2,1)S(1)}, bf16[4,7168]{1,0:T(4,128)(2,1)}, u32[]{:S(2)}) copy-start(bf16[4,7168]{1,0:T(4,128)(2,1)} %param.6) | copy-start | bytes 172036
  0.0 2.5 %copy-start.1 = (s32[4,8]{1,0:T(4,128)S(1)}, s32[4,8]{1,0:T(4,128)}, u32[]{:S(2)}) copy-start(s32[4,8]{1,0:T(4,128)} %param.7) | copy-start | bytes 388
  82.9 45.9 %all-to-all-start.1 = ((bf16[32,2,2,7168]{3,2,1,0:T(2,128)(2,1)}), bf16[32,2,2,7168]{3,2,1,0:T(2,128)(2,1)S(1)}, u32[]{:S(2)}, u32[]{:S(2)}) async-start(bf16[32,2,2,7168]{3,2,1,0:T(2,128)(2,1)} %bitcast.10), calls=%async_computation.1 | async-start | bytes 3670016 | tf_op jit(solution)/shard_map/all_to_all | solution.py:40
  130.9 0.9 copy-start.2
where the time goes:
time: 133 us
  blocking collectives  50.9 us (38%)
  waiting for transfers between devices  42.9 us (32%)
  matrix products  23.5 us (18%)
  local copies, waits for them, and re-layouts  7.87 us (6%)
  other arithmetic  4.59 us (3%)
  starting transfers between devices  2.89 us (2%)
    all_to_all x1, blocking collectives, body(): lax.all_to_all(copies, ('sect', 'grp', 'dev'), split_axis=0, concat_axis=...  50.9 us
    all_to_all x1, waiting for transfers between devices, body(): lax.all_to_all(flattened, ('sect', 'grp', 'dev'), split_axis=0, concat_ax...  42.9 us
    dot_general x1, matrix products, body(): jnp.einsum('jabcf,jfd->abjcd', hidden, w_down, preferred_element_type=jnp...  15.7 us
    dot_general x1, matrix products, body(): jnp.einsum('abjcd,jdf->jabcf', arrived, w_gate, preferred_element_type=jn...  7.47 us
    convert_element_type x1, local copies, waits for them, and re-layouts, body(): partial_value = jnp.einsum('jabcf,jfd->abjcd', hidden, w_down, preferred_...  4.61 us
    all_to_all x1, starting transfers between devices, body(): lax.all_to_all(flattened, ('sect', 'grp', 'dev'), split_axis=0, concat_ax...  2.89 us
  transfers between devices with their start and end apart: 1, of which 1 were waited for; matrix products, arithmetic and copies ran while one was open for 0% of the time, Pallas kernels for 0%

commit v1 on v0

v1 whole, which is shorter than its diff:
```python
import jax
import jax.numpy as jnp
from jax import lax
from jax.sharding import PartitionSpec as P

AXES = ("sect", "grp", "dev")


def body(tokens, expert_ids, gate_weights, w_gate, w_up, w_down):
    local_experts = w_gate.shape[0]
    first = lax.axis_index(("sect", "grp")) * local_experts
    rows = lax.all_gather(tokens, AXES, axis=0, tiled=True)
    ids = lax.all_gather(expert_ids, AXES, axis=0, tiled=True)
    weights = lax.all_gather(gate_weights, AXES, axis=0, tiled=True)
    local = first + jnp.arange(local_experts, dtype=jnp.int32)
    scale = jnp.sum(
        jnp.where(ids[None] == local[:, None, None], weights[None], 0.0), axis=2
    )
    gate_proj = jnp.einsum("rd,jdf->jrf", rows, w_gate, preferred_element_type=jnp.float32)
    up_proj = jnp.einsum("rd,jdf->jrf", rows, w_up, preferred_element_type=jnp.float32)
    hidden = (jax.nn.silu(gate_proj) * up_proj * scale[:, :, None]).astype(jnp.bfloat16)
    partial = jnp.einsum(
        "jrf,jfd->rd", hidden, w_down, preferred_element_type=jnp.float32
    ).astype(jnp.bfloat16)
    return lax.psum_scatter(partial, AXES, scatter_dimension=0, tiled=True)


def solution(mesh):
    in_specs = (
        P(AXES, None),
        P(AXES, None),
        P(AXES, None),
        P(("sect", "grp"), None, "dev"),
        P(("sect", "grp"), None, "dev"),
        P(("sect", "grp"), "dev", None),
    )
    return jax.shard_map(
        body, mesh=mesh, in_specs=in_specs, out_specs=P(AXES, None), check_vma=False
    )
```

time: 133 us -> 327 us (2.46)
  waiting for transfers between devices: 42.9 us -> 144 us
  blocking collectives: 50.9 us -> 137 us
  between operations: 0.1 us -> 13.4 us
  other arithmetic: 4.59 us -> 0.09 us
  matrix products: 23.5 us -> 27.6 us
  local copies, waits for them, and re-layouts: 7.87 us -> 4.59 us
    unnamed x0 -> x3, waiting for transfers between devices: none -> 144 us
    all_gather x0 -> x2, blocking collectives: none -> 137 us  [the longest x1 71 us: body(): ids = lax.all_gather(expert_ids, AXES, axis=0, tiled=True)]
    all_to_all x1 -> x0, blocking collectives: 50.9 us -> none  [body(): lax.all_to_all(copies, ('sect', 'grp', 'dev'), split_axis=0, concat_axis=...]
    all_to_all x1 -> x0, waiting for transfers between devices: 42.9 us -> none  [body(): lax.all_to_all(flattened, ('sect', 'grp', 'dev'), split_axis=0, concat_ax...]
    convert_element_type x1 -> x0, local copies, waits for them, and re-layouts: 4.61 us -> none  [body(): partial_value = jnp.einsum('jabcf,jfd->abjcd', hidden, w_down, preferred_...]
    unnamed x6 -> x4, local copies, waits for them, and re-layouts: 0.01 us -> 4.59 us
    dot_general x3 -> x2, matrix products: 23.5 us -> 27.6 us  [the longest x1 20.3 us: body(): jnp.einsum('jrf,jfd->rd', hidden, w_down, preferred_element_type=jnp.floa...]
    reduce_sum x4 -> x1, other arithmetic: 3.83 us -> 0.09 us  [body(): jnp.sum(jnp.where(ids[None] == local[:, None, None], weights[None], 0.0),...]
  transfers between devices with their start and end apart: 1 -> 2, of which waited for: 1 -> 1; matrix products, arithmetic and copies ran while one was open for 0% -> 0% of each run, Pallas kernels for 0% -> 0%
where the time goes in v1:
time: 327 us
  waiting for transfers between devices  144 us (44%)
  blocking collectives  137 us (42%)
  matrix products  27.6 us (8%)
  between operations  13.4 us (4%)
  local copies, waits for them, and re-layouts  4.59 us (1%)
    unnamed x3, waiting for transfers between devices  144 us
    all_gather x1, blocking collectives, body(): ids = lax.all_gather(expert_ids, AXES, axis=0, tiled=True)  71 us
    all_gather x1, blocking collectives, body(): weights = lax.all_gather(gate_weights, AXES, axis=0, tiled=True)  66.2 us
    dot_general x1, matrix products, body(): jnp.einsum('jrf,jfd->rd', hidden, w_down, preferred_element_type=jnp.floa...  20.3 us
    dot_general x1, matrix products, body(): jnp.einsum('rd,jdf->jrf', rows, w_gate, preferred_element_type=jnp.float32)  7.35 us
  transfers between devices with their start and end apart: 2, of which 1 were waited for; matrix products, arithmetic and copies ran while one was open for 0% of the time, Pallas kernels for 0%

profile of v1, /device:TPU:0, one launch (start us, length us, event | category | flops | bytes accessed | tf_op | source)
XLA Modules:
  0.0 326.6 jit_solution(8380860105048672223)
XLA Ops:
  6.5 0.0 all-gather.5.cloned.1.call-start
  6.5 0.7 all-gather.5.cloned.1.call-update
  7.3 0.0 all-reduce.3.cloned.1.call-start
  7.3 71.0 %all-gather.1 = s32[32,4,8]{2,1,0:T(4,128)S(1)} all-gather(s32[1,4,8]{2,1,0:T(4,128)} %bitcast.29), channel_id=1, replica_groups=mesh['sect'=2,'grp'=4,'dev'=4] {'sect','grp','dev'}, dimensions={0}, use_global_device_ids=true | all-gather | bytes 4224 | tf_op jit(solution)/shard_map/all_gather | solution.py:13
  78.3 66.2 %all-gather.2 = f32[32,4,8]{2,1,0:T(4,128)S(1)} all-gather(f32[1,4,8]{2,1,0:T(4,128)} %bitcast.30), channel_id=1, replica_groups=mesh['sect'=2,'grp'=4,'dev'=4] {'sect','grp','dev'}, dimensions={0}, use_global_device_ids=true | all-gather | bytes 4224 | tf_op jit(solution)/shard_map/all_gather | solution.py:14
  144.6 0.1 select_reduce_fusion
  144.7 0.0 all-gather.5.cloned.1.call-done
  144.7 2.9 reshape.13
  147.7 7.4 %convolution_bitcast_fusion.2 = f32[2,128,512]{1,2,0:T(8,128)S(1)} fusion(bf16[2,7168,512]{2,1,0:T(8,128)(2,1)} %param.9, bf16[128,7168,1]{1,0,2:T(8,128)(2,1)S(1)} %reshape.13), kind=kOutput, calls=%fused_computation.5 | convolution fusion | flops 1879048192 | bytes 17039360 | tf_op jit(solution)/shard_map/rd,jdf->jrf/dot_general | solution.py:19
  155.1 20.3 %fusion = bf16[128,7168]{1,0:T(8,128)(2,1)} fusion(bf16[2,512,7168]{2,1,0:T(8,128)(2,1)} %param.11, bf16[2,7168,512]{2,1,0:T(8,128)(2,1)} %param.10, bf16[128,7168,1]{1,0,2:T(8,128)(2,1)S(1)} %reshape.13, f32[2,128,512]{1,2,0:T(8,128)S(1)} %convolution_bitcast_fusion.2, f32[2,128]{1,0:T(2,128)S(1)} %select_reduce_fusion), kind=kOutput, calls=%fused_computation.1 | convolution fusion | flops 3759931392 | bytes 33555456 | tf_op jit(solution)/shard_map/jrf,jfd->rd/dot_general | solution.py:22
  175.3 0.0 all-reduce.3.cloned.1.call-update
  175.4 142.8 %all-reduce.3.cloned.1.call-done = bf16[128,7168]{1,0:T(8,128)(2,1)} async-done(((bf16[128,7168]{1,0:T(8,128)(2,1)}), bf16[128,7168]{1,0:T(8,128)(2,1)}) %all-reduce.3.cloned.1.call-update) | async-done | bytes 1835024
  318.2 1.6 constant_dynamic-slice_fusion
  (3 shorter events, 0.1 us)
Async XLA Ops:
  6.5 138.2 %all-gather.5.cloned.1.call-start = ((), (), s32[]{:S(2)}) async-start(), calls=%async_computation | async-start | bytes 1892352 | tf_op jit(solution)/shard_map/all_gather | solution.py:12
  7.3 310.9 %all-reduce.3.cloned.1.call-start = ((), (), s32[]{:S(2)}) async-start(), calls=%async_computation.1 | async-start | bytes 3670016
Sparse Core Ops, SparseCore 0:
  10.2 58.5 all-gather.4
  175.5 142.6 all-reduce.2

commit v2 on v1

v2 whole, which is shorter than its diff:
```python
import functools

import jax
import jax.numpy as jnp
from jax import lax
from jax.experimental import pallas as pl
from jax.experimental.pallas import tpu as pltpu
from jax.sharding import PartitionSpec as P

AXES = ("sect", "grp", "dev")
CHUNKS = 2


def swap(value, axis, mask):
    return lax.ppermute(value, axis, [(i, i ^ mask) for i in range(lax.axis_size(axis))])


def bits_of(size):
    return [1 << b for b in range(size.bit_length() - 1)]


def split_columns(width):
    half = width // 256 * 128
    return half


def gather_rows(block):
    lanes, groups, sects = (lax.axis_size(a) for a in ("dev", "grp", "sect"))
    line = jnp.concatenate([block] + [swap(block, "dev", m) for m in range(1, lanes)], axis=0)
    half = split_columns(block.shape[1])
    if groups == 4:
        by_x, by_y = swap(line, "grp", 1), swap(line, "grp", 2)
        corner = [swap(by_x[:, :half], "grp", 2), swap(by_y[:, half:], "grp", 1)]
        entries = [[line], [by_x], [by_y], corner]
    else:
        entries = [[line]]
        for bit in bits_of(groups):
            entries = entries + [[swap(p, "grp", bit) for p in e] for e in entries]
    for bit in bits_of(sects):
        entries = entries + [[swap(p, "sect", bit) for p in e] for e in entries]
    return entries


def up_kernel(layout, width, first_ref, *refs):
    pieces = refs[: sum(layout)]
    gate_ref, upw_ref, hidden_ref, rows_ref, acc_ref = refs[sum(layout):]
    step = pl.program_id(0)
    experts, depth, hidden = gate_ref.shape
    line = pieces[0].shape[0]

    @pl.when(step == 0)
    def _():
        at = 0
        for entry, count in enumerate(layout):
            left = 0
            for piece in pieces[at:at + count]:
                rows_ref[pl.ds(entry * line, line), pl.ds(left, piece.shape[1])] = piece[...]
                left += piece.shape[1]
            at += count
        acc_ref[...] = jnp.zeros_like(acc_ref)

    here = rows_ref[:, pl.ds(pl.multiple_of(step * depth, 128), depth)]
    for e in range(experts):
        acc_ref[2 * e] += jnp.dot(here, gate_ref[e], preferred_element_type=jnp.float32)
        acc_ref[2 * e + 1] += jnp.dot(here, upw_ref[e], preferred_element_type=jnp.float32)

    @pl.when(step == pl.num_programs(0) - 1)
    def _():
        extra = rows_ref[:, width:].astype(jnp.float32)
        lane = lax.broadcasted_iota(jnp.int32, extra.shape, 1)
        for e in range(experts):
            mine = lax.rem(lane, extra.shape[1] // 2) == first_ref[0] + e
            scale = jnp.sum(jnp.where(mine, extra, 0.0), axis=1, keepdims=True)
            gate = acc_ref[2 * e]
            value = gate / (1.0 + jnp.exp(-gate)) * acc_ref[2 * e + 1] * scale
            hidden_ref[:, pl.ds(e * hidden, hidden)] = value.astype(jnp.bfloat16)


def up_call(first, entries, w_gate, w_up):
    layout = [len(e) for e in entries]
    flat = [p for e in entries for p in e]
    experts, width, hidden = w_gate.shape
    line = flat[0].shape[0]
    full = sum(p.shape[1] for p in entries[0])
    rows = line * len(entries)
    depth = 1024 if width % 1024 == 0 else 128
    weight = pl.BlockSpec((experts, depth, hidden), lambda i: (0, i, 0))
    return pl.pallas_call(
        functools.partial(up_kernel, layout, width),
        out_shape=jax.ShapeDtypeStruct((rows, experts * hidden), jnp.bfloat16),
        grid=(width // depth,),
        in_specs=[pl.BlockSpec(memory_space=pltpu.SMEM)]
        + [pl.BlockSpec(p.shape, lambda i: (0, 0)) for p in flat]
        + [weight, weight],
        out_specs=pl.BlockSpec((rows, experts * hidden), lambda i: (0, 0)),
        scratch_shapes=[
            pltpu.VMEM((rows, full), jnp.bfloat16),
            pltpu.VMEM((2 * experts, rows, hidden), jnp.float32),
        ],
        compiler_params=pltpu.CompilerParams(vmem_limit_bytes=48 * 2**20),
        cost_estimate=pl.CostEstimate(
            flops=4 * rows * experts * width * hidden,
            bytes_accessed=4 * experts * width * hidden,
            transcendentals=0,
        ),
        name="gate_up",
    )(first, *flat, w_gate, w_up)


def down_kernel(order, line, hidden_ref, down_ref, keep_ref, send_ref):
    experts, hidden, _ = down_ref.shape
    total = None
    for e in range(experts):
        part = jnp.dot(
            hidden_ref[:, pl.ds(e * hidden, hidden)], down_ref[e],
            preferred_element_type=jnp.float32,
        )
        total = part if total is None else total + part
    total = total.astype(jnp.bfloat16)
    groups = len(order)
    for place, entry in enumerate(order):
        keep_ref[pl.ds(place * line, line), :] = total[entry * line:(entry + 1) * line]
        low = (groups + entry) * line
        send_ref[pl.ds(place * line, line), :] = total[low:low + line]


def down_call(order, line, hidden, w_down, start, columns):
    experts, depth, _ = w_down.shape
    rows = line * len(order)
    block = 896 if columns % 896 == 0 else 128
    offset = start // block
    out = jax.ShapeDtypeStruct((rows, columns), jnp.bfloat16)
    out_block = pl.BlockSpec((rows, block), lambda i: (0, i))
    return pl.pallas_call(
        functools.partial(down_kernel, order, line),
        out_shape=(out, out),
        grid=(columns // block,),
        in_specs=[
            pl.BlockSpec(hidden.shape, lambda i: (0, 0)),
            pl.BlockSpec((experts, depth, block), lambda i: (0, 0, offset + i)),
        ],
        out_specs=(out_block, out_block),
        compiler_params=pltpu.CompilerParams(vmem_limit_bytes=32 * 2**20),
        cost_estimate=pl.CostEstimate(
            flops=2 * hidden.shape[0] * experts * depth * columns,
            bytes_accessed=2 * experts * depth * columns,
            transcendentals=0,
        ),
        name="down",
    )(hidden, w_down)


def add(*values):
    total = values[0].astype(jnp.float32)
    for value in values[1:]:
        total = total + value.astype(jnp.float32)
    return total.astype(jnp.bfloat16)


def body(tokens, expert_ids, gate_weights, w_gate, w_up, w_down):
    sects, groups, lanes = (lax.axis_size(a) for a in AXES)
    row_count, width = tokens.shape
    experts = w_gate.shape[0]
    expert_count = sects * groups * experts
    first = lax.axis_index(("sect", "grp")).astype(jnp.int32) * experts

    half = -(-expert_count // 64) * 64
    catalog = jnp.arange(half, dtype=jnp.int32)
    dense = jnp.sum(
        jnp.where(expert_ids[:, :, None] == catalog, gate_weights[:, :, None], 0.0), axis=1
    )
    high = lax.reduce_precision(dense, 8, 7)
    extra = jnp.concatenate([high, dense - high], axis=1).astype(jnp.bfloat16)
    entries = gather_rows(jnp.concatenate([tokens, extra], axis=1))

    hidden = up_call(first.reshape(1), entries, w_gate, w_up)

    line = lanes * row_count
    results = []
    chunk = width // CHUNKS
    for c in range(CHUNKS):
        bits = bits_of(groups)
        bits = bits if c % 2 else bits[::-1]
        order = [0]
        for bit in bits:
            order = order + [o | bit for o in order]
        keep, send = down_call(order, line, hidden, w_down, c * chunk, chunk)
        value = add(keep, swap(send, "sect", 1))
        for bit in bits[::-1]:
            middle = value.shape[0] // 2
            arrived = swap(value[middle:], "grp", bit)
            value = add(value[:middle], arrived)
        pieces = [value[:row_count]]
        for m in range(1, lanes):
            pieces.append(swap(value[m * row_count:(m + 1) * row_count], "dev", m))
        results.append(add(*pieces))
    return jnp.concatenate(results, axis=1)


def solution(mesh):
    in_specs = (
        P(AXES, None),
        P(AXES, None),
        P(AXES, None),
        P(("sect", "grp"), None, "dev"),
        P(("sect", "grp"), None, "dev"),
        P(("sect", "grp"), "dev", None),
    )
    return jax.shard_map(
        body, mesh=mesh, in_specs=in_specs, out_specs=P(AXES, None), check_vma=False
    )
```

time: 327 us -> 78.2 us (0.24)
  blocking collectives: 137 us -> 0 us
  waiting for transfers between devices: 144 us -> 25.8 us
  matrix products: 27.6 us -> 0 us
  starting transfers between devices: 0.04 us -> 26 us
  Pallas kernels: 0 us -> 17.8 us
  between operations: 13.4 us -> 0.16 us
    unnamed x3 -> x0, waiting for transfers between devices: 144 us -> none
    all_gather x2 -> x0, blocking collectives: 137 us -> none  [the longest x1 71 us: body(): ids = lax.all_gather(expert_ids, AXES, axis=0, tiled=True)]
    dot_general x2 -> x0, matrix products: 27.6 us -> none  [the longest x1 20.3 us: body(): jnp.einsum('jrf,jfd->rd', hidden, w_down, preferred_element_type=jnp.floa...]
    ppermute x0 -> x24, starting transfers between devices: none -> 26 us  [swap(): lax.ppermute(value, axis, [(i, i ^ mask) for i in range(lax.axis_size(axi...]
    ppermute x0 -> x24, waiting for transfers between devices: none -> 25.8 us  [swap(): lax.ppermute(value, axis, [(i, i ^ mask) for i in range(lax.axis_size(axi...]
    pallas_call x0 -> x3, Pallas kernels: none -> 17.8 us  [the longest x1 12.6 us: up_call(): pl.pallas_call(functools.partial(up_kernel, layout, width), out_shape=jax...]
  transfers between devices with their start and end apart: 2 -> 24, of which waited for: 1 -> 12; matrix products, arithmetic and copies ran while one was open for 0% -> 1% of each run, Pallas kernels for 0% -> 3%
where the time goes in v2:
time: 78.2 us; the launch traced here: 78 us
  starting transfers between devices  26 us (33%)
  waiting for transfers between devices  25.8 us (33%)
  Pallas kernels  17.8 us (23%)
  local copies, waits for them, and re-layouts  6.25 us (8%)
  other arithmetic  2.04 us (3%)
    ppermute x24, starting transfers between devices, swap(): lax.ppermute(value, axis, [(i, i ^ mask) for i in range(lax.axis_size(axi...  26 us
    ppermute x24, waiting for transfers between devices, swap(): lax.ppermute(value, axis, [(i, i ^ mask) for i in range(lax.axis_size(axi...  25.8 us
    pallas_call x1, Pallas kernels, up_call(): pl.pallas_call(functools.partial(up_kernel, layout, width), out_shape=jax...  12.6 us
    pallas_call x2, Pallas kernels, down_call(): pl.pallas_call(functools.partial(down_kernel, order, line), out_shape=(ou...  5.19 us
    unnamed x2, local copies, waits for them, and re-layouts  5.17 us
  transfers between devices with their start and end apart: 24, of which 12 were waited for; matrix products, arithmetic and copies ran while one was open for 1% of the time, Pallas kernels for 3%

profile of v2, /device:TPU:0, one launch (start us, length us, event | category | flops | bytes accessed | tf_op | source)
XLA Modules:
  0.0 78.0 jit_solution(10888977379873408816)
XLA Ops:
  0.0 0.8 %select_reduce_fusion = f32[4,64]{1,0:T(4,128)S(1)} fusion(f32[4,8]{1,0:T(4,128)} %param.8, s32[4,8]{1,0:T(4,128)} %param.7), kind=kLoop, calls=%fused_computation.10 | loop fusion | flops 5888 | bytes 1280 | tf_op jit(solution)/shard_map/reduce_sum | solution.py:169
  0.8 0.9 %concatenate.12 = bf16[4,7296]{1,0:T(4,128)(2,1)S(1)} concatenate(bf16[4,7168]{1,0:T(4,128)(2,1)} %param.6, bf16[4,64]{1,0:T(4,128)(2,1)S(1)} %get-tuple-element.20, bf16[4,64]{1,0:T(4,128)(2,1)S(1)} %get-tuple-element.19), dimensions={1} | concatenate | bytes 116736 | tf_op jit(solution)/shard_map/concatenate | solution.py:174
  1.7 5.1 %collective-permute-start.2 = (bf16[4,7296]{1,0:T(4,128)(2,1)S(1)}, bf16[4,7296]{1,0:T(4,128)(2,1)S(1)}, u32[]{:S(2)}, u32[]{:S(2)}) collective-permute-start(bf16[4,7296]{1,0:T(4,128)(2,1)S(1)} %concatenate.12), channel_id=1, source_target_pairs={{0,3},{1,2},{2,1},{3,0},{4,7},{5,6},{6,5},{7,4},{8,11},{9,10},{10,... | collective-permute-start | bytes 175112 | tf_op jit(solution)/shard_map/ppermute | solution.py:15
  6.8 0.0 collective-permute-start.1
  6.8 0.6 collective-permute-start
  7.4 1.8 %collective-permute-done.2 = bf16[4,7296]{1,0:T(4,128)(2,1)S(1)} collective-permute-done((bf16[4,7296]{1,0:T(4,128)(2,1)S(1)}, bf16[4,7296]{1,0:T(4,128)(2,1)S(1)}, u32[]{:S(2)}, u32[]{:S(2)}) %collective-permute-start.2) | collective-permute-done | bytes 58400 | tf_op jit(solution)/shard_map/ppermute | solution.py:15
  9.2 2.7 %collective-permute-done.1 = bf16[4,7296]{1,0:T(4,128)(2,1)S(1)} collective-permute-done((bf16[4,7296]{1,0:T(4,128)(2,1)S(1)}, bf16[4,7296]{1,0:T(4,128)(2,1)S(1)}, u32[]{:S(2)}, u32[]{:S(2)}) %collective-permute-start.1) | collective-permute-done | bytes 58400 | tf_op jit(solution)/shard_map/ppermute | solution.py:15
  11.9 0.0 collective-permute-done
  11.9 0.1 pad_maximum_fusion.refs_0_
  12.0 1.7 %collective-permute-start.4 = (bf16[16,7296]{1,0:T(8,128)(2,1)S(1)}, bf16[16,7296]{1,0:T(8,128)(2,1)S(1)}, u32[]{:S(2)}, u32[]{:S(2)}) collective-permute-start(bf16[16,7296]{1,0:T(8,128)(2,1)S(1)} %pad_maximum_fusion.refs_0_), channel_id=1, source_target_pairs={{0,8},{4,12},{8,0},{12,4},{1,9},{5,13},{9,1},{13,5},{2,10},{6,14},... | collective-permute-start | bytes 700424 | tf_op jit(solution)/shard_map/ppermute | solution.py:15
  13.7 1.5 %collective-permute-start.3 = (bf16[16,7296]{1,0:T(8,128)(2,1)S(1)}, bf16[16,7296]{1,0:T(8,128)(2,1)S(1)}, u32[]{:S(2)}, u32[]{:S(2)}) collective-permute-start(bf16[16,7296]{1,0:T(8,128)(2,1)S(1)} %pad_maximum_fusion.refs_0_), channel_id=1, source_target_pairs={{0,4},{4,0},{8,12},{12,8},{1,5},{5,1},{9,13},{13,9},{2,6},{6,2},{1... | collective-permute-start | bytes 700424 | tf_op jit(solution)/shard_map/ppermute | solution.py:15
  15.2 3.7 %collective-permute-done.4.refs_2_ = bf16[16,7296]{1,0:T(8,128)(2,1)S(1)} collective-permute-done((bf16[16,7296]{1,0:T(8,128)(2,1)S(1)}, bf16[16,7296]{1,0:T(8,128)(2,1)S(1)}, u32[]{:S(2)}, u32[]{:S(2)}) %collective-permute-start.4) | collective-permute-done | bytes 233504 | tf_op jit(solution)/shard_map/ppermute | solution.py:15
  18.9 1.6 %collective-permute-start.6 = (bf16[16,3712]{1,0:T(8,128)(2,1)S(1)}, bf16[16,3712]{1,0:T(8,128)(2,1)S(1)}, u32[]{:S(2)}, u32[]{:S(2)}) collective-permute-start(bf16[16,3712]{1,0:T(8,128)(2,1)S(1)} %slice.73), channel_id=1, source_target_pairs={{0,4},{4,0},{8,12},{12,8},{1,5},{5,1},{9,13},{13,9},{2,6},{6,2},{1... | collective-permute-start | bytes 356360 | tf_op jit(solution)/shard_map/ppermute | solution.py:15
  20.5 0.0 collective-permute-start.7
  20.5 0.5 collective-permute-start.9
  21.1 0.0 collective-permute-done.3.refs_1_
  21.1 0.0 collective-permute-start.8
  21.1 1.6 %collective-permute-start.5 = (bf16[16,3584]{1,0:T(8,128)(2,1)S(1)}, bf16[16,3584]{1,0:T(8,128)(2,1)S(1)}, u32[]{:S(2)}, u32[]{:S(2)}) collective-permute-start(bf16[16,3584]{1,0:T(8,128)(2,1)S(1)} %slice.72), channel_id=1, source_target_pairs={{0,8},{4,12},{8,0},{12,4},{1,9},{5,13},{9,1},{13,5},{2,10},{6,14},... | collective-permute-start | bytes 344072 | tf_op jit(solution)/shard_map/ppermute | solution.py:15
  22.7 1.1 %collective-permute-done.6.refs_4_ = bf16[16,3712]{1,0:T(8,128)(2,1)S(1)} collective-permute-done((bf16[16,3712]{1,0:T(8,128)(2,1)S(1)}, bf16[16,3712]{1,0:T(8,128)(2,1)S(1)}, u32[]{:S(2)}, u32[]{:S(2)}) %collective-permute-start.6) | collective-permute-done | bytes 118816 | tf_op jit(solution)/shard_map/ppermute | solution.py:15
  23.8 0.0 collective-permute-start.11
  23.8 2.9 %collective-permute-done.5.refs_3_ = bf16[16,3584]{1,0:T(8,128)(2,1)S(1)} collective-permute-done((bf16[16,3584]{1,0:T(8,128)(2,1)S(1)}, bf16[16,3584]{1,0:T(8,128)(2,1)S(1)}, u32[]{:S(2)}, u32[]{:S(2)}) %collective-permute-start.5) | collective-permute-done | bytes 114720 | tf_op jit(solution)/shard_map/ppermute | solution.py:15
  26.7 0.0 collective-permute-start.10
  26.7 0.0 collective-permute-done.7.refs_5_
  26.7 1.3 %collective-permute-done.10.refs_8_ = bf16[16,3584]{1,0:T(8,128)(2,1)S(1)} collective-permute-done((bf16[16,3584]{1,0:T(8,128)(2,1)S(1)}, bf16[16,3584]{1,0:T(8,128)(2,1)S(1)}, u32[]{:S(2)}, u32[]{:S(2)}) %collective-permute-start.10) | collective-permute-done | bytes 114720 | tf_op jit(solution)/shard_map/ppermute | solution.py:15
  28.0 0.0 collective-permute-done.9.refs_7_
  28.0 0.0 collective-permute-done.8.refs_6_
  28.0 0.0 collective-permute-done.11.refs_9_
  28.0 12.6 %gate_up.1.hidden_ref = bf16[128,1024]{1,0:T(8,128)(2,1)S(1)} custom-call(s32[1]{0:T(128)} %bitcast.first_ref, bf16[16,7296]{1,0:T(8,128)(2,1)S(1)} %pad_maximum_fusion.refs_0_, bf16[16,7296]{1,0:T(8,128)(2,1)S(1)} %collective-permute-done.3.refs_1_, bf16[16,7296]{1,0:T(8,128)(2,1)S(1)} %collective-permute-done.4.refs_2_, ...), custom_call_target="tpu_custom_call" | custom-call | flops 3758096384 | bytes 29360128 | tf_op jit(solution)/shard_map/gate_up/pallas_call | solution.py:88
  40.6 0.0 copy-start
  40.6 5.2 %copy-done = bf16[2,512,7168]{2,1,0:T(8,128)(2,1)S(1)} copy-done((bf16[2,512,7168]{2,1,0:T(8,128)(2,1)S(1)}, bf16[2,512,7168]{2,1,0:T(8,128)(2,1)}, u32[]{:S(2)}) %copy-start) | copy-done | bytes 14680088
  45.8 2.6 %down.3 = (bf16[64,3584]{1,0:T(8,128)(2,1)S(1)}, bf16[64,3584]{1,0:T(8,128)(2,1)S(1)}) custom-call(bf16[128,1024]{1,0:T(8,128)(2,1)S(1)} %gate_up.1.hidden_ref, bf16[2,512,7168]{2,1,0:T(8,128)(2,1)S(1)} %copy-done), custom_call_target="tpu_custom_call" | custom-call | flops 939524096 | bytes 7340032 | tf_op jit(solution)/shard_map/down/pallas_call | solution.py:134
  48.4 0.2 collective-permute-start.18
  48.6 2.6 %down.2 = (bf16[64,3584]{1,0:T(8,128)(2,1)S(1)}, bf16[64,3584]{1,0:T(8,128)(2,1)S(1)}) custom-call(bf16[128,1024]{1,0:T(8,128)(2,1)S(1)} %gate_up.1.hidden_ref, bf16[2,512,7168]{2,1,0:T(8,128)(2,1)S(1)} %copy-done), custom_call_target="tpu_custom_call" | custom-call | flops 939524096 | bytes 7340032 | tf_op jit(solution)/shard_map/down/pallas_call | solution.py:134
  51.2 0.4 collective-permute-start.12
  51.6 0.0 collective-permute-done.18
  51.6 0.1 add_convert_fusion
  51.8 1.6 %collective-permute-start.19 = (bf16[32,3584]{1,0:T(8,128)(2,1)S(1)}, bf16[32,3584]{1,0:T(8,128)(2,1)S(1)}, u32[]{:S(2)}, u32[]{:S(2)}) collective-permute-start(bf16[32,3584]{1,0:T(8,128)(2,1)S(1)} %slice.83), channel_id=1, source_target_pairs={{0,8},{4,12},{8,0},{12,4},{1,9},{5,13},{9,1},{13,5},{2,10},{6,14},... | collective-permute-start | bytes 688136 | tf_op jit(solution)/shard_map/ppermute | solution.py:15
  53.3 0.0 collective-permute-done.12
  53.4 0.1 add_convert_fusion.1
  53.5 0.7 collective-permute-start.13
  54.2 5.3 %collective-permute-done.19 = bf16[32,3584]{1,0:T(8,128)(2,1)S(1)} collective-permute-done((bf16[32,3584]{1,0:T(8,128)(2,1)S(1)}, bf16[32,3584]{1,0:T(8,128)(2,1)S(1)}, u32[]{:S(2)}, u32[]{:S(2)}) %collective-permute-start.19) | collective-permute-done | bytes 229408 | tf_op jit(solution)/shard_map/ppermute | solution.py:15
  59.5 0.1 add_convert_fusion.2
  59.6 0.9 %collective-permute-start.20 = (bf16[16,3584]{1,0:T(8,128)(2,1)S(1)}, bf16[16,3584]{1,0:T(8,128)(2,1)S(1)}, u32[]{:S(2)}, u32[]{:S(2)}) collective-permute-start(bf16[16,3584]{1,0:T(8,128)(2,1)S(1)} %slice.85), channel_id=1, source_target_pairs={{0,4},{4,0},{8,12},{12,8},{1,5},{5,1},{9,13},{13,9},{2,6},{6,2},{1... | collective-permute-start | bytes 344072 | tf_op jit(solution)/shard_map/ppermute | solution.py:15
  60.5 0.6 collective-permute-done.13
  61.2 0.1 add_convert_fusion.3
  61.2 1.6 %collective-permute-start.14 = (bf16[16,3584]{1,0:T(8,128)(2,1)S(1)}, bf16[16,3584]{1,0:T(8,128)(2,1)S(1)}, u32[]{:S(2)}, u32[]{:S(2)}) collective-permute-start(bf16[16,3584]{1,0:T(8,128)(2,1)S(1)} %slice.77), channel_id=1, source_target_pairs={{0,8},{4,12},{8,0},{12,4},{1,9},{5,13},{9,1},{13,5},{2,10},{6,14},... | collective-permute-start | bytes 344072 | tf_op jit(solution)/shard_map/ppermute | solution.py:15
  62.8 1.6 %collective-permute-done.20 = bf16[16,3584]{1,0:T(8,128)(2,1)S(1)} collective-permute-done((bf16[16,3584]{1,0:T(8,128)(2,1)S(1)}, bf16[16,3584]{1,0:T(8,128)(2,1)S(1)}, u32[]{:S(2)}, u32[]{:S(2)}) %collective-permute-start.20) | collective-permute-done | bytes 114720 | tf_op jit(solution)/shard_map/ppermute | solution.py:15
  64.5 0.6 collective-permute-start.21
  65.1 2.8 %collective-permute-start.23 = (bf16[4,3584]{1,0:T(4,128)(2,1)S(1)}, bf16[4,3584]{1,0:T(4,128)(2,1)S(1)}, u32[]{:S(2)}, u32[]{:S(2)}) collective-permute-start(bf16[4,3584]{1,0:T(4,128)(2,1)S(1)} %get-tuple-element.17), channel_id=1, source_target_pairs={{0,3},{1,2},{2,1},{3,0},{4,7},{5,6},{6,5},{7,4},{8,11},{9,10},{10,... | collective-permute-start | bytes 86024 | tf_op jit(solution)/shard_map/ppermute | solution.py:15
  68.0 0.1 collective-permute-start.22
  68.1 0.0 collective-permute-done.14
  68.2 1.5 %collective-permute-start.15 = (bf16[4,3584]{1,0:T(4,128)(2,1)S(1)}, bf16[4,3584]{1,0:T(4,128)(2,1)S(1)}, u32[]{:S(2)}, u32[]{:S(2)}) collective-permute-start(bf16[4,3584]{1,0:T(4,128)(2,1)S(1)} %get-tuple-element.13), channel_id=1, source_target_pairs={{0,1},{1,0},{2,3},{3,2},{4,5},{5,4},{6,7},{7,6},{8,9},{9,8},{10,11... | collective-permute-start | bytes 86024 | tf_op jit(solution)/shard_map/ppermute | solution.py:15
  69.7 2.8 %collective-permute-start.17 = (bf16[4,3584]{1,0:T(4,128)(2,1)S(1)}, bf16[4,3584]{1,0:T(4,128)(2,1)S(1)}, u32[]{:S(2)}, u32[]{:S(2)}) collective-permute-start(bf16[4,3584]{1,0:T(4,128)(2,1)S(1)} %get-tuple-element.14), channel_id=1, source_target_pairs={{0,3},{1,2},{2,1},{3,0},{4,7},{5,6},{6,5},{7,4},{8,11},{9,10},{10,... | collective-permute-start | bytes 86024 | tf_op jit(solution)/shard_map/ppermute | solution.py:15
  72.5 0.0 collective-permute-done.21
  72.5 0.0 collective-permute-start.16
  72.5 0.0 collective-permute-done.23
  72.5 0.2 collective-permute-done.22
  72.8 0.0 collective-permute-done.15
  72.8 2.5 %collective-permute-done.17 = bf16[4,3584]{1,0:T(4,128)(2,1)S(1)} collective-permute-done((bf16[4,3584]{1,0:T(4,128)(2,1)S(1)}, bf16[4,3584]{1,0:T(4,128)(2,1)S(1)}, u32[]{:S(2)}, u32[]{:S(2)}) %collective-permute-start.17) | collective-permute-done | bytes 28704 | tf_op jit(solution)/shard_map/ppermute | solution.py:15
  75.3 1.9 %collective-permute-done.16 = bf16[4,3584]{1,0:T(4,128)(2,1)S(1)} collective-permute-done((bf16[4,3584]{1,0:T(4,128)(2,1)S(1)}, bf16[4,3584]{1,0:T(4,128)(2,1)S(1)}, u32[]{:S(2)}, u32[]{:S(2)}) %collective-permute-start.16) | collective-permute-done | bytes 28704 | tf_op jit(solution)/shard_map/ppermute | solution.py:15
  77.3 0.7 pad_maximum_fusion.1
  (13 shorter events, 0.3 us)
Async XLA Ops:
  1.7 7.5 %collective-permute-start.2 = (bf16[4,7296]{1,0:T(4,128)(2,1)S(1)}, bf16[4,7296]{1,0:T(4,128)(2,1)S(1)}, u32[]{:S(2)}, u32[]{:S(2)}) collective-permute-start(bf16[4,7296]{1,0:T(4,128)(2,1)S(1)} %concatenate.12), channel_id=1, source_target_pairs={{0,3},{1,2},{2,1},{3,0},{4,7},{5,6},{6,5},{7,4},{8,11},{9,10},{10,... | collective-permute-start | bytes 175112 | tf_op jit(solution)/shard_map/ppermute | solution.py:15
  6.8 5.1 %collective-permute-start.1 = (bf16[4,7296]{1,0:T(4,128)(2,1)S(1)}, bf16[4,7296]{1,0:T(4,128)(2,1)S(1)}, u32[]{:S(2)}, u32[]{:S(2)}) collective-permute-start(bf16[4,7296]{1,0:T(4,128)(2,1)S(1)} %concatenate.12), channel_id=1, source_target_pairs={{0,2},{1,3},{2,0},{3,1},{4,6},{5,7},{6,4},{7,5},{8,10},{9,11},{10,... | collective-permute-start | bytes 175112 | tf_op jit(solution)/shard_map/ppermute | solution.py:15
  6.8 5.1 %collective-permute-start = (bf16[4,7296]{1,0:T(4,128)(2,1)S(1)}, bf16[4,7296]{1,0:T(4,128)(2,1)S(1)}, u32[]{:S(2)}, u32[]{:S(2)}) collective-permute-start(bf16[4,7296]{1,0:T(4,128)(2,1)S(1)} %concatenate.12), channel_id=1, source_target_pairs={{0,1},{1,0},{2,3},{3,2},{4,5},{5,4},{6,7},{7,6},{8,9},{9,8},{10,11... | collective-permute-start | bytes 175112 | tf_op jit(solution)/shard_map/ppermute | solution.py:15
  12.0 6.8 %collective-permute-start.4 = (bf16[16,7296]{1,0:T(8,128)(2,1)S(1)}, bf16[16,7296]{1,0:T(8,128)(2,1)S(1)}, u32[]{:S(2)}, u32[]{:S(2)}) collective-permute-start(bf16[16,7296]{1,0:T(8,128)(2,1)S(1)} %pad_maximum_fusion.refs_0_), channel_id=1, source_target_pairs={{0,8},{4,12},{8,0},{12,4},{1,9},{5,13},{9,1},{13,5},{2,10},{6,14},... | collective-permute-start | bytes 700424 | tf_op jit(solution)/shard_map/ppermute | solution.py:15
  13.7 7.3 %collective-permute-start.3 = (bf16[16,7296]{1,0:T(8,128)(2,1)S(1)}, bf16[16,7296]{1,0:T(8,128)(2,1)S(1)}, u32[]{:S(2)}, u32[]{:S(2)}) collective-permute-start(bf16[16,7296]{1,0:T(8,128)(2,1)S(1)} %pad_maximum_fusion.refs_0_), channel_id=1, source_target_pairs={{0,4},{4,0},{8,12},{12,8},{1,5},{5,1},{9,13},{13,9},{2,6},{6,2},{1... | collective-permute-start | bytes 700424 | tf_op jit(solution)/shard_map/ppermute | solution.py:15
  18.9 4.9 %collective-permute-start.6 = (bf16[16,3712]{1,0:T(8,128)(2,1)S(1)}, bf16[16,3712]{1,0:T(8,128)(2,1)S(1)}, u32[]{:S(2)}, u32[]{:S(2)}) collective-permute-start(bf16[16,3712]{1,0:T(8,128)(2,1)S(1)} %slice.73), channel_id=1, source_target_pairs={{0,4},{4,0},{8,12},{12,8},{1,5},{5,1},{9,13},{13,9},{2,6},{6,2},{1... | collective-permute-start | bytes 356360 | tf_op jit(solution)/shard_map/ppermute | solution.py:15
  20.5 6.2 %collective-permute-start.7 = (bf16[16,7296]{1,0:T(8,128)(2,1)S(1)}, bf16[16,7296]{1,0:T(8,128)(2,1)S(1)}, u32[]{:S(2)}, u32[]{:S(2)}) collective-permute-start(bf16[16,7296]{1,0:T(8,128)(2,1)S(1)} %pad_maximum_fusion.refs_0_), channel_id=1, source_target_pairs={{0,16},{16,0},{1,17},{17,1},{2,18},{18,2},{3,19},{19,3},{4,20},{20... | collective-permute-start | bytes 700424 | tf_op jit(solution)/shard_map/ppermute | solution.py:15
  20.5 7.5 %collective-permute-start.9 = (bf16[16,7296]{1,0:T(8,128)(2,1)S(1)}, bf16[16,7296]{1,0:T(8,128)(2,1)S(1)}, u32[]{:S(2)}, u32[]{:S(2)}) collective-permute-start(bf16[16,7296]{1,0:T(8,128)(2,1)S(1)} %collective-permute-done.4.refs_2_), channel_id=1, source_target_pairs={{0,16},{16,0},{1,17},{17,1},{2,18},{18,2},{3,19},{19,3},{4,20},{20... | collective-permute-start | bytes 700424 | tf_op jit(solution)/shard_map/ppermute | solution.py:15
  21.1 7.0 %collective-permute-start.8 = (bf16[16,7296]{1,0:T(8,128)(2,1)S(1)}, bf16[16,7296]{1,0:T(8,128)(2,1)S(1)}, u32[]{:S(2)}, u32[]{:S(2)}) collective-permute-start(bf16[16,7296]{1,0:T(8,128)(2,1)S(1)} %collective-permute-done.3.refs_1_), channel_id=1, source_target_pairs={{0,16},{16,0},{1,17},{17,1},{2,18},{18,2},{3,19},{19,3},{4,20},{20... | collective-permute-start | bytes 700424 | tf_op jit(solution)/shard_map/ppermute | solution.py:15
  21.1 5.6 %collective-permute-start.5 = (bf16[16,3584]{1,0:T(8,128)(2,1)S(1)}, bf16[16,3584]{1,0:T(8,128)(2,1)S(1)}, u32[]{:S(2)}, u32[]{:S(2)}) collective-permute-start(bf16[16,3584]{1,0:T(8,128)(2,1)S(1)} %slice.72), channel_id=1, source_target_pairs={{0,8},{4,12},{8,0},{12,4},{1,9},{5,13},{9,1},{13,5},{2,10},{6,14},... | collective-permute-start | bytes 344072 | tf_op jit(solution)/shard_map/ppermute | solution.py:15
  23.8 4.2 %collective-permute-start.11 = (bf16[16,3712]{1,0:T(8,128)(2,1)S(1)}, bf16[16,3712]{1,0:T(8,128)(2,1)S(1)}, u32[]{:S(2)}, u32[]{:S(2)}) collective-permute-start(bf16[16,3712]{1,0:T(8,128)(2,1)S(1)} %collective-permute-done.6.refs_4_), channel_id=1, source_target_pairs={{0,16},{16,0},{1,17},{17,1},{2,18},{18,2},{3,19},{19,3},{4,20},{20... | collective-permute-start | bytes 356360 | tf_op jit(solution)/shard_map/ppermute | solution.py:15
  26.7 1.3 %collective-permute-start.10 = (bf16[16,3584]{1,0:T(8,128)(2,1)S(1)}, bf16[16,3584]{1,0:T(8,128)(2,1)S(1)}, u32[]{:S(2)}, u32[]{:S(2)}) collective-permute-start(bf16[16,3584]{1,0:T(8,128)(2,1)S(1)} %collective-permute-done.5.refs_3_), channel_id=1, source_target_pairs={{0,16},{16,0},{1,17},{17,1},{2,18},{18,2},{3,19},{19,3},{4,20},{20... | collective-permute-start | bytes 344072 | tf_op jit(solution)/shard_map/ppermute | solution.py:15
  40.6 5.2 %copy-start = (bf16[2,512,7168]{2,1,0:T(8,128)(2,1)S(1)}, bf16[2,512,7168]{2,1,0:T(8,128)(2,1)}, u32[]{:S(2)}) copy-start(bf16[2,512,7168]{2,1,0:T(8,128)(2,1)} %down_ref.3) | copy-start | bytes 44040196
  48.4 3.2 %collective-permute-start.18 = (bf16[64,3584]{1,0:T(8,128)(2,1)S(1)}, bf16[64,3584]{1,0:T(8,128)(2,1)S(1)}, u32[]{:S(2)}, u32[]{:S(2)}) collective-permute-start(bf16[64,3584]{1,0:T(8,128)(2,1)S(1)} %get-tuple-element.12), channel_id=1, source_target_pairs={{0,16},{16,0},{1,17},{17,1},{2,18},{18,2},{3,19},{19,3},{4,20},{20... | collective-permute-start | bytes 1376264 | tf_op jit(solution)/shard_map/ppermute | solution.py:15
  51.2 2.1 %collective-permute-start.12 = (bf16[64,3584]{1,0:T(8,128)(2,1)S(1)}, bf16[64,3584]{1,0:T(8,128)(2,1)S(1)}, u32[]{:S(2)}, u32[]{:S(2)}) collective-permute-start(bf16[64,3584]{1,0:T(8,128)(2,1)S(1)} %get-tuple-element.10), channel_id=1, source_target_pairs={{0,16},{16,0},{1,17},{17,1},{2,18},{18,2},{3,19},{19,3},{4,20},{20... | collective-permute-start | bytes 1376264 | tf_op jit(solution)/shard_map/ppermute | solution.py:15
  51.8 7.7 %collective-permute-start.19 = (bf16[32,3584]{1,0:T(8,128)(2,1)S(1)}, bf16[32,3584]{1,0:T(8,128)(2,1)S(1)}, u32[]{:S(2)}, u32[]{:S(2)}) collective-permute-start(bf16[32,3584]{1,0:T(8,128)(2,1)S(1)} %slice.83), channel_id=1, source_target_pairs={{0,8},{4,12},{8,0},{12,4},{1,9},{5,13},{9,1},{13,5},{2,10},{6,14},... | collective-permute-start | bytes 688136 | tf_op jit(solution)/shard_map/ppermute | solution.py:15
  53.5 7.7 %collective-permute-start.13 = (bf16[32,3584]{1,0:T(8,128)(2,1)S(1)}, bf16[32,3584]{1,0:T(8,128)(2,1)S(1)}, u32[]{:S(2)}, u32[]{:S(2)}) collective-permute-start(bf16[32,3584]{1,0:T(8,128)(2,1)S(1)} %slice.75), channel_id=1, source_target_pairs={{0,4},{4,0},{8,12},{12,8},{1,5},{5,1},{9,13},{13,9},{2,6},{6,2},{1... | collective-permute-start | bytes 688136 | tf_op jit(solution)/shard_map/ppermute | solution.py:15
  59.6 4.9 %collective-permute-start.20 = (bf16[16,3584]{1,0:T(8,128)(2,1)S(1)}, bf16[16,3584]{1,0:T(8,128)(2,1)S(1)}, u32[]{:S(2)}, u32[]{:S(2)}) collective-permute-start(bf16[16,3584]{1,0:T(8,128)(2,1)S(1)} %slice.85), channel_id=1, source_target_pairs={{0,4},{4,0},{8,12},{12,8},{1,5},{5,1},{9,13},{13,9},{2,6},{6,2},{1... | collective-permute-start | bytes 344072 | tf_op jit(solution)/shard_map/ppermute | solution.py:15
  61.2 6.8 %collective-permute-start.14 = (bf16[16,3584]{1,0:T(8,128)(2,1)S(1)}, bf16[16,3584]{1,0:T(8,128)(2,1)S(1)}, u32[]{:S(2)}, u32[]{:S(2)}) collective-permute-start(bf16[16,3584]{1,0:T(8,128)(2,1)S(1)} %slice.77), channel_id=1, source_target_pairs={{0,8},{4,12},{8,0},{12,4},{1,9},{5,13},{9,1},{13,5},{2,10},{6,14},... | collective-permute-start | bytes 344072 | tf_op jit(solution)/shard_map/ppermute | solution.py:15
  64.5 8.0 %collective-permute-start.21 = (bf16[4,3584]{1,0:T(4,128)(2,1)S(1)}, bf16[4,3584]{1,0:T(4,128)(2,1)S(1)}, u32[]{:S(2)}, u32[]{:S(2)}) collective-permute-start(bf16[4,3584]{1,0:T(4,128)(2,1)S(1)} %get-tuple-element.16), channel_id=1, source_target_pairs={{0,1},{1,0},{2,3},{3,2},{4,5},{5,4},{6,7},{7,6},{8,9},{9,8},{10,11... | collective-permute-start | bytes 86024 | tf_op jit(solution)/shard_map/ppermute | solution.py:15
  65.1 7.4 %collective-permute-start.23 = (bf16[4,3584]{1,0:T(4,128)(2,1)S(1)}, bf16[4,3584]{1,0:T(4,128)(2,1)S(1)}, u32[]{:S(2)}, u32[]{:S(2)}) collective-permute-start(bf16[4,3584]{1,0:T(4,128)(2,1)S(1)} %get-tuple-element.17), channel_id=1, source_target_pairs={{0,3},{1,2},{2,1},{3,0},{4,7},{5,6},{6,5},{7,4},{8,11},{9,10},{10,... | collective-permute-start | bytes 86024 | tf_op jit(solution)/shard_map/ppermute | solution.py:15
  68.0 4.8 %collective-permute-start.22 = (bf16[4,3584]{1,0:T(4,128)(2,1)S(1)}, bf16[4,3584]{1,0:T(4,128)(2,1)S(1)}, u32[]{:S(2)}, u32[]{:S(2)}) collective-permute-start(bf16[4,3584]{1,0:T(4,128)(2,1)S(1)} %get-tuple-element.18), channel_id=1, source_target_pairs={{0,2},{1,3},{2,0},{3,1},{4,6},{5,7},{6,4},{7,5},{8,10},{9,11},{10,... | collective-permute-start | bytes 86024 | tf_op jit(solution)/shard_map/ppermute | solution.py:15
  68.2 4.6 %collective-permute-start.15 = (bf16[4,3584]{1,0:T(4,128)(2,1)S(1)}, bf16[4,3584]{1,0:T(4,128)(2,1)S(1)}, u32[]{:S(2)}, u32[]{:S(2)}) collective-permute-start(bf16[4,3584]{1,0:T(4,128)(2,1)S(1)} %get-tuple-element.13), channel_id=1, source_target_pairs={{0,1},{1,0},{2,3},{3,2},{4,5},{5,4},{6,7},{7,6},{8,9},{9,8},{10,11... | collective-permute-start | bytes 86024 | tf_op jit(solution)/shard_map/ppermute | solution.py:15
  69.7 5.7 %collective-permute-start.17 = (bf16[4,3584]{1,0:T(4,128)(2,1)S(1)}, bf16[4,3584]{1,0:T(4,128)(2,1)S(1)}, u32[]{:S(2)}, u32[]{:S(2)}) collective-permute-start(bf16[4,3584]{1,0:T(4,128)(2,1)S(1)} %get-tuple-element.14), channel_id=1, source_target_pairs={{0,3},{1,2},{2,1},{3,0},{4,7},{5,6},{6,5},{7,4},{8,11},{9,10},{10,... | collective-permute-start | bytes 86024 | tf_op jit(solution)/shard_map/ppermute | solution.py:15
  72.5 4.8 %collective-permute-start.16 = (bf16[4,3584]{1,0:T(4,128)(2,1)S(1)}, bf16[4,3584]{1,0:T(4,128)(2,1)S(1)}, u32[]{:S(2)}, u32[]{:S(2)}) collective-permute-start(bf16[4,3584]{1,0:T(4,128)(2,1)S(1)} %get-tuple-element.15), channel_id=1, source_target_pairs={{0,2},{1,3},{2,0},{3,1},{4,6},{5,7},{6,4},{7,5},{8,10},{9,11},{10,... | collective-permute-start | bytes 86024 | tf_op jit(solution)/shard_map/ppermute | solution.py:15

commit v3 on v2

--- a/solution.py
+++ b/solution.py
@@ -44,36 +44,43 @@
 def up_kernel(layout, width, first_ref, *refs):
     pieces = refs[: sum(layout)]
     gate_ref, upw_ref, hidden_ref, rows_ref, acc_ref = refs[sum(layout):]
-    step = pl.program_id(0)
-    experts, depth, hidden = gate_ref.shape
+    experts, _, hidden = gate_ref.shape
     line = pieces[0].shape[0]
-
-    @pl.when(step == 0)
-    def _():
-        at = 0
-        for entry, count in enumerate(layout):
-            left = 0
-            for piece in pieces[at:at + count]:
-                rows_ref[pl.ds(entry * line, line), pl.ds(left, piece.shape[1])] = piece[...]
-                left += piece.shape[1]
-            at += count
-        acc_ref[...] = jnp.zeros_like(acc_ref)
-
-    here = rows_ref[:, pl.ds(pl.multiple_of(step * depth, 128), depth)]
+    depth = 1024 if width % 1024 == 0 else 128
+
+    at = 0
+    for entry, count in enumerate(layout):
+        left = 0
+        for piece in pieces[at:at + count]:
+            rows_ref[pl.ds(entry * line, line), pl.ds(left, piece.shape[1])] = piece[...]
+            left += piece.shape[1]
+        at += count
+    acc_ref[...] = jnp.zeros_like(acc_ref)
+
+    @pl.loop(0, width // depth)
+    def _(step):
+        span = pl.ds(pl.multiple_of(step * depth, depth), depth)
+        here = rows_ref[:, span]
+        for e in range(experts):
+            acc_ref[2 * e] += jnp.dot(
+                here, gate_ref[e, span, :], preferred_element_type=jnp.float32
+            )
+            acc_ref[2 * e + 1] += jnp.dot(
+                here, upw_ref[e, span, :], preferred_element_type=jnp.float32
+            )
+
+    extra = rows_ref[:, width:].astype(jnp.float32)
+    lane = lax.broadcasted_iota(jnp.int32, extra.shape, 1)
     for e in range(experts):
-        acc_ref[2 * e] += jnp.dot(here, gate_ref[e], preferred_element_type=jnp.float32)
-        acc_ref[2 * e + 1] += jnp.dot(here, upw_ref[e], preferred_element_type=jnp.float32)
-
-    @pl.when(step == pl.num_programs(0) - 1)
-    def _():
-        extra = rows_ref[:, width:].astype(jnp.float32)
-        lane = lax.broadcasted_iota(jnp.int32, extra.shape, 1)
-        for e in range(experts):
-            mine = lax.rem(lane, extra.shape[1] // 2) == first_ref[0] + e
-            scale = jnp.sum(jnp.where(mine, extra, 0.0), axis=1, keepdims=True)
-            gate = acc_ref[2 * e]
-            value = gate / (1.0 + jnp.exp(-gate)) * acc_ref[2 * e + 1] * scale
-            hidden_ref[:, pl.ds(e * hidden, hidden)] = value.astype(jnp.bfloat16)
+        mine = lax.rem(lane, extra.shape[1] // 2) == first_ref[0] + e
+        scale = jnp.sum(jnp.where(mine, extra, 0.0), axis=1, keepdims=True)
+        gate = acc_ref[2 * e]
+        value = gate / (1.0 + jnp.exp(-gate)) * acc_ref[2 * e + 1] * scale
+        hidden_ref[:, pl.ds(e * hidden, hidden)] = value.astype(jnp.bfloat16)
+
+
+def in_vmem(value):
+    return pltpu.with_memory_space_constraint(value, pltpu.VMEM)
 
 
 def up_call(first, entries, w_gate, w_up):
@@ -83,71 +90,75 @@
     line = flat[0].shape[0]
     full = sum(p.shape[1] for p in entries[0])
     rows = line * len(entries)
-    depth = 1024 if width % 1024 == 0 else 128
-    weight = pl.BlockSpec((experts, depth, hidden), lambda i: (0, i, 0))
+    whole = pl.BlockSpec(memory_space=pltpu.VMEM)
     return pl.pallas_call(
         functools.partial(up_kernel, layout, width),
         out_shape=jax.ShapeDtypeStruct((rows, experts * hidden), jnp.bfloat16),
-        grid=(width // depth,),
-        in_specs=[pl.BlockSpec(memory_space=pltpu.SMEM)]
-        + [pl.BlockSpec(p.shape, lambda i: (0, 0)) for p in flat]
-        + [weight, weight],
-        out_specs=pl.BlockSpec((rows, experts * hidden), lambda i: (0, 0)),
+        in_specs=[pl.BlockSpec(memory_space=pltpu.SMEM)] + [whole] * (len(flat) + 2),
+        out_specs=whole,
         scratch_shapes=[
             pltpu.VMEM((rows, full), jnp.bfloat16),
             pltpu.VMEM((2 * experts, rows, hidden), jnp.float32),
         ],
-        compiler_params=pltpu.CompilerParams(vmem_limit_bytes=48 * 2**20),
+        compiler_params=pltpu.CompilerParams(vmem_limit_bytes=kernel_bytes(rows, full)),
         cost_estimate=pl.CostEstimate(
             flops=4 * rows * experts * width * hidden,
-            bytes_accessed=4 * experts * width * hidden,
-            transcendentals=0,
+            bytes_accessed=2 * rows * width,
+            transcendentals=rows * experts * hidden,
         ),
         name="gate_up",
-    )(first, *flat, w_gate, w_up)
-
-
-def down_kernel(order, line, hidden_ref, down_ref, keep_ref, send_ref):
+    )(first, *flat, in_vmem(w_gate), in_vmem(w_up))
+
+
+def kernel_bytes(rows, width):
+    return 6 * rows * width + 6 * 2**20
+
+
+def down_kernel(order, line, start, hidden_ref, down_ref, keep_ref, send_ref):
     experts, hidden, _ = down_ref.shape
-    total = None
-    for e in range(experts):
-        part = jnp.dot(
-            hidden_ref[:, pl.ds(e * hidden, hidden)], down_ref[e],
-            preferred_element_type=jnp.float32,
-        )
-        total = part if total is None else total + part
-    total = total.astype(jnp.bfloat16)
+    columns = keep_ref.shape[1]
+    block = 512 if columns % 512 == 0 else 128
     groups = len(order)
-    for place, entry in enumerate(order):
-        keep_ref[pl.ds(place * line, line), :] = total[entry * line:(entry + 1) * line]
-        low = (groups + entry) * line
-        send_ref[pl.ds(place * line, line), :] = total[low:low + line]
+
+    @pl.loop(0, columns // block)
+    def _(step):
+        at = pl.multiple_of(step * block, block)
+        total = None
+        for e in range(experts):
+            part = jnp.dot(
+                hidden_ref[:, pl.ds(e * hidden, hidden)],
+                down_ref[e, :, pl.ds(start + at, block)],
+                preferred_element_type=jnp.float32,
+            )
+            total = part if total is None else total + part
+        total = total.astype(jnp.bfloat16)
+        for place, entry in enumerate(order):
+            rows = pl.ds(place * line, line)
+            keep_ref[rows, pl.ds(at, block)] = total[entry * line:(entry + 1) * line]
+            low = (groups + entry) * line
+            send_ref[rows, pl.ds(at, block)] = total[low:low + line]
 
 
 def down_call(order, line, hidden, w_down, start, columns):
     experts, depth, _ = w_down.shape
     rows = line * len(order)
-    block = 896 if columns % 896 == 0 else 128
-    offset = start // block
     out = jax.ShapeDtypeStruct((rows, columns), jnp.bfloat16)
-    out_block = pl.BlockSpec((rows, block), lambda i: (0, i))
+    whole = pl.BlockSpec(memory_space=pltpu.VMEM)
     return pl.pallas_call(
-        functools.partial(down_kernel, order, line),
+        functools.partial(down_kernel, order, line, start),
         out_shape=(out, out),
-        grid=(columns // block,),
-        in_specs=[
-            pl.BlockSpec(hidden.shape, lambda i: (0, 0)),
-            pl.BlockSpec((experts, depth, block), lambda i: (0, 0, offset + i)),
-        ],
-        out_specs=(out_block, out_block),
-        compiler_params=pltpu.CompilerParams(vmem_limit_bytes=32 * 2**20),
+        in_specs=[whole, whole],
+        out_specs=(whole, whole),
+        compiler_params=pltpu.CompilerParams(
+            vmem_limit_bytes=kernel_bytes(2 * rows, columns)
+        ),
         cost_estimate=pl.CostEstimate(
             flops=2 * hidden.shape[0] * experts * depth * columns,
-            bytes_accessed=2 * experts * depth * columns,
+            bytes_accessed=4 * rows * columns,
             transcendentals=0,
         ),
         name="down",
-    )(hidden, w_down)
+    )(hidden, in_vmem(w_down))
 
 
 def add(*values):

time: 78.2 us -> 77.8 us (level)
  Pallas kernels: 17.8 us -> 11.6 us
  local copies, waits for them, and re-layouts: 6.25 us -> 11.4 us
    pallas_call x1, Pallas kernels: 12.6 us -> 7.11 us  [up_call(): pl.pallas_call(functools.partial(up_kernel, layout, width), out_shape=jax...]
    unnamed x2 -> x12, local copies, waits for them, and re-layouts: 5.17 us -> 10.4 us
where the time goes in v3:
time: 77.8 us; the launch traced here: 77.5 us
  waiting for transfers between devices  26.3 us (34%)
  starting transfers between devices  25.9 us (33%)
  Pallas kernels  11.6 us (15%)
  local copies, waits for them, and re-layouts  11.4 us (15%)
  other arithmetic  2.05 us (3%)
    ppermute x24, waiting for transfers between devices, swap(): lax.ppermute(value, axis, [(i, i ^ mask) for i in range(lax.axis_size(axi...  26.3 us
    ppermute x24, starting transfers between devices, swap(): lax.ppermute(value, axis, [(i, i ^ mask) for i in range(lax.axis_size(axi...  25.9 us
    unnamed x12, local copies, waits for them, and re-layouts  10.4 us
    pallas_call x1, Pallas kernels, up_call(): pl.pallas_call(functools.partial(up_kernel, layout, width), out_shape=jax...  7.11 us
    pallas_call x2, Pallas kernels, down_call(): pl.pallas_call(functools.partial(down_kernel, order, line, start), out_sh...  4.51 us
  transfers between devices with their start and end apart: 24, of which 12 were waited for; matrix products, arithmetic and copies ran while one was open for 1% of the time, Pallas kernels for 3%

profile of v3, /device:TPU:0, one launch (start us, length us, event | category | flops | bytes accessed | tf_op | source)
XLA Modules:
  0.0 77.5 jit_solution(13897785347659612266)
XLA Ops:
  0.0 0.8 %select_reduce_fusion = f32[4,64]{1,0:T(4,128)S(1)} fusion(f32[4,8]{1,0:T(4,128)} %param.8, s32[4,8]{1,0:T(4,128)} %param.7), kind=kLoop, calls=%fused_computation.10 | loop fusion | flops 5888 | bytes 1280 | tf_op jit(solution)/shard_map/reduce_sum | solution.py:180
  0.8 0.9 %concatenate.12 = bf16[4,7296]{1,0:T(4,128)(2,1)S(1)} concatenate(bf16[4,7168]{1,0:T(4,128)(2,1)} %param.6, bf16[4,64]{1,0:T(4,128)(2,1)S(1)} %get-tuple-element.20, bf16[4,64]{1,0:T(4,128)(2,1)S(1)} %get-tuple-element.19), dimensions={1} | concatenate | bytes 116736 | tf_op jit(solution)/shard_map/concatenate | solution.py:185
  1.7 5.1 %collective-permute-start.2 = (bf16[4,7296]{1,0:T(4,128)(2,1)S(1)}, bf16[4,7296]{1,0:T(4,128)(2,1)S(1)}, u32[]{:S(2)}, u32[]{:S(2)}) collective-permute-start(bf16[4,7296]{1,0:T(4,128)(2,1)S(1)} %concatenate.12), channel_id=1, source_target_pairs={{0,3},{1,2},{2,1},{3,0},{4,7},{5,6},{6,5},{7,4},{8,11},{9,10},{10,... | collective-permute-start | bytes 175112 | tf_op jit(solution)/shard_map/ppermute | solution.py:15
  6.8 0.0 collective-permute-start.1
  6.8 0.6 collective-permute-start
  7.4 1.8 %collective-permute-done.2 = bf16[4,7296]{1,0:T(4,128)(2,1)S(1)} collective-permute-done((bf16[4,7296]{1,0:T(4,128)(2,1)S(1)}, bf16[4,7296]{1,0:T(4,128)(2,1)S(1)}, u32[]{:S(2)}, u32[]{:S(2)}) %collective-permute-start.2) | collective-permute-done | bytes 58400 | tf_op jit(solution)/shard_map/ppermute | solution.py:15
  9.2 2.7 %collective-permute-done.1 = bf16[4,7296]{1,0:T(4,128)(2,1)S(1)} collective-permute-done((bf16[4,7296]{1,0:T(4,128)(2,1)S(1)}, bf16[4,7296]{1,0:T(4,128)(2,1)S(1)}, u32[]{:S(2)}, u32[]{:S(2)}) %collective-permute-start.1) | collective-permute-done | bytes 58400 | tf_op jit(solution)/shard_map/ppermute | solution.py:15
  11.9 0.0 collective-permute-done
  11.9 0.1 pad_maximum_fusion.refs_0_
  12.0 1.7 %collective-permute-start.4 = (bf16[16,7296]{1,0:T(8,128)(2,1)S(1)}, bf16[16,7296]{1,0:T(8,128)(2,1)S(1)}, u32[]{:S(2)}, u32[]{:S(2)}) collective-permute-start(bf16[16,7296]{1,0:T(8,128)(2,1)S(1)} %pad_maximum_fusion.refs_0_), channel_id=1, source_target_pairs={{0,8},{4,12},{8,0},{12,4},{1,9},{5,13},{9,1},{13,5},{2,10},{6,14},... | collective-permute-start | bytes 700424 | tf_op jit(solution)/shard_map/ppermute | solution.py:15
  13.7 1.5 %collective-permute-start.3 = (bf16[16,7296]{1,0:T(8,128)(2,1)S(1)}, bf16[16,7296]{1,0:T(8,128)(2,1)S(1)}, u32[]{:S(2)}, u32[]{:S(2)}) collective-permute-start(bf16[16,7296]{1,0:T(8,128)(2,1)S(1)} %pad_maximum_fusion.refs_0_), channel_id=1, source_target_pairs={{0,4},{4,0},{8,12},{12,8},{1,5},{5,1},{9,13},{13,9},{2,6},{6,2},{1... | collective-permute-start | bytes 700424 | tf_op jit(solution)/shard_map/ppermute | solution.py:15
  15.2 3.7 %collective-permute-done.4.refs_2_ = bf16[16,7296]{1,0:T(8,128)(2,1)S(1)} collective-permute-done((bf16[16,7296]{1,0:T(8,128)(2,1)S(1)}, bf16[16,7296]{1,0:T(8,128)(2,1)S(1)}, u32[]{:S(2)}, u32[]{:S(2)}) %collective-permute-start.4) | collective-permute-done | bytes 233504 | tf_op jit(solution)/shard_map/ppermute | solution.py:15
  18.9 1.6 %collective-permute-start.6 = (bf16[16,3712]{1,0:T(8,128)(2,1)S(1)}, bf16[16,3712]{1,0:T(8,128)(2,1)}, u32[]{:S(2)}, u32[]{:S(2)}) collective-permute-start(bf16[16,3712]{1,0:T(8,128)(2,1)S(1)} %slice.73), channel_id=1, source_target_pairs={{0,4},{4,0},{8,12},{12,8},{1,5},{5,1},{9,13},{13,9},{2,6},{6,2},{1... | collective-permute-start | bytes 356360 | tf_op jit(solution)/shard_map/ppermute | solution.py:15
  20.5 0.0 collective-permute-start.7
  20.5 0.5 collective-permute-start.9
  21.1 0.0 collective-permute-done.3.refs_1_
  21.1 0.0 collective-permute-start.8
  21.1 1.6 %collective-permute-start.5 = (bf16[16,3584]{1,0:T(8,128)(2,1)S(1)}, bf16[16,3584]{1,0:T(8,128)(2,1)}, u32[]{:S(2)}, u32[]{:S(2)}) collective-permute-start(bf16[16,3584]{1,0:T(8,128)(2,1)S(1)} %slice.72), channel_id=1, source_target_pairs={{0,8},{4,12},{8,0},{12,4},{1,9},{5,13},{9,1},{13,5},{2,10},{6,14},... | collective-permute-start | bytes 344072 | tf_op jit(solution)/shard_map/ppermute | solution.py:15
  22.7 1.2 %collective-permute-done.6.refs_4_ = bf16[16,3712]{1,0:T(8,128)(2,1)} collective-permute-done((bf16[16,3712]{1,0:T(8,128)(2,1)S(1)}, bf16[16,3712]{1,0:T(8,128)(2,1)}, u32[]{:S(2)}, u32[]{:S(2)}) %collective-permute-start.6) | collective-permute-done | bytes 118816 | tf_op jit(solution)/shard_map/ppermute | solution.py:15
  23.9 0.0 collective-permute-start.11
  23.9 2.9 %collective-permute-done.5.refs_3_ = bf16[16,3584]{1,0:T(8,128)(2,1)} collective-permute-done((bf16[16,3584]{1,0:T(8,128)(2,1)S(1)}, bf16[16,3584]{1,0:T(8,128)(2,1)}, u32[]{:S(2)}, u32[]{:S(2)}) %collective-permute-start.5) | collective-permute-done | bytes 114720 | tf_op jit(solution)/shard_map/ppermute | solution.py:15
  26.8 0.0 collective-permute-start.10
  26.8 0.0 collective-permute-done.7.refs_5_
  26.8 1.7 %collective-permute-done.10.refs_8_ = bf16[16,3584]{1,0:T(8,128)(2,1)} collective-permute-done((bf16[16,3584]{1,0:T(8,128)(2,1)}, bf16[16,3584]{1,0:T(8,128)(2,1)}, u32[]{:S(2)}, u32[]{:S(2)}) %collective-permute-start.10) | collective-permute-done | bytes 114720 | tf_op jit(solution)/shard_map/ppermute | solution.py:15
  28.5 0.0 collective-permute-done.9.refs_7_
  28.5 0.0 collective-permute-done.8.refs_6_
  28.5 0.0 collective-permute-done.11.refs_9_
  28.5 0.0 copy-start
  28.5 5.2 %copy-done = bf16[2,7168,512]{2,1,0:T(8,128)(2,1)S(1)} copy-done((bf16[2,7168,512]{2,1,0:T(8,128)(2,1)S(1)}, bf16[2,7168,512]{2,1,0:T(8,128)(2,1)}, u32[]{:S(2)}) %copy-start) | copy-done | bytes 14680088
  33.7 5.2 %copy-done.1 = bf16[2,7168,512]{2,1,0:T(8,128)(2,1)S(1)} copy-done((bf16[2,7168,512]{2,1,0:T(8,128)(2,1)S(1)}, bf16[2,7168,512]{2,1,0:T(8,128)(2,1)}, u32[]{:S(2)}) %copy-start.1) | copy-done | bytes 14680088
  38.8 7.1 %gate_up.1.hidden_ref = bf16[128,1024]{1,0:T(8,128)(2,1)S(1)} custom-call(s32[1]{0:T(128)} %bitcast.first_ref, bf16[16,7296]{1,0:T(8,128)(2,1)S(1)} %pad_maximum_fusion.refs_0_, bf16[16,7296]{1,0:T(8,128)(2,1)S(1)} %collective-permute-done.3.refs_1_, bf16[16,7296]{1,0:T(8,128)(2,1)S(1)} %collective-permute-done.4.refs_2_, ...), custom_call_target="tpu_custom_call" | custom-call | flops 3758096384 | bytes 1835008 | tf_op jit(solution)/shard_map/gate_up/pallas_call | solution.py:94
  46.0 0.0 slice-done
  46.0 0.0 slice-done.1
  46.0 2.3 %down.3 = (bf16[64,3584]{1,0:T(8,128)(2,1)S(1)}, bf16[64,3584]{1,0:T(8,128)(2,1)S(1)}) custom-call(bf16[128,1024]{1,0:T(8,128)(2,1)S(1)} %gate_up.1.hidden_ref, bf16[2,512,7168]{2,1,0:T(8,128)(2,1)S(1)} %bitcast.2), custom_call_target="tpu_custom_call" | custom-call | flops 939524096 | bytes 917504 | tf_op jit(solution)/shard_map/down/pallas_call | solution.py:147
  48.3 0.2 collective-permute-start.18
  48.5 2.2 %down.2 = (bf16[64,3584]{1,0:T(8,128)(2,1)S(1)}, bf16[64,3584]{1,0:T(8,128)(2,1)S(1)}) custom-call(bf16[128,1024]{1,0:T(8,128)(2,1)S(1)} %gate_up.1.hidden_ref, bf16[2,512,7168]{2,1,0:T(8,128)(2,1)S(1)} %bitcast.2), custom_call_target="tpu_custom_call" | custom-call | flops 939524096 | bytes 917504 | tf_op jit(solution)/shard_map/down/pallas_call | solution.py:147
  50.7 0.4 collective-permute-start.12
  51.2 0.0 collective-permute-done.18
  51.2 0.1 add_convert_fusion
  51.3 1.6 %collective-permute-start.19 = (bf16[32,3584]{1,0:T(8,128)(2,1)S(1)}, bf16[32,3584]{1,0:T(8,128)(2,1)S(1)}, u32[]{:S(2)}, u32[]{:S(2)}) collective-permute-start(bf16[32,3584]{1,0:T(8,128)(2,1)S(1)} %slice.83), channel_id=1, source_target_pairs={{0,8},{4,12},{8,0},{12,4},{1,9},{5,13},{9,1},{13,5},{2,10},{6,14},... | collective-permute-start | bytes 688136 | tf_op jit(solution)/shard_map/ppermute | solution.py:15
  52.9 0.0 collective-permute-done.12
  52.9 0.1 add_convert_fusion.1
  53.0 0.7 collective-permute-start.13
  53.7 5.3 %collective-permute-done.19 = bf16[32,3584]{1,0:T(8,128)(2,1)S(1)} collective-permute-done((bf16[32,3584]{1,0:T(8,128)(2,1)S(1)}, bf16[32,3584]{1,0:T(8,128)(2,1)S(1)}, u32[]{:S(2)}, u32[]{:S(2)}) %collective-permute-start.19) | collective-permute-done | bytes 229408 | tf_op jit(solution)/shard_map/ppermute | solution.py:15
  59.0 0.1 add_convert_fusion.2
  59.1 0.9 %collective-permute-start.20 = (bf16[16,3584]{1,0:T(8,128)(2,1)S(1)}, bf16[16,3584]{1,0:T(8,128)(2,1)S(1)}, u32[]{:S(2)}, u32[]{:S(2)}) collective-permute-start(bf16[16,3584]{1,0:T(8,128)(2,1)S(1)} %slice.85), channel_id=1, source_target_pairs={{0,4},{4,0},{8,12},{12,8},{1,5},{5,1},{9,13},{13,9},{2,6},{6,2},{1... | collective-permute-start | bytes 344072 | tf_op jit(solution)/shard_map/ppermute | solution.py:15
  60.0 0.7 collective-permute-done.13
  60.7 0.1 add_convert_fusion.3
  60.8 1.6 %collective-permute-start.14 = (bf16[16,3584]{1,0:T(8,128)(2,1)S(1)}, bf16[16,3584]{1,0:T(8,128)(2,1)S(1)}, u32[]{:S(2)}, u32[]{:S(2)}) collective-permute-start(bf16[16,3584]{1,0:T(8,128)(2,1)S(1)} %slice.77), channel_id=1, source_target_pairs={{0,8},{4,12},{8,0},{12,4},{1,9},{5,13},{9,1},{13,5},{2,10},{6,14},... | collective-permute-start | bytes 344072 | tf_op jit(solution)/shard_map/ppermute | solution.py:15
  62.3 1.6 %collective-permute-done.20 = bf16[16,3584]{1,0:T(8,128)(2,1)S(1)} collective-permute-done((bf16[16,3584]{1,0:T(8,128)(2,1)S(1)}, bf16[16,3584]{1,0:T(8,128)(2,1)S(1)}, u32[]{:S(2)}, u32[]{:S(2)}) %collective-permute-start.20) | collective-permute-done | bytes 114720 | tf_op jit(solution)/shard_map/ppermute | solution.py:15
  64.0 0.6 collective-permute-start.21
  64.7 2.8 %collective-permute-start.23 = (bf16[4,3584]{1,0:T(4,128)(2,1)S(1)}, bf16[4,3584]{1,0:T(4,128)(2,1)S(1)}, u32[]{:S(2)}, u32[]{:S(2)}) collective-permute-start(bf16[4,3584]{1,0:T(4,128)(2,1)S(1)} %get-tuple-element.17), channel_id=1, source_target_pairs={{0,3},{1,2},{2,1},{3,0},{4,7},{5,6},{6,5},{7,4},{8,11},{9,10},{10,... | collective-permute-start | bytes 86024 | tf_op jit(solution)/shard_map/ppermute | solution.py:15
  67.5 0.1 collective-permute-start.22
  67.6 0.0 collective-permute-done.14
  67.7 1.5 %collective-permute-start.15 = (bf16[4,3584]{1,0:T(4,128)(2,1)S(1)}, bf16[4,3584]{1,0:T(4,128)(2,1)S(1)}, u32[]{:S(2)}, u32[]{:S(2)}) collective-permute-start(bf16[4,3584]{1,0:T(4,128)(2,1)S(1)} %get-tuple-element.13), channel_id=1, source_target_pairs={{0,1},{1,0},{2,3},{3,2},{4,5},{5,4},{6,7},{7,6},{8,9},{9,8},{10,11... | collective-permute-start | bytes 86024 | tf_op jit(solution)/shard_map/ppermute | solution.py:15
  69.2 2.8 %collective-permute-start.17 = (bf16[4,3584]{1,0:T(4,128)(2,1)S(1)}, bf16[4,3584]{1,0:T(4,128)(2,1)S(1)}, u32[]{:S(2)}, u32[]{:S(2)}) collective-permute-start(bf16[4,3584]{1,0:T(4,128)(2,1)S(1)} %get-tuple-element.14), channel_id=1, source_target_pairs={{0,3},{1,2},{2,1},{3,0},{4,7},{5,6},{6,5},{7,4},{8,11},{9,10},{10,... | collective-permute-start | bytes 86024 | tf_op jit(solution)/shard_map/ppermute | solution.py:15
  72.0 0.0 collective-permute-done.21
  72.0 0.0 collective-permute-start.16
  72.0 0.0 collective-permute-done.23
  72.0 0.2 collective-permute-done.22
  72.3 0.0 collective-permute-done.15
  72.3 2.6 %collective-permute-done.17 = bf16[4,3584]{1,0:T(4,128)(2,1)S(1)} collective-permute-done((bf16[4,3584]{1,0:T(4,128)(2,1)S(1)}, bf16[4,3584]{1,0:T(4,128)(2,1)S(1)}, u32[]{:S(2)}, u32[]{:S(2)}) %collective-permute-start.17) | collective-permute-done | bytes 28704 | tf_op jit(solution)/shard_map/ppermute | solution.py:15
  74.9 1.9 %collective-permute-done.16 = bf16[4,3584]{1,0:T(4,128)(2,1)S(1)} collective-permute-done((bf16[4,3584]{1,0:T(4,128)(2,1)S(1)}, bf16[4,3584]{1,0:T(4,128)(2,1)S(1)}, u32[]{:S(2)}, u32[]{:S(2)}) %collective-permute-start.16) | collective-permute-done | bytes 28704 | tf_op jit(solution)/shard_map/ppermute | solution.py:15
  76.8 0.7 pad_maximum_fusion.1
  (21 shorter events, 0.3 us)
Async XLA Ops:
  1.7 7.5 %collective-permute-start.2 = (bf16[4,7296]{1,0:T(4,128)(2,1)S(1)}, bf16[4,7296]{1,0:T(4,128)(2,1)S(1)}, u32[]{:S(2)}, u32[]{:S(2)}) collective-permute-start(bf16[4,7296]{1,0:T(4,128)(2,1)S(1)} %concatenate.12), channel_id=1, source_target_pairs={{0,3},{1,2},{2,1},{3,0},{4,7},{5,6},{6,5},{7,4},{8,11},{9,10},{10,... | collective-permute-start | bytes 175112 | tf_op jit(solution)/shard_map/ppermute | solution.py:15
  6.8 5.1 %collective-permute-start.1 = (bf16[4,7296]{1,0:T(4,128)(2,1)S(1)}, bf16[4,7296]{1,0:T(4,128)(2,1)S(1)}, u32[]{:S(2)}, u32[]{:S(2)}) collective-permute-start(bf16[4,7296]{1,0:T(4,128)(2,1)S(1)} %concatenate.12), channel_id=1, source_target_pairs={{0,2},{1,3},{2,0},{3,1},{4,6},{5,7},{6,4},{7,5},{8,10},{9,11},{10,... | collective-permute-start | bytes 175112 | tf_op jit(solution)/shard_map/ppermute | solution.py:15
  6.8 5.1 %collective-permute-start = (bf16[4,7296]{1,0:T(4,128)(2,1)S(1)}, bf16[4,7296]{1,0:T(4,128)(2,1)S(1)}, u32[]{:S(2)}, u32[]{:S(2)}) collective-permute-start(bf16[4,7296]{1,0:T(4,128)(2,1)S(1)} %concatenate.12), channel_id=1, source_target_pairs={{0,1},{1,0},{2,3},{3,2},{4,5},{5,4},{6,7},{7,6},{8,9},{9,8},{10,11... | collective-permute-start | bytes 175112 | tf_op jit(solution)/shard_map/ppermute | solution.py:15
  12.0 6.8 %collective-permute-start.4 = (bf16[16,7296]{1,0:T(8,128)(2,1)S(1)}, bf16[16,7296]{1,0:T(8,128)(2,1)S(1)}, u32[]{:S(2)}, u32[]{:S(2)}) collective-permute-start(bf16[16,7296]{1,0:T(8,128)(2,1)S(1)} %pad_maximum_fusion.refs_0_), channel_id=1, source_target_pairs={{0,8},{4,12},{8,0},{12,4},{1,9},{5,13},{9,1},{13,5},{2,10},{6,14},... | collective-permute-start | bytes 700424 | tf_op jit(solution)/shard_map/ppermute | solution.py:15
  13.7 7.4 %collective-permute-start.3 = (bf16[16,7296]{1,0:T(8,128)(2,1)S(1)}, bf16[16,7296]{1,0:T(8,128)(2,1)S(1)}, u32[]{:S(2)}, u32[]{:S(2)}) collective-permute-start(bf16[16,7296]{1,0:T(8,128)(2,1)S(1)} %pad_maximum_fusion.refs_0_), channel_id=1, source_target_pairs={{0,4},{4,0},{8,12},{12,8},{1,5},{5,1},{9,13},{13,9},{2,6},{6,2},{1... | collective-permute-start | bytes 700424 | tf_op jit(solution)/shard_map/ppermute | solution.py:15
  18.9 27.1 %slice-start = ((s8[14680064]{0:T(1024)(128)(4,1)}), s8[2097152]{0:T(1024)(128)(4,1)S(1)}, s32[]{:S(2)}) async-start(s8[14680064]{0:T(1024)(128)(4,1)} %bitcast.1), calls=%async_computation | async-start | bytes 4194304
  18.9 5.0 %collective-permute-start.6 = (bf16[16,3712]{1,0:T(8,128)(2,1)S(1)}, bf16[16,3712]{1,0:T(8,128)(2,1)}, u32[]{:S(2)}, u32[]{:S(2)}) collective-permute-start(bf16[16,3712]{1,0:T(8,128)(2,1)S(1)} %slice.73), channel_id=1, source_target_pairs={{0,4},{4,0},{8,12},{12,8},{1,5},{5,1},{9,13},{13,9},{2,6},{6,2},{1... | collective-permute-start | bytes 356360 | tf_op jit(solution)/shard_map/ppermute | solution.py:15
  20.5 6.3 %collective-permute-start.7 = (bf16[16,7296]{1,0:T(8,128)(2,1)S(1)}, bf16[16,7296]{1,0:T(8,128)(2,1)S(1)}, u32[]{:S(2)}, u32[]{:S(2)}) collective-permute-start(bf16[16,7296]{1,0:T(8,128)(2,1)S(1)} %pad_maximum_fusion.refs_0_), channel_id=1, source_target_pairs={{0,16},{16,0},{1,17},{17,1},{2,18},{18,2},{3,19},{19,3},{4,20},{20... | collective-permute-start | bytes 700424 | tf_op jit(solution)/shard_map/ppermute | solution.py:15
  20.5 7.9 %collective-permute-start.9 = (bf16[16,7296]{1,0:T(8,128)(2,1)S(1)}, bf16[16,7296]{1,0:T(8,128)(2,1)S(1)}, u32[]{:S(2)}, u32[]{:S(2)}) collective-permute-start(bf16[16,7296]{1,0:T(8,128)(2,1)S(1)} %collective-permute-done.4.refs_2_), channel_id=1, source_target_pairs={{0,16},{16,0},{1,17},{17,1},{2,18},{18,2},{3,19},{19,3},{4,20},{20... | collective-permute-start | bytes 700424 | tf_op jit(solution)/shard_map/ppermute | solution.py:15
  21.1 7.4 %collective-permute-start.8 = (bf16[16,7296]{1,0:T(8,128)(2,1)S(1)}, bf16[16,7296]{1,0:T(8,128)(2,1)S(1)}, u32[]{:S(2)}, u32[]{:S(2)}) collective-permute-start(bf16[16,7296]{1,0:T(8,128)(2,1)S(1)} %collective-permute-done.3.refs_1_), channel_id=1, source_target_pairs={{0,16},{16,0},{1,17},{17,1},{2,18},{18,2},{3,19},{19,3},{4,20},{20... | collective-permute-start | bytes 700424 | tf_op jit(solution)/shard_map/ppermute | solution.py:15
  21.1 5.7 %collective-permute-start.5 = (bf16[16,3584]{1,0:T(8,128)(2,1)S(1)}, bf16[16,3584]{1,0:T(8,128)(2,1)}, u32[]{:S(2)}, u32[]{:S(2)}) collective-permute-start(bf16[16,3584]{1,0:T(8,128)(2,1)S(1)} %slice.72), channel_id=1, source_target_pairs={{0,8},{4,12},{8,0},{12,4},{1,9},{5,13},{9,1},{13,5},{2,10},{6,14},... | collective-permute-start | bytes 344072 | tf_op jit(solution)/shard_map/ppermute | solution.py:15
  23.9 4.6 %collective-permute-start.11 = (bf16[16,3712]{1,0:T(8,128)(2,1)}, bf16[16,3712]{1,0:T(8,128)(2,1)}, u32[]{:S(2)}, u32[]{:S(2)}) collective-permute-start(bf16[16,3712]{1,0:T(8,128)(2,1)} %collective-permute-done.6.refs_4_), channel_id=1, source_target_pairs={{0,16},{16,0},{1,17},{17,1},{2,18},{18,2},{3,19},{19,3},{4,20},{20... | collective-permute-start | bytes 356360 | tf_op jit(solution)/shard_map/ppermute | solution.py:15
  26.8 1.7 %collective-permute-start.10 = (bf16[16,3584]{1,0:T(8,128)(2,1)}, bf16[16,3584]{1,0:T(8,128)(2,1)}, u32[]{:S(2)}, u32[]{:S(2)}) collective-permute-start(bf16[16,3584]{1,0:T(8,128)(2,1)} %collective-permute-done.5.refs_3_), channel_id=1, source_target_pairs={{0,16},{16,0},{1,17},{17,1},{2,18},{18,2},{3,19},{19,3},{4,20},{20... | collective-permute-start | bytes 344072 | tf_op jit(solution)/shard_map/ppermute | solution.py:15
  28.5 5.2 %copy-start = (bf16[2,7168,512]{2,1,0:T(8,128)(2,1)S(1)}, bf16[2,7168,512]{2,1,0:T(8,128)(2,1)}, u32[]{:S(2)}) copy-start(bf16[2,7168,512]{2,1,0:T(8,128)(2,1)} %refs_10_.1) | copy-start | bytes 44040196
  33.7 5.2 %copy-start.1 = (bf16[2,7168,512]{2,1,0:T(8,128)(2,1)S(1)}, bf16[2,7168,512]{2,1,0:T(8,128)(2,1)}, u32[]{:S(2)}) copy-start(bf16[2,7168,512]{2,1,0:T(8,128)(2,1)} %refs_11_.1) | copy-start | bytes 44040196
  38.8 7.1 %slice-start.1 = ((s8[14680064]{0:T(1024)(128)(4,1)}), s8[4194304]{0:T(1024)(128)(4,1)S(1)}, s32[]{:S(2)}) async-start(s8[14680064]{0:T(1024)(128)(4,1)} %bitcast.1), calls=%async_computation.1 | async-start | bytes 8388608
  38.8 7.1 %slice-start.2 = ((s8[14680064]{0:T(1024)(128)(4,1)}), s8[4194304]{0:T(1024)(128)(4,1)S(1)}, s32[]{:S(2)}) async-start(s8[14680064]{0:T(1024)(128)(4,1)} %bitcast.1), calls=%async_computation.2 | async-start | bytes 8388608
  38.8 7.1 %slice-start.3 = ((s8[14680064]{0:T(1024)(128)(4,1)}), s8[4194304]{0:T(1024)(128)(4,1)S(1)}, s32[]{:S(2)}) async-start(s8[14680064]{0:T(1024)(128)(4,1)} %bitcast.1), calls=%async_computation.3 | async-start | bytes 8388608
  48.3 2.9 %collective-permute-start.18 = (bf16[64,3584]{1,0:T(8,128)(2,1)S(1)}, bf16[64,3584]{1,0:T(8,128)(2,1)S(1)}, u32[]{:S(2)}, u32[]{:S(2)}) collective-permute-start(bf16[64,3584]{1,0:T(8,128)(2,1)S(1)} %get-tuple-element.12), channel_id=1, source_target_pairs={{0,16},{16,0},{1,17},{17,1},{2,18},{18,2},{3,19},{19,3},{4,20},{20... | collective-permute-start | bytes 1376264 | tf_op jit(solution)/shard_map/ppermute | solution.py:15
  50.7 2.2 %collective-permute-start.12 = (bf16[64,3584]{1,0:T(8,128)(2,1)S(1)}, bf16[64,3584]{1,0:T(8,128)(2,1)S(1)}, u32[]{:S(2)}, u32[]{:S(2)}) collective-permute-start(bf16[64,3584]{1,0:T(8,128)(2,1)S(1)} %get-tuple-element.10), channel_id=1, source_target_pairs={{0,16},{16,0},{1,17},{17,1},{2,18},{18,2},{3,19},{19,3},{4,20},{20... | collective-permute-start | bytes 1376264 | tf_op jit(solution)/shard_map/ppermute | solution.py:15
  51.3 7.7 %collective-permute-start.19 = (bf16[32,3584]{1,0:T(8,128)(2,1)S(1)}, bf16[32,3584]{1,0:T(8,128)(2,1)S(1)}, u32[]{:S(2)}, u32[]{:S(2)}) collective-permute-start(bf16[32,3584]{1,0:T(8,128)(2,1)S(1)} %slice.83), channel_id=1, source_target_pairs={{0,8},{4,12},{8,0},{12,4},{1,9},{5,13},{9,1},{13,5},{2,10},{6,14},... | collective-permute-start | bytes 688136 | tf_op jit(solution)/shard_map/ppermute | solution.py:15
  53.0 7.7 %collective-permute-start.13 = (bf16[32,3584]{1,0:T(8,128)(2,1)S(1)}, bf16[32,3584]{1,0:T(8,128)(2,1)S(1)}, u32[]{:S(2)}, u32[]{:S(2)}) collective-permute-start(bf16[32,3584]{1,0:T(8,128)(2,1)S(1)} %slice.75), channel_id=1, source_target_pairs={{0,4},{4,0},{8,12},{12,8},{1,5},{5,1},{9,13},{13,9},{2,6},{6,2},{1... | collective-permute-start | bytes 688136 | tf_op jit(solution)/shard_map/ppermute | solution.py:15
  59.1 4.9 %collective-permute-start.20 = (bf16[16,3584]{1,0:T(8,128)(2,1)S(1)}, bf16[16,3584]{1,0:T(8,128)(2,1)S(1)}, u32[]{:S(2)}, u32[]{:S(2)}) collective-permute-start(bf16[16,3584]{1,0:T(8,128)(2,1)S(1)} %slice.85), channel_id=1, source_target_pairs={{0,4},{4,0},{8,12},{12,8},{1,5},{5,1},{9,13},{13,9},{2,6},{6,2},{1... | collective-permute-start | bytes 344072 | tf_op jit(solution)/shard_map/ppermute | solution.py:15
  60.8 6.8 %collective-permute-start.14 = (bf16[16,3584]{1,0:T(8,128)(2,1)S(1)}, bf16[16,3584]{1,0:T(8,128)(2,1)S(1)}, u32[]{:S(2)}, u32[]{:S(2)}) collective-permute-start(bf16[16,3584]{1,0:T(8,128)(2,1)S(1)} %slice.77), channel_id=1, source_target_pairs={{0,8},{4,12},{8,0},{12,4},{1,9},{5,13},{9,1},{13,5},{2,10},{6,14},... | collective-permute-start | bytes 344072 | tf_op jit(solution)/shard_map/ppermute | solution.py:15
  64.0 8.0 %collective-permute-start.21 = (bf16[4,3584]{1,0:T(4,128)(2,1)S(1)}, bf16[4,3584]{1,0:T(4,128)(2,1)S(1)}, u32[]{:S(2)}, u32[]{:S(2)}) collective-permute-start(bf16[4,3584]{1,0:T(4,128)(2,1)S(1)} %get-tuple-element.16), channel_id=1, source_target_pairs={{0,1},{1,0},{2,3},{3,2},{4,5},{5,4},{6,7},{7,6},{8,9},{9,8},{10,11... | collective-permute-start | bytes 86024 | tf_op jit(solution)/shard_map/ppermute | solution.py:15
  64.7 7.4 %collective-permute-start.23 = (bf16[4,3584]{1,0:T(4,128)(2,1)S(1)}, bf16[4,3584]{1,0:T(4,128)(2,1)S(1)}, u32[]{:S(2)}, u32[]{:S(2)}) collective-permute-start(bf16[4,3584]{1,0:T(4,128)(2,1)S(1)} %get-tuple-element.17), channel_id=1, source_target_pairs={{0,3},{1,2},{2,1},{3,0},{4,7},{5,6},{6,5},{7,4},{8,11},{9,10},{10,... | collective-permute-start | bytes 86024 | tf_op jit(solution)/shard_map/ppermute | solution.py:15
  67.5 4.8 %collective-permute-start.22 = (bf16[4,3584]{1,0:T(4,128)(2,1)S(1)}, bf16[4,3584]{1,0:T(4,128)(2,1)S(1)}, u32[]{:S(2)}, u32[]{:S(2)}) collective-permute-start(bf16[4,3584]{1,0:T(4,128)(2,1)S(1)} %get-tuple-element.18), channel_id=1, source_target_pairs={{0,2},{1,3},{2,0},{3,1},{4,6},{5,7},{6,4},{7,5},{8,10},{9,11},{10,... | collective-permute-start | bytes 86024 | tf_op jit(solution)/shard_map/ppermute | solution.py:15
  67.7 4.6 %collective-permute-start.15 = (bf16[4,3584]{1,0:T(4,128)(2,1)S(1)}, bf16[4,3584]{1,0:T(4,128)(2,1)S(1)}, u32[]{:S(2)}, u32[]{:S(2)}) collective-permute-start(bf16[4,3584]{1,0:T(4,128)(2,1)S(1)} %get-tuple-element.13), channel_id=1, source_target_pairs={{0,1},{1,0},{2,3},{3,2},{4,5},{5,4},{6,7},{7,6},{8,9},{9,8},{10,11... | collective-permute-start | bytes 86024 | tf_op jit(solution)/shard_map/ppermute | solution.py:15
  69.2 5.7 %collective-permute-start.17 = (bf16[4,3584]{1,0:T(4,128)(2,1)S(1)}, bf16[4,3584]{1,0:T(4,128)(2,1)S(1)}, u32[]{:S(2)}, u32[]{:S(2)}) collective-permute-start(bf16[4,3584]{1,0:T(4,128)(2,1)S(1)} %get-tuple-element.14), channel_id=1, source_target_pairs={{0,3},{1,2},{2,1},{3,0},{4,7},{5,6},{6,5},{7,4},{8,11},{9,10},{10,... | collective-permute-start | bytes 86024 | tf_op jit(solution)/shard_map/ppermute | solution.py:15
  72.0 4.8 %collective-permute-start.16 = (bf16[4,3584]{1,0:T(4,128)(2,1)S(1)}, bf16[4,3584]{1,0:T(4,128)(2,1)S(1)}, u32[]{:S(2)}, u32[]{:S(2)}) collective-permute-start(bf16[4,3584]{1,0:T(4,128)(2,1)S(1)} %get-tuple-element.15), channel_id=1, source_target_pairs={{0,2},{1,3},{2,0},{3,1},{4,6},{5,7},{6,4},{7,5},{8,10},{9,11},{10,... | collective-permute-start | bytes 86024 | tf_op jit(solution)/shard_map/ppermute | solution.py:15

commit v4 on v3

v4 whole, which is shorter than its diff:
```python
import functools

import jax
import jax.numpy as jnp
from jax import lax
from jax.experimental import pallas as pl
from jax.experimental.pallas import tpu as pltpu
from jax.sharding import PartitionSpec as P

AXES = ("sect", "grp", "dev")
CHUNKS = 2


def swap(value, axis, mask):
    return lax.ppermute(value, axis, [(i, i ^ mask) for i in range(lax.axis_size(axis))])


def bits_of(size):
    return [1 << b for b in range(size.bit_length() - 1)]


def split_columns(width):
    half = width // 256 * 128
    return half


def gather_rows(block, w_up):
    lanes, groups, sects = (lax.axis_size(a) for a in ("dev", "grp", "sect"))
    arrived = [swap(block, "dev", m) for m in range(1, lanes)]
    w_up, token = fetch(w_up, block)
    arrived, token = lax.optimization_barrier((arrived, token))
    line = jnp.concatenate([block] + arrived, axis=0)
    half = split_columns(block.shape[1])
    if groups == 4:
        by_x, by_y = swap(line, "grp", 1), swap(line, "grp", 2)
        corner = [swap(by_x[:, :half], "grp", 2), swap(by_y[:, half:], "grp", 1)]
        entries = [[line], [by_x], [by_y], corner]
    else:
        entries = [[line]]
        for bit in bits_of(groups):
            entries = entries + [[swap(p, "grp", bit) for p in e] for e in entries]
    for bit in bits_of(sects):
        entries = entries + [[swap(p, "sect", bit) for p in e] for e in entries]
    return entries, w_up, token


def up_kernel(layout, width, first_ref, token_ref, *refs):
    pieces = refs[: sum(layout)]
    gate_hbm, upw_ref, hidden_ref, rows_ref, gate_ref, up_ref, sems = refs[sum(layout):]
    experts, _, hidden = upw_ref.shape
    line = pieces[0].shape[0]
    block = min(256, hidden)
    steps = hidden // block

    def span_of(step):
        return pl.ds(pl.multiple_of(step * block, block), block)

    def copy_of(e, step):
        span = span_of(step)
        return pltpu.make_async_copy(
            gate_hbm.at[e, :, span], gate_ref.at[e, :, span], sems.at[e, step]
        )

    for e in range(experts):
        for step in range(steps):
            copy_of(e, step).start()

    at = 0
    for entry, count in enumerate(layout):
        left = 0
        for piece in pieces[at:at + count]:
            rows_ref[pl.ds(entry * line, line), pl.ds(left, piece.shape[1])] = piece[...]
            left += piece.shape[1]
        at += count

    for e in range(experts):

        @pl.loop(0, steps)
        def _(step):
            span = span_of(step)
            up_ref[e, :, span] = jnp.dot(
                rows_ref[:, :width], upw_ref[e, :, span], preferred_element_type=jnp.float32
            )

    extra = rows_ref[:, width:].astype(jnp.float32)
    lane = lax.broadcasted_iota(jnp.int32, extra.shape, 1)
    for e in range(experts):
        mine = lax.rem(lane, extra.shape[1] // 2) == first_ref[0] + e
        scale = jnp.sum(jnp.where(mine, extra, 0.0), axis=1, keepdims=True)

        @pl.loop(0, steps)
        def _(step):
            span = span_of(step)
            copy_of(e, step).wait()
            gate = jnp.dot(
                rows_ref[:, :width], gate_ref[e, :, span], preferred_element_type=jnp.float32
            )
            value = gate / (1.0 + jnp.exp(-gate)) * up_ref[e, :, span] * scale
            out = pl.ds(pl.multiple_of(e * hidden + step * block, block), block)
            hidden_ref[:, out] = value.astype(jnp.bfloat16)


def fetch_kernel(parts, *refs):
    source_ref, target_ref, token_ref, sems = refs[-4:]
    depth = source_ref.shape[1] // parts
    copies = [
        pltpu.make_async_copy(
            source_ref.at[e, pl.ds(p * depth, depth)],
            target_ref.at[e, pl.ds(p * depth, depth)],
            sems.at[e * parts + p],
        )
        for e in range(source_ref.shape[0])
        for p in range(parts)
    ]
    for copy in copies:
        copy.start()
    token_ref[...] = jnp.zeros_like(token_ref)
    for copy in copies:
        copy.wait()


def fetch(weight, *after):
    parts = 4
    return pl.pallas_call(
        functools.partial(fetch_kernel, parts),
        out_shape=(
            pltpu.VMEM(weight.shape, weight.dtype),
            jax.ShapeDtypeStruct((8, 128), jnp.float32),
        ),
        in_specs=[pl.BlockSpec(memory_space=pl.ANY)] * (len(after) + 1),
        out_specs=(pl.BlockSpec(memory_space=pltpu.VMEM),) * 2,
        scratch_shapes=[pltpu.SemaphoreType.DMA((weight.shape[0] * parts,))],
        compiler_params=pltpu.CompilerParams(vmem_limit_bytes=2**20),
        cost_estimate=pl.CostEstimate(
            flops=0, bytes_accessed=2 * weight.size, transcendentals=0
        ),
        name="fetch",
    )(*after, pltpu.with_memory_space_constraint(weight, pltpu.HBM))


def up_call(first, entries, w_gate, w_up, token):
    layout = [len(e) for e in entries]
    flat = [p for e in entries for p in e]
    experts, width, hidden = w_gate.shape
    line = flat[0].shape[0]
    full = sum(p.shape[1] for p in entries[0])
    rows = line * len(entries)
    whole = pl.BlockSpec(memory_space=pltpu.VMEM)
    return pl.pallas_call(
        functools.partial(up_kernel, layout, width),
        out_shape=jax.ShapeDtypeStruct((rows, experts * hidden), jnp.bfloat16),
        in_specs=[pl.BlockSpec(memory_space=pltpu.SMEM), pl.BlockSpec(memory_space=pl.ANY)]
        + [whole] * len(flat)
        + [pl.BlockSpec(memory_space=pl.ANY), whole],
        out_specs=whole,
        scratch_shapes=[
            pltpu.VMEM((rows, full), jnp.bfloat16),
            pltpu.VMEM(w_gate.shape, w_gate.dtype),
            pltpu.VMEM((experts, rows, hidden), jnp.float32),
            pltpu.SemaphoreType.DMA((experts, hidden // min(256, hidden))),
        ],
        compiler_params=pltpu.CompilerParams(
            vmem_limit_bytes=kernel_bytes(rows, full) + 2 * w_gate.size
        ),
        cost_estimate=pl.CostEstimate(
            flops=4 * rows * experts * width * hidden,
            bytes_accessed=2 * rows * width,
            transcendentals=rows * experts * hidden,
        ),
        name="gate_up",
    )(
        first,
        token,
        *flat,
        pltpu.with_memory_space_constraint(w_gate, pltpu.HBM),
        pltpu.with_memory_space_constraint(w_up, pltpu.VMEM),
    )


def kernel_bytes(rows, width):
    return 4 * rows * width + 4 * 2**20


def down_kernel(order, line, hidden_ref, down_ref, keep_ref, send_ref):
    experts, hidden, block = down_ref.shape
    groups = len(order)
    weight = down_ref[...].reshape(experts * hidden, block)
    total = jnp.dot(hidden_ref[...], weight, preferred_element_type=jnp.float32)
    total = total.astype(jnp.bfloat16)
    for place, entry in enumerate(order):
        rows = pl.ds(place * line, line)
        keep_ref[rows, :] = total[entry * line:(entry + 1) * line]
        low = (groups + entry) * line
        send_ref[rows, :] = total[low:low + line]


def down_call(order, line, hidden, w_down, start, columns):
    experts, depth, _ = w_down.shape
    rows = line * len(order)
    block = 512 if columns % 512 == 0 else 128
    offset = start // block
    out = jax.ShapeDtypeStruct((rows, columns), jnp.bfloat16)
    out_block = pl.BlockSpec((rows, block), lambda i: (0, i))
    return pl.pallas_call(
        functools.partial(down_kernel, order, line),
        out_shape=(out, out),
        grid=(columns // block,),
        in_specs=[
            pl.BlockSpec(hidden.shape, lambda i: (0, 0)),
            pl.BlockSpec((experts, depth, block), lambda i: (0, 0, offset + i)),
        ],
        out_specs=(out_block, out_block),
        compiler_params=pltpu.CompilerParams(vmem_limit_bytes=kernel_bytes(2 * rows, 4096)),
        cost_estimate=pl.CostEstimate(
            flops=2 * hidden.shape[0] * experts * depth * columns,
            bytes_accessed=2 * experts * depth * columns,
            transcendentals=0,
        ),
        name="down",
    )(hidden, pltpu.with_memory_space_constraint(w_down, pltpu.HBM))


def add(*values):
    total = values[0].astype(jnp.float32)
    for value in values[1:]:
        total = total + value.astype(jnp.float32)
    return total.astype(jnp.bfloat16)


def body(tokens, expert_ids, gate_weights, w_gate, w_up, w_down):
    sects, groups, lanes = (lax.axis_size(a) for a in AXES)
    row_count, width = tokens.shape
    experts = w_gate.shape[0]
    expert_count = sects * groups * experts
    first = lax.axis_index(("sect", "grp")).astype(jnp.int32) * experts

    half = -(-expert_count // 64) * 64
    catalog = jnp.arange(half, dtype=jnp.int32)
    dense = jnp.sum(
        jnp.where(expert_ids[:, :, None] == catalog, gate_weights[:, :, None], 0.0), axis=1
    )
    high = lax.reduce_precision(dense, 8, 7)
    extra = jnp.concatenate([high, dense - high], axis=1).astype(jnp.bfloat16)
    entries, w_up, token = gather_rows(jnp.concatenate([tokens, extra], axis=1), w_up)

    hidden = up_call(first.reshape(1), entries, w_gate, w_up, token)

    line = lanes * row_count
    results = []
    chunk = width // CHUNKS
    for c in range(CHUNKS):
        bits = bits_of(groups)
        bits = bits if c % 2 else bits[::-1]
        order = [0]
        for bit in bits:
            order = order + [o | bit for o in order]
        keep, send = down_call(order, line, hidden, w_down, c * chunk, chunk)
        value = add(keep, swap(send, "sect", 1))
        for bit in bits[::-1]:
            middle = value.shape[0] // 2
            arrived = swap(value[middle:], "grp", bit)
            value = add(value[:middle], arrived)
        pieces = [value[:row_count]]
        for m in range(1, lanes):
            pieces.append(swap(value[m * row_count:(m + 1) * row_count], "dev", m))
        results.append(add(*pieces))
    return jnp.concatenate(results, axis=1)


def solution(mesh):
    in_specs = (
        P(AXES, None),
        P(AXES, None),
        P(AXES, None),
        P(("sect", "grp"), None, "dev"),
        P(("sect", "grp"), None, "dev"),
        P(("sect", "grp"), "dev", None),
    )
    return jax.shard_map(
        body, mesh=mesh, in_specs=in_specs, out_specs=P(AXES, None), check_vma=False
    )
```

time: 77.8 us -> 85.7 us (1.10)
  Pallas kernels: 11.6 us -> 23.9 us
  waiting for transfers between devices: 26.3 us -> 21.3 us
    pallas_call x2 -> x3, Pallas kernels: 4.51 us -> 17.9 us  [the longest x2 12.6 us: down_call(): pl.pallas_call(functools.partial(down_kernel, order, line), out_shape=(ou...]
    ppermute x24, waiting for transfers between devices: 26.3 us -> 21.3 us  [swap(): lax.ppermute(value, axis, [(i, i ^ mask) for i in range(lax.axis_size(axi...]
    pallas_call x1, Pallas kernels: 7.11 us -> 6 us  [up_call(): pl.pallas_call(functools.partial(up_kernel, layout, width), out_shape=jax...]
    unnamed x12 -> x4, local copies, waits for them, and re-layouts: 10.4 us -> 10.4 us
  transfers between devices with their start and end apart: 24 -> 24, of which waited for: 12 -> 10; matrix products, arithmetic and copies ran while one was open for 1% -> 1% of each run, Pallas kernels for 3% -> 14%
where the time goes in v4:
time: 85.7 us; the launch traced here: 85.2 us
  starting transfers between devices  26.4 us (31%)
  Pallas kernels  23.9 us (28%)
  waiting for transfers between devices  21.3 us (25%)
  local copies, waits for them, and re-layouts  11.4 us (13%)
  other arithmetic  2.04 us (2%)
    ppermute x24, starting transfers between devices, swap(): lax.ppermute(value, axis, [(i, i ^ mask) for i in range(lax.axis_size(axi...  26.4 us
    ppermute x24, waiting for transfers between devices, swap(): lax.ppermute(value, axis, [(i, i ^ mask) for i in range(lax.axis_size(axi...  21.3 us
    pallas_call x2, Pallas kernels, down_call(): pl.pallas_call(functools.partial(down_kernel, order, line), out_shape=(ou...  12.6 us
    unnamed x4, local copies, waits for them, and re-layouts  10.4 us
    pallas_call x1, Pallas kernels, up_call(): pl.pallas_call(functools.partial(up_kernel, layout, width), out_shape=jax...  6 us
    pallas_call x1, Pallas kernels, fetch(): pl.pallas_call(functools.partial(fetch_kernel, parts), out_shape=(pltpu.V...  5.31 us
  transfers between devices with their start and end apart: 24, of which 10 were waited for; matrix products, arithmetic and copies ran while one was open for 1% of the time, Pallas kernels for 14%

profile of v4, /device:TPU:0, one launch (start us, length us, event | category | flops | bytes accessed | tf_op | source)
XLA Modules:
  0.0 85.2 jit_solution(10747084592773453808)
XLA Ops:
  0.0 0.8 select_reduce_fusion
  0.8 0.9 %concatenate.12.refs_0_ = bf16[4,7296]{1,0:T(4,128)(2,1)S(1)} concatenate(bf16[4,7168]{1,0:T(4,128)(2,1)} %param.6, bf16[4,64]{1,0:T(4,128)(2,1)S(1)} %get-tuple-element.32, bf16[4,64]{1,0:T(4,128)(2,1)S(1)} %get-tuple-element.31), dimensions={1} | concatenate | bytes 116736 | tf_op jit(solution)/shard_map/concatenate | solution.py:244
  1.7 5.1 %collective-permute-start.2 = (bf16[4,7296]{1,0:T(4,128)(2,1)S(1)}, bf16[4,7296]{1,0:T(4,128)(2,1)S(1)}, u32[]{:S(2)}, u32[]{:S(2)}) collective-permute-start(bf16[4,7296]{1,0:T(4,128)(2,1)S(1)} %concatenate.12.refs_0_), channel_id=1, source_target_pairs={{0,3},{1,2},{2,1},{3,0},{4,7},{5,6},{6,5},{7,4},{8,11},{9,10},{10,... | collective-permute-start | bytes 175112 | tf_op jit(solution)/shard_map/ppermute | solution.py:15
  6.8 0.0 collective-permute-start.1
  6.8 0.6 collective-permute-start
  7.4 5.3 %fetch.1 = (bf16[2,7168,512]{2,1,0:T(8,128)(2,1)S(1)}, f32[8,128]{1,0:T(8,128)S(1)}) custom-call(bf16[4,7296]{1,0:T(4,128)(2,1)S(1)} %concatenate.12.refs_0_, bf16[2,7168,512]{2,1,0:T(8,128)(2,1)} %refs_1_.1), custom_call_target="tpu_custom_call" | custom-call | bytes 14680064 | tf_op jit(solution)/shard_map/fetch/pallas_call | solution.py:124
  12.8 0.0 copy-start
  12.8 5.2 %copy-done = bf16[2,7168,512]{2,1,0:T(8,128)(2,1)} copy-done((bf16[2,7168,512]{2,1,0:T(8,128)(2,1)}, bf16[2,7168,512]{2,1,0:T(8,128)(2,1)S(1)}, u32[]{:S(2)}) %copy-start) | copy-done | bytes 14680088
  18.0 0.0 collective-permute-done.2
  18.0 0.0 collective-permute-done.1
  18.0 0.0 collective-permute-done
  18.0 0.1 pad_maximum_fusion.refs_0_
  18.1 1.7 %collective-permute-start.4 = (bf16[16,7296]{1,0:T(8,128)(2,1)S(1)}, bf16[16,7296]{1,0:T(8,128)(2,1)S(1)}, u32[]{:S(2)}, u32[]{:S(2)}) collective-permute-start(bf16[16,7296]{1,0:T(8,128)(2,1)S(1)} %pad_maximum_fusion.refs_0_), channel_id=1, source_target_pairs={{0,8},{4,12},{8,0},{12,4},{1,9},{5,13},{9,1},{13,5},{2,10},{6,14},... | collective-permute-start | bytes 700424 | tf_op jit(solution)/shard_map/ppermute | solution.py:15
  19.8 1.5 %collective-permute-start.3 = (bf16[16,7296]{1,0:T(8,128)(2,1)S(1)}, bf16[16,7296]{1,0:T(8,128)(2,1)S(1)}, u32[]{:S(2)}, u32[]{:S(2)}) collective-permute-start(bf16[16,7296]{1,0:T(8,128)(2,1)S(1)} %pad_maximum_fusion.refs_0_), channel_id=1, source_target_pairs={{0,4},{4,0},{8,12},{12,8},{1,5},{5,1},{9,13},{13,9},{2,6},{6,2},{1... | collective-permute-start | bytes 700424 | tf_op jit(solution)/shard_map/ppermute | solution.py:15
  21.3 3.7 %collective-permute-done.4.refs_2_ = bf16[16,7296]{1,0:T(8,128)(2,1)S(1)} collective-permute-done((bf16[16,7296]{1,0:T(8,128)(2,1)S(1)}, bf16[16,7296]{1,0:T(8,128)(2,1)S(1)}, u32[]{:S(2)}, u32[]{:S(2)}) %collective-permute-start.4) | collective-permute-done | bytes 233504 | tf_op jit(solution)/shard_map/ppermute | solution.py:15
  25.1 1.6 %collective-permute-start.6 = (bf16[16,3712]{1,0:T(8,128)(2,1)S(1)}, bf16[16,3712]{1,0:T(8,128)(2,1)S(1)}, u32[]{:S(2)}, u32[]{:S(2)}) collective-permute-start(bf16[16,3712]{1,0:T(8,128)(2,1)S(1)} %slice.73), channel_id=1, source_target_pairs={{0,4},{4,0},{8,12},{12,8},{1,5},{5,1},{9,13},{13,9},{2,6},{6,2},{1... | collective-permute-start | bytes 356360 | tf_op jit(solution)/shard_map/ppermute | solution.py:15
  26.6 0.0 collective-permute-start.7
  26.6 0.5 collective-permute-start.9
  27.1 0.0 collective-permute-done.3.refs_1_
  27.1 0.0 collective-permute-start.8
  27.2 1.6 %collective-permute-start.5 = (bf16[16,3584]{1,0:T(8,128)(2,1)S(1)}, bf16[16,3584]{1,0:T(8,128)(2,1)S(1)}, u32[]{:S(2)}, u32[]{:S(2)}) collective-permute-start(bf16[16,3584]{1,0:T(8,128)(2,1)S(1)} %slice.72), channel_id=1, source_target_pairs={{0,8},{4,12},{8,0},{12,4},{1,9},{5,13},{9,1},{13,5},{2,10},{6,14},... | collective-permute-start | bytes 344072 | tf_op jit(solution)/shard_map/ppermute | solution.py:15
  28.7 1.2 %collective-permute-done.6.refs_4_ = bf16[16,3712]{1,0:T(8,128)(2,1)S(1)} collective-permute-done((bf16[16,3712]{1,0:T(8,128)(2,1)S(1)}, bf16[16,3712]{1,0:T(8,128)(2,1)S(1)}, u32[]{:S(2)}, u32[]{:S(2)}) %collective-permute-start.6) | collective-permute-done | bytes 118816 | tf_op jit(solution)/shard_map/ppermute | solution.py:15
  30.0 0.0 collective-permute-start.11
  30.0 2.8 %collective-permute-done.5.refs_3_ = bf16[16,3584]{1,0:T(8,128)(2,1)S(1)} collective-permute-done((bf16[16,3584]{1,0:T(8,128)(2,1)S(1)}, bf16[16,3584]{1,0:T(8,128)(2,1)S(1)}, u32[]{:S(2)}, u32[]{:S(2)}) %collective-permute-start.5) | collective-permute-done | bytes 114720 | tf_op jit(solution)/shard_map/ppermute | solution.py:15
  32.8 0.0 collective-permute-start.10
  32.8 0.0 collective-permute-done.7.refs_5_
  32.8 1.3 %collective-permute-done.10.refs_8_ = bf16[16,3584]{1,0:T(8,128)(2,1)S(1)} collective-permute-done((bf16[16,3584]{1,0:T(8,128)(2,1)S(1)}, bf16[16,3584]{1,0:T(8,128)(2,1)S(1)}, u32[]{:S(2)}, u32[]{:S(2)}) %collective-permute-start.10) | collective-permute-done | bytes 114720 | tf_op jit(solution)/shard_map/ppermute | solution.py:15
  34.1 0.0 collective-permute-done.9.refs_7_
  34.1 0.0 collective-permute-done.8.refs_6_
  34.1 0.0 collective-permute-done.11.refs_9_
  34.1 0.0 copy-start.1
  34.1 5.2 %copy-done.1 = bf16[2,7168,512]{2,1,0:T(8,128)(2,1)S(1)} copy-done((bf16[2,7168,512]{2,1,0:T(8,128)(2,1)S(1)}, bf16[2,7168,512]{2,1,0:T(8,128)(2,1)}, u32[]{:S(2)}) %copy-start.1) | copy-done | bytes 14680088
  39.3 6.0 %gate_up.1.hidden_ref = bf16[128,1024]{1,0:T(8,128)(2,1)S(1)} custom-call(s32[1]{0:T(128)} %bitcast.first_ref, f32[8,128]{1,0:T(8,128)S(1)} %get-tuple-element.16.token_ref, bf16[16,7296]{1,0:T(8,128)(2,1)S(1)} %pad_maximum_fusion.refs_0_, bf16[16,7296]{1,0:T(8,128)(2,1)S(1)} %collective-permute-done.3.refs_1_, ...), custom_call_target="tpu_custom_call" | custom-call | flops 3758096384 | bytes 1835008 | tf_op jit(solution)/shard_map/gate_up/pallas_call | solution.py:149
  45.3 6.3 %down.3 = (bf16[64,3584]{1,0:T(8,128)(2,1)S(1)}, bf16[64,3584]{1,0:T(8,128)(2,1)S(1)}) custom-call(bf16[128,1024]{1,0:T(8,128)(2,1)S(1)} %gate_up.1.hidden_ref, bf16[2,512,7168]{2,1,0:T(8,128)(2,1)} %down_ref.3), custom_call_target="tpu_custom_call" | custom-call | flops 939524096 | bytes 7340032 | tf_op jit(solution)/shard_map/down/pallas_call | solution.py:204
  51.6 0.2 collective-permute-start.18
  51.8 6.3 %down.2 = (bf16[64,3584]{1,0:T(8,128)(2,1)S(1)}, bf16[64,3584]{1,0:T(8,128)(2,1)S(1)}) custom-call(bf16[128,1024]{1,0:T(8,128)(2,1)S(1)} %gate_up.1.hidden_ref, bf16[2,512,7168]{2,1,0:T(8,128)(2,1)} %down_ref.3), custom_call_target="tpu_custom_call" | custom-call | flops 939524096 | bytes 7340032 | tf_op jit(solution)/shard_map/down/pallas_call | solution.py:204
  58.1 0.4 collective-permute-start.12
  58.5 0.0 collective-permute-done.18
  58.5 0.1 add_convert_fusion
  58.7 1.6 %collective-permute-start.19 = (bf16[32,3584]{1,0:T(8,128)(2,1)S(1)}, bf16[32,3584]{1,0:T(8,128)(2,1)S(1)}, u32[]{:S(2)}, u32[]{:S(2)}) collective-permute-start(bf16[32,3584]{1,0:T(8,128)(2,1)S(1)} %slice.83), channel_id=1, source_target_pairs={{0,8},{4,12},{8,0},{12,4},{1,9},{5,13},{9,1},{13,5},{2,10},{6,14},... | collective-permute-start | bytes 688136 | tf_op jit(solution)/shard_map/ppermute | solution.py:15
  60.3 0.0 collective-permute-done.12
  60.3 0.1 add_convert_fusion.1
  60.4 0.7 collective-permute-start.13
  61.2 5.3 %collective-permute-done.19 = bf16[32,3584]{1,0:T(8,128)(2,1)S(1)} collective-permute-done((bf16[32,3584]{1,0:T(8,128)(2,1)S(1)}, bf16[32,3584]{1,0:T(8,128)(2,1)S(1)}, u32[]{:S(2)}, u32[]{:S(2)}) %collective-permute-start.19) | collective-permute-done | bytes 229408 | tf_op jit(solution)/shard_map/ppermute | solution.py:15
  66.4 0.1 add_convert_fusion.2
  66.5 1.0 %collective-permute-start.20 = (bf16[16,3584]{1,0:T(8,128)(2,1)S(1)}, bf16[16,3584]{1,0:T(8,128)(2,1)S(1)}, u32[]{:S(2)}, u32[]{:S(2)}) collective-permute-start(bf16[16,3584]{1,0:T(8,128)(2,1)S(1)} %slice.85), channel_id=1, source_target_pairs={{0,4},{4,0},{8,12},{12,8},{1,5},{5,1},{9,13},{13,9},{2,6},{6,2},{1... | collective-permute-start | bytes 344072 | tf_op jit(solution)/shard_map/ppermute | solution.py:15
  67.5 0.6 collective-permute-done.13
  68.1 0.1 add_convert_fusion.3
  68.1 1.6 %collective-permute-start.14 = (bf16[16,3584]{1,0:T(8,128)(2,1)S(1)}, bf16[16,3584]{1,0:T(8,128)(2,1)S(1)}, u32[]{:S(2)}, u32[]{:S(2)}) collective-permute-start(bf16[16,3584]{1,0:T(8,128)(2,1)S(1)} %slice.77), channel_id=1, source_target_pairs={{0,8},{4,12},{8,0},{12,4},{1,9},{5,13},{9,1},{13,5},{2,10},{6,14},... | collective-permute-start | bytes 344072 | tf_op jit(solution)/shard_map/ppermute | solution.py:15
  69.7 1.6 %collective-permute-done.20 = bf16[16,3584]{1,0:T(8,128)(2,1)S(1)} collective-permute-done((bf16[16,3584]{1,0:T(8,128)(2,1)S(1)}, bf16[16,3584]{1,0:T(8,128)(2,1)S(1)}, u32[]{:S(2)}, u32[]{:S(2)}) %collective-permute-start.20) | collective-permute-done | bytes 114720 | tf_op jit(solution)/shard_map/ppermute | solution.py:15
  71.4 1.4 %collective-permute-start.21 = (bf16[4,3584]{1,0:T(4,128)(2,1)S(1)}, bf16[4,3584]{1,0:T(4,128)(2,1)S(1)}, u32[]{:S(2)}, u32[]{:S(2)}) collective-permute-start(bf16[4,3584]{1,0:T(4,128)(2,1)S(1)} %get-tuple-element.28), channel_id=1, source_target_pairs={{0,1},{1,0},{2,3},{3,2},{4,5},{5,4},{6,7},{7,6},{8,9},{9,8},{10,11... | collective-permute-start | bytes 86024 | tf_op jit(solution)/shard_map/ppermute | solution.py:15
  72.9 2.4 %collective-permute-start.23 = (bf16[4,3584]{1,0:T(4,128)(2,1)S(1)}, bf16[4,3584]{1,0:T(4,128)(2,1)S(1)}, u32[]{:S(2)}, u32[]{:S(2)}) collective-permute-start(bf16[4,3584]{1,0:T(4,128)(2,1)S(1)} %get-tuple-element.29), channel_id=1, source_target_pairs={{0,3},{1,2},{2,1},{3,0},{4,7},{5,6},{6,5},{7,4},{8,11},{9,10},{10,... | collective-permute-start | bytes 86024 | tf_op jit(solution)/shard_map/ppermute | solution.py:15
  75.2 0.3 collective-permute-start.22
  75.5 0.0 collective-permute-done.14
  75.6 1.8 %collective-permute-start.15 = (bf16[4,3584]{1,0:T(4,128)(2,1)S(1)}, bf16[4,3584]{1,0:T(4,128)(2,1)S(1)}, u32[]{:S(2)}, u32[]{:S(2)}) collective-permute-start(bf16[4,3584]{1,0:T(4,128)(2,1)S(1)} %get-tuple-element.25), channel_id=1, source_target_pairs={{0,1},{1,0},{2,3},{3,2},{4,5},{5,4},{6,7},{7,6},{8,9},{9,8},{10,11... | collective-permute-start | bytes 86024 | tf_op jit(solution)/shard_map/ppermute | solution.py:15
  77.4 2.4 %collective-permute-start.17 = (bf16[4,3584]{1,0:T(4,128)(2,1)S(1)}, bf16[4,3584]{1,0:T(4,128)(2,1)S(1)}, u32[]{:S(2)}, u32[]{:S(2)}) collective-permute-start(bf16[4,3584]{1,0:T(4,128)(2,1)S(1)} %get-tuple-element.26), channel_id=1, source_target_pairs={{0,3},{1,2},{2,1},{3,0},{4,7},{5,6},{6,5},{7,4},{8,11},{9,10},{10,... | collective-permute-start | bytes 86024 | tf_op jit(solution)/shard_map/ppermute | solution.py:15
  79.8 0.0 collective-permute-done.21
  79.8 0.0 collective-permute-start.16
  79.8 0.0 collective-permute-done.23
  79.8 0.6 collective-permute-done.22
  80.5 0.0 collective-permute-done.15
  80.5 2.6 %collective-permute-done.17 = bf16[4,3584]{1,0:T(4,128)(2,1)S(1)} collective-permute-done((bf16[4,3584]{1,0:T(4,128)(2,1)S(1)}, bf16[4,3584]{1,0:T(4,128)(2,1)S(1)}, u32[]{:S(2)}, u32[]{:S(2)}) %collective-permute-start.17) | collective-permute-done | bytes 28704 | tf_op jit(solution)/shard_map/ppermute | solution.py:15
  83.1 1.5 %collective-permute-done.16 = bf16[4,3584]{1,0:T(4,128)(2,1)S(1)} collective-permute-done((bf16[4,3584]{1,0:T(4,128)(2,1)S(1)}, bf16[4,3584]{1,0:T(4,128)(2,1)S(1)}, u32[]{:S(2)}, u32[]{:S(2)}) %collective-permute-start.16) | collective-permute-done | bytes 28704 | tf_op jit(solution)/shard_map/ppermute | solution.py:15
  84.6 0.7 pad_maximum_fusion.1
  (13 shorter events, 0.3 us)
Async XLA Ops:
  1.7 16.2 %collective-permute-start.2 = (bf16[4,7296]{1,0:T(4,128)(2,1)S(1)}, bf16[4,7296]{1,0:T(4,128)(2,1)S(1)}, u32[]{:S(2)}, u32[]{:S(2)}) collective-permute-start(bf16[4,7296]{1,0:T(4,128)(2,1)S(1)} %concatenate.12.refs_0_), channel_id=1, source_target_pairs={{0,3},{1,2},{2,1},{3,0},{4,7},{5,6},{6,5},{7,4},{8,11},{9,10},{10,... | collective-permute-start | bytes 175112 | tf_op jit(solution)/shard_map/ppermute | solution.py:15
  6.8 11.2 %collective-permute-start.1 = (bf16[4,7296]{1,0:T(4,128)(2,1)S(1)}, bf16[4,7296]{1,0:T(4,128)(2,1)S(1)}, u32[]{:S(2)}, u32[]{:S(2)}) collective-permute-start(bf16[4,7296]{1,0:T(4,128)(2,1)S(1)} %concatenate.12.refs_0_), channel_id=1, source_target_pairs={{0,2},{1,3},{2,0},{3,1},{4,6},{5,7},{6,4},{7,5},{8,10},{9,11},{10,... | collective-permute-start | bytes 175112 | tf_op jit(solution)/shard_map/ppermute | solution.py:15
  6.8 11.2 %collective-permute-start = (bf16[4,7296]{1,0:T(4,128)(2,1)S(1)}, bf16[4,7296]{1,0:T(4,128)(2,1)S(1)}, u32[]{:S(2)}, u32[]{:S(2)}) collective-permute-start(bf16[4,7296]{1,0:T(4,128)(2,1)S(1)} %concatenate.12.refs_0_), channel_id=1, source_target_pairs={{0,1},{1,0},{2,3},{3,2},{4,5},{5,4},{6,7},{7,6},{8,9},{9,8},{10,11... | collective-permute-start | bytes 175112 | tf_op jit(solution)/shard_map/ppermute | solution.py:15
  12.8 5.2 %copy-start = (bf16[2,7168,512]{2,1,0:T(8,128)(2,1)}, bf16[2,7168,512]{2,1,0:T(8,128)(2,1)S(1)}, u32[]{:S(2)}) copy-start(bf16[2,7168,512]{2,1,0:T(8,128)(2,1)S(1)} %get-tuple-element.20.refs_11_) | copy-start | bytes 44040196
  18.1 6.9 %collective-permute-start.4 = (bf16[16,7296]{1,0:T(8,128)(2,1)S(1)}, bf16[16,7296]{1,0:T(8,128)(2,1)S(1)}, u32[]{:S(2)}, u32[]{:S(2)}) collective-permute-start(bf16[16,7296]{1,0:T(8,128)(2,1)S(1)} %pad_maximum_fusion.refs_0_), channel_id=1, source_target_pairs={{0,8},{4,12},{8,0},{12,4},{1,9},{5,13},{9,1},{13,5},{2,10},{6,14},... | collective-permute-start | bytes 700424 | tf_op jit(solution)/shard_map/ppermute | solution.py:15
  19.8 7.3 %collective-permute-start.3 = (bf16[16,7296]{1,0:T(8,128)(2,1)S(1)}, bf16[16,7296]{1,0:T(8,128)(2,1)S(1)}, u32[]{:S(2)}, u32[]{:S(2)}) collective-permute-start(bf16[16,7296]{1,0:T(8,128)(2,1)S(1)} %pad_maximum_fusion.refs_0_), channel_id=1, source_target_pairs={{0,4},{4,0},{8,12},{12,8},{1,5},{5,1},{9,13},{13,9},{2,6},{6,2},{1... | collective-permute-start | bytes 700424 | tf_op jit(solution)/shard_map/ppermute | solution.py:15
  25.1 4.9 %collective-permute-start.6 = (bf16[16,3712]{1,0:T(8,128)(2,1)S(1)}, bf16[16,3712]{1,0:T(8,128)(2,1)S(1)}, u32[]{:S(2)}, u32[]{:S(2)}) collective-permute-start(bf16[16,3712]{1,0:T(8,128)(2,1)S(1)} %slice.73), channel_id=1, source_target_pairs={{0,4},{4,0},{8,12},{12,8},{1,5},{5,1},{9,13},{13,9},{2,6},{6,2},{1... | collective-permute-start | bytes 356360 | tf_op jit(solution)/shard_map/ppermute | solution.py:15
  26.6 6.2 %collective-permute-start.7 = (bf16[16,7296]{1,0:T(8,128)(2,1)S(1)}, bf16[16,7296]{1,0:T(8,128)(2,1)S(1)}, u32[]{:S(2)}, u32[]{:S(2)}) collective-permute-start(bf16[16,7296]{1,0:T(8,128)(2,1)S(1)} %pad_maximum_fusion.refs_0_), channel_id=1, source_target_pairs={{0,16},{16,0},{1,17},{17,1},{2,18},{18,2},{3,19},{19,3},{4,20},{20... | collective-permute-start | bytes 700424 | tf_op jit(solution)/shard_map/ppermute | solution.py:15
  26.6 7.5 %collective-permute-start.9 = (bf16[16,7296]{1,0:T(8,128)(2,1)S(1)}, bf16[16,7296]{1,0:T(8,128)(2,1)S(1)}, u32[]{:S(2)}, u32[]{:S(2)}) collective-permute-start(bf16[16,7296]{1,0:T(8,128)(2,1)S(1)} %collective-permute-done.4.refs_2_), channel_id=1, source_target_pairs={{0,16},{16,0},{1,17},{17,1},{2,18},{18,2},{3,19},{19,3},{4,20},{20... | collective-permute-start | bytes 700424 | tf_op jit(solution)/shard_map/ppermute | solution.py:15
  27.1 7.0 %collective-permute-start.8 = (bf16[16,7296]{1,0:T(8,128)(2,1)S(1)}, bf16[16,7296]{1,0:T(8,128)(2,1)S(1)}, u32[]{:S(2)}, u32[]{:S(2)}) collective-permute-start(bf16[16,7296]{1,0:T(8,128)(2,1)S(1)} %collective-permute-done.3.refs_1_), channel_id=1, source_target_pairs={{0,16},{16,0},{1,17},{17,1},{2,18},{18,2},{3,19},{19,3},{4,20},{20... | collective-permute-start | bytes 700424 | tf_op jit(solution)/shard_map/ppermute | solution.py:15
  27.2 5.6 %collective-permute-start.5 = (bf16[16,3584]{1,0:T(8,128)(2,1)S(1)}, bf16[16,3584]{1,0:T(8,128)(2,1)S(1)}, u32[]{:S(2)}, u32[]{:S(2)}) collective-permute-start(bf16[16,3584]{1,0:T(8,128)(2,1)S(1)} %slice.72), channel_id=1, source_target_pairs={{0,8},{4,12},{8,0},{12,4},{1,9},{5,13},{9,1},{13,5},{2,10},{6,14},... | collective-permute-start | bytes 344072 | tf_op jit(solution)/shard_map/ppermute | solution.py:15
  30.0 4.1 %collective-permute-start.11 = (bf16[16,3712]{1,0:T(8,128)(2,1)S(1)}, bf16[16,3712]{1,0:T(8,128)(2,1)S(1)}, u32[]{:S(2)}, u32[]{:S(2)}) collective-permute-start(bf16[16,3712]{1,0:T(8,128)(2,1)S(1)} %collective-permute-done.6.refs_4_), channel_id=1, source_target_pairs={{0,16},{16,0},{1,17},{17,1},{2,18},{18,2},{3,19},{19,3},{4,20},{20... | collective-permute-start | bytes 356360 | tf_op jit(solution)/shard_map/ppermute | solution.py:15
  32.8 1.3 %collective-permute-start.10 = (bf16[16,3584]{1,0:T(8,128)(2,1)S(1)}, bf16[16,3584]{1,0:T(8,128)(2,1)S(1)}, u32[]{:S(2)}, u32[]{:S(2)}) collective-permute-start(bf16[16,3584]{1,0:T(8,128)(2,1)S(1)} %collective-permute-done.5.refs_3_), channel_id=1, source_target_pairs={{0,16},{16,0},{1,17},{17,1},{2,18},{18,2},{3,19},{19,3},{4,20},{20... | collective-permute-start | bytes 344072 | tf_op jit(solution)/shard_map/ppermute | solution.py:15
  34.1 5.2 %copy-start.1 = (bf16[2,7168,512]{2,1,0:T(8,128)(2,1)S(1)}, bf16[2,7168,512]{2,1,0:T(8,128)(2,1)}, u32[]{:S(2)}) copy-start(bf16[2,7168,512]{2,1,0:T(8,128)(2,1)} %copy-done) | copy-start | bytes 44040196
  51.6 6.9 %collective-permute-start.18 = (bf16[64,3584]{1,0:T(8,128)(2,1)S(1)}, bf16[64,3584]{1,0:T(8,128)(2,1)S(1)}, u32[]{:S(2)}, u32[]{:S(2)}) collective-permute-start(bf16[64,3584]{1,0:T(8,128)(2,1)S(1)} %get-tuple-element.24), channel_id=1, source_target_pairs={{0,16},{16,0},{1,17},{17,1},{2,18},{18,2},{3,19},{19,3},{4,20},{20... | collective-permute-start | bytes 1376264 | tf_op jit(solution)/shard_map/ppermute | solution.py:15
  58.1 2.1 %collective-permute-start.12 = (bf16[64,3584]{1,0:T(8,128)(2,1)S(1)}, bf16[64,3584]{1,0:T(8,128)(2,1)S(1)}, u32[]{:S(2)}, u32[]{:S(2)}) collective-permute-start(bf16[64,3584]{1,0:T(8,128)(2,1)S(1)} %get-tuple-element.22), channel_id=1, source_target_pairs={{0,16},{16,0},{1,17},{17,1},{2,18},{18,2},{3,19},{19,3},{4,20},{20... | collective-permute-start | bytes 1376264 | tf_op jit(solution)/shard_map/ppermute | solution.py:15
  58.7 7.7 %collective-permute-start.19 = (bf16[32,3584]{1,0:T(8,128)(2,1)S(1)}, bf16[32,3584]{1,0:T(8,128)(2,1)S(1)}, u32[]{:S(2)}, u32[]{:S(2)}) collective-permute-start(bf16[32,3584]{1,0:T(8,128)(2,1)S(1)} %slice.83), channel_id=1, source_target_pairs={{0,8},{4,12},{8,0},{12,4},{1,9},{5,13},{9,1},{13,5},{2,10},{6,14},... | collective-permute-start | bytes 688136 | tf_op jit(solution)/shard_map/ppermute | solution.py:15
  60.4 7.7 %collective-permute-start.13 = (bf16[32,3584]{1,0:T(8,128)(2,1)S(1)}, bf16[32,3584]{1,0:T(8,128)(2,1)S(1)}, u32[]{:S(2)}, u32[]{:S(2)}) collective-permute-start(bf16[32,3584]{1,0:T(8,128)(2,1)S(1)} %slice.75), channel_id=1, source_target_pairs={{0,4},{4,0},{8,12},{12,8},{1,5},{5,1},{9,13},{13,9},{2,6},{6,2},{1... | collective-permute-start | bytes 688136 | tf_op jit(solution)/shard_map/ppermute | solution.py:15
  66.5 4.9 %collective-permute-start.20 = (bf16[16,3584]{1,0:T(8,128)(2,1)S(1)}, bf16[16,3584]{1,0:T(8,128)(2,1)S(1)}, u32[]{:S(2)}, u32[]{:S(2)}) collective-permute-start(bf16[16,3584]{1,0:T(8,128)(2,1)S(1)} %slice.85), channel_id=1, source_target_pairs={{0,4},{4,0},{8,12},{12,8},{1,5},{5,1},{9,13},{13,9},{2,6},{6,2},{1... | collective-permute-start | bytes 344072 | tf_op jit(solution)/shard_map/ppermute | solution.py:15
  68.1 7.4 %collective-permute-start.14 = (bf16[16,3584]{1,0:T(8,128)(2,1)S(1)}, bf16[16,3584]{1,0:T(8,128)(2,1)S(1)}, u32[]{:S(2)}, u32[]{:S(2)}) collective-permute-start(bf16[16,3584]{1,0:T(8,128)(2,1)S(1)} %slice.77), channel_id=1, source_target_pairs={{0,8},{4,12},{8,0},{12,4},{1,9},{5,13},{9,1},{13,5},{2,10},{6,14},... | collective-permute-start | bytes 344072 | tf_op jit(solution)/shard_map/ppermute | solution.py:15
  71.4 8.3 %collective-permute-start.21 = (bf16[4,3584]{1,0:T(4,128)(2,1)S(1)}, bf16[4,3584]{1,0:T(4,128)(2,1)S(1)}, u32[]{:S(2)}, u32[]{:S(2)}) collective-permute-start(bf16[4,3584]{1,0:T(4,128)(2,1)S(1)} %get-tuple-element.28), channel_id=1, source_target_pairs={{0,1},{1,0},{2,3},{3,2},{4,5},{5,4},{6,7},{7,6},{8,9},{9,8},{10,11... | collective-permute-start | bytes 86024 | tf_op jit(solution)/shard_map/ppermute | solution.py:15
  72.9 6.9 %collective-permute-start.23 = (bf16[4,3584]{1,0:T(4,128)(2,1)S(1)}, bf16[4,3584]{1,0:T(4,128)(2,1)S(1)}, u32[]{:S(2)}, u32[]{:S(2)}) collective-permute-start(bf16[4,3584]{1,0:T(4,128)(2,1)S(1)} %get-tuple-element.29), channel_id=1, source_target_pairs={{0,3},{1,2},{2,1},{3,0},{4,7},{5,6},{6,5},{7,4},{8,11},{9,10},{10,... | collective-permute-start | bytes 86024 | tf_op jit(solution)/shard_map/ppermute | solution.py:15
  75.2 5.2 %collective-permute-start.22 = (bf16[4,3584]{1,0:T(4,128)(2,1)S(1)}, bf16[4,3584]{1,0:T(4,128)(2,1)S(1)}, u32[]{:S(2)}, u32[]{:S(2)}) collective-permute-start(bf16[4,3584]{1,0:T(4,128)(2,1)S(1)} %get-tuple-element.30), channel_id=1, source_target_pairs={{0,2},{1,3},{2,0},{3,1},{4,6},{5,7},{6,4},{7,5},{8,10},{9,11},{10,... | collective-permute-start | bytes 86024 | tf_op jit(solution)/shard_map/ppermute | solution.py:15
  75.6 4.9 %collective-permute-start.15 = (bf16[4,3584]{1,0:T(4,128)(2,1)S(1)}, bf16[4,3584]{1,0:T(4,128)(2,1)S(1)}, u32[]{:S(2)}, u32[]{:S(2)}) collective-permute-start(bf16[4,3584]{1,0:T(4,128)(2,1)S(1)} %get-tuple-element.25), channel_id=1, source_target_pairs={{0,1},{1,0},{2,3},{3,2},{4,5},{5,4},{6,7},{7,6},{8,9},{9,8},{10,11... | collective-permute-start | bytes 86024 | tf_op jit(solution)/shard_map/ppermute | solution.py:15
  77.4 5.7 %collective-permute-start.17 = (bf16[4,3584]{1,0:T(4,128)(2,1)S(1)}, bf16[4,3584]{1,0:T(4,128)(2,1)S(1)}, u32[]{:S(2)}, u32[]{:S(2)}) collective-permute-start(bf16[4,3584]{1,0:T(4,128)(2,1)S(1)} %get-tuple-element.26), channel_id=1, source_target_pairs={{0,3},{1,2},{2,1},{3,0},{4,7},{5,6},{6,5},{7,4},{8,11},{9,10},{10,... | collective-permute-start | bytes 86024 | tf_op jit(solution)/shard_map/ppermute | solution.py:15
  79.8 4.8 %collective-permute-start.16 = (bf16[4,3584]{1,0:T(4,128)(2,1)S(1)}, bf16[4,3584]{1,0:T(4,128)(2,1)S(1)}, u32[]{:S(2)}, u32[]{:S(2)}) collective-permute-start(bf16[4,3584]{1,0:T(4,128)(2,1)S(1)} %get-tuple-element.27), channel_id=1, source_target_pairs={{0,2},{1,3},{2,0},{3,1},{4,6},{5,7},{6,4},{7,5},{8,10},{9,11},{10,... | collective-permute-start | bytes 86024 | tf_op jit(solution)/shard_map/ppermute | solution.py:15

commit v5 on v4

v5 whole, which is shorter than its diff:
```python
import functools

import jax
import jax.numpy as jnp
from jax import lax
from jax.experimental import pallas as pl
from jax.experimental.pallas import tpu as pltpu
from jax.sharding import PartitionSpec as P

AXES = ("sect", "grp", "dev")
CHUNKS = 2


def swap(value, axis, mask):
    return lax.ppermute(value, axis, [(i, i ^ mask) for i in range(lax.axis_size(axis))])


def bits_of(size):
    return [1 << b for b in range(size.bit_length() - 1)]


def vmem_call(kernel, out_shape, name, *operands):
    whole = pl.BlockSpec(memory_space=pltpu.VMEM)
    return pl.pallas_call(
        kernel,
        out_shape=out_shape,
        in_specs=[whole] * len(operands),
        out_specs=jax.tree.map(lambda _: whole, out_shape),
        compiler_params=pltpu.CompilerParams(vmem_limit_bytes=4 * 2**20),
        name=name,
    )(*operands)


def extend_kernel(tokens_ref, ids_ref, weights_ref, out_ref):
    rows, width = tokens_ref.shape
    half = (out_ref.shape[1] - width) // 2
    lane = lax.broadcasted_iota(jnp.int32, (rows, half * 2), 1)
    dense = jnp.zeros((rows, half * 2), jnp.float32)
    for k in range(ids_ref.shape[1]):
        mine = lax.rem(lane, half) == ids_ref[:, k:k + 1]
        dense = dense + jnp.where(mine, weights_ref[:, k:k + 1], 0.0)
    high = dense.astype(jnp.bfloat16).astype(jnp.float32)
    out_ref[:, :width] = tokens_ref[...]
    out_ref[:, width:] = jnp.where(lane < half, high, dense - high).astype(jnp.bfloat16)


def extend(tokens, ids, weights, half):
    rows, width = tokens.shape
    out = jax.ShapeDtypeStruct((rows, width + 2 * half), tokens.dtype)
    return vmem_call(extend_kernel, out, "extend", tokens, ids, weights)


def join_kernel(*refs):
    pieces, out_ref = refs[:-1], refs[-1]
    values = [p[...].astype(jnp.float32) for p in pieces]
    out_ref[...] = jnp.concatenate(values, axis=0).astype(out_ref.dtype)


def join(pieces):
    rows, width = pieces[0].shape
    out = jax.ShapeDtypeStruct((rows * len(pieces), width), pieces[0].dtype)
    return vmem_call(join_kernel, out, "join", *pieces)


def halves_kernel(left_ref, right_ref, left_out, right_out):
    half = left_out.shape[1]
    left_out[...] = left_ref[:, :half]
    right_out[...] = right_ref[:, half:]


def halves(left, right):
    rows, width = left.shape
    half = width // 256 * 128
    out = (
        jax.ShapeDtypeStruct((rows, half), left.dtype),
        jax.ShapeDtypeStruct((rows, width - half), left.dtype),
    )
    return vmem_call(halves_kernel, out, "halves", left, right)


def gather_rows(block, w_gate, w_up):
    lanes, groups, sects = (lax.axis_size(a) for a in ("dev", "grp", "sect"))
    arrived = [swap(block, "dev", m) for m in range(1, lanes)]
    w_gate, token = fetch(w_gate, (block,))
    arrived, token = lax.optimization_barrier((arrived, token))
    line = join([block] + arrived)
    if groups == 4:
        by_x, by_y = swap(line, "grp", 1), swap(line, "grp", 2)
        w_up, token, w_gate = fetch(w_up, (line, token), (w_gate,))
        by_x, by_y, token = lax.optimization_barrier((by_x, by_y, token))
        from_x, from_y = halves(by_x, by_y)
        corner = [swap(from_x, "grp", 2), swap(from_y, "grp", 1)]
        entries = [[line], [by_x], [by_y], corner]
    else:
        entries = [[line]]
        w_up, token, w_gate = fetch(w_up, (line, token), (w_gate,))
        for bit in bits_of(groups):
            entries = entries + [[swap(p, "grp", bit) for p in e] for e in entries]
    for bit in bits_of(sects):
        entries = entries + [[swap(p, "sect", bit) for p in e] for e in entries]
    return entries, w_gate, w_up, token


def up_kernel(layout, width, first_ref, token_ref, *refs):
    pieces = refs[: sum(layout)]
    gate_ref, upw_ref, down_hbm, hidden_ref, down_ref, rows_ref, value_ref, sems = refs[
        sum(layout):
    ]
    experts, _, hidden = upw_ref.shape
    line = pieces[0].shape[0]
    block = min(256, hidden)

    def copies(e):
        for c in range(width // hidden):
            yield pltpu.make_async_copy(
                down_hbm.at[e, :, pl.ds(c * hidden, hidden)],
                down_ref.at[e, pl.ds(c * hidden, hidden)],
                sems.at[e, c],
            )

    at = 0
    for entry, count in enumerate(layout):
        left = 0
        for piece in pieces[at:at + count]:
            rows_ref[pl.ds(entry * line, line), pl.ds(left, piece.shape[1])] = piece[...]
            left += piece.shape[1]
        at += count

    for e in range(experts):

        @pl.loop(0, hidden // block)
        def _(step):
            span = pl.ds(pl.multiple_of(step * block, block), block)
            gate = jnp.dot(
                rows_ref[:, :width], gate_ref[e, :, span], preferred_element_type=jnp.float32
            )
            value_ref[e, :, span] = gate / (1.0 + jnp.exp(-gate))

        for copy in copies(e):
            copy.start()

    extra = rows_ref[:, width:].astype(jnp.float32)
    lane = lax.broadcasted_iota(jnp.int32, extra.shape, 1)
    for e in range(experts):
        mine = lax.rem(lane, extra.shape[1] // 2) == first_ref[0] + e
        scale = jnp.sum(jnp.where(mine, extra, 0.0), axis=1, keepdims=True)

        @pl.loop(0, hidden // block)
        def _(step):
            span = pl.ds(pl.multiple_of(step * block, block), block)
            up = jnp.dot(
                rows_ref[:, :width], upw_ref[e, :, span], preferred_element_type=jnp.float32
            )
            out = pl.ds(pl.multiple_of(e * hidden + step * block, block), block)
            hidden_ref[:, out] = (value_ref[e, :, span] * up * scale).astype(jnp.bfloat16)

    for e in range(experts):
        for copy in copies(e):
            copy.wait()


def fetch_kernel(parts, *refs):
    source_ref, target_ref, token_ref, *_, sems = refs
    depth = source_ref.shape[1] // parts
    copies = [
        pltpu.make_async_copy(
            source_ref.at[e, pl.ds(p * depth, depth)],
            target_ref.at[e, pl.ds(p * depth, depth)],
            sems.at[e * parts + p],
        )
        for e in range(source_ref.shape[0])
        for p in range(parts)
    ]
    for copy in copies:
        copy.start()
    token_ref[...] = jnp.zeros_like(token_ref)
    for copy in copies:
        copy.wait()


def fetch(weight, after, carried=()):
    parts = 4
    in_hbm = pl.BlockSpec(memory_space=pl.ANY)
    in_vmem = pl.BlockSpec(memory_space=pltpu.VMEM)
    carry, pins = len(carried), [pltpu.with_memory_space_constraint(c, pltpu.VMEM) for c in carried]

    def kernel(*refs):
        fetch_kernel(parts, *refs[len(after) + carry:])

    return pl.pallas_call(
        kernel,
        out_shape=(
            pltpu.VMEM(weight.shape, weight.dtype),
            jax.ShapeDtypeStruct((8, 128), jnp.float32),
        )
        + tuple(pltpu.VMEM(c.shape, c.dtype) for c in carried),
        in_specs=[in_hbm] * len(after) + [in_vmem] * carry + [in_hbm],
        out_specs=(in_vmem,) * (2 + carry),
        input_output_aliases={len(after) + i: 2 + i for i in range(carry)},
        scratch_shapes=[pltpu.SemaphoreType.DMA((weight.shape[0] * parts,))],
        compiler_params=pltpu.CompilerParams(vmem_limit_bytes=2**20),
        cost_estimate=pl.CostEstimate(
            flops=0, bytes_accessed=2 * weight.size, transcendentals=0
        ),
        name="fetch",
    )(*after, *pins, pltpu.with_memory_space_constraint(weight, pltpu.HBM))


def up_call(first, entries, w_gate, w_up, w_down, token):
    layout = [len(e) for e in entries]
    flat = [p for e in entries for p in e]
    experts, width, hidden = w_up.shape
    line = flat[0].shape[0]
    full = sum(p.shape[1] for p in entries[0])
    rows = line * len(entries)
    whole = pl.BlockSpec(memory_space=pltpu.VMEM)
    anywhere = pl.BlockSpec(memory_space=pl.ANY)
    return pl.pallas_call(
        functools.partial(up_kernel, layout, width),
        out_shape=(
            jax.ShapeDtypeStruct((rows, experts * hidden), jnp.bfloat16),
            pltpu.VMEM(w_gate.shape, w_gate.dtype),
        ),
        in_specs=[pl.BlockSpec(memory_space=pltpu.SMEM), anywhere]
        + [whole] * (len(flat) + 2)
        + [anywhere],
        out_specs=(whole, whole),
        scratch_shapes=[
            pltpu.VMEM((rows, full), jnp.bfloat16),
            pltpu.VMEM((experts, rows, hidden), jnp.float32),
            pltpu.SemaphoreType.DMA((experts, width // hidden)),
        ],
        input_output_aliases={2 + len(flat): 1},
        compiler_params=pltpu.CompilerParams(vmem_limit_bytes=kernel_bytes(rows, full)),
        cost_estimate=pl.CostEstimate(
            flops=4 * rows * experts * width * hidden,
            bytes_accessed=2 * w_down.size,
            transcendentals=rows * experts * hidden,
        ),
        name="gate_up",
    )(
        first,
        token,
        *flat,
        pltpu.with_memory_space_constraint(w_gate, pltpu.VMEM),
        pltpu.with_memory_space_constraint(w_up, pltpu.VMEM),
        pltpu.with_memory_space_constraint(w_down, pltpu.HBM),
    )


def kernel_bytes(rows, width):
    return 2 * rows * width + 4 * 2**20


def down_kernel(order, line, start, hidden_ref, down_ref, keep_ref, send_ref):
    experts, _, hidden = down_ref.shape
    groups = len(order)

    @pl.loop(0, keep_ref.shape[1] // hidden)
    def _(step):
        rows = pl.ds(pl.multiple_of((start // hidden + step) * hidden, hidden), hidden)
        weight = down_ref[:, rows, :].reshape(experts * hidden, hidden)
        total = jnp.dot(hidden_ref[...], weight, preferred_element_type=jnp.float32)
        total = total.astype(jnp.bfloat16)
        columns = pl.ds(pl.multiple_of(step * hidden, hidden), hidden)
        for place, entry in enumerate(order):
            rows = pl.ds(place * line, line)
            keep_ref[rows, columns] = total[entry * line:(entry + 1) * line]
            low = (groups + entry) * line
            send_ref[rows, columns] = total[low:low + line]


def down_call(order, line, hidden, w_down, start, columns):
    rows = line * len(order)
    out = jax.ShapeDtypeStruct((rows, columns), jnp.bfloat16)
    whole = pl.BlockSpec(memory_space=pltpu.VMEM)
    return pl.pallas_call(
        functools.partial(down_kernel, order, line, start),
        out_shape=(out, out),
        in_specs=[whole, whole],
        out_specs=(whole, whole),
        compiler_params=pltpu.CompilerParams(vmem_limit_bytes=4 * 2**20),
        cost_estimate=pl.CostEstimate(
            flops=2 * hidden.size * columns,
            bytes_accessed=4 * rows * columns,
            transcendentals=0,
        ),
        name="down",
    )(hidden, pltpu.with_memory_space_constraint(w_down, pltpu.VMEM))


def add(*values):
    total = values[0].astype(jnp.float32)
    for value in values[1:]:
        total = total + value.astype(jnp.float32)
    return total.astype(jnp.bfloat16)


def body(tokens, expert_ids, gate_weights, w_gate, w_up, w_down):
    sects, groups, lanes = (lax.axis_size(a) for a in AXES)
    row_count, width = tokens.shape
    experts = w_gate.shape[0]
    expert_count = sects * groups * experts
    first = lax.axis_index(("sect", "grp")).astype(jnp.int32) * experts

    half = -(-expert_count // 64) * 64
    block = extend(tokens, expert_ids, gate_weights, half)
    entries, w_gate, w_up, token = gather_rows(block, w_gate, w_up)
    hidden, w_down = up_call(first.reshape(1), entries, w_gate, w_up, w_down, token)

    line = lanes * row_count
    results = []
    chunk = width // CHUNKS
    for c in range(CHUNKS):
        bits = bits_of(groups)
        bits = bits if c % 2 else bits[::-1]
        order = [0]
        for bit in bits:
            order = order + [o | bit for o in order]
        keep, send = down_call(order, line, hidden, w_down, c * chunk, chunk)
        value = add(keep, swap(send, "sect", 1))
        for bit in bits[::-1]:
            middle = value.shape[0] // 2
            arrived = swap(value[middle:], "grp", bit)
            value = add(value[:middle], arrived)
        pieces = [value[:row_count]]
        for m in range(1, lanes):
            pieces.append(swap(value[m * row_count:(m + 1) * row_count], "dev", m))
        results.append(add(*pieces))
    return jnp.concatenate(results, axis=1)


def solution(mesh):
    in_specs = (
        P(AXES, None),
        P(AXES, None),
        P(AXES, None),
        P(("sect", "grp"), None, "dev"),
        P(("sect", "grp"), None, "dev"),
        P(("sect", "grp"), "dev", None),
    )
    return jax.shard_map(
        body, mesh=mesh, in_specs=in_specs, out_specs=P(AXES, None), check_vma=False
    )
```

time: 85.7 us -> 100 us (1.17)
  local copies, waits for them, and re-layouts: 11.4 us -> 33.4 us
  starting transfers between devices: 26.4 us -> 23.4 us
  waiting for transfers between devices: 21.3 us -> 19.5 us
  Pallas kernels: 23.9 us -> 22.3 us
    unnamed x4 -> x18, local copies, waits for them, and re-layouts: 10.4 us -> 33.3 us
    ppermute x24, starting transfers between devices: 26.4 us -> 23.4 us  [swap(): lax.ppermute(value, axis, [(i, i ^ mask) for i in range(lax.axis_size(axi...]
    ppermute x24, waiting for transfers between devices: 21.3 us -> 19.5 us  [swap(): lax.ppermute(value, axis, [(i, i ^ mask) for i in range(lax.axis_size(axi...]
    pallas_call x4 -> x8, Pallas kernels: 23.9 us -> 22.3 us  [the longest x2 10.6 us: fetch(): pl.pallas_call(kernel, out_shape=(pltpu.VMEM(weight.shape, weight.dtype),...]
  transfers between devices with their start and end apart: 24 -> 24, of which waited for: 10 -> 9; matrix products, arithmetic and copies ran while one was open for 1% -> 1% of each run, Pallas kernels for 14% -> 13%
where the time goes in v5:
time: 100 us
  local copies, waits for them, and re-layouts  33.4 us (33%)
  starting transfers between devices  23.4 us (23%)
  Pallas kernels  22.3 us (22%)
  waiting for transfers between devices  19.5 us (20%)
  other arithmetic  1.1 us (1%)
    unnamed x18, local copies, waits for them, and re-layouts  33.3 us
    ppermute x24, starting transfers between devices, swap(): lax.ppermute(value, axis, [(i, i ^ mask) for i in range(lax.axis_size(axi...  23.4 us
    ppermute x24, waiting for transfers between devices, swap(): lax.ppermute(value, axis, [(i, i ^ mask) for i in range(lax.axis_size(axi...  19.5 us
    pallas_call x2, Pallas kernels, fetch(): pl.pallas_call(kernel, out_shape=(pltpu.VMEM(weight.shape, weight.dtype),...  10.6 us
    pallas_call x1, Pallas kernels, up_call(): pl.pallas_call(functools.partial(up_kernel, layout, width), out_shape=(ja...  7.07 us
    pallas_call x2, Pallas kernels, down_call(): pl.pallas_call(functools.partial(down_kernel, order, line, start), out_sh...  4.47 us
  transfers between devices with their start and end apart: 24, of which 9 were waited for; matrix products, arithmetic and copies ran while one was open for 1% of the time, Pallas kernels for 13%

profile of v5, /device:TPU:0, one launch (start us, length us, event | category | flops | bytes accessed | tf_op | source)
XLA Modules:
  0.0 100.0 jit_solution(8013748057069087011)
XLA Ops:
  0.0 0.8 copy-done.6
  0.8 0.7 copy-done.7
  1.5 0.7 copy-done.8
  2.2 0.1 extend.1.refs_0_
  2.3 5.1 %collective-permute-start.2 = (bf16[4,7296]{1,0:T(4,128)(2,1)S(1)}, bf16[4,7296]{1,0:T(4,128)(2,1)S(1)}, u32[]{:S(2)}, u32[]{:S(2)}) collective-permute-start(bf16[4,7296]{1,0:T(4,128)(2,1)S(1)} %extend.1.refs_0_), channel_id=1, source_target_pairs={{0,3},{1,2},{2,1},{3,0},{4,7},{5,6},{6,5},{7,4},{8,11},{9,10},{10,... | collective-permute-start | bytes 175112 | tf_op jit(solution)/shard_map/ppermute | solution.py:15
  7.4 0.0 collective-permute-start.1
  7.4 0.6 collective-permute-start
  8.0 5.3 %fetch.2 = (bf16[2,7168,512]{2,1,0:T(8,128)(2,1)S(1)}, f32[8,128]{1,0:T(8,128)S(1)}) custom-call(bf16[4,7296]{1,0:T(4,128)(2,1)S(1)} %extend.1.refs_0_, bf16[2,7168,512]{2,1,0:T(8,128)(2,1)} %refs_1_.1), custom_call_target="tpu_custom_call" | custom-call | bytes 14680064 | tf_op jit(solution)/shard_map/fetch/pallas_call | solution.py:190
  13.4 0.0 collective-permute-done.refs_1_
  13.4 0.1 join.1.refs_0_
  13.5 1.7 %collective-permute-start.4 = (bf16[16,7296]{1,0:T(8,128)(2,1)S(1)}, bf16[16,7296]{1,0:T(8,128)(2,1)S(1)}, u32[]{:S(2)}, u32[]{:S(2)}) collective-permute-start(bf16[16,7296]{1,0:T(8,128)(2,1)S(1)} %join.1.refs_0_), channel_id=1, source_target_pairs={{0,8},{4,12},{8,0},{12,4},{1,9},{5,13},{9,1},{13,5},{2,10},{6,14},... | collective-permute-start | bytes 700424 | tf_op jit(solution)/shard_map/ppermute | solution.py:15
  15.2 1.5 %collective-permute-start.3 = (bf16[16,7296]{1,0:T(8,128)(2,1)S(1)}, bf16[16,7296]{1,0:T(8,128)(2,1)S(1)}, u32[]{:S(2)}, u32[]{:S(2)}) collective-permute-start(bf16[16,7296]{1,0:T(8,128)(2,1)S(1)} %join.1.refs_0_), channel_id=1, source_target_pairs={{0,4},{4,0},{8,12},{12,8},{1,5},{5,1},{9,13},{13,9},{2,6},{6,2},{1... | collective-permute-start | bytes 700424 | tf_op jit(solution)/shard_map/ppermute | solution.py:15
  16.7 5.3 %fetch.3 = (bf16[2,7168,512]{2,1,0:T(8,128)(2,1)S(1)}, f32[8,128]{1,0:T(8,128)S(1)}, bf16[2,7168,512]{2,1,0:T(8,128)(2,1)S(1)}) custom-call(bf16[16,7296]{1,0:T(8,128)(2,1)S(1)} %join.1.refs_0_, f32[8,128]{1,0:T(8,128)S(1)} %get-tuple-element.29.refs_1_, bf16[2,7168,512]{2,1,0:T(8,128)(2,1)S(1)} %get-tuple-element.30.refs_2_, ...), custom_call_target="tpu_custom_call", output_to_operand_aliasing={{2}: (2, {})} | custom-call | bytes 14680064 | tf_op jit(solution)/shard_map/fetch/pallas_call | solution.py:190
  22.0 5.2 %copy-done = bf16[2,7168,512]{2,1,0:T(8,128)(2,1)} copy-done((bf16[2,7168,512]{2,1,0:T(8,128)(2,1)}, bf16[2,7168,512]{2,1,0:T(8,128)(2,1)S(1)}, u32[]{:S(2)}) %copy-start) | copy-done | bytes 14680088
  27.2 5.1 %copy-done.4 = bf16[2,7168,512]{2,1,0:T(8,128)(2,1)} copy-done((bf16[2,7168,512]{2,1,0:T(8,128)(2,1)}, bf16[2,7168,512]{2,1,0:T(8,128)(2,1)S(1)}, u32[]{:S(2)}) %copy-start.4) | copy-done | bytes 14680088
  32.4 0.0 collective-permute-done.4.right_ref.refs_2_
  32.4 0.0 collective-permute-done.3.left_ref.refs_1_
  32.4 0.6 collective-permute-start.6
  33.0 0.0 collective-permute-start.7
  33.0 0.5 collective-permute-start.8
  33.5 0.4 collective-permute-start.5
  33.9 3.4 %collective-permute-done.6.refs_4_ = bf16[16,3712]{1,0:T(8,128)(2,1)S(1)} collective-permute-done((bf16[16,3712]{1,0:T(8,128)(2,1)S(1)}, bf16[16,3712]{1,0:T(8,128)(2,1)S(1)}, u32[]{:S(2)}, u32[]{:S(2)}) %collective-permute-start.6) | collective-permute-done | bytes 118816 | tf_op jit(solution)/shard_map/ppermute | solution.py:15
  37.3 0.0 collective-permute-start.11
  37.3 1.8 %collective-permute-done.5.refs_3_ = bf16[16,3584]{1,0:T(8,128)(2,1)S(1)} collective-permute-done((bf16[16,3584]{1,0:T(8,128)(2,1)S(1)}, bf16[16,3584]{1,0:T(8,128)(2,1)S(1)}, u32[]{:S(2)}, u32[]{:S(2)}) %collective-permute-start.5) | collective-permute-done | bytes 114720 | tf_op jit(solution)/shard_map/ppermute | solution.py:15
  39.1 0.0 collective-permute-start.10
  39.1 0.0 collective-permute-done.7.refs_5_
  39.1 1.3 %collective-permute-done.10.refs_8_ = bf16[16,3584]{1,0:T(8,128)(2,1)S(1)} collective-permute-done((bf16[16,3584]{1,0:T(8,128)(2,1)S(1)}, bf16[16,3584]{1,0:T(8,128)(2,1)S(1)}, u32[]{:S(2)}, u32[]{:S(2)}) %collective-permute-start.10) | collective-permute-done | bytes 114720 | tf_op jit(solution)/shard_map/ppermute | solution.py:15
  40.4 0.0 collective-permute-done.8.refs_6_
  40.4 0.0 collective-permute-done.9.refs_7_
  40.4 0.0 collective-permute-done.11.refs_9_
  40.4 5.2 %copy-done.1 = bf16[2,7168,512]{2,1,0:T(8,128)(2,1)S(1)} copy-done((bf16[2,7168,512]{2,1,0:T(8,128)(2,1)S(1)}, bf16[2,7168,512]{2,1,0:T(8,128)(2,1)}, u32[]{:S(2)}) %copy-start.1) | copy-done | bytes 14680088
  45.6 5.2 %copy-done.5 = bf16[2,7168,512]{2,1,0:T(8,128)(2,1)S(1)} copy-done((bf16[2,7168,512]{2,1,0:T(8,128)(2,1)S(1)}, bf16[2,7168,512]{2,1,0:T(8,128)(2,1)}, u32[]{:S(2)}) %copy-start.5) | copy-done | bytes 14680088
  50.7 7.1 %gate_up.1 = (bf16[128,1024]{1,0:T(8,128)(2,1)S(1)}, bf16[2,7168,512]{2,1,0:T(8,128)(2,1)S(1)}) custom-call(s32[1]{0:T(128)} %bitcast.first_ref, f32[8,128]{1,0:T(8,128)S(1)} %get-tuple-element.32.token_ref, bf16[16,7296]{1,0:T(8,128)(2,1)S(1)} %join.1.refs_0_, ...), custom_call_target="tpu_custom_call", output_to_operand_aliasing={{1}: (12, {})} | custom-call | flops 3758096384 | bytes 14680064 | tf_op jit(solution)/shard_map/gate_up/pallas_call | solution.py:218
  57.8 5.2 %copy-done.2 = bf16[2,7168,512]{2,1,0:T(8,128)(2,1)} copy-done((bf16[2,7168,512]{2,1,0:T(8,128)(2,1)}, bf16[2,7168,512]{2,1,0:T(8,128)(2,1)S(1)}, u32[]{:S(2)}) %copy-start.2) | copy-done | bytes 14680088
  63.0 5.2 %copy-done.3 = bf16[2,7168,512]{2,1,0:T(8,128)(2,1)S(1)} copy-done((bf16[2,7168,512]{2,1,0:T(8,128)(2,1)S(1)}, bf16[2,7168,512]{2,1,0:T(8,128)(2,1)}, u32[]{:S(2)}) %copy-start.3) | copy-done | bytes 14680088
  68.2 2.2 %down.3 = (bf16[64,3584]{1,0:T(8,128)(2,1)S(1)}, bf16[64,3584]{1,0:T(8,128)(2,1)S(1)}) custom-call(bf16[128,1024]{1,0:T(8,128)(2,1)S(1)} %get-tuple-element.39.hidden_ref, bf16[2,7168,512]{2,1,0:T(8,128)(2,1)S(1)} %copy-done.3), custom_call_target="tpu_custom_call" | custom-call | flops 939524096 | bytes 917504 | tf_op jit(solution)/shard_map/down/pallas_call | solution.py:277
  70.5 0.2 collective-permute-start.18
  70.7 2.2 %down.2 = (bf16[64,3584]{1,0:T(8,128)(2,1)S(1)}, bf16[64,3584]{1,0:T(8,128)(2,1)S(1)}) custom-call(bf16[128,1024]{1,0:T(8,128)(2,1)S(1)} %get-tuple-element.39.hidden_ref, bf16[2,7168,512]{2,1,0:T(8,128)(2,1)S(1)} %copy-done.3), custom_call_target="tpu_custom_call" | custom-call | flops 939524096 | bytes 917504 | tf_op jit(solution)/shard_map/down/pallas_call | solution.py:277
  72.9 0.4 collective-permute-start.12
  73.3 0.1 add_convert_fusion
  73.5 0.4 collective-permute-start.19
  73.9 0.9 collective-permute-done.12
  74.8 0.1 add_convert_fusion.1
  74.9 1.6 %collective-permute-start.13 = (bf16[32,3584]{1,0:T(8,128)(2,1)S(1)}, bf16[32,3584]{1,0:T(8,128)(2,1)S(1)}, u32[]{:S(2)}, u32[]{:S(2)}) collective-permute-start(bf16[32,3584]{1,0:T(8,128)(2,1)S(1)} %slice.65), channel_id=1, source_target_pairs={{0,4},{4,0},{8,12},{12,8},{1,5},{5,1},{9,13},{13,9},{2,6},{6,2},{1... | collective-permute-start | bytes 688136 | tf_op jit(solution)/shard_map/ppermute | solution.py:15
  76.5 4.7 %collective-permute-done.19 = bf16[32,3584]{1,0:T(8,128)(2,1)S(1)} collective-permute-done((bf16[32,3584]{1,0:T(8,128)(2,1)S(1)}, bf16[32,3584]{1,0:T(8,128)(2,1)S(1)}, u32[]{:S(2)}, u32[]{:S(2)}) %collective-permute-start.19) | collective-permute-done | bytes 229408 | tf_op jit(solution)/shard_map/ppermute | solution.py:15
  81.2 0.1 add_convert_fusion.2
  81.3 1.5 %collective-permute-start.20 = (bf16[16,3584]{1,0:T(8,128)(2,1)S(1)}, bf16[16,3584]{1,0:T(8,128)(2,1)S(1)}, u32[]{:S(2)}, u32[]{:S(2)}) collective-permute-start(bf16[16,3584]{1,0:T(8,128)(2,1)S(1)} %slice.75), channel_id=1, source_target_pairs={{0,4},{4,0},{8,12},{12,8},{1,5},{5,1},{9,13},{13,9},{2,6},{6,2},{1... | collective-permute-start | bytes 344072 | tf_op jit(solution)/shard_map/ppermute | solution.py:15
  82.8 0.0 collective-permute-done.13
  82.9 0.1 add_convert_fusion.3
  82.9 0.5 collective-permute-start.14
  83.5 2.6 %collective-permute-done.20 = bf16[16,3584]{1,0:T(8,128)(2,1)S(1)} collective-permute-done((bf16[16,3584]{1,0:T(8,128)(2,1)S(1)}, bf16[16,3584]{1,0:T(8,128)(2,1)S(1)}, u32[]{:S(2)}, u32[]{:S(2)}) %collective-permute-start.20) | collective-permute-done | bytes 114720 | tf_op jit(solution)/shard_map/ppermute | solution.py:15
  86.2 1.3 %collective-permute-start.21 = (bf16[4,3584]{1,0:T(4,128)(2,1)S(1)}, bf16[4,3584]{1,0:T(4,128)(2,1)S(1)}, u32[]{:S(2)}, u32[]{:S(2)}) collective-permute-start(bf16[4,3584]{1,0:T(4,128)(2,1)S(1)} %get-tuple-element.48), channel_id=1, source_target_pairs={{0,1},{1,0},{2,3},{3,2},{4,5},{5,4},{6,7},{7,6},{8,9},{9,8},{10,11... | collective-permute-start | bytes 86024 | tf_op jit(solution)/shard_map/ppermute | solution.py:15
  87.5 2.5 %collective-permute-start.23 = (bf16[4,3584]{1,0:T(4,128)(2,1)S(1)}, bf16[4,3584]{1,0:T(4,128)(2,1)S(1)}, u32[]{:S(2)}, u32[]{:S(2)}) collective-permute-start(bf16[4,3584]{1,0:T(4,128)(2,1)S(1)} %get-tuple-element.49), channel_id=1, source_target_pairs={{0,3},{1,2},{2,1},{3,0},{4,7},{5,6},{6,5},{7,4},{8,11},{9,10},{10,... | collective-permute-start | bytes 86024 | tf_op jit(solution)/shard_map/ppermute | solution.py:15
  90.0 0.5 collective-permute-start.22
  90.4 0.0 collective-permute-done.14
  90.5 1.5 %collective-permute-start.15 = (bf16[4,3584]{1,0:T(4,128)(2,1)S(1)}, bf16[4,3584]{1,0:T(4,128)(2,1)S(1)}, u32[]{:S(2)}, u32[]{:S(2)}) collective-permute-start(bf16[4,3584]{1,0:T(4,128)(2,1)S(1)} %get-tuple-element.45), channel_id=1, source_target_pairs={{0,1},{1,0},{2,3},{3,2},{4,5},{5,4},{6,7},{7,6},{8,9},{9,8},{10,11... | collective-permute-start | bytes 86024 | tf_op jit(solution)/shard_map/ppermute | solution.py:15
  92.0 2.5 %collective-permute-start.17 = (bf16[4,3584]{1,0:T(4,128)(2,1)S(1)}, bf16[4,3584]{1,0:T(4,128)(2,1)S(1)}, u32[]{:S(2)}, u32[]{:S(2)}) collective-permute-start(bf16[4,3584]{1,0:T(4,128)(2,1)S(1)} %get-tuple-element.46), channel_id=1, source_target_pairs={{0,3},{1,2},{2,1},{3,0},{4,7},{5,6},{6,5},{7,4},{8,11},{9,10},{10,... | collective-permute-start | bytes 86024 | tf_op jit(solution)/shard_map/ppermute | solution.py:15
  94.5 0.0 collective-permute-done.21
  94.5 0.0 collective-permute-start.16
  94.5 0.0 collective-permute-done.23
  94.5 0.9 collective-permute-done.22
  95.4 2.3 %collective-permute-done.17 = bf16[4,3584]{1,0:T(4,128)(2,1)S(1)} collective-permute-done((bf16[4,3584]{1,0:T(4,128)(2,1)S(1)}, bf16[4,3584]{1,0:T(4,128)(2,1)S(1)}, u32[]{:S(2)}, u32[]{:S(2)}) %collective-permute-start.17) | collective-permute-done | bytes 28704 | tf_op jit(solution)/shard_map/ppermute | solution.py:15
  97.7 1.6 %collective-permute-done.16 = bf16[4,3584]{1,0:T(4,128)(2,1)S(1)} collective-permute-done((bf16[4,3584]{1,0:T(4,128)(2,1)S(1)}, bf16[4,3584]{1,0:T(4,128)(2,1)S(1)}, u32[]{:S(2)}, u32[]{:S(2)}) %collective-permute-start.16) | collective-permute-done | bytes 28704 | tf_op jit(solution)/shard_map/ppermute | solution.py:15
  99.3 0.7 pad_maximum_fusion
  (25 shorter events, 0.3 us)
Async XLA Ops:
  0.0 0.8 copy-start.6
  0.8 0.7 copy-start.7
  1.5 0.7 copy-start.8
  2.3 11.1 %collective-permute-start.2 = (bf16[4,7296]{1,0:T(4,128)(2,1)S(1)}, bf16[4,7296]{1,0:T(4,128)(2,1)S(1)}, u32[]{:S(2)}, u32[]{:S(2)}) collective-permute-start(bf16[4,7296]{1,0:T(4,128)(2,1)S(1)} %extend.1.refs_0_), channel_id=1, source_target_pairs={{0,3},{1,2},{2,1},{3,0},{4,7},{5,6},{6,5},{7,4},{8,11},{9,10},{10,... | collective-permute-start | bytes 175112 | tf_op jit(solution)/shard_map/ppermute | solution.py:15
  7.4 6.0 %collective-permute-start.1 = (bf16[4,7296]{1,0:T(4,128)(2,1)S(1)}, bf16[4,7296]{1,0:T(4,128)(2,1)S(1)}, u32[]{:S(2)}, u32[]{:S(2)}) collective-permute-start(bf16[4,7296]{1,0:T(4,128)(2,1)S(1)} %extend.1.refs_0_), channel_id=1, source_target_pairs={{0,2},{1,3},{2,0},{3,1},{4,6},{5,7},{6,4},{7,5},{8,10},{9,11},{10,... | collective-permute-start | bytes 175112 | tf_op jit(solution)/shard_map/ppermute | solution.py:15
  7.4 6.0 %collective-permute-start = (bf16[4,7296]{1,0:T(4,128)(2,1)S(1)}, bf16[4,7296]{1,0:T(4,128)(2,1)S(1)}, u32[]{:S(2)}, u32[]{:S(2)}) collective-permute-start(bf16[4,7296]{1,0:T(4,128)(2,1)S(1)} %extend.1.refs_0_), channel_id=1, source_target_pairs={{0,1},{1,0},{2,3},{3,2},{4,5},{5,4},{6,7},{7,6},{8,9},{9,8},{10,11... | collective-permute-start | bytes 175112 | tf_op jit(solution)/shard_map/ppermute | solution.py:15
  13.5 18.9 %collective-permute-start.4 = (bf16[16,7296]{1,0:T(8,128)(2,1)S(1)}, bf16[16,7296]{1,0:T(8,128)(2,1)S(1)}, u32[]{:S(2)}, u32[]{:S(2)}) collective-permute-start(bf16[16,7296]{1,0:T(8,128)(2,1)S(1)} %join.1.refs_0_), channel_id=1, source_target_pairs={{0,8},{4,12},{8,0},{12,4},{1,9},{5,13},{9,1},{13,5},{2,10},{6,14},... | collective-permute-start | bytes 700424 | tf_op jit(solution)/shard_map/ppermute | solution.py:15
  15.2 17.2 %collective-permute-start.3 = (bf16[16,7296]{1,0:T(8,128)(2,1)S(1)}, bf16[16,7296]{1,0:T(8,128)(2,1)S(1)}, u32[]{:S(2)}, u32[]{:S(2)}) collective-permute-start(bf16[16,7296]{1,0:T(8,128)(2,1)S(1)} %join.1.refs_0_), channel_id=1, source_target_pairs={{0,4},{4,0},{8,12},{12,8},{1,5},{5,1},{9,13},{13,9},{2,6},{6,2},{1... | collective-permute-start | bytes 700424 | tf_op jit(solution)/shard_map/ppermute | solution.py:15
  22.0 5.2 %copy-start = (bf16[2,7168,512]{2,1,0:T(8,128)(2,1)}, bf16[2,7168,512]{2,1,0:T(8,128)(2,1)S(1)}, u32[]{:S(2)}) copy-start(bf16[2,7168,512]{2,1,0:T(8,128)(2,1)S(1)} %get-tuple-element.37.refs_10_) | copy-start | bytes 44040196
  27.2 5.2 %copy-start.4 = (bf16[2,7168,512]{2,1,0:T(8,128)(2,1)}, bf16[2,7168,512]{2,1,0:T(8,128)(2,1)S(1)}, u32[]{:S(2)}) copy-start(bf16[2,7168,512]{2,1,0:T(8,128)(2,1)S(1)} %get-tuple-element.38.refs_11_) | copy-start | bytes 44040196
  32.4 4.9 %collective-permute-start.6 = (bf16[16,3712]{1,0:T(8,128)(2,1)S(1)}, bf16[16,3712]{1,0:T(8,128)(2,1)S(1)}, u32[]{:S(2)}, u32[]{:S(2)}) collective-permute-start(bf16[16,3712]{1,0:T(8,128)(2,1)S(1)} %get-tuple-element.36), channel_id=1, source_target_pairs={{0,4},{4,0},{8,12},{12,8},{1,5},{5,1},{9,13},{13,9},{2,6},{6,2},{1... | collective-permute-start | bytes 356360 | tf_op jit(solution)/shard_map/ppermute | solution.py:15
  33.0 6.1 %collective-permute-start.7 = (bf16[16,7296]{1,0:T(8,128)(2,1)S(1)}, bf16[16,7296]{1,0:T(8,128)(2,1)S(1)}, u32[]{:S(2)}, u32[]{:S(2)}) collective-permute-start(bf16[16,7296]{1,0:T(8,128)(2,1)S(1)} %join.1.refs_0_), channel_id=1, source_target_pairs={{0,16},{16,0},{1,17},{17,1},{2,18},{18,2},{3,19},{19,3},{4,20},{20... | collective-permute-start | bytes 700424 | tf_op jit(solution)/shard_map/ppermute | solution.py:15
  33.0 7.4 %collective-permute-start.8 = (bf16[16,7296]{1,0:T(8,128)(2,1)S(1)}, bf16[16,7296]{1,0:T(8,128)(2,1)S(1)}, u32[]{:S(2)}, u32[]{:S(2)}) collective-permute-start(bf16[16,7296]{1,0:T(8,128)(2,1)S(1)} %collective-permute-done.3.left_ref.refs_1_), channel_id=1, source_target_pairs={{0,16},{16,0},{1,17},{17,1},{2,18},{18,2},{3,19},{19,3},{4,20},{20... | collective-permute-start | bytes 700424 | tf_op jit(solution)/shard_map/ppermute | solution.py:15
  33.5 6.9 %collective-permute-start.9 = (bf16[16,7296]{1,0:T(8,128)(2,1)S(1)}, bf16[16,7296]{1,0:T(8,128)(2,1)S(1)}, u32[]{:S(2)}, u32[]{:S(2)}) collective-permute-start(bf16[16,7296]{1,0:T(8,128)(2,1)S(1)} %collective-permute-done.4.right_ref.refs_2_), channel_id=1, source_target_pairs={{0,16},{16,0},{1,17},{17,1},{2,18},{18,2},{3,19},{19,3},{4,20},{20... | collective-permute-start | bytes 700424 | tf_op jit(solution)/shard_map/ppermute | solution.py:15
  33.5 5.6 %collective-permute-start.5 = (bf16[16,3584]{1,0:T(8,128)(2,1)S(1)}, bf16[16,3584]{1,0:T(8,128)(2,1)S(1)}, u32[]{:S(2)}, u32[]{:S(2)}) collective-permute-start(bf16[16,3584]{1,0:T(8,128)(2,1)S(1)} %get-tuple-element.35), channel_id=1, source_target_pairs={{0,8},{4,12},{8,0},{12,4},{1,9},{5,13},{9,1},{13,5},{2,10},{6,14},... | collective-permute-start | bytes 344072 | tf_op jit(solution)/shard_map/ppermute | solution.py:15
  37.3 3.1 %collective-permute-start.11 = (bf16[16,3712]{1,0:T(8,128)(2,1)S(1)}, bf16[16,3712]{1,0:T(8,128)(2,1)S(1)}, u32[]{:S(2)}, u32[]{:S(2)}) collective-permute-start(bf16[16,3712]{1,0:T(8,128)(2,1)S(1)} %collective-permute-done.6.refs_4_), channel_id=1, source_target_pairs={{0,16},{16,0},{1,17},{17,1},{2,18},{18,2},{3,19},{19,3},{4,20},{20... | collective-permute-start | bytes 356360 | tf_op jit(solution)/shard_map/ppermute | solution.py:15
  39.1 1.3 %collective-permute-start.10 = (bf16[16,3584]{1,0:T(8,128)(2,1)S(1)}, bf16[16,3584]{1,0:T(8,128)(2,1)S(1)}, u32[]{:S(2)}, u32[]{:S(2)}) collective-permute-start(bf16[16,3584]{1,0:T(8,128)(2,1)S(1)} %collective-permute-done.5.refs_3_), channel_id=1, source_target_pairs={{0,16},{16,0},{1,17},{17,1},{2,18},{18,2},{3,19},{19,3},{4,20},{20... | collective-permute-start | bytes 344072 | tf_op jit(solution)/shard_map/ppermute | solution.py:15
  40.4 5.2 %copy-start.1 = (bf16[2,7168,512]{2,1,0:T(8,128)(2,1)S(1)}, bf16[2,7168,512]{2,1,0:T(8,128)(2,1)}, u32[]{:S(2)}) copy-start(bf16[2,7168,512]{2,1,0:T(8,128)(2,1)} %copy-done) | copy-start | bytes 44040196
  45.6 5.2 %copy-start.5 = (bf16[2,7168,512]{2,1,0:T(8,128)(2,1)S(1)}, bf16[2,7168,512]{2,1,0:T(8,128)(2,1)}, u32[]{:S(2)}) copy-start(bf16[2,7168,512]{2,1,0:T(8,128)(2,1)} %copy-done.4) | copy-start | bytes 44040196
  57.8 5.2 %copy-start.2 = (bf16[2,7168,512]{2,1,0:T(8,128)(2,1)}, bf16[2,7168,512]{2,1,0:T(8,128)(2,1)S(1)}, u32[]{:S(2)}) copy-start(bf16[2,7168,512]{2,1,0:T(8,128)(2,1)S(1)} %get-tuple-element.40.down_ref) | copy-start | bytes 44040196
  63.0 5.2 %copy-start.3 = (bf16[2,7168,512]{2,1,0:T(8,128)(2,1)S(1)}, bf16[2,7168,512]{2,1,0:T(8,128)(2,1)}, u32[]{:S(2)}) copy-start(bf16[2,7168,512]{2,1,0:T(8,128)(2,1)} %copy-done.2) | copy-start | bytes 44040196
  70.5 2.9 %collective-permute-start.18 = (bf16[64,3584]{1,0:T(8,128)(2,1)S(1)}, bf16[64,3584]{1,0:T(8,128)(2,1)S(1)}, u32[]{:S(2)}, u32[]{:S(2)}) collective-permute-start(bf16[64,3584]{1,0:T(8,128)(2,1)S(1)} %get-tuple-element.44), channel_id=1, source_target_pairs={{0,16},{16,0},{1,17},{17,1},{2,18},{18,2},{3,19},{19,3},{4,20},{20... | collective-permute-start | bytes 1376264 | tf_op jit(solution)/shard_map/ppermute | solution.py:15
  72.9 1.9 %collective-permute-start.12 = (bf16[64,3584]{1,0:T(8,128)(2,1)S(1)}, bf16[64,3584]{1,0:T(8,128)(2,1)S(1)}, u32[]{:S(2)}, u32[]{:S(2)}) collective-permute-start(bf16[64,3584]{1,0:T(8,128)(2,1)S(1)} %get-tuple-element.42), channel_id=1, source_target_pairs={{0,16},{16,0},{1,17},{17,1},{2,18},{18,2},{3,19},{19,3},{4,20},{20... | collective-permute-start | bytes 1376264 | tf_op jit(solution)/shard_map/ppermute | solution.py:15
  73.5 7.7 %collective-permute-start.19 = (bf16[32,3584]{1,0:T(8,128)(2,1)S(1)}, bf16[32,3584]{1,0:T(8,128)(2,1)S(1)}, u32[]{:S(2)}, u32[]{:S(2)}) collective-permute-start(bf16[32,3584]{1,0:T(8,128)(2,1)S(1)} %slice.73), channel_id=1, source_target_pairs={{0,8},{4,12},{8,0},{12,4},{1,9},{5,13},{9,1},{13,5},{2,10},{6,14},... | collective-permute-start | bytes 688136 | tf_op jit(solution)/shard_map/ppermute | solution.py:15
  74.9 7.9 %collective-permute-start.13 = (bf16[32,3584]{1,0:T(8,128)(2,1)S(1)}, bf16[32,3584]{1,0:T(8,128)(2,1)S(1)}, u32[]{:S(2)}, u32[]{:S(2)}) collective-permute-start(bf16[32,3584]{1,0:T(8,128)(2,1)S(1)} %slice.65), channel_id=1, source_target_pairs={{0,4},{4,0},{8,12},{12,8},{1,5},{5,1},{9,13},{13,9},{2,6},{6,2},{1... | collective-permute-start | bytes 688136 | tf_op jit(solution)/shard_map/ppermute | solution.py:15
  81.3 4.9 %collective-permute-start.20 = (bf16[16,3584]{1,0:T(8,128)(2,1)S(1)}, bf16[16,3584]{1,0:T(8,128)(2,1)S(1)}, u32[]{:S(2)}, u32[]{:S(2)}) collective-permute-start(bf16[16,3584]{1,0:T(8,128)(2,1)S(1)} %slice.75), channel_id=1, source_target_pairs={{0,4},{4,0},{8,12},{12,8},{1,5},{5,1},{9,13},{13,9},{2,6},{6,2},{1... | collective-permute-start | bytes 344072 | tf_op jit(solution)/shard_map/ppermute | solution.py:15
  82.9 7.5 %collective-permute-start.14 = (bf16[16,3584]{1,0:T(8,128)(2,1)S(1)}, bf16[16,3584]{1,0:T(8,128)(2,1)S(1)}, u32[]{:S(2)}, u32[]{:S(2)}) collective-permute-start(bf16[16,3584]{1,0:T(8,128)(2,1)S(1)} %slice.67), channel_id=1, source_target_pairs={{0,8},{4,12},{8,0},{12,4},{1,9},{5,13},{9,1},{13,5},{2,10},{6,14},... | collective-permute-start | bytes 344072 | tf_op jit(solution)/shard_map/ppermute | solution.py:15
  86.2 8.3 %collective-permute-start.21 = (bf16[4,3584]{1,0:T(4,128)(2,1)S(1)}, bf16[4,3584]{1,0:T(4,128)(2,1)S(1)}, u32[]{:S(2)}, u32[]{:S(2)}) collective-permute-start(bf16[4,3584]{1,0:T(4,128)(2,1)S(1)} %get-tuple-element.48), channel_id=1, source_target_pairs={{0,1},{1,0},{2,3},{3,2},{4,5},{5,4},{6,7},{7,6},{8,9},{9,8},{10,11... | collective-permute-start | bytes 86024 | tf_op jit(solution)/shard_map/ppermute | solution.py:15
  87.5 7.0 %collective-permute-start.23 = (bf16[4,3584]{1,0:T(4,128)(2,1)S(1)}, bf16[4,3584]{1,0:T(4,128)(2,1)S(1)}, u32[]{:S(2)}, u32[]{:S(2)}) collective-permute-start(bf16[4,3584]{1,0:T(4,128)(2,1)S(1)} %get-tuple-element.49), channel_id=1, source_target_pairs={{0,3},{1,2},{2,1},{3,0},{4,7},{5,6},{6,5},{7,4},{8,11},{9,10},{10,... | collective-permute-start | bytes 86024 | tf_op jit(solution)/shard_map/ppermute | solution.py:15
  90.0 5.4 %collective-permute-start.22 = (bf16[4,3584]{1,0:T(4,128)(2,1)S(1)}, bf16[4,3584]{1,0:T(4,128)(2,1)S(1)}, u32[]{:S(2)}, u32[]{:S(2)}) collective-permute-start(bf16[4,3584]{1,0:T(4,128)(2,1)S(1)} %get-tuple-element.50), channel_id=1, source_target_pairs={{0,2},{1,3},{2,0},{3,1},{4,6},{5,7},{6,4},{7,5},{8,10},{9,11},{10,... | collective-permute-start | bytes 86024 | tf_op jit(solution)/shard_map/ppermute | solution.py:15
  90.5 4.9 %collective-permute-start.15 = (bf16[4,3584]{1,0:T(4,128)(2,1)S(1)}, bf16[4,3584]{1,0:T(4,128)(2,1)S(1)}, u32[]{:S(2)}, u32[]{:S(2)}) collective-permute-start(bf16[4,3584]{1,0:T(4,128)(2,1)S(1)} %get-tuple-element.45), channel_id=1, source_target_pairs={{0,1},{1,0},{2,3},{3,2},{4,5},{5,4},{6,7},{7,6},{8,9},{9,8},{10,11... | collective-permute-start | bytes 86024 | tf_op jit(solution)/shard_map/ppermute | solution.py:15
  92.0 5.7 %collective-permute-start.17 = (bf16[4,3584]{1,0:T(4,128)(2,1)S(1)}, bf16[4,3584]{1,0:T(4,128)(2,1)S(1)}, u32[]{:S(2)}, u32[]{:S(2)}) collective-permute-start(bf16[4,3584]{1,0:T(4,128)(2,1)S(1)} %get-tuple-element.46), channel_id=1, source_target_pairs={{0,3},{1,2},{2,1},{3,0},{4,7},{5,6},{6,5},{7,4},{8,11},{9,10},{10,... | collective-permute-start | bytes 86024 | tf_op jit(solution)/shard_map/ppermute | solution.py:15
  94.5 4.8 %collective-permute-start.16 = (bf16[4,3584]{1,0:T(4,128)(2,1)S(1)}, bf16[4,3584]{1,0:T(4,128)(2,1)S(1)}, u32[]{:S(2)}, u32[]{:S(2)}) collective-permute-start(bf16[4,3584]{1,0:T(4,128)(2,1)S(1)} %get-tuple-element.47), channel_id=1, source_target_pairs={{0,2},{1,3},{2,0},{3,1},{4,6},{5,7},{6,4},{7,5},{8,10},{9,11},{10,... | collective-permute-start | bytes 86024 | tf_op jit(solution)/shard_map/ppermute | solution.py:15

commit v6 on v5

v6 whole, which is shorter than its diff:
```python
import functools

import jax
import jax.numpy as jnp
from jax import lax
from jax.experimental import pallas as pl
from jax.experimental.pallas import tpu as pltpu
from jax.sharding import PartitionSpec as P

AXES = ("sect", "grp", "dev")
CHUNKS = 2
VMEM_LIMIT = 30 * 2**20


def swap(value, axis, mask):
    return lax.ppermute(value, axis, [(i, i ^ mask) for i in range(lax.axis_size(axis))])


def bits_of(size):
    return [1 << b for b in range(size.bit_length() - 1)]


def vmem_call(kernel, out_shape, name, *operands):
    whole = pl.BlockSpec(memory_space=pltpu.VMEM)
    return pl.pallas_call(
        kernel,
        out_shape=out_shape,
        in_specs=[whole] * len(operands),
        out_specs=jax.tree.map(lambda _: whole, out_shape),
        compiler_params=pltpu.CompilerParams(vmem_limit_bytes=VMEM_LIMIT),
        name=name,
    )(*operands)


def extend_kernel(tokens_hbm, ids_hbm, weights_hbm, out_ref, tokens_ref, ids_ref, weights_ref, sems):
    pairs = ((ids_hbm, ids_ref), (weights_hbm, weights_ref), (tokens_hbm, tokens_ref))
    copies = [pltpu.make_async_copy(a, b, sems.at[i]) for i, (a, b) in enumerate(pairs)]
    for copy in copies:
        copy.start()
    rows, width = tokens_ref.shape
    half = (out_ref.shape[1] - width) // 2
    lane = lax.broadcasted_iota(jnp.int32, (rows, half * 2), 1)
    dense = jnp.zeros((rows, half * 2), jnp.float32)
    for copy in copies:
        copy.wait()
    for k in range(ids_ref.shape[1]):
        mine = lax.rem(lane, half) == ids_ref[:, k:k + 1]
        dense = dense + jnp.where(mine, weights_ref[:, k:k + 1], 0.0)
    high = dense.astype(jnp.bfloat16).astype(jnp.float32)
    out_ref[:, :width] = tokens_ref[...]
    out_ref[:, width:] = jnp.where(lane < half, high, dense - high).astype(jnp.bfloat16)


def extend(tokens, ids, weights, half):
    rows, width = tokens.shape
    return pl.pallas_call(
        extend_kernel,
        out_shape=jax.ShapeDtypeStruct((rows, width + 2 * half), tokens.dtype),
        in_specs=[pl.BlockSpec(memory_space=pl.ANY)] * 3,
        out_specs=pl.BlockSpec(memory_space=pltpu.VMEM),
        scratch_shapes=[pltpu.VMEM(v.shape, v.dtype) for v in (tokens, ids, weights)]
        + [pltpu.SemaphoreType.DMA((3,))],
        compiler_params=pltpu.CompilerParams(vmem_limit_bytes=VMEM_LIMIT),
        name="extend",
    )(*(pltpu.with_memory_space_constraint(v, pltpu.HBM) for v in (tokens, ids, weights)))


def join_kernel(*refs):
    pieces, out_ref = refs[:-1], refs[-1]
    values = [p[...].astype(jnp.float32) for p in pieces]
    out_ref[...] = jnp.concatenate(values, axis=0).astype(out_ref.dtype)


def join(pieces):
    rows, width = pieces[0].shape
    out = jax.ShapeDtypeStruct((rows * len(pieces), width), pieces[0].dtype)
    return vmem_call(join_kernel, out, "join", *pieces)


def halves_kernel(left_ref, right_ref, left_out, right_out):
    half = left_out.shape[1]
    left_out[...] = left_ref[:, :half]
    right_out[...] = right_ref[:, half:]


def halves(left, right):
    rows, width = left.shape
    half = width // 256 * 128
    out = (
        jax.ShapeDtypeStruct((rows, half), left.dtype),
        jax.ShapeDtypeStruct((rows, width - half), left.dtype),
    )
    return vmem_call(halves_kernel, out, "halves", left, right)


def gather_rows(block, w_up):
    lanes, groups, sects = (lax.axis_size(a) for a in ("dev", "grp", "sect"))
    arrived = [swap(block, "dev", m) for m in range(1, lanes)]
    w_up, token = fetch(w_up, block)
    arrived, token = lax.optimization_barrier((arrived, token))
    line = join([block] + arrived)
    if groups == 4:
        by_x, by_y = swap(line, "grp", 1), swap(line, "grp", 2)
        from_x, from_y = halves(by_x, by_y)
        corner = [swap(from_x, "grp", 2), swap(from_y, "grp", 1)]
        entries = [[line], [by_x], [by_y], corner]
    else:
        entries = [[line]]
        for bit in bits_of(groups):
            entries = entries + [[swap(p, "grp", bit) for p in e] for e in entries]
    for bit in bits_of(sects):
        entries = entries + [[swap(p, "sect", bit) for p in e] for e in entries]
    return entries, w_up, token


def down_product(order, line, hidden_ref, down_ref, keep_ref, send_ref, sems, copy_of):
    blocks = sems.shape[0]
    block = keep_ref.shape[1] // blocks
    experts, depth, _ = down_ref.shape
    groups = len(order)

    @pl.loop(0, blocks)
    def _(step):
        columns = pl.ds(pl.multiple_of(step * block, block), block)
        copy_of(step).wait()
        weight = down_ref[:, :, columns].reshape(experts * depth, block)
        total = jnp.dot(hidden_ref[...], weight, preferred_element_type=jnp.float32)
        total = total.astype(jnp.bfloat16)
        for place, entry in enumerate(order):
            rows = pl.ds(place * line, line)
            keep_ref[rows, columns] = total[entry * line:(entry + 1) * line]
            low = (groups + entry) * line
            send_ref[rows, columns] = total[low:low + line]


def down_copy(start, down_hbm, down_ref, sems):
    block = down_ref.shape[2] // sems.shape[0]

    def copy(step):
        at = pl.multiple_of(step * block, block)
        return pltpu.make_async_copy(
            down_hbm.at[:, :, pl.ds(start + at, block)],
            down_ref.at[:, :, pl.ds(at, block)],
            sems.at[step],
        )

    return copy


def up_kernel(layout, width, order, start, token_ref, *refs):
    pieces = refs[: sum(layout)]
    (upw_ref, gate_hbm, down_hbm, hidden_ref, keep_ref, send_ref,
     rows_ref, up_ref, gate_ref, gate_sems, down_ref, sems) = refs[sum(layout):]
    experts, _, hidden = upw_ref.shape
    place = lax.axis_index("sect") * lax.axis_size("grp") + lax.axis_index("grp")
    first = place * experts
    line = pieces[0].shape[0]
    block = min(256, hidden)
    gate_copies = weight_copies(gate_hbm, gate_ref, gate_sems)
    for gate_copy in gate_copies:
        gate_copy.start()
    copy = down_copy(start, down_hbm, down_ref, sems)
    for step in range(sems.shape[0]):
        copy(step).start()

    at = 0
    for entry, count in enumerate(layout):
        left = 0
        for piece in pieces[at:at + count]:
            rows_ref[pl.ds(entry * line, line), pl.ds(left, piece.shape[1])] = piece[...]
            left += piece.shape[1]
        at += count

    for e in range(experts):

        @pl.loop(0, hidden // block)
        def _(step):
            span = pl.ds(pl.multiple_of(step * block, block), block)
            up_ref[e, :, span] = jnp.dot(
                rows_ref[:, :width], upw_ref[e, :, span], preferred_element_type=jnp.float32
            )

    extra = rows_ref[:, width:].astype(jnp.float32)
    lane = lax.broadcasted_iota(jnp.int32, extra.shape, 1)
    parts = gate_sems.shape[1]
    for e in range(experts):
        mine = lax.rem(lane, extra.shape[1] // 2) == first + e
        scale = jnp.sum(jnp.where(mine, extra, 0.0), axis=1, keepdims=True)
        for gate_copy in gate_copies[e * parts:(e + 1) * parts]:
            gate_copy.wait()

        @pl.loop(0, hidden // block)
        def _(step):
            span = pl.ds(pl.multiple_of(step * block, block), block)
            gate = jnp.dot(
                rows_ref[:, :width], gate_ref[e, :, span], preferred_element_type=jnp.float32
            )
            value = gate / (1.0 + jnp.exp(-gate)) * up_ref[e, :, span] * scale
            out = pl.ds(pl.multiple_of(e * hidden + step * block, block), block)
            hidden_ref[:, out] = value.astype(jnp.bfloat16)

    down_product(order, line, hidden_ref, down_ref, keep_ref, send_ref, sems, copy)


def fetch_kernel(after_ref, source_ref, target_ref, token_ref, sems):
    copies = weight_copies(source_ref, target_ref, sems)
    for copy in copies:
        copy.start()
    token_ref[...] = jnp.zeros_like(token_ref)
    for copy in copies:
        copy.wait()


def weight_copies(source_ref, target_ref, sems):
    experts, parts = sems.shape
    depth = source_ref.shape[1] // parts
    return [
        pltpu.make_async_copy(
            source_ref.at[e, pl.ds(p * depth, depth)],
            target_ref.at[e, pl.ds(p * depth, depth)],
            sems.at[e, p],
        )
        for e in range(experts)
        for p in range(parts)
    ]


def fetch(weight, after):
    in_hbm = pl.BlockSpec(memory_space=pl.ANY)
    in_vmem = pl.BlockSpec(memory_space=pltpu.VMEM)
    return pl.pallas_call(
        fetch_kernel,
        out_shape=(
            pltpu.VMEM(weight.shape, weight.dtype),
            jax.ShapeDtypeStruct((8, 128), jnp.float32),
        ),
        in_specs=[in_hbm, in_hbm],
        out_specs=(in_vmem, in_vmem),
        scratch_shapes=[pltpu.SemaphoreType.DMA((weight.shape[0], 4))],
        compiler_params=pltpu.CompilerParams(vmem_limit_bytes=VMEM_LIMIT),
        cost_estimate=pl.CostEstimate(
            flops=0, bytes_accessed=2 * weight.size, transcendentals=0
        ),
        name="fetch",
    )(after, pltpu.with_memory_space_constraint(weight, pltpu.HBM))


def down_scratch(w_down, columns):
    experts, depth, _ = w_down.shape
    block = 512 if columns % 512 == 0 else 128
    return [
        pltpu.VMEM((experts, depth, columns), w_down.dtype),
        pltpu.SemaphoreType.DMA((columns // block,)),
    ]


def up_call(entries, w_gate, w_up, w_down, token, order, start, columns):
    layout = [len(e) for e in entries]
    flat = [p for e in entries for p in e]
    experts, width, hidden = w_up.shape
    line = flat[0].shape[0]
    full = sum(p.shape[1] for p in entries[0])
    rows = line * len(entries)
    whole = pl.BlockSpec(memory_space=pltpu.VMEM)
    anywhere = pl.BlockSpec(memory_space=pl.ANY)
    out = jax.ShapeDtypeStruct((rows // 2, columns), jnp.bfloat16)
    return pl.pallas_call(
        functools.partial(up_kernel, layout, width, order, start),
        out_shape=(jax.ShapeDtypeStruct((rows, experts * hidden), jnp.bfloat16), out, out),
        in_specs=[anywhere] + [whole] * (len(flat) + 1) + [anywhere] * 2,
        out_specs=(whole,) * 3,
        scratch_shapes=[
            pltpu.VMEM((rows, full), jnp.bfloat16),
            pltpu.VMEM((experts, rows, hidden), jnp.float32),
            pltpu.VMEM(w_gate.shape, w_gate.dtype),
            pltpu.SemaphoreType.DMA((experts, 4)),
        ]
        + down_scratch(w_down, columns),
        compiler_params=pltpu.CompilerParams(vmem_limit_bytes=VMEM_LIMIT),
        cost_estimate=pl.CostEstimate(
            flops=4 * rows * experts * width * hidden + 2 * rows * experts * hidden * columns,
            bytes_accessed=2 * experts * hidden * columns,
            transcendentals=rows * experts * hidden,
        ),
        name="gate_up",
    )(
        token,
        *flat,
        pltpu.with_memory_space_constraint(w_up, pltpu.VMEM),
        pltpu.with_memory_space_constraint(w_gate, pltpu.HBM),
        pltpu.with_memory_space_constraint(w_down, pltpu.HBM),
    )


def down_kernel(order, line, start, hidden_ref, down_hbm, keep_ref, send_ref, down_ref, sems):
    copy = down_copy(start, down_hbm, down_ref, sems)
    for step in range(sems.shape[0]):
        copy(step).start()
    down_product(order, line, hidden_ref, down_ref, keep_ref, send_ref, sems, copy)


def down_call(order, line, hidden, w_down, start, columns):
    rows = line * len(order)
    out = jax.ShapeDtypeStruct((rows, columns), jnp.bfloat16)
    whole = pl.BlockSpec(memory_space=pltpu.VMEM)
    return pl.pallas_call(
        functools.partial(down_kernel, order, line, start),
        out_shape=(out, out),
        in_specs=[whole, pl.BlockSpec(memory_space=pl.ANY)],
        out_specs=(whole, whole),
        scratch_shapes=down_scratch(w_down, columns),
        compiler_params=pltpu.CompilerParams(vmem_limit_bytes=VMEM_LIMIT),
        cost_estimate=pl.CostEstimate(
            flops=2 * hidden.size * columns,
            bytes_accessed=2 * hidden.shape[1] * columns,
            transcendentals=0,
        ),
        name="down",
    )(hidden, pltpu.with_memory_space_constraint(w_down, pltpu.HBM))


def add(*values):
    total = values[0].astype(jnp.float32)
    for value in values[1:]:
        total = total + value.astype(jnp.float32)
    return total.astype(jnp.bfloat16)


def body(tokens, expert_ids, gate_weights, w_gate, w_up, w_down):
    sects, groups, lanes = (lax.axis_size(a) for a in AXES)
    row_count, width = tokens.shape
    experts = w_gate.shape[0]
    expert_count = sects * groups * experts

    half = -(-expert_count // 64) * 64
    block = extend(tokens, expert_ids, gate_weights, half)
    entries, w_up, token = gather_rows(block, w_up)

    line = lanes * row_count
    results = []
    chunk = width // CHUNKS
    hidden = None
    for c in range(CHUNKS):
        bits = bits_of(groups)
        bits = bits if c % 2 else bits[::-1]
        order = [0]
        for bit in bits:
            order = order + [o | bit for o in order]
        if c == 0:
            hidden, keep, send = up_call(
                entries, w_gate, w_up, w_down, token, order, 0, chunk
            )
        else:
            keep, send = down_call(order, line, hidden, w_down, c * chunk, chunk)
        value = add(keep, swap(send, "sect", 1))
        for bit in bits[::-1]:
            middle = value.shape[0] // 2
            arrived = swap(value[middle:], "grp", bit)
            value = add(value[:middle], arrived)
        pieces = [value[:row_count]]
        for m in range(1, lanes):
            pieces.append(swap(value[m * row_count:(m + 1) * row_count], "dev", m))
        results.append(add(*pieces))
    return jnp.concatenate(results, axis=1)


def solution(mesh):
    in_specs = (
        P(AXES, None),
        P(AXES, None),
        P(AXES, None),
        P(("sect", "grp"), None, "dev"),
        P(("sect", "grp"), None, "dev"),
        P(("sect", "grp"), "dev", None),
    )
    return jax.shard_map(
        body, mesh=mesh, in_specs=in_specs, out_specs=P(AXES, None), check_vma=False
    )
```

time: 100 us -> 71.3 us (0.71)
  local copies, waits for them, and re-layouts: 33.4 us -> 0.13 us
  waiting for transfers between devices: 19.5 us -> 26 us
  Pallas kernels: 22.3 us -> 20.8 us
    unnamed x18 -> x0, local copies, waits for them, and re-layouts: 33.3 us -> none
    ppermute x24, waiting for transfers between devices: 19.5 us -> 26 us  [swap(): lax.ppermute(value, axis, [(i, i ^ mask) for i in range(lax.axis_size(axi...]
    pallas_call x2 -> x1, Pallas kernels: 4.47 us -> 3.55 us  [down_call(): pl.pallas_call(functools.partial(down_kernel, order, line, start), out_sh...]
  transfers between devices with their start and end apart: 24 -> 24, of which waited for: 9 -> 12; matrix products, arithmetic and copies ran while one was open for 1% -> 1% of each run, Pallas kernels for 13% -> 12%
where the time goes in v6:
time: 71.3 us; the launch traced here: 71.1 us
  waiting for transfers between devices  26 us (36%)
  starting transfers between devices  22.9 us (32%)
  Pallas kernels  20.8 us (29%)
  other arithmetic  1.11 us (2%)
    ppermute x24, waiting for transfers between devices, swap(): lax.ppermute(value, axis, [(i, i ^ mask) for i in range(lax.axis_size(axi...  26 us
    ppermute x24, starting transfers between devices, swap(): lax.ppermute(value, axis, [(i, i ^ mask) for i in range(lax.axis_size(axi...  22.9 us
    pallas_call x1, Pallas kernels, up_call(): pl.pallas_call(functools.partial(up_kernel, layout, width, order, start),...  10.9 us
    pallas_call x1, Pallas kernels, fetch(): pl.pallas_call(fetch_kernel, out_shape=(pltpu.VMEM(weight.shape, weight.d...  5.31 us
    pallas_call x1, Pallas kernels, down_call(): pl.pallas_call(functools.partial(down_kernel, order, line, start), out_sh...  3.55 us
  transfers between devices with their start and end apart: 24, of which 12 were waited for; matrix products, arithmetic and copies ran while one was open for 1% of the time, Pallas kernels for 12%

profile of v6, /device:TPU:0, one launch (start us, length us, event | category | flops | bytes accessed | tf_op | source)
XLA Modules:
  0.0 71.1 jit_solution(12389387379381894224)
XLA Ops:
  0.0 1.0 %extend.1.after_ref.refs_0_ = bf16[4,7296]{1,0:T(4,128)(2,1)S(1)} custom-call(bf16[4,7168]{1,0:T(4,128)(2,1)} %tokens_hbm.1, s32[4,8]{1,0:T(4,128)} %ids_hbm.1, f32[4,8]{1,0:T(4,128)} %weights_hbm.1), custom_call_target="tpu_custom_call" | custom-call | tf_op jit(solution)/shard_map/extend/pallas_call | solution.py:56
  1.0 5.1 %collective-permute-start.2 = (bf16[4,7296]{1,0:T(4,128)(2,1)S(1)}, bf16[4,7296]{1,0:T(4,128)(2,1)S(1)}, u32[]{:S(2)}, u32[]{:S(2)}) collective-permute-start(bf16[4,7296]{1,0:T(4,128)(2,1)S(1)} %extend.1.after_ref.refs_0_), channel_id=1, source_target_pairs={{0,3},{1,2},{2,1},{3,0},{4,7},{5,6},{6,5},{7,4},{8,11},{9,10},{10,... | collective-permute-start | bytes 175112 | tf_op jit(solution)/shard_map/ppermute | solution.py:16
  6.1 0.0 collective-permute-start.1
  6.1 0.6 collective-permute-start
  6.7 5.3 %fetch.1 = (bf16[2,7168,512]{2,1,0:T(8,128)(2,1)S(1)}, f32[8,128]{1,0:T(8,128)S(1)}) custom-call(bf16[4,7296]{1,0:T(4,128)(2,1)S(1)} %extend.1.after_ref.refs_0_, bf16[2,7168,512]{2,1,0:T(8,128)(2,1)} %source_ref.1), custom_call_target="tpu_custom_call" | custom-call | bytes 14680064 | tf_op jit(solution)/shard_map/fetch/pallas_call | solution.py:231
  12.1 0.0 collective-permute-done.2.refs_3_
  12.1 0.0 collective-permute-done.1.refs_2_
  12.1 0.0 collective-permute-done.refs_1_
  12.1 0.1 join.1.refs_0_
  12.2 1.7 %collective-permute-start.4 = (bf16[16,7296]{1,0:T(8,128)(2,1)S(1)}, bf16[16,7296]{1,0:T(8,128)(2,1)S(1)}, u32[]{:S(2)}, u32[]{:S(2)}) collective-permute-start(bf16[16,7296]{1,0:T(8,128)(2,1)S(1)} %join.1.refs_0_), channel_id=1, source_target_pairs={{0,8},{4,12},{8,0},{12,4},{1,9},{5,13},{9,1},{13,5},{2,10},{6,14},... | collective-permute-start | bytes 700424 | tf_op jit(solution)/shard_map/ppermute | solution.py:16
  13.9 1.5 %collective-permute-start.3 = (bf16[16,7296]{1,0:T(8,128)(2,1)S(1)}, bf16[16,7296]{1,0:T(8,128)(2,1)S(1)}, u32[]{:S(2)}, u32[]{:S(2)}) collective-permute-start(bf16[16,7296]{1,0:T(8,128)(2,1)S(1)} %join.1.refs_0_), channel_id=1, source_target_pairs={{0,4},{4,0},{8,12},{12,8},{1,5},{5,1},{9,13},{13,9},{2,6},{6,2},{1... | collective-permute-start | bytes 700424 | tf_op jit(solution)/shard_map/ppermute | solution.py:16
  15.4 3.7 %collective-permute-done.4.right_ref.refs_2_ = bf16[16,7296]{1,0:T(8,128)(2,1)S(1)} collective-permute-done((bf16[16,7296]{1,0:T(8,128)(2,1)S(1)}, bf16[16,7296]{1,0:T(8,128)(2,1)S(1)}, u32[]{:S(2)}, u32[]{:S(2)}) %collective-permute-start.4) | collective-permute-done | bytes 233504 | tf_op jit(solution)/shard_map/ppermute | solution.py:16
  19.1 1.2 %collective-permute-done.3.left_ref.refs_1_ = bf16[16,7296]{1,0:T(8,128)(2,1)S(1)} collective-permute-done((bf16[16,7296]{1,0:T(8,128)(2,1)S(1)}, bf16[16,7296]{1,0:T(8,128)(2,1)S(1)}, u32[]{:S(2)}, u32[]{:S(2)}) %collective-permute-start.3) | collective-permute-done | bytes 233504 | tf_op jit(solution)/shard_map/ppermute | solution.py:16
  20.4 1.6 %collective-permute-start.6 = (bf16[16,3712]{1,0:T(8,128)(2,1)S(1)}, bf16[16,3712]{1,0:T(8,128)(2,1)S(1)}, u32[]{:S(2)}, u32[]{:S(2)}) collective-permute-start(bf16[16,3712]{1,0:T(8,128)(2,1)S(1)} %get-tuple-element.24), channel_id=1, source_target_pairs={{0,4},{4,0},{8,12},{12,8},{1,5},{5,1},{9,13},{13,9},{2,6},{6,2},{1... | collective-permute-start | bytes 356360 | tf_op jit(solution)/shard_map/ppermute | solution.py:16
  21.9 0.0 collective-permute-start.7
  21.9 0.5 collective-permute-start.9
  22.4 0.0 collective-permute-start.8
  22.4 0.5 collective-permute-start.5
  22.9 2.3 %collective-permute-done.6.refs_4_ = bf16[16,3712]{1,0:T(8,128)(2,1)S(1)} collective-permute-done((bf16[16,3712]{1,0:T(8,128)(2,1)S(1)}, bf16[16,3712]{1,0:T(8,128)(2,1)S(1)}, u32[]{:S(2)}, u32[]{:S(2)}) %collective-permute-start.6) | collective-permute-done | bytes 118816 | tf_op jit(solution)/shard_map/ppermute | solution.py:16
  25.3 0.0 collective-permute-start.11
  25.3 2.7 %collective-permute-done.5.refs_3_ = bf16[16,3584]{1,0:T(8,128)(2,1)S(1)} collective-permute-done((bf16[16,3584]{1,0:T(8,128)(2,1)S(1)}, bf16[16,3584]{1,0:T(8,128)(2,1)S(1)}, u32[]{:S(2)}, u32[]{:S(2)}) %collective-permute-start.5) | collective-permute-done | bytes 114720 | tf_op jit(solution)/shard_map/ppermute | solution.py:16
  28.0 0.0 collective-permute-start.10
  28.0 0.0 collective-permute-done.7.refs_5_
  28.0 1.3 %collective-permute-done.10.refs_8_ = bf16[16,3584]{1,0:T(8,128)(2,1)S(1)} collective-permute-done((bf16[16,3584]{1,0:T(8,128)(2,1)S(1)}, bf16[16,3584]{1,0:T(8,128)(2,1)S(1)}, u32[]{:S(2)}, u32[]{:S(2)}) %collective-permute-start.10) | collective-permute-done | bytes 114720 | tf_op jit(solution)/shard_map/ppermute | solution.py:16
  29.3 0.0 collective-permute-done.9.refs_7_
  29.3 0.0 collective-permute-done.8.refs_6_
  29.3 0.0 collective-permute-done.11.refs_9_
  29.3 10.9 %gate_up.1 = (bf16[128,1024]{1,0:T(8,128)(2,1)S(1)}, bf16[64,3584]{1,0:T(8,128)(2,1)S(1)}, bf16[64,3584]{1,0:T(8,128)(2,1)S(1)}) custom-call(f32[8,128]{1,0:T(8,128)S(1)} %get-tuple-element.19.token_ref, bf16[16,7296]{1,0:T(8,128)(2,1)S(1)} %join.1.refs_0_, bf16[16,7296]{1,0:T(8,128)(2,1)S(1)} %collective-permute-done.3.left_ref.refs_1_, ...), custom_call_target="tpu_custom_call" | custom-call | flops 4697620480 | bytes 7340032 | tf_op jit(solution)/shard_map/gate_up/pallas_call | solution.py:267
  40.2 0.2 collective-permute-start.12
  40.4 3.6 %down.1 = (bf16[64,3584]{1,0:T(8,128)(2,1)S(1)}, bf16[64,3584]{1,0:T(8,128)(2,1)S(1)}) custom-call(bf16[128,1024]{1,0:T(8,128)(2,1)S(1)} %get-tuple-element.28.hidden_ref, bf16[2,512,7168]{2,1,0:T(8,128)(2,1)} %down_hbm.1), custom_call_target="tpu_custom_call" | custom-call | flops 939524096 | bytes 7340032 | tf_op jit(solution)/shard_map/down/pallas_call | solution.py:306
  44.0 0.4 collective-permute-start.18
  44.4 0.0 collective-permute-done.12
  44.4 0.1 add_convert_fusion.1
  44.6 0.6 collective-permute-start.13
  45.2 0.7 collective-permute-done.18
  45.9 0.1 add_convert_fusion
  46.0 0.6 collective-permute-start.19
  46.6 5.7 %collective-permute-done.13 = bf16[32,3584]{1,0:T(8,128)(2,1)S(1)} collective-permute-done((bf16[32,3584]{1,0:T(8,128)(2,1)S(1)}, bf16[32,3584]{1,0:T(8,128)(2,1)S(1)}, u32[]{:S(2)}, u32[]{:S(2)}) %collective-permute-start.13) | collective-permute-done | bytes 229408 | tf_op jit(solution)/shard_map/ppermute | solution.py:16
  52.3 0.1 add_convert_fusion.3
  52.4 0.6 collective-permute-start.14
  52.9 1.0 %collective-permute-done.19 = bf16[32,3584]{1,0:T(8,128)(2,1)S(1)} collective-permute-done((bf16[32,3584]{1,0:T(8,128)(2,1)S(1)}, bf16[32,3584]{1,0:T(8,128)(2,1)S(1)}, u32[]{:S(2)}, u32[]{:S(2)}) %collective-permute-start.19) | collective-permute-done | bytes 229408 | tf_op jit(solution)/shard_map/ppermute | solution.py:16
  53.9 0.1 add_convert_fusion.2
  54.0 0.6 collective-permute-start.20
  54.6 2.6 %collective-permute-done.14 = bf16[16,3584]{1,0:T(8,128)(2,1)S(1)} collective-permute-done((bf16[16,3584]{1,0:T(8,128)(2,1)S(1)}, bf16[16,3584]{1,0:T(8,128)(2,1)S(1)}, u32[]{:S(2)}, u32[]{:S(2)}) %collective-permute-start.14) | collective-permute-done | bytes 114720 | tf_op jit(solution)/shard_map/ppermute | solution.py:16
  57.3 1.5 %collective-permute-start.15 = (bf16[4,3584]{1,0:T(4,128)(2,1)S(1)}, bf16[4,3584]{1,0:T(4,128)(2,1)S(1)}, u32[]{:S(2)}, u32[]{:S(2)}) collective-permute-start(bf16[4,3584]{1,0:T(4,128)(2,1)S(1)} %get-tuple-element.31), channel_id=1, source_target_pairs={{0,1},{1,0},{2,3},{3,2},{4,5},{5,4},{6,7},{7,6},{8,9},{9,8},{10,11... | collective-permute-start | bytes 86024 | tf_op jit(solution)/shard_map/ppermute | solution.py:16
  58.8 2.4 %collective-permute-start.17 = (bf16[4,3584]{1,0:T(4,128)(2,1)S(1)}, bf16[4,3584]{1,0:T(4,128)(2,1)S(1)}, u32[]{:S(2)}, u32[]{:S(2)}) collective-permute-start(bf16[4,3584]{1,0:T(4,128)(2,1)S(1)} %get-tuple-element.32), channel_id=1, source_target_pairs={{0,3},{1,2},{2,1},{3,0},{4,7},{5,6},{6,5},{7,4},{8,11},{9,10},{10,... | collective-permute-start | bytes 86024 | tf_op jit(solution)/shard_map/ppermute | solution.py:16
  61.1 0.3 collective-permute-start.16
  61.4 0.0 collective-permute-done.20
  61.5 1.8 %collective-permute-start.21 = (bf16[4,3584]{1,0:T(4,128)(2,1)S(1)}, bf16[4,3584]{1,0:T(4,128)(2,1)S(1)}, u32[]{:S(2)}, u32[]{:S(2)}) collective-permute-start(bf16[4,3584]{1,0:T(4,128)(2,1)S(1)} %get-tuple-element.34), channel_id=1, source_target_pairs={{0,1},{1,0},{2,3},{3,2},{4,5},{5,4},{6,7},{7,6},{8,9},{9,8},{10,11... | collective-permute-start | bytes 86024 | tf_op jit(solution)/shard_map/ppermute | solution.py:16
  63.3 2.4 %collective-permute-start.23 = (bf16[4,3584]{1,0:T(4,128)(2,1)S(1)}, bf16[4,3584]{1,0:T(4,128)(2,1)S(1)}, u32[]{:S(2)}, u32[]{:S(2)}) collective-permute-start(bf16[4,3584]{1,0:T(4,128)(2,1)S(1)} %get-tuple-element.35), channel_id=1, source_target_pairs={{0,3},{1,2},{2,1},{3,0},{4,7},{5,6},{6,5},{7,4},{8,11},{9,10},{10,... | collective-permute-start | bytes 86024 | tf_op jit(solution)/shard_map/ppermute | solution.py:16
  65.7 0.0 collective-permute-done.15
  65.7 0.0 collective-permute-start.22
  65.7 0.0 collective-permute-done.17
  65.7 0.6 collective-permute-done.16
  66.3 0.0 collective-permute-done.21
  66.4 2.6 %collective-permute-done.23 = bf16[4,3584]{1,0:T(4,128)(2,1)S(1)} collective-permute-done((bf16[4,3584]{1,0:T(4,128)(2,1)S(1)}, bf16[4,3584]{1,0:T(4,128)(2,1)S(1)}, u32[]{:S(2)}, u32[]{:S(2)}) %collective-permute-start.23) | collective-permute-done | bytes 28704 | tf_op jit(solution)/shard_map/ppermute | solution.py:16
  69.0 1.5 %collective-permute-done.22 = bf16[4,3584]{1,0:T(4,128)(2,1)S(1)} collective-permute-done((bf16[4,3584]{1,0:T(4,128)(2,1)S(1)}, bf16[4,3584]{1,0:T(4,128)(2,1)S(1)}, u32[]{:S(2)}, u32[]{:S(2)}) %collective-permute-start.22) | collective-permute-done | bytes 28704 | tf_op jit(solution)/shard_map/ppermute | solution.py:16
  70.5 0.7 pad_maximum_fusion
  (11 shorter events, 0.3 us)
Async XLA Ops:
  1.0 11.1 %collective-permute-start.2 = (bf16[4,7296]{1,0:T(4,128)(2,1)S(1)}, bf16[4,7296]{1,0:T(4,128)(2,1)S(1)}, u32[]{:S(2)}, u32[]{:S(2)}) collective-permute-start(bf16[4,7296]{1,0:T(4,128)(2,1)S(1)} %extend.1.after_ref.refs_0_), channel_id=1, source_target_pairs={{0,3},{1,2},{2,1},{3,0},{4,7},{5,6},{6,5},{7,4},{8,11},{9,10},{10,... | collective-permute-start | bytes 175112 | tf_op jit(solution)/shard_map/ppermute | solution.py:16
  6.1 6.0 %collective-permute-start.1 = (bf16[4,7296]{1,0:T(4,128)(2,1)S(1)}, bf16[4,7296]{1,0:T(4,128)(2,1)S(1)}, u32[]{:S(2)}, u32[]{:S(2)}) collective-permute-start(bf16[4,7296]{1,0:T(4,128)(2,1)S(1)} %extend.1.after_ref.refs_0_), channel_id=1, source_target_pairs={{0,2},{1,3},{2,0},{3,1},{4,6},{5,7},{6,4},{7,5},{8,10},{9,11},{10,... | collective-permute-start | bytes 175112 | tf_op jit(solution)/shard_map/ppermute | solution.py:16
  6.1 6.0 %collective-permute-start = (bf16[4,7296]{1,0:T(4,128)(2,1)S(1)}, bf16[4,7296]{1,0:T(4,128)(2,1)S(1)}, u32[]{:S(2)}, u32[]{:S(2)}) collective-permute-start(bf16[4,7296]{1,0:T(4,128)(2,1)S(1)} %extend.1.after_ref.refs_0_), channel_id=1, source_target_pairs={{0,1},{1,0},{2,3},{3,2},{4,5},{5,4},{6,7},{7,6},{8,9},{9,8},{10,11... | collective-permute-start | bytes 175112 | tf_op jit(solution)/shard_map/ppermute | solution.py:16
  12.2 6.9 %collective-permute-start.4 = (bf16[16,7296]{1,0:T(8,128)(2,1)S(1)}, bf16[16,7296]{1,0:T(8,128)(2,1)S(1)}, u32[]{:S(2)}, u32[]{:S(2)}) collective-permute-start(bf16[16,7296]{1,0:T(8,128)(2,1)S(1)} %join.1.refs_0_), channel_id=1, source_target_pairs={{0,8},{4,12},{8,0},{12,4},{1,9},{5,13},{9,1},{13,5},{2,10},{6,14},... | collective-permute-start | bytes 700424 | tf_op jit(solution)/shard_map/ppermute | solution.py:16
  13.9 6.4 %collective-permute-start.3 = (bf16[16,7296]{1,0:T(8,128)(2,1)S(1)}, bf16[16,7296]{1,0:T(8,128)(2,1)S(1)}, u32[]{:S(2)}, u32[]{:S(2)}) collective-permute-start(bf16[16,7296]{1,0:T(8,128)(2,1)S(1)} %join.1.refs_0_), channel_id=1, source_target_pairs={{0,4},{4,0},{8,12},{12,8},{1,5},{5,1},{9,13},{13,9},{2,6},{6,2},{1... | collective-permute-start | bytes 700424 | tf_op jit(solution)/shard_map/ppermute | solution.py:16
  20.4 4.9 %collective-permute-start.6 = (bf16[16,3712]{1,0:T(8,128)(2,1)S(1)}, bf16[16,3712]{1,0:T(8,128)(2,1)S(1)}, u32[]{:S(2)}, u32[]{:S(2)}) collective-permute-start(bf16[16,3712]{1,0:T(8,128)(2,1)S(1)} %get-tuple-element.24), channel_id=1, source_target_pairs={{0,4},{4,0},{8,12},{12,8},{1,5},{5,1},{9,13},{13,9},{2,6},{6,2},{1... | collective-permute-start | bytes 356360 | tf_op jit(solution)/shard_map/ppermute | solution.py:16
  21.9 6.1 %collective-permute-start.7 = (bf16[16,7296]{1,0:T(8,128)(2,1)S(1)}, bf16[16,7296]{1,0:T(8,128)(2,1)S(1)}, u32[]{:S(2)}, u32[]{:S(2)}) collective-permute-start(bf16[16,7296]{1,0:T(8,128)(2,1)S(1)} %join.1.refs_0_), channel_id=1, source_target_pairs={{0,16},{16,0},{1,17},{17,1},{2,18},{18,2},{3,19},{19,3},{4,20},{20... | collective-permute-start | bytes 700424 | tf_op jit(solution)/shard_map/ppermute | solution.py:16
  21.9 7.4 %collective-permute-start.9 = (bf16[16,7296]{1,0:T(8,128)(2,1)S(1)}, bf16[16,7296]{1,0:T(8,128)(2,1)S(1)}, u32[]{:S(2)}, u32[]{:S(2)}) collective-permute-start(bf16[16,7296]{1,0:T(8,128)(2,1)S(1)} %collective-permute-done.4.right_ref.refs_2_), channel_id=1, source_target_pairs={{0,16},{16,0},{1,17},{17,1},{2,18},{18,2},{3,19},{19,3},{4,20},{20... | collective-permute-start | bytes 700424 | tf_op jit(solution)/shard_map/ppermute | solution.py:16
  22.4 6.9 %collective-permute-start.8 = (bf16[16,7296]{1,0:T(8,128)(2,1)S(1)}, bf16[16,7296]{1,0:T(8,128)(2,1)S(1)}, u32[]{:S(2)}, u32[]{:S(2)}) collective-permute-start(bf16[16,7296]{1,0:T(8,128)(2,1)S(1)} %collective-permute-done.3.left_ref.refs_1_), channel_id=1, source_target_pairs={{0,16},{16,0},{1,17},{17,1},{2,18},{18,2},{3,19},{19,3},{4,20},{20... | collective-permute-start | bytes 700424 | tf_op jit(solution)/shard_map/ppermute | solution.py:16
  22.4 5.6 %collective-permute-start.5 = (bf16[16,3584]{1,0:T(8,128)(2,1)S(1)}, bf16[16,3584]{1,0:T(8,128)(2,1)S(1)}, u32[]{:S(2)}, u32[]{:S(2)}) collective-permute-start(bf16[16,3584]{1,0:T(8,128)(2,1)S(1)} %get-tuple-element.23), channel_id=1, source_target_pairs={{0,8},{4,12},{8,0},{12,4},{1,9},{5,13},{9,1},{13,5},{2,10},{6,14},... | collective-permute-start | bytes 344072 | tf_op jit(solution)/shard_map/ppermute | solution.py:16
  25.3 4.1 %collective-permute-start.11 = (bf16[16,3712]{1,0:T(8,128)(2,1)S(1)}, bf16[16,3712]{1,0:T(8,128)(2,1)S(1)}, u32[]{:S(2)}, u32[]{:S(2)}) collective-permute-start(bf16[16,3712]{1,0:T(8,128)(2,1)S(1)} %collective-permute-done.6.refs_4_), channel_id=1, source_target_pairs={{0,16},{16,0},{1,17},{17,1},{2,18},{18,2},{3,19},{19,3},{4,20},{20... | collective-permute-start | bytes 356360 | tf_op jit(solution)/shard_map/ppermute | solution.py:16
  28.0 1.3 %collective-permute-start.10 = (bf16[16,3584]{1,0:T(8,128)(2,1)S(1)}, bf16[16,3584]{1,0:T(8,128)(2,1)S(1)}, u32[]{:S(2)}, u32[]{:S(2)}) collective-permute-start(bf16[16,3584]{1,0:T(8,128)(2,1)S(1)} %collective-permute-done.5.refs_3_), channel_id=1, source_target_pairs={{0,16},{16,0},{1,17},{17,1},{2,18},{18,2},{3,19},{19,3},{4,20},{20... | collective-permute-start | bytes 344072 | tf_op jit(solution)/shard_map/ppermute | solution.py:16
  40.2 4.2 %collective-permute-start.12 = (bf16[64,3584]{1,0:T(8,128)(2,1)S(1)}, bf16[64,3584]{1,0:T(8,128)(2,1)S(1)}, u32[]{:S(2)}, u32[]{:S(2)}) collective-permute-start(bf16[64,3584]{1,0:T(8,128)(2,1)S(1)} %get-tuple-element.27), channel_id=1, source_target_pairs={{0,16},{16,0},{1,17},{17,1},{2,18},{18,2},{3,19},{19,3},{4,20},{20... | collective-permute-start | bytes 1376264 | tf_op jit(solution)/shard_map/ppermute | solution.py:16
  44.0 1.9 %collective-permute-start.18 = (bf16[64,3584]{1,0:T(8,128)(2,1)S(1)}, bf16[64,3584]{1,0:T(8,128)(2,1)S(1)}, u32[]{:S(2)}, u32[]{:S(2)}) collective-permute-start(bf16[64,3584]{1,0:T(8,128)(2,1)S(1)} %get-tuple-element.30), channel_id=1, source_target_pairs={{0,16},{16,0},{1,17},{17,1},{2,18},{18,2},{3,19},{19,3},{4,20},{20... | collective-permute-start | bytes 1376264 | tf_op jit(solution)/shard_map/ppermute | solution.py:16
  44.6 7.7 %collective-permute-start.13 = (bf16[32,3584]{1,0:T(8,128)(2,1)S(1)}, bf16[32,3584]{1,0:T(8,128)(2,1)S(1)}, u32[]{:S(2)}, u32[]{:S(2)}) collective-permute-start(bf16[32,3584]{1,0:T(8,128)(2,1)S(1)} %slice.65), channel_id=1, source_target_pairs={{0,4},{4,0},{8,12},{12,8},{1,5},{5,1},{9,13},{13,9},{2,6},{6,2},{1... | collective-permute-start | bytes 688136 | tf_op jit(solution)/shard_map/ppermute | solution.py:16
  46.0 7.9 %collective-permute-start.19 = (bf16[32,3584]{1,0:T(8,128)(2,1)S(1)}, bf16[32,3584]{1,0:T(8,128)(2,1)S(1)}, u32[]{:S(2)}, u32[]{:S(2)}) collective-permute-start(bf16[32,3584]{1,0:T(8,128)(2,1)S(1)} %slice.73), channel_id=1, source_target_pairs={{0,8},{4,12},{8,0},{12,4},{1,9},{5,13},{9,1},{13,5},{2,10},{6,14},... | collective-permute-start | bytes 688136 | tf_op jit(solution)/shard_map/ppermute | solution.py:16
  52.4 4.9 %collective-permute-start.14 = (bf16[16,3584]{1,0:T(8,128)(2,1)S(1)}, bf16[16,3584]{1,0:T(8,128)(2,1)S(1)}, u32[]{:S(2)}, u32[]{:S(2)}) collective-permute-start(bf16[16,3584]{1,0:T(8,128)(2,1)S(1)} %slice.67), channel_id=1, source_target_pairs={{0,8},{4,12},{8,0},{12,4},{1,9},{5,13},{9,1},{13,5},{2,10},{6,14},... | collective-permute-start | bytes 344072 | tf_op jit(solution)/shard_map/ppermute | solution.py:16
  54.0 7.4 %collective-permute-start.20 = (bf16[16,3584]{1,0:T(8,128)(2,1)S(1)}, bf16[16,3584]{1,0:T(8,128)(2,1)S(1)}, u32[]{:S(2)}, u32[]{:S(2)}) collective-permute-start(bf16[16,3584]{1,0:T(8,128)(2,1)S(1)} %slice.75), channel_id=1, source_target_pairs={{0,4},{4,0},{8,12},{12,8},{1,5},{5,1},{9,13},{13,9},{2,6},{6,2},{1... | collective-permute-start | bytes 344072 | tf_op jit(solution)/shard_map/ppermute | solution.py:16
  57.3 8.4 %collective-permute-start.15 = (bf16[4,3584]{1,0:T(4,128)(2,1)S(1)}, bf16[4,3584]{1,0:T(4,128)(2,1)S(1)}, u32[]{:S(2)}, u32[]{:S(2)}) collective-permute-start(bf16[4,3584]{1,0:T(4,128)(2,1)S(1)} %get-tuple-element.31), channel_id=1, source_target_pairs={{0,1},{1,0},{2,3},{3,2},{4,5},{5,4},{6,7},{7,6},{8,9},{9,8},{10,11... | collective-permute-start | bytes 86024 | tf_op jit(solution)/shard_map/ppermute | solution.py:16
  58.8 6.9 %collective-permute-start.17 = (bf16[4,3584]{1,0:T(4,128)(2,1)S(1)}, bf16[4,3584]{1,0:T(4,128)(2,1)S(1)}, u32[]{:S(2)}, u32[]{:S(2)}) collective-permute-start(bf16[4,3584]{1,0:T(4,128)(2,1)S(1)} %get-tuple-element.32), channel_id=1, source_target_pairs={{0,3},{1,2},{2,1},{3,0},{4,7},{5,6},{6,5},{7,4},{8,11},{9,10},{10,... | collective-permute-start | bytes 86024 | tf_op jit(solution)/shard_map/ppermute | solution.py:16
  61.1 5.2 %collective-permute-start.16 = (bf16[4,3584]{1,0:T(4,128)(2,1)S(1)}, bf16[4,3584]{1,0:T(4,128)(2,1)S(1)}, u32[]{:S(2)}, u32[]{:S(2)}) collective-permute-start(bf16[4,3584]{1,0:T(4,128)(2,1)S(1)} %get-tuple-element.33), channel_id=1, source_target_pairs={{0,2},{1,3},{2,0},{3,1},{4,6},{5,7},{6,4},{7,5},{8,10},{9,11},{10,... | collective-permute-start | bytes 86024 | tf_op jit(solution)/shard_map/ppermute | solution.py:16
  61.5 4.9 %collective-permute-start.21 = (bf16[4,3584]{1,0:T(4,128)(2,1)S(1)}, bf16[4,3584]{1,0:T(4,128)(2,1)S(1)}, u32[]{:S(2)}, u32[]{:S(2)}) collective-permute-start(bf16[4,3584]{1,0:T(4,128)(2,1)S(1)} %get-tuple-element.34), channel_id=1, source_target_pairs={{0,1},{1,0},{2,3},{3,2},{4,5},{5,4},{6,7},{7,6},{8,9},{9,8},{10,11... | collective-permute-start | bytes 86024 | tf_op jit(solution)/shard_map/ppermute | solution.py:16
  63.3 5.7 %collective-permute-start.23 = (bf16[4,3584]{1,0:T(4,128)(2,1)S(1)}, bf16[4,3584]{1,0:T(4,128)(2,1)S(1)}, u32[]{:S(2)}, u32[]{:S(2)}) collective-permute-start(bf16[4,3584]{1,0:T(4,128)(2,1)S(1)} %get-tuple-element.35), channel_id=1, source_target_pairs={{0,3},{1,2},{2,1},{3,0},{4,7},{5,6},{6,5},{7,4},{8,11},{9,10},{10,... | collective-permute-start | bytes 86024 | tf_op jit(solution)/shard_map/ppermute | solution.py:16
  65.7 4.8 %collective-permute-start.22 = (bf16[4,3584]{1,0:T(4,128)(2,1)S(1)}, bf16[4,3584]{1,0:T(4,128)(2,1)S(1)}, u32[]{:S(2)}, u32[]{:S(2)}) collective-permute-start(bf16[4,3584]{1,0:T(4,128)(2,1)S(1)} %get-tuple-element.36), channel_id=1, source_target_pairs={{0,2},{1,3},{2,0},{3,1},{4,6},{5,7},{6,4},{7,5},{8,10},{9,11},{10,... | collective-permute-start | bytes 86024 | tf_op jit(solution)/shard_map/ppermute | solution.py:16

commit v7 on v6

--- a/solution.py
+++ b/solution.py
@@ -38,7 +38,7 @@
     for copy in copies:
         copy.start()
     rows, width = tokens_ref.shape
-    half = (out_ref.shape[1] - width) // 2
+    half = (out_ref.shape[2] - width) // 2
     lane = lax.broadcasted_iota(jnp.int32, (rows, half * 2), 1)
     dense = jnp.zeros((rows, half * 2), jnp.float32)
     for copy in copies:
@@ -47,15 +47,17 @@
         mine = lax.rem(lane, half) == ids_ref[:, k:k + 1]
         dense = dense + jnp.where(mine, weights_ref[:, k:k + 1], 0.0)
     high = dense.astype(jnp.bfloat16).astype(jnp.float32)
-    out_ref[:, :width] = tokens_ref[...]
-    out_ref[:, width:] = jnp.where(lane < half, high, dense - high).astype(jnp.bfloat16)
-
-
-def extend(tokens, ids, weights, half):
+    extra = jnp.where(lane < half, high, dense - high).astype(jnp.bfloat16)
+    for copy in range(out_ref.shape[0]):
+        out_ref[copy, :, :width] = tokens_ref[...]
+        out_ref[copy, :, width:] = extra
+
+
+def extend(tokens, ids, weights, half, copies):
     rows, width = tokens.shape
     return pl.pallas_call(
         extend_kernel,
-        out_shape=jax.ShapeDtypeStruct((rows, width + 2 * half), tokens.dtype),
+        out_shape=jax.ShapeDtypeStruct((copies, rows, width + 2 * half), tokens.dtype),
         in_specs=[pl.BlockSpec(memory_space=pl.ANY)] * 3,
         out_specs=pl.BlockSpec(memory_space=pltpu.VMEM),
         scratch_shapes=[pltpu.VMEM(v.shape, v.dtype) for v in (tokens, ids, weights)]
@@ -65,59 +67,40 @@
     )(*(pltpu.with_memory_space_constraint(v, pltpu.HBM) for v in (tokens, ids, weights)))
 
 
-def join_kernel(*refs):
-    pieces, out_ref = refs[:-1], refs[-1]
-    values = [p[...].astype(jnp.float32) for p in pieces]
-    out_ref[...] = jnp.concatenate(values, axis=0).astype(out_ref.dtype)
-
-
-def join(pieces):
-    rows, width = pieces[0].shape
-    out = jax.ShapeDtypeStruct((rows * len(pieces), width), pieces[0].dtype)
-    return vmem_call(join_kernel, out, "join", *pieces)
-
-
-def halves_kernel(left_ref, right_ref, left_out, right_out):
-    half = left_out.shape[1]
-    left_out[...] = left_ref[:, :half]
-    right_out[...] = right_ref[:, half:]
-
-
-def halves(left, right):
-    rows, width = left.shape
-    half = width // 256 * 128
-    out = (
-        jax.ShapeDtypeStruct((rows, half), left.dtype),
-        jax.ShapeDtypeStruct((rows, width - half), left.dtype),
-    )
-    return vmem_call(halves_kernel, out, "halves", left, right)
+def join_kernel(pieces_ref, out_ref):
+    values = [pieces_ref[i].astype(jnp.float32) for i in range(pieces_ref.shape[0])]
+    line = jnp.concatenate(values, axis=0).astype(out_ref.dtype)
+    for copy in range(out_ref.shape[0]):
+        out_ref[copy] = line
+
+
+def join(pieces, copies):
+    count, rows, width = pieces.shape
+    out = jax.ShapeDtypeStruct((copies, count * rows, width), pieces.dtype)
+    return vmem_call(join_kernel, out, "join", pieces)
+
+
+def everywhere(value, axis):
+    return lax.all_to_all(value, axis, split_axis=0, concat_axis=0, tiled=True)
 
 
 def gather_rows(block, w_up):
-    lanes, groups, sects = (lax.axis_size(a) for a in ("dev", "grp", "sect"))
-    arrived = [swap(block, "dev", m) for m in range(1, lanes)]
+    groups, sects = lax.axis_size("grp"), lax.axis_size("sect")
+    arrived = everywhere(block, "dev")
     w_up, token = fetch(w_up, block)
     arrived, token = lax.optimization_barrier((arrived, token))
-    line = join([block] + arrived)
-    if groups == 4:
-        by_x, by_y = swap(line, "grp", 1), swap(line, "grp", 2)
-        from_x, from_y = halves(by_x, by_y)
-        corner = [swap(from_x, "grp", 2), swap(from_y, "grp", 1)]
-        entries = [[line], [by_x], [by_y], corner]
-    else:
-        entries = [[line]]
-        for bit in bits_of(groups):
-            entries = entries + [[swap(p, "grp", bit) for p in e] for e in entries]
+    lines = everywhere(join(arrived, groups), "grp")
+    entries = [lines]
     for bit in bits_of(sects):
-        entries = entries + [[swap(p, "sect", bit) for p in e] for e in entries]
+        entries = entries + [swap(e, "sect", bit) for e in entries]
     return entries, w_up, token
 
 
-def down_product(order, line, hidden_ref, down_ref, keep_ref, send_ref, sems, copy_of):
+def down_product(hidden_ref, down_ref, keep_ref, send_ref, sems, copy_of):
     blocks = sems.shape[0]
     block = keep_ref.shape[1] // blocks
     experts, depth, _ = down_ref.shape
-    groups = len(order)
+    middle = keep_ref.shape[0]
 
     @pl.loop(0, blocks)
     def _(step):
@@ -126,11 +109,8 @@
         weight = down_ref[:, :, columns].reshape(experts * depth, block)
         total = jnp.dot(hidden_ref[...], weight, preferred_element_type=jnp.float32)
         total = total.astype(jnp.bfloat16)
-        for place, entry in enumerate(order):
-            rows = pl.ds(place * line, line)
-            keep_ref[rows, columns] = total[entry * line:(entry + 1) * line]
-            low = (groups + entry) * line
-            send_ref[rows, columns] = total[low:low + line]
+        keep_ref[:, columns] = total[:middle]
+        send_ref[:, columns] = total[middle:]
 
 
 def down_copy(start, down_hbm, down_ref, sems):
@@ -147,29 +127,24 @@
     return copy
 
 
-def up_kernel(layout, width, order, start, token_ref, *refs):
-    pieces = refs[: sum(layout)]
+def up_kernel(entry_count, width, start, token_ref, *refs):
+    entries = refs[:entry_count]
     (upw_ref, gate_hbm, down_hbm, hidden_ref, keep_ref, send_ref,
-     rows_ref, up_ref, gate_ref, gate_sems, down_ref, sems) = refs[sum(layout):]
+     rows_ref, up_ref, gate_ref, gate_sems, down_ref, sems) = refs[entry_count:]
     experts, _, hidden = upw_ref.shape
     place = lax.axis_index("sect") * lax.axis_size("grp") + lax.axis_index("grp")
     first = place * experts
-    line = pieces[0].shape[0]
     block = min(256, hidden)
     gate_copies = weight_copies(gate_hbm, gate_ref, gate_sems)
     for gate_copy in gate_copies:
         gate_copy.start()
     copy = down_copy(start, down_hbm, down_ref, sems)
-    for step in range(sems.shape[0]):
-        copy(step).start()
 
     at = 0
-    for entry, count in enumerate(layout):
-        left = 0
-        for piece in pieces[at:at + count]:
-            rows_ref[pl.ds(entry * line, line), pl.ds(left, piece.shape[1])] = piece[...]
-            left += piece.shape[1]
-        at += count
+    for entry in entries:
+        for i in range(entry.shape[0]):
+            rows_ref[pl.ds(at, entry.shape[1])] = entry[i]
+            at += entry.shape[1]
 
     for e in range(experts):
 
@@ -188,6 +163,9 @@
         scale = jnp.sum(jnp.where(mine, extra, 0.0), axis=1, keepdims=True)
         for gate_copy in gate_copies[e * parts:(e + 1) * parts]:
             gate_copy.wait()
+        if e == 0:
+            for step in range(sems.shape[0]):
+                copy(step).start()
 
         @pl.loop(0, hidden // block)
         def _(step):
@@ -199,7 +177,7 @@
             out = pl.ds(pl.multiple_of(e * hidden + step * block, block), block)
             hidden_ref[:, out] = value.astype(jnp.bfloat16)
 
-    down_product(order, line, hidden_ref, down_ref, keep_ref, send_ref, sems, copy)
+    down_product(hidden_ref, down_ref, keep_ref, send_ref, sems, copy)
 
 
 def fetch_kernel(after_ref, source_ref, target_ref, token_ref, sems):
@@ -254,20 +232,17 @@
     ]
 
 
-def up_call(entries, w_gate, w_up, w_down, token, order, start, columns):
-    layout = [len(e) for e in entries]
-    flat = [p for e in entries for p in e]
+def up_call(entries, w_gate, w_up, w_down, token, start, columns):
     experts, width, hidden = w_up.shape
-    line = flat[0].shape[0]
-    full = sum(p.shape[1] for p in entries[0])
-    rows = line * len(entries)
+    groups, line, full = entries[0].shape
+    rows = groups * line * len(entries)
     whole = pl.BlockSpec(memory_space=pltpu.VMEM)
     anywhere = pl.BlockSpec(memory_space=pl.ANY)
     out = jax.ShapeDtypeStruct((rows // 2, columns), jnp.bfloat16)
     return pl.pallas_call(
-        functools.partial(up_kernel, layout, width, order, start),
+        functools.partial(up_kernel, len(entries), width, start),
         out_shape=(jax.ShapeDtypeStruct((rows, experts * hidden), jnp.bfloat16), out, out),
-        in_specs=[anywhere] + [whole] * (len(flat) + 1) + [anywhere] * 2,
+        in_specs=[anywhere] + [whole] * (len(entries) + 1) + [anywhere] * 2,
         out_specs=(whole,) * 3,
         scratch_shapes=[
             pltpu.VMEM((rows, full), jnp.bfloat16),
@@ -285,26 +260,26 @@
         name="gate_up",
     )(
         token,
-        *flat,
+        *entries,
         pltpu.with_memory_space_constraint(w_up, pltpu.VMEM),
         pltpu.with_memory_space_constraint(w_gate, pltpu.HBM),
         pltpu.with_memory_space_constraint(w_down, pltpu.HBM),
     )
 
 
-def down_kernel(order, line, start, hidden_ref, down_hbm, keep_ref, send_ref, down_ref, sems):
+def down_kernel(start, hidden_ref, down_hbm, keep_ref, send_ref, down_ref, sems):
     copy = down_copy(start, down_hbm, down_ref, sems)
     for step in range(sems.shape[0]):
         copy(step).start()
-    down_product(order, line, hidden_ref, down_ref, keep_ref, send_ref, sems, copy)
-
-
-def down_call(order, line, hidden, w_down, start, columns):
-    rows = line * len(order)
+    down_product(hidden_ref, down_ref, keep_ref, send_ref, sems, copy)
+
+
+def down_call(hidden, w_down, start, columns):
+    rows = hidden.shape[0] // 2
     out = jax.ShapeDtypeStruct((rows, columns), jnp.bfloat16)
     whole = pl.BlockSpec(memory_space=pltpu.VMEM)
     return pl.pallas_call(
-        functools.partial(down_kernel, order, line, start),
+        functools.partial(down_kernel, start),
         out_shape=(out, out),
         in_specs=[whole, pl.BlockSpec(memory_space=pl.ANY)],
         out_specs=(whole, whole),
@@ -333,35 +308,22 @@
     expert_count = sects * groups * experts
 
     half = -(-expert_count // 64) * 64
-    block = extend(tokens, expert_ids, gate_weights, half)
+    block = extend(tokens, expert_ids, gate_weights, half, lanes)
     entries, w_up, token = gather_rows(block, w_up)
 
+    chunk = width // CHUNKS
+    sums = []
+    for c in range(CHUNKS):
+        if c == 0:
+            hidden, keep, send = up_call(entries, w_gate, w_up, w_down, token, 0, chunk)
+        else:
+            keep, send = down_call(hidden, w_down, c * chunk, chunk)
+        sums.append(add(keep, swap(send, "sect", 1)))
     line = lanes * row_count
-    results = []
-    chunk = width // CHUNKS
-    hidden = None
-    for c in range(CHUNKS):
-        bits = bits_of(groups)
-        bits = bits if c % 2 else bits[::-1]
-        order = [0]
-        for bit in bits:
-            order = order + [o | bit for o in order]
-        if c == 0:
-            hidden, keep, send = up_call(
-                entries, w_gate, w_up, w_down, token, order, 0, chunk
-            )
-        else:
-            keep, send = down_call(order, line, hidden, w_down, c * chunk, chunk)
-        value = add(keep, swap(send, "sect", 1))
-        for bit in bits[::-1]:
-            middle = value.shape[0] // 2
-            arrived = swap(value[middle:], "grp", bit)
-            value = add(value[:middle], arrived)
-        pieces = [value[:row_count]]
-        for m in range(1, lanes):
-            pieces.append(swap(value[m * row_count:(m + 1) * row_count], "dev", m))
-        results.append(add(*pieces))
-    return jnp.concatenate(results, axis=1)
+    arrived = everywhere(jnp.concatenate(sums, axis=1), "grp").reshape(groups, line, width)
+    value = add(*(arrived[g] for g in range(groups)))
+    arrived = everywhere(value.reshape(lanes, row_count, width), "dev")
+    return add(*(arrived[d] for d in range(lanes)))
 
 
 def solution(mesh):

time: 71.3 us -> 86.6 us (1.21)
  blocking collectives: 0 us -> 44.2 us
  waiting for transfers between devices: 26 us -> 3.83 us
  starting transfers between devices: 22.9 us -> 6.97 us
  local copies, waits for them, and re-layouts: 0.13 us -> 10.5 us
  Pallas kernels: 20.8 us -> 19.7 us
    all_to_all x0 -> x3, blocking collectives: none -> 44.2 us  [everywhere(): return lax.all_to_all(value, axis, split_axis=0, concat_axis=0, tiled=True)]
    ppermute x24 -> x3, waiting for transfers between devices: 26 us -> 3.82 us  [swap(): lax.ppermute(value, axis, [(i, i ^ mask) for i in range(lax.axis_size(axi...]
    ppermute x24 -> x3, starting transfers between devices: 22.9 us -> 0.64 us  [swap(): lax.ppermute(value, axis, [(i, i ^ mask) for i in range(lax.axis_size(axi...]
    unnamed x0 -> x4, local copies, waits for them, and re-layouts: none -> 10.4 us
    all_to_all x0 -> x1, starting transfers between devices: none -> 6.33 us  [everywhere(): return lax.all_to_all(value, axis, split_axis=0, concat_axis=0, tiled=True)]
    pallas_call x3, Pallas kernels: 15.4 us -> 14.3 us  [the longest x1 9.05 us: up_call(): pl.pallas_call(functools.partial(up_kernel, len(entries), width, start),...]
  transfers between devices with their start and end apart: 24 -> 4, of which waited for: 12 -> 2; matrix products, arithmetic and copies ran while one was open for 1% -> 0% of each run, Pallas kernels for 12% -> 10%
where the time goes in v7:
time: 86.6 us; the launch traced here: 86.2 us
  blocking collectives  44.2 us (51%)
  Pallas kernels  19.7 us (23%)
  local copies, waits for them, and re-layouts  10.5 us (12%)
  starting transfers between devices  6.97 us (8%)
  waiting for transfers between devices  3.83 us (4%)
  other arithmetic  1.08 us (1%)
    all_to_all x3, blocking collectives, everywhere(): return lax.all_to_all(value, axis, split_axis=0, concat_axis=0, tiled=True)  44.2 us
    unnamed x4, local copies, waits for them, and re-layouts  10.4 us
    pallas_call x1, Pallas kernels, up_call(): pl.pallas_call(functools.partial(up_kernel, len(entries), width, start),...  9.05 us
    all_to_all x1, starting transfers between devices, everywhere(): return lax.all_to_all(value, axis, split_axis=0, concat_axis=0, tiled=True)  6.33 us
    pallas_call x1, Pallas kernels, fetch(): pl.pallas_call(fetch_kernel, out_shape=(pltpu.VMEM(weight.shape, weight.d...  5.31 us
    ppermute x3, waiting for transfers between devices, swap(): lax.ppermute(value, axis, [(i, i ^ mask) for i in range(lax.axis_size(axi...  3.82 us
    pallas_call x1, Pallas kernels, down_call(): pl.pallas_call(functools.partial(down_kernel, start), out_shape=(out, out...  3.55 us
  transfers between devices with their start and end apart: 4, of which 2 were waited for; matrix products, arithmetic and copies ran while one was open for 0% of the time, Pallas kernels for 10%

profile of v7, /device:TPU:0, one launch (start us, length us, event | category | flops | bytes accessed | tf_op | source)
XLA Modules:
  0.0 86.2 jit_solution(13242895457699864603)
XLA Ops:
  0.0 1.7 %extend.1.after_ref = bf16[4,4,7296]{2,1,0:T(4,128)(2,1)} custom-call(bf16[4,7168]{1,0:T(4,128)(2,1)} %tokens_hbm.1, s32[4,8]{1,0:T(4,128)} %ids_hbm.1, f32[4,8]{1,0:T(4,128)} %weights_hbm.1), custom_call_target="tpu_custom_call" | custom-call | tf_op jit(solution)/shard_map/extend/pallas_call | solution.py:58
  1.7 6.3 %all-to-all-start = ((bf16[4,4,7296]{2,1,0:T(4,128)(2,1)}), bf16[4,4,7296]{2,1,0:T(4,128)(2,1)S(1)}, u32[]{:S(2)}, u32[]{:S(2)}) async-start(bf16[4,4,7296]{2,1,0:T(4,128)(2,1)} %extend.1.after_ref), calls=%async_computation | async-start | bytes 466944 | tf_op jit(solution)/shard_map/all_to_all | solution.py:84
  8.0 5.3 %fetch.1 = (bf16[2,7168,512]{2,1,0:T(8,128)(2,1)S(1)}, f32[8,128]{1,0:T(8,128)S(1)}) custom-call(bf16[4,4,7296]{2,1,0:T(4,128)(2,1)} %extend.1.after_ref, bf16[2,7168,512]{2,1,0:T(8,128)(2,1)} %source_ref.1), custom_call_target="tpu_custom_call" | custom-call | bytes 14680064 | tf_op jit(solution)/shard_map/fetch/pallas_call | solution.py:209
  13.3 0.0 copy-start
  13.3 5.2 %copy-done = bf16[2,7168,512]{2,1,0:T(8,128)(2,1)} copy-done((bf16[2,7168,512]{2,1,0:T(8,128)(2,1)}, bf16[2,7168,512]{2,1,0:T(8,128)(2,1)S(1)}, u32[]{:S(2)}) %copy-start) | copy-done | bytes 14680088
  18.5 0.0 all-to-all-done.pieces_ref
  18.5 0.1 join.1
  18.6 16.5 %all_to_all.24.refs_0_ = bf16[4,16,7296]{2,1,0:T(8,128)(2,1)S(1)} all-to-all(bf16[4,16,7296]{2,1,0:T(8,128)(2,1)S(1)} %join.1), channel_id=1, replica_groups=mesh['sect'=2,'grp'=4,'dev'=4] {'grp'}, dimensions={0} | all-to-all | bytes 1867776 | tf_op jit(solution)/shard_map/all_to_all | solution.py:84
  35.1 0.0 collective-permute-start
  35.1 2.5 %collective-permute-done.refs_1_ = bf16[4,16,7296]{2,1,0:T(8,128)(2,1)S(1)} collective-permute-done((bf16[4,16,7296]{2,1,0:T(8,128)(2,1)S(1)}, bf16[4,16,7296]{2,1,0:T(8,128)(2,1)S(1)}, u32[]{:S(2)}, u32[]{:S(2)}) %collective-permute-start) | collective-permute-done | bytes 933920 | tf_op jit(solution)/shard_map/ppermute | solution.py:16
  37.6 0.0 copy-start.1
  37.6 5.2 %copy-done.1 = bf16[2,7168,512]{2,1,0:T(8,128)(2,1)S(1)} copy-done((bf16[2,7168,512]{2,1,0:T(8,128)(2,1)S(1)}, bf16[2,7168,512]{2,1,0:T(8,128)(2,1)}, u32[]{:S(2)}) %copy-start.1) | copy-done | bytes 14680088
  42.7 9.0 %gate_up.1 = (bf16[128,1024]{1,0:T(8,128)(2,1)S(1)}, bf16[64,3584]{1,0:T(8,128)(2,1)S(1)}, bf16[64,3584]{1,0:T(8,128)(2,1)S(1)}) custom-call(f32[8,128]{1,0:T(8,128)S(1)} %get-tuple-element.15.token_ref, bf16[4,16,7296]{2,1,0:T(8,128)(2,1)S(1)} %all_to_all.24.refs_0_, bf16[4,16,7296]{2,1,0:T(8,128)(2,1)S(1)} %collective-permute-done.refs_1_, ...), custom_call_target="tpu_custom_call" | custom-call | flops 4697620480 | bytes 7340032 | tf_op jit(solution)/shard_map/gate_up/pallas_call | solution.py:242
  51.8 0.2 collective-permute-start.1
  52.0 3.6 %down.1 = (bf16[64,3584]{1,0:T(8,128)(2,1)S(1)}, bf16[64,3584]{1,0:T(8,128)(2,1)S(1)}) custom-call(bf16[128,1024]{1,0:T(8,128)(2,1)S(1)} %get-tuple-element.20.hidden_ref, bf16[2,512,7168]{2,1,0:T(8,128)(2,1)} %down_hbm.1), custom_call_target="tpu_custom_call" | custom-call | flops 939524096 | bytes 7340032 | tf_op jit(solution)/shard_map/down/pallas_call | solution.py:281
  55.6 0.4 collective-permute-start.2
  56.0 0.0 collective-permute-done.1
  56.0 0.1 add_convert_fusion.1
  56.1 1.3 %collective-permute-done.2 = bf16[64,3584]{1,0:T(8,128)(2,1)S(1)} collective-permute-done((bf16[64,3584]{1,0:T(8,128)(2,1)S(1)}, bf16[64,3584]{1,0:T(8,128)(2,1)S(1)}, u32[]{:S(2)}, u32[]{:S(2)}) %collective-permute-start.2) | collective-permute-done | bytes 458784 | tf_op jit(solution)/shard_map/ppermute | solution.py:16
  57.4 0.1 add_convert_fusion
  57.6 0.1 pad_maximum_fusion
  57.6 16.0 %all_to_all.25 = bf16[4,16,7168]{2,1,0:T(8,128)(2,1)S(1)} all-to-all(bf16[4,16,7168]{2,1,0:T(8,128)(2,1)S(1)} %bitcast.3), channel_id=1, replica_groups=mesh['sect'=2,'grp'=4,'dev'=4] {'grp'}, dimensions={0} | all-to-all | bytes 1835008 | tf_op jit(solution)/shard_map/all_to_all | solution.py:84
  73.6 0.1 add_convert_fusion.2
  73.7 0.1 add.42
  73.8 11.7 %all_to_all.26 = bf16[4,4,7168]{2,1,0:T(4,128)(2,1)S(1)} all-to-all(bf16[4,4,7168]{2,1,0:T(4,128)(2,1)S(1)} %add.42), channel_id=1, replica_groups=mesh['sect'=2,'grp'=4,'dev'=4] {'dev'}, dimensions={0} | all-to-all | bytes 458752 | tf_op jit(solution)/shard_map/all_to_all | solution.py:84
  85.5 0.7 fusion
Async XLA Ops:
  1.7 16.9 %all-to-all-start = ((bf16[4,4,7296]{2,1,0:T(4,128)(2,1)}), bf16[4,4,7296]{2,1,0:T(4,128)(2,1)S(1)}, u32[]{:S(2)}, u32[]{:S(2)}) async-start(bf16[4,4,7296]{2,1,0:T(4,128)(2,1)} %extend.1.after_ref), calls=%async_computation | async-start | bytes 466944 | tf_op jit(solution)/shard_map/all_to_all | solution.py:84
  13.3 5.2 %copy-start = (bf16[2,7168,512]{2,1,0:T(8,128)(2,1)}, bf16[2,7168,512]{2,1,0:T(8,128)(2,1)S(1)}, u32[]{:S(2)}) copy-start(bf16[2,7168,512]{2,1,0:T(8,128)(2,1)S(1)} %get-tuple-element.17.refs_2_) | copy-start | bytes 44040196
  35.1 2.5 %collective-permute-start = (bf16[4,16,7296]{2,1,0:T(8,128)(2,1)S(1)}, bf16[4,16,7296]{2,1,0:T(8,128)(2,1)S(1)}, u32[]{:S(2)}, u32[]{:S(2)}) collective-permute-start(bf16[4,16,7296]{2,1,0:T(8,128)(2,1)S(1)} %all_to_all.24.refs_0_), channel_id=1, source_target_pairs={{0,16},{16,0},{1,17},{17,1},{2,18},{18,2},{3,19},{19,3},{4,20},{20... | collective-permute-start | bytes 2801672 | tf_op jit(solution)/shard_map/ppermute | solution.py:16
  37.6 5.2 %copy-start.1 = (bf16[2,7168,512]{2,1,0:T(8,128)(2,1)S(1)}, bf16[2,7168,512]{2,1,0:T(8,128)(2,1)}, u32[]{:S(2)}) copy-start(bf16[2,7168,512]{2,1,0:T(8,128)(2,1)} %copy-done) | copy-start | bytes 44040196
  51.8 4.2 %collective-permute-start.1 = (bf16[64,3584]{1,0:T(8,128)(2,1)S(1)}, bf16[64,3584]{1,0:T(8,128)(2,1)S(1)}, u32[]{:S(2)}, u32[]{:S(2)}) collective-permute-start(bf16[64,3584]{1,0:T(8,128)(2,1)S(1)} %get-tuple-element.19), channel_id=1, source_target_pairs={{0,16},{16,0},{1,17},{17,1},{2,18},{18,2},{3,19},{19,3},{4,20},{20... | collective-permute-start | bytes 1376264 | tf_op jit(solution)/shard_map/ppermute | solution.py:16
  55.6 1.9 %collective-permute-start.2 = (bf16[64,3584]{1,0:T(8,128)(2,1)S(1)}, bf16[64,3584]{1,0:T(8,128)(2,1)S(1)}, u32[]{:S(2)}, u32[]{:S(2)}) collective-permute-start(bf16[64,3584]{1,0:T(8,128)(2,1)S(1)} %get-tuple-element.22), channel_id=1, source_target_pairs={{0,16},{16,0},{1,17},{17,1},{2,18},{18,2},{3,19},{19,3},{4,20},{20... | collective-permute-start | bytes 1376264 | tf_op jit(solution)/shard_map/ppermute | solution.py:16

commit v8 on v6

--- a/solution.py
+++ b/solution.py
@@ -65,16 +65,16 @@
     )(*(pltpu.with_memory_space_constraint(v, pltpu.HBM) for v in (tokens, ids, weights)))
 
 
-def join_kernel(*refs):
+def stack_kernel(*refs):
     pieces, out_ref = refs[:-1], refs[-1]
     values = [p[...].astype(jnp.float32) for p in pieces]
     out_ref[...] = jnp.concatenate(values, axis=0).astype(out_ref.dtype)
 
 
-def join(pieces):
-    rows, width = pieces[0].shape
-    out = jax.ShapeDtypeStruct((rows * len(pieces), width), pieces[0].dtype)
-    return vmem_call(join_kernel, out, "join", *pieces)
+def stack(*pieces):
+    rows = sum(p.shape[0] for p in pieces)
+    out = jax.ShapeDtypeStruct((rows, pieces[0].shape[1]), pieces[0].dtype)
+    return vmem_call(stack_kernel, out, "stack", *pieces)
 
 
 def halves_kernel(left_ref, right_ref, left_out, right_out):
@@ -93,31 +93,51 @@
     return vmem_call(halves_kernel, out, "halves", left, right)
 
 
+def gather_kernel(by_x_ref, by_y_ref, left_ref, right_ref, out_ref):
+    line, half = left_ref.shape
+    out_ref[:line] = by_x_ref[...]
+    out_ref[line:2 * line] = by_y_ref[...]
+    out_ref[2 * line:, :half] = left_ref[...]
+    out_ref[2 * line:, half:] = right_ref[...]
+
+
 def gather_rows(block, w_up):
     lanes, groups, sects = (lax.axis_size(a) for a in ("dev", "grp", "sect"))
-    arrived = [swap(block, "dev", m) for m in range(1, lanes)]
-    w_up, token = fetch(w_up, block)
-    arrived, token = lax.optimization_barrier((arrived, token))
-    line = join([block] + arrived)
+    line, weights, token = block, [], block
+    experts = list(range(w_up.shape[0]))
+    for bit in bits_of(lanes)[::-1]:
+        arrived = swap(line, "dev", bit)
+        if experts:
+            weight, token = fetch(w_up, experts.pop(0), token)
+            weights.append(weight)
+            arrived, token = lax.optimization_barrier((arrived, token))
+        line = stack(line, arrived)
+    while experts:
+        weight, token = fetch(w_up, experts.pop(0), token)
+        weights.append(weight)
     if groups == 4:
-        by_x, by_y = swap(line, "grp", 1), swap(line, "grp", 2)
+        by_x, by_y, mine = swap(line, "grp", 1), swap(line, "grp", 2), swap(line, "sect", 1)
+        by_x, by_y, mine = lax.optimization_barrier((by_x, by_y, mine))
         from_x, from_y = halves(by_x, by_y)
-        corner = [swap(from_x, "grp", 2), swap(from_y, "grp", 1)]
-        entries = [[line], [by_x], [by_y], corner]
+        left, right = swap(from_x, "grp", 2), swap(from_y, "grp", 1)
+        out = jax.ShapeDtypeStruct((3 * line.shape[0], line.shape[1]), line.dtype)
+        rest = vmem_call(gather_kernel, out, "gather", by_x, by_y, left, right)
+        entries = [line, rest, mine, swap(rest, "sect", 1)]
     else:
-        entries = [[line]]
+        entries = [line]
         for bit in bits_of(groups):
-            entries = entries + [[swap(p, "grp", bit) for p in e] for e in entries]
-    for bit in bits_of(sects):
-        entries = entries + [[swap(p, "sect", bit) for p in e] for e in entries]
-    return entries, w_up, token
-
-
-def down_product(order, line, hidden_ref, down_ref, keep_ref, send_ref, sems, copy_of):
+            entries = entries + [swap(e, "grp", bit) for e in entries]
+        for bit in bits_of(sects):
+            entries = entries + [swap(e, "sect", bit) for e in entries]
+    return entries, weights, token
+
+
+def down_product(order, hidden_ref, down_ref, keep_ref, send_ref, sems, copy_of):
     blocks = sems.shape[0]
     block = keep_ref.shape[1] // blocks
     experts, depth, _ = down_ref.shape
     groups = len(order)
+    line = keep_ref.shape[0] // groups
 
     @pl.loop(0, blocks)
     def _(step):
@@ -147,29 +167,23 @@
     return copy
 
 
-def up_kernel(layout, width, order, start, token_ref, *refs):
-    pieces = refs[: sum(layout)]
-    (upw_ref, gate_hbm, down_hbm, hidden_ref, keep_ref, send_ref,
-     rows_ref, up_ref, gate_ref, gate_sems, down_ref, sems) = refs[sum(layout):]
-    experts, _, hidden = upw_ref.shape
+def up_kernel(counts, width, order, start, token_ref, *refs):
+    pieces, up_refs = refs[:counts[0]], refs[counts[0]:sum(counts)]
+    (gate_hbm, down_hbm, hidden_ref, keep_ref, send_ref,
+     rows_ref, up_ref, gate_ref, gate_sems, down_ref, sems) = refs[sum(counts):]
+    experts, _, hidden = gate_ref.shape
     place = lax.axis_index("sect") * lax.axis_size("grp") + lax.axis_index("grp")
     first = place * experts
-    line = pieces[0].shape[0]
     block = min(256, hidden)
     gate_copies = weight_copies(gate_hbm, gate_ref, gate_sems)
     for gate_copy in gate_copies:
         gate_copy.start()
     copy = down_copy(start, down_hbm, down_ref, sems)
-    for step in range(sems.shape[0]):
-        copy(step).start()
 
     at = 0
-    for entry, count in enumerate(layout):
-        left = 0
-        for piece in pieces[at:at + count]:
-            rows_ref[pl.ds(entry * line, line), pl.ds(left, piece.shape[1])] = piece[...]
-            left += piece.shape[1]
-        at += count
+    for piece in pieces:
+        rows_ref[pl.ds(at, piece.shape[0])] = piece[...]
+        at += piece.shape[0]
 
     for e in range(experts):
 
@@ -177,7 +191,7 @@
         def _(step):
             span = pl.ds(pl.multiple_of(step * block, block), block)
             up_ref[e, :, span] = jnp.dot(
-                rows_ref[:, :width], upw_ref[e, :, span], preferred_element_type=jnp.float32
+                rows_ref[:, :width], up_refs[e][0, :, span], preferred_element_type=jnp.float32
             )
 
     extra = rows_ref[:, width:].astype(jnp.float32)
@@ -188,6 +202,9 @@
         scale = jnp.sum(jnp.where(mine, extra, 0.0), axis=1, keepdims=True)
         for gate_copy in gate_copies[e * parts:(e + 1) * parts]:
             gate_copy.wait()
+        if e == 0:
+            for step in range(sems.shape[0]):
+                copy(step).start()
 
         @pl.loop(0, hidden // block)
         def _(step):
@@ -199,11 +216,11 @@
             out = pl.ds(pl.multiple_of(e * hidden + step * block, block), block)
             hidden_ref[:, out] = value.astype(jnp.bfloat16)
 
-    down_product(order, line, hidden_ref, down_ref, keep_ref, send_ref, sems, copy)
-
-
-def fetch_kernel(after_ref, source_ref, target_ref, token_ref, sems):
-    copies = weight_copies(source_ref, target_ref, sems)
+    down_product(order, hidden_ref, down_ref, keep_ref, send_ref, sems, copy)
+
+
+def fetch_kernel(expert, after_ref, source_ref, target_ref, token_ref, sems):
+    copies = weight_copies(source_ref.at[pl.ds(expert, 1)], target_ref, sems)
     for copy in copies:
         copy.start()
     token_ref[...] = jnp.zeros_like(token_ref)
@@ -225,21 +242,21 @@
     ]
 
 
-def fetch(weight, after):
+def fetch(weight, expert, after):
     in_hbm = pl.BlockSpec(memory_space=pl.ANY)
     in_vmem = pl.BlockSpec(memory_space=pltpu.VMEM)
     return pl.pallas_call(
-        fetch_kernel,
+        functools.partial(fetch_kernel, expert),
         out_shape=(
-            pltpu.VMEM(weight.shape, weight.dtype),
+            pltpu.VMEM((1, *weight.shape[1:]), weight.dtype),
             jax.ShapeDtypeStruct((8, 128), jnp.float32),
         ),
         in_specs=[in_hbm, in_hbm],
         out_specs=(in_vmem, in_vmem),
-        scratch_shapes=[pltpu.SemaphoreType.DMA((weight.shape[0], 4))],
+        scratch_shapes=[pltpu.SemaphoreType.DMA((1, 8))],
         compiler_params=pltpu.CompilerParams(vmem_limit_bytes=VMEM_LIMIT),
         cost_estimate=pl.CostEstimate(
-            flops=0, bytes_accessed=2 * weight.size, transcendentals=0
+            flops=0, bytes_accessed=2 * weight.size // weight.shape[0], transcendentals=0
         ),
         name="fetch",
     )(after, pltpu.with_memory_space_constraint(weight, pltpu.HBM))
@@ -254,20 +271,18 @@
     ]
 
 
-def up_call(entries, w_gate, w_up, w_down, token, order, start, columns):
-    layout = [len(e) for e in entries]
-    flat = [p for e in entries for p in e]
-    experts, width, hidden = w_up.shape
-    line = flat[0].shape[0]
-    full = sum(p.shape[1] for p in entries[0])
-    rows = line * len(entries)
+def up_call(entries, w_gate, w_ups, w_down, token, order, start, columns):
+    experts, width, hidden = w_gate.shape
+    full = entries[0].shape[1]
+    rows = sum(e.shape[0] for e in entries)
+    counts = (len(entries), len(w_ups))
     whole = pl.BlockSpec(memory_space=pltpu.VMEM)
     anywhere = pl.BlockSpec(memory_space=pl.ANY)
     out = jax.ShapeDtypeStruct((rows // 2, columns), jnp.bfloat16)
     return pl.pallas_call(
-        functools.partial(up_kernel, layout, width, order, start),
+        functools.partial(up_kernel, counts, width, order, start),
         out_shape=(jax.ShapeDtypeStruct((rows, experts * hidden), jnp.bfloat16), out, out),
-        in_specs=[anywhere] + [whole] * (len(flat) + 1) + [anywhere] * 2,
+        in_specs=[anywhere] + [whole] * sum(counts) + [anywhere] * 2,
         out_specs=(whole,) * 3,
         scratch_shapes=[
             pltpu.VMEM((rows, full), jnp.bfloat16),
@@ -285,26 +300,26 @@
         name="gate_up",
     )(
         token,
-        *flat,
-        pltpu.with_memory_space_constraint(w_up, pltpu.VMEM),
+        *entries,
+        *(pltpu.with_memory_space_constraint(w, pltpu.VMEM) for w in w_ups),
         pltpu.with_memory_space_constraint(w_gate, pltpu.HBM),
         pltpu.with_memory_space_constraint(w_down, pltpu.HBM),
     )
 
 
-def down_kernel(order, line, start, hidden_ref, down_hbm, keep_ref, send_ref, down_ref, sems):
+def down_kernel(order, start, hidden_ref, down_hbm, keep_ref, send_ref, down_ref, sems):
     copy = down_copy(start, down_hbm, down_ref, sems)
     for step in range(sems.shape[0]):
         copy(step).start()
-    down_product(order, line, hidden_ref, down_ref, keep_ref, send_ref, sems, copy)
-
-
-def down_call(order, line, hidden, w_down, start, columns):
-    rows = line * len(order)
+    down_product(order, hidden_ref, down_ref, keep_ref, send_ref, sems, copy)
+
+
+def down_call(order, hidden, w_down, start, columns):
+    rows = hidden.shape[0] // 2
     out = jax.ShapeDtypeStruct((rows, columns), jnp.bfloat16)
     whole = pl.BlockSpec(memory_space=pltpu.VMEM)
     return pl.pallas_call(
-        functools.partial(down_kernel, order, line, start),
+        functools.partial(down_kernel, order, start),
         out_shape=(out, out),
         in_specs=[whole, pl.BlockSpec(memory_space=pl.ANY)],
         out_specs=(whole, whole),
@@ -334,9 +349,8 @@
 
     half = -(-expert_count // 64) * 64
     block = extend(tokens, expert_ids, gate_weights, half)
-    entries, w_up, token = gather_rows(block, w_up)
-
-    line = lanes * row_count
+    entries, w_ups, token = gather_rows(block, w_up)
+
     results = []
     chunk = width // CHUNKS
     hidden = None
@@ -348,20 +362,21 @@
             order = order + [o | bit for o in order]
         if c == 0:
             hidden, keep, send = up_call(
-                entries, w_gate, w_up, w_down, token, order, 0, chunk
+                entries, w_gate, w_ups, w_down, token, order, 0, chunk
             )
         else:
-            keep, send = down_call(order, line, hidden, w_down, c * chunk, chunk)
+            keep, send = down_call(order, hidden, w_down, c * chunk, chunk)
         value = add(keep, swap(send, "sect", 1))
         for bit in bits[::-1]:
             middle = value.shape[0] // 2
             arrived = swap(value[middle:], "grp", bit)
             value = add(value[:middle], arrived)
-        pieces = [value[:row_count]]
-        for m in range(1, lanes):
-            pieces.append(swap(value[m * row_count:(m + 1) * row_count], "dev", m))
-        results.append(add(*pieces))
-    return jnp.concatenate(results, axis=1)
+        results.append(value)
+    value = jnp.concatenate(results, axis=1)
+    for bit in bits_of(lanes):
+        middle = value.shape[0] // 2
+        value = add(value[:middle], swap(value[middle:], "dev", bit))
+    return value
 
 
 def solution(mesh):

time: 71.3 us -> 70.4 us (0.987)
  starting transfers between devices: 22.9 us -> 17.7 us
  waiting for transfers between devices: 26 us -> 31.1 us
  Pallas kernels: 20.8 us -> 20 us
    ppermute x24 -> x16, starting transfers between devices: 22.9 us -> 17.7 us  [swap(): lax.ppermute(value, axis, [(i, i ^ mask) for i in range(lax.axis_size(axi...]
    ppermute x24 -> x16, waiting for transfers between devices: 26 us -> 31.1 us  [swap(): lax.ppermute(value, axis, [(i, i ^ mask) for i in range(lax.axis_size(axi...]
    pallas_call x3 -> x4, Pallas kernels: 19.8 us -> 18.9 us  [the longest x1 9.05 us: up_call(): pl.pallas_call(functools.partial(up_kernel, counts, width, order, start),...]
  transfers between devices with their start and end apart: 24 -> 16, of which waited for: 12 -> 12; matrix products, arithmetic and copies ran while one was open for 1% -> 1% of each run, Pallas kernels for 12% -> 14%
where the time goes in v8:
time: 70.4 us; the launch traced here: 70.2 us
  waiting for transfers between devices  31.1 us (44%)
  Pallas kernels  20 us (28%)
  starting transfers between devices  17.7 us (25%)
  other arithmetic  1.09 us (2%)
    ppermute x16, waiting for transfers between devices, swap(): lax.ppermute(value, axis, [(i, i ^ mask) for i in range(lax.axis_size(axi...  31.1 us
    ppermute x16, starting transfers between devices, swap(): lax.ppermute(value, axis, [(i, i ^ mask) for i in range(lax.axis_size(axi...  17.7 us
    pallas_call x1, Pallas kernels, up_call(): pl.pallas_call(functools.partial(up_kernel, counts, width, order, start),...  9.05 us
    pallas_call x2, Pallas kernels, fetch(): pl.pallas_call(functools.partial(fetch_kernel, expert), out_shape=(pltpu....  6.33 us
    pallas_call x1, Pallas kernels, down_call(): pl.pallas_call(functools.partial(down_kernel, order, start), out_shape=(o...  3.55 us
  transfers between devices with their start and end apart: 16, of which 12 were waited for; matrix products, arithmetic and copies ran while one was open for 1% of the time, Pallas kernels for 14%

profile of v8, /device:TPU:0, one launch (start us, length us, event | category | flops | bytes accessed | tf_op | source)
XLA Modules:
  0.0 70.2 jit_solution(8360600981604836511)
XLA Ops:
  0.0 1.0 %extend.1.after_ref.refs_0_ = bf16[4,7296]{1,0:T(4,128)(2,1)S(1)} custom-call(bf16[4,7168]{1,0:T(4,128)(2,1)} %tokens_hbm.1, s32[4,8]{1,0:T(4,128)} %ids_hbm.1, f32[4,8]{1,0:T(4,128)} %weights_hbm.1), custom_call_target="tpu_custom_call" | custom-call | tf_op jit(solution)/shard_map/extend/pallas_call | solution.py:56
  1.0 4.1 %collective-permute-start = (bf16[4,7296]{1,0:T(4,128)(2,1)S(1)}, bf16[4,7296]{1,0:T(4,128)(2,1)S(1)}, u32[]{:S(2)}, u32[]{:S(2)}) collective-permute-start(bf16[4,7296]{1,0:T(4,128)(2,1)S(1)} %extend.1.after_ref.refs_0_), channel_id=1, source_target_pairs={{0,2},{1,3},{2,0},{3,1},{4,6},{5,7},{6,4},{7,5},{8,10},{9,11},{10,... | collective-permute-start | bytes 175112 | tf_op jit(solution)/shard_map/ppermute | solution.py:16
  5.1 3.2 %fetch.2 = (bf16[1,7168,512]{2,1,0:T(8,128)(2,1)S(1)}, f32[8,128]{1,0:T(8,128)S(1)}) custom-call(bf16[4,7296]{1,0:T(4,128)(2,1)S(1)} %extend.1.after_ref.refs_0_, bf16[2,7168,512]{2,1,0:T(8,128)(2,1)} %source_ref.3), custom_call_target="tpu_custom_call" | custom-call | bytes 7340032 | tf_op jit(solution)/shard_map/fetch/pallas_call | solution.py:248
  8.3 0.0 collective-permute-done.refs_1_
  8.3 1.6 %collective-permute-start.1 = (bf16[8,7296]{1,0:T(8,128)(2,1)S(1)}, bf16[8,7296]{1,0:T(8,128)(2,1)S(1)}, u32[]{:S(2)}, u32[]{:S(2)}) collective-permute-start(bf16[8,7296]{1,0:T(8,128)(2,1)S(1)} %stack.2.refs_0_), channel_id=1, source_target_pairs={{0,1},{1,0},{2,3},{3,2},{4,5},{5,4},{6,7},{7,6},{8,9},{9,8},{10,11... | collective-permute-start | bytes 350216 | tf_op jit(solution)/shard_map/ppermute | solution.py:16
  10.0 3.2 %fetch.3 = (bf16[1,7168,512]{2,1,0:T(8,128)(2,1)S(1)}, f32[8,128]{1,0:T(8,128)S(1)}) custom-call(f32[8,128]{1,0:T(8,128)S(1)} %get-tuple-element.25.after_ref, bf16[2,7168,512]{2,1,0:T(8,128)(2,1)} %source_ref.3), custom_call_target="tpu_custom_call" | custom-call | bytes 7340032 | tf_op jit(solution)/shard_map/fetch/pallas_call | solution.py:248
  13.1 0.1 collective-permute-done.1.refs_1_
  13.2 0.1 collective-permute-start.4
  13.3 2.0 %collective-permute-start.3 = (bf16[16,7296]{1,0:T(8,128)(2,1)S(1)}, bf16[16,7296]{1,0:T(8,128)(2,1)S(1)}, u32[]{:S(2)}, u32[]{:S(2)}) collective-permute-start(bf16[16,7296]{1,0:T(8,128)(2,1)S(1)} %stack.3.refs_0_), channel_id=1, source_target_pairs={{0,8},{4,12},{8,0},{12,4},{1,9},{5,13},{9,1},{13,5},{2,10},{6,14},... | collective-permute-start | bytes 700424 | tf_op jit(solution)/shard_map/ppermute | solution.py:16
  15.3 1.5 %collective-permute-start.2 = (bf16[16,7296]{1,0:T(8,128)(2,1)S(1)}, bf16[16,7296]{1,0:T(8,128)(2,1)S(1)}, u32[]{:S(2)}, u32[]{:S(2)}) collective-permute-start(bf16[16,7296]{1,0:T(8,128)(2,1)S(1)} %stack.3.refs_0_), channel_id=1, source_target_pairs={{0,4},{4,0},{8,12},{12,8},{1,5},{5,1},{9,13},{13,9},{2,6},{6,2},{1... | collective-permute-start | bytes 700424 | tf_op jit(solution)/shard_map/ppermute | solution.py:16
  16.8 0.0 collective-permute-done.4.refs_2_
  16.8 4.8 %collective-permute-done.3.right_ref.by_y_ref = bf16[16,7296]{1,0:T(8,128)(2,1)S(1)} collective-permute-done((bf16[16,7296]{1,0:T(8,128)(2,1)S(1)}, bf16[16,7296]{1,0:T(8,128)(2,1)S(1)}, u32[]{:S(2)}, u32[]{:S(2)}) %collective-permute-start.3) | collective-permute-done | bytes 233504 | tf_op jit(solution)/shard_map/ppermute | solution.py:16
  21.6 1.5 %collective-permute-done.2.left_ref.by_x_ref = bf16[16,7296]{1,0:T(8,128)(2,1)S(1)} collective-permute-done((bf16[16,7296]{1,0:T(8,128)(2,1)S(1)}, bf16[16,7296]{1,0:T(8,128)(2,1)S(1)}, u32[]{:S(2)}, u32[]{:S(2)}) %collective-permute-start.2) | collective-permute-done | bytes 233504 | tf_op jit(solution)/shard_map/ppermute | solution.py:16
  23.1 1.6 %collective-permute-start.6 = (bf16[16,3712]{1,0:T(8,128)(2,1)S(1)}, bf16[16,3712]{1,0:T(8,128)(2,1)S(1)}, u32[]{:S(2)}, u32[]{:S(2)}) collective-permute-start(bf16[16,3712]{1,0:T(8,128)(2,1)S(1)} %get-tuple-element.32), channel_id=1, source_target_pairs={{0,4},{4,0},{8,12},{12,8},{1,5},{5,1},{9,13},{13,9},{2,6},{6,2},{1... | collective-permute-start | bytes 356360 | tf_op jit(solution)/shard_map/ppermute | solution.py:16
  24.7 0.5 collective-permute-start.5
  25.2 4.3 %collective-permute-done.5.left_ref = bf16[16,3584]{1,0:T(8,128)(2,1)S(1)} collective-permute-done((bf16[16,3584]{1,0:T(8,128)(2,1)S(1)}, bf16[16,3584]{1,0:T(8,128)(2,1)S(1)}, u32[]{:S(2)}, u32[]{:S(2)}) %collective-permute-start.5) | collective-permute-done | bytes 114720 | tf_op jit(solution)/shard_map/ppermute | solution.py:16
  29.4 0.0 collective-permute-done.6.right_ref
  29.5 0.1 collective-permute-start.7
  29.6 2.1 %collective-permute-done.7.refs_3_ = bf16[48,7296]{1,0:T(8,128)(2,1)S(1)} collective-permute-done((bf16[48,7296]{1,0:T(8,128)(2,1)S(1)}, bf16[48,7296]{1,0:T(8,128)(2,1)S(1)}, u32[]{:S(2)}, u32[]{:S(2)}) %collective-permute-start.7) | collective-permute-done | bytes 700448 | tf_op jit(solution)/shard_map/ppermute | solution.py:16
  31.7 9.0 %gate_up.1 = (bf16[128,1024]{1,0:T(8,128)(2,1)S(1)}, bf16[64,3584]{1,0:T(8,128)(2,1)S(1)}, bf16[64,3584]{1,0:T(8,128)(2,1)S(1)}) custom-call(f32[8,128]{1,0:T(8,128)S(1)} %get-tuple-element.27.token_ref, bf16[16,7296]{1,0:T(8,128)(2,1)S(1)} %stack.3.refs_0_, bf16[48,7296]{1,0:T(8,128)(2,1)S(1)} %gather.1.refs_1_, ...), custom_call_target="tpu_custom_call" | custom-call | flops 4697620480 | bytes 7340032 | tf_op jit(solution)/shard_map/gate_up/pallas_call | solution.py:282
  40.8 0.2 collective-permute-start.8
  41.0 3.6 %down.1 = (bf16[64,3584]{1,0:T(8,128)(2,1)S(1)}, bf16[64,3584]{1,0:T(8,128)(2,1)S(1)}) custom-call(bf16[128,1024]{1,0:T(8,128)(2,1)S(1)} %get-tuple-element.38.hidden_ref, bf16[2,512,7168]{2,1,0:T(8,128)(2,1)} %down_hbm.1), custom_call_target="tpu_custom_call" | custom-call | flops 939524096 | bytes 7340032 | tf_op jit(solution)/shard_map/down/pallas_call | solution.py:321
  44.5 0.4 collective-permute-start.11
  45.0 0.0 collective-permute-done.8
  45.0 0.1 add_convert_fusion.1
  45.1 0.6 collective-permute-start.9
  45.7 0.7 collective-permute-done.11
  46.4 0.1 add_convert_fusion
  46.6 0.6 collective-permute-start.12
  47.1 5.7 %collective-permute-done.9 = bf16[32,3584]{1,0:T(8,128)(2,1)S(1)} collective-permute-done((bf16[32,3584]{1,0:T(8,128)(2,1)S(1)}, bf16[32,3584]{1,0:T(8,128)(2,1)S(1)}, u32[]{:S(2)}, u32[]{:S(2)}) %collective-permute-start.9) | collective-permute-done | bytes 229408 | tf_op jit(solution)/shard_map/ppermute | solution.py:16
  52.8 0.1 add_convert_fusion.3
  52.9 0.5 collective-permute-start.10
  53.5 1.0 %collective-permute-done.12 = bf16[32,3584]{1,0:T(8,128)(2,1)S(1)} collective-permute-done((bf16[32,3584]{1,0:T(8,128)(2,1)S(1)}, bf16[32,3584]{1,0:T(8,128)(2,1)S(1)}, u32[]{:S(2)}, u32[]{:S(2)}) %collective-permute-start.12) | collective-permute-done | bytes 229408 | tf_op jit(solution)/shard_map/ppermute | solution.py:16
  54.5 0.1 add_convert_fusion.2
  54.6 0.6 collective-permute-start.13
  55.2 2.6 %collective-permute-done.10 = bf16[16,3584]{1,0:T(8,128)(2,1)S(1)} collective-permute-done((bf16[16,3584]{1,0:T(8,128)(2,1)S(1)}, bf16[16,3584]{1,0:T(8,128)(2,1)S(1)}, u32[]{:S(2)}, u32[]{:S(2)}) %collective-permute-start.10) | collective-permute-done | bytes 114720 | tf_op jit(solution)/shard_map/ppermute | solution.py:16
  57.8 1.6 %collective-permute-done.13 = bf16[16,3584]{1,0:T(8,128)(2,1)S(1)} collective-permute-done((bf16[16,3584]{1,0:T(8,128)(2,1)S(1)}, bf16[16,3584]{1,0:T(8,128)(2,1)S(1)}, u32[]{:S(2)}, u32[]{:S(2)}) %collective-permute-start.13) | collective-permute-done | bytes 114720 | tf_op jit(solution)/shard_map/ppermute | solution.py:16
  59.5 1.2 %collective-permute-start.14 = (bf16[8,7168]{1,0:T(8,128)(2,1)S(1)}, bf16[8,7168]{1,0:T(8,128)(2,1)S(1)}, u32[]{:S(2)}, u32[]{:S(2)}) collective-permute-start(bf16[8,7168]{1,0:T(8,128)(2,1)S(1)} %pad_maximum_fusion), channel_id=1, source_target_pairs={{0,1},{1,0},{2,3},{3,2},{4,5},{5,4},{6,7},{7,6},{8,9},{9,8},{10,11... | collective-permute-start | bytes 344072 | tf_op jit(solution)/shard_map/ppermute | solution.py:16
  60.7 3.7 %collective-permute-done.14 = bf16[8,7168]{1,0:T(8,128)(2,1)S(1)} collective-permute-done((bf16[8,7168]{1,0:T(8,128)(2,1)S(1)}, bf16[8,7168]{1,0:T(8,128)(2,1)S(1)}, u32[]{:S(2)}, u32[]{:S(2)}) %collective-permute-start.14) | collective-permute-done | bytes 114720 | tf_op jit(solution)/shard_map/ppermute | solution.py:16
  64.4 2.1 %collective-permute-start.15 = (bf16[4,7168]{1,0:T(4,128)(2,1)S(1)}, bf16[4,7168]{1,0:T(4,128)(2,1)S(1)}, u32[]{:S(2)}, u32[]{:S(2)}) collective-permute-start(bf16[4,7168]{1,0:T(4,128)(2,1)S(1)} %slice.59), channel_id=1, source_target_pairs={{0,2},{1,3},{2,0},{3,1},{4,6},{5,7},{6,4},{7,5},{8,10},{9,11},{10,... | collective-permute-start | bytes 172040 | tf_op jit(solution)/shard_map/ppermute | solution.py:16
  66.5 3.0 %collective-permute-done.15 = bf16[4,7168]{1,0:T(4,128)(2,1)S(1)} collective-permute-done((bf16[4,7168]{1,0:T(4,128)(2,1)S(1)}, bf16[4,7168]{1,0:T(4,128)(2,1)S(1)}, u32[]{:S(2)}, u32[]{:S(2)}) %collective-permute-start.15) | collective-permute-done | bytes 57376 | tf_op jit(solution)/shard_map/ppermute | solution.py:16
  69.6 0.7 add_convert_fusion.7
  (13 shorter events, 0.3 us)
Async XLA Ops:
  1.0 7.3 %collective-permute-start = (bf16[4,7296]{1,0:T(4,128)(2,1)S(1)}, bf16[4,7296]{1,0:T(4,128)(2,1)S(1)}, u32[]{:S(2)}, u32[]{:S(2)}) collective-permute-start(bf16[4,7296]{1,0:T(4,128)(2,1)S(1)} %extend.1.after_ref.refs_0_), channel_id=1, source_target_pairs={{0,2},{1,3},{2,0},{3,1},{4,6},{5,7},{6,4},{7,5},{8,10},{9,11},{10,... | collective-permute-start | bytes 175112 | tf_op jit(solution)/shard_map/ppermute | solution.py:16
  8.3 4.9 %collective-permute-start.1 = (bf16[8,7296]{1,0:T(8,128)(2,1)S(1)}, bf16[8,7296]{1,0:T(8,128)(2,1)S(1)}, u32[]{:S(2)}, u32[]{:S(2)}) collective-permute-start(bf16[8,7296]{1,0:T(8,128)(2,1)S(1)} %stack.2.refs_0_), channel_id=1, source_target_pairs={{0,1},{1,0},{2,3},{3,2},{4,5},{5,4},{6,7},{7,6},{8,9},{9,8},{10,11... | collective-permute-start | bytes 350216 | tf_op jit(solution)/shard_map/ppermute | solution.py:16
  13.2 3.6 %collective-permute-start.4 = (bf16[16,7296]{1,0:T(8,128)(2,1)S(1)}, bf16[16,7296]{1,0:T(8,128)(2,1)S(1)}, u32[]{:S(2)}, u32[]{:S(2)}) collective-permute-start(bf16[16,7296]{1,0:T(8,128)(2,1)S(1)} %stack.3.refs_0_), channel_id=1, source_target_pairs={{0,16},{16,0},{1,17},{17,1},{2,18},{18,2},{3,19},{19,3},{4,20},{20... | collective-permute-start | bytes 700424 | tf_op jit(solution)/shard_map/ppermute | solution.py:16
  13.3 8.3 %collective-permute-start.3 = (bf16[16,7296]{1,0:T(8,128)(2,1)S(1)}, bf16[16,7296]{1,0:T(8,128)(2,1)S(1)}, u32[]{:S(2)}, u32[]{:S(2)}) collective-permute-start(bf16[16,7296]{1,0:T(8,128)(2,1)S(1)} %stack.3.refs_0_), channel_id=1, source_target_pairs={{0,8},{4,12},{8,0},{12,4},{1,9},{5,13},{9,1},{13,5},{2,10},{6,14},... | collective-permute-start | bytes 700424 | tf_op jit(solution)/shard_map/ppermute | solution.py:16
  15.3 7.8 %collective-permute-start.2 = (bf16[16,7296]{1,0:T(8,128)(2,1)S(1)}, bf16[16,7296]{1,0:T(8,128)(2,1)S(1)}, u32[]{:S(2)}, u32[]{:S(2)}) collective-permute-start(bf16[16,7296]{1,0:T(8,128)(2,1)S(1)} %stack.3.refs_0_), channel_id=1, source_target_pairs={{0,4},{4,0},{8,12},{12,8},{1,5},{5,1},{9,13},{13,9},{2,6},{6,2},{1... | collective-permute-start | bytes 700424 | tf_op jit(solution)/shard_map/ppermute | solution.py:16
  23.1 6.4 %collective-permute-start.6 = (bf16[16,3712]{1,0:T(8,128)(2,1)S(1)}, bf16[16,3712]{1,0:T(8,128)(2,1)S(1)}, u32[]{:S(2)}, u32[]{:S(2)}) collective-permute-start(bf16[16,3712]{1,0:T(8,128)(2,1)S(1)} %get-tuple-element.32), channel_id=1, source_target_pairs={{0,4},{4,0},{8,12},{12,8},{1,5},{5,1},{9,13},{13,9},{2,6},{6,2},{1... | collective-permute-start | bytes 356360 | tf_op jit(solution)/shard_map/ppermute | solution.py:16
  24.7 4.8 %collective-permute-start.5 = (bf16[16,3584]{1,0:T(8,128)(2,1)S(1)}, bf16[16,3584]{1,0:T(8,128)(2,1)S(1)}, u32[]{:S(2)}, u32[]{:S(2)}) collective-permute-start(bf16[16,3584]{1,0:T(8,128)(2,1)S(1)} %get-tuple-element.31), channel_id=1, source_target_pairs={{0,8},{4,12},{8,0},{12,4},{1,9},{5,13},{9,1},{13,5},{2,10},{6,14},... | collective-permute-start | bytes 344072 | tf_op jit(solution)/shard_map/ppermute | solution.py:16
  29.5 2.2 %collective-permute-start.7 = (bf16[48,7296]{1,0:T(8,128)(2,1)S(1)}, bf16[48,7296]{1,0:T(8,128)(2,1)S(1)}, u32[]{:S(2)}, u32[]{:S(2)}) collective-permute-start(bf16[48,7296]{1,0:T(8,128)(2,1)S(1)} %gather.1.refs_1_), channel_id=1, source_target_pairs={{0,16},{16,0},{1,17},{17,1},{2,18},{18,2},{3,19},{19,3},{4,20},{20... | collective-permute-start | bytes 2101256 | tf_op jit(solution)/shard_map/ppermute | solution.py:16
  40.8 4.2 %collective-permute-start.8 = (bf16[64,3584]{1,0:T(8,128)(2,1)S(1)}, bf16[64,3584]{1,0:T(8,128)(2,1)S(1)}, u32[]{:S(2)}, u32[]{:S(2)}) collective-permute-start(bf16[64,3584]{1,0:T(8,128)(2,1)S(1)} %get-tuple-element.37), channel_id=1, source_target_pairs={{0,16},{16,0},{1,17},{17,1},{2,18},{18,2},{3,19},{19,3},{4,20},{20... | collective-permute-start | bytes 1376264 | tf_op jit(solution)/shard_map/ppermute | solution.py:16
  44.5 1.9 %collective-permute-start.11 = (bf16[64,3584]{1,0:T(8,128)(2,1)S(1)}, bf16[64,3584]{1,0:T(8,128)(2,1)S(1)}, u32[]{:S(2)}, u32[]{:S(2)}) collective-permute-start(bf16[64,3584]{1,0:T(8,128)(2,1)S(1)} %get-tuple-element.40), channel_id=1, source_target_pairs={{0,16},{16,0},{1,17},{17,1},{2,18},{18,2},{3,19},{19,3},{4,20},{20... | collective-permute-start | bytes 1376264 | tf_op jit(solution)/shard_map/ppermute | solution.py:16
  45.1 7.7 %collective-permute-start.9 = (bf16[32,3584]{1,0:T(8,128)(2,1)S(1)}, bf16[32,3584]{1,0:T(8,128)(2,1)S(1)}, u32[]{:S(2)}, u32[]{:S(2)}) collective-permute-start(bf16[32,3584]{1,0:T(8,128)(2,1)S(1)} %slice.49), channel_id=1, source_target_pairs={{0,4},{4,0},{8,12},{12,8},{1,5},{5,1},{9,13},{13,9},{2,6},{6,2},{1... | collective-permute-start | bytes 688136 | tf_op jit(solution)/shard_map/ppermute | solution.py:16
  46.6 7.9 %collective-permute-start.12 = (bf16[32,3584]{1,0:T(8,128)(2,1)S(1)}, bf16[32,3584]{1,0:T(8,128)(2,1)S(1)}, u32[]{:S(2)}, u32[]{:S(2)}) collective-permute-start(bf16[32,3584]{1,0:T(8,128)(2,1)S(1)} %slice.53), channel_id=1, source_target_pairs={{0,8},{4,12},{8,0},{12,4},{1,9},{5,13},{9,1},{13,5},{2,10},{6,14},... | collective-permute-start | bytes 688136 | tf_op jit(solution)/shard_map/ppermute | solution.py:16
  52.9 4.9 %collective-permute-start.10 = (bf16[16,3584]{1,0:T(8,128)(2,1)S(1)}, bf16[16,3584]{1,0:T(8,128)(2,1)S(1)}, u32[]{:S(2)}, u32[]{:S(2)}) collective-permute-start(bf16[16,3584]{1,0:T(8,128)(2,1)S(1)} %slice.51), channel_id=1, source_target_pairs={{0,8},{4,12},{8,0},{12,4},{1,9},{5,13},{9,1},{13,5},{2,10},{6,14},... | collective-permute-start | bytes 344072 | tf_op jit(solution)/shard_map/ppermute | solution.py:16
  54.6 4.9 %collective-permute-start.13 = (bf16[16,3584]{1,0:T(8,128)(2,1)S(1)}, bf16[16,3584]{1,0:T(8,128)(2,1)S(1)}, u32[]{:S(2)}, u32[]{:S(2)}) collective-permute-start(bf16[16,3584]{1,0:T(8,128)(2,1)S(1)} %slice.55), channel_id=1, source_target_pairs={{0,4},{4,0},{8,12},{12,8},{1,5},{5,1},{9,13},{13,9},{2,6},{6,2},{1... | collective-permute-start | bytes 344072 | tf_op jit(solution)/shard_map/ppermute | solution.py:16
  59.5 4.9 %collective-permute-start.14 = (bf16[8,7168]{1,0:T(8,128)(2,1)S(1)}, bf16[8,7168]{1,0:T(8,128)(2,1)S(1)}, u32[]{:S(2)}, u32[]{:S(2)}) collective-permute-start(bf16[8,7168]{1,0:T(8,128)(2,1)S(1)} %pad_maximum_fusion), channel_id=1, source_target_pairs={{0,1},{1,0},{2,3},{3,2},{4,5},{5,4},{6,7},{7,6},{8,9},{9,8},{10,11... | collective-permute-start | bytes 344072 | tf_op jit(solution)/shard_map/ppermute | solution.py:16
  64.4 5.2 %collective-permute-start.15 = (bf16[4,7168]{1,0:T(4,128)(2,1)S(1)}, bf16[4,7168]{1,0:T(4,128)(2,1)S(1)}, u32[]{:S(2)}, u32[]{:S(2)}) collective-permute-start(bf16[4,7168]{1,0:T(4,128)(2,1)S(1)} %slice.59), channel_id=1, source_target_pairs={{0,2},{1,3},{2,0},{3,1},{4,6},{5,7},{6,4},{7,5},{8,10},{9,11},{10,... | collective-permute-start | bytes 172040 | tf_op jit(solution)/shard_map/ppermute | solution.py:16

commit v9 on v8

v9 whole, which is shorter than its diff:
```python
import functools

import jax
import jax.numpy as jnp
from jax import lax
from jax.experimental import pallas as pl
from jax.experimental.pallas import tpu as pltpu
from jax.sharding import PartitionSpec as P

AXES = ("sect", "grp", "dev")
VMEM_LIMIT = 20 * 2**20


def rounds_of():
    sects, groups, lanes = (lax.axis_size(a) for a in AXES)
    near = [1 << b for b in range(lanes.bit_length() - 1)][::-1]
    far = [lanes << b for b in range(groups.bit_length() - 1)][::-1]
    orders = [near + far, far[-1:] + near + far[:-1]]
    return [orders[s % 2] for s in range(sects)]


def swap(value, masks):
    count = lax.axis_size(("grp", "dev"))
    pairs = [
        (s * count + i, s * count + (i ^ mask)) for s, mask in enumerate(masks) for i in range(count)
    ]
    return lax.ppermute(value, AXES, pairs)


def swap_core(value):
    return lax.ppermute(value, "sect", [(0, 1), (1, 0)])


def vmem_call(kernel, out_shape, name, *operands):
    whole = pl.BlockSpec(memory_space=pltpu.VMEM)
    return pl.pallas_call(
        kernel,
        out_shape=out_shape,
        in_specs=[whole] * len(operands),
        out_specs=jax.tree.map(lambda _: whole, out_shape),
        compiler_params=pltpu.CompilerParams(vmem_limit_bytes=VMEM_LIMIT),
        name=name,
    )(*operands)


def extend_kernel(tokens_hbm, ids_hbm, weights_hbm, out_ref, tokens_ref, ids_ref, weights_ref, sems):
    pairs = ((ids_hbm, ids_ref), (weights_hbm, weights_ref), (tokens_hbm, tokens_ref))
    copies = [pltpu.make_async_copy(a, b, sems.at[i]) for i, (a, b) in enumerate(pairs)]
    for copy in copies:
        copy.start()
    rows, width = tokens_ref.shape
    half = (out_ref.shape[1] - width) // 2
    lane = lax.broadcasted_iota(jnp.int32, (rows, half * 2), 1)
    dense = jnp.zeros((rows, half * 2), jnp.float32)
    for copy in copies:
        copy.wait()
    for k in range(ids_ref.shape[1]):
        mine = lax.rem(lane, half) == ids_ref[:, k:k + 1]
        dense = dense + jnp.where(mine, weights_ref[:, k:k + 1], 0.0)
    high = dense.astype(jnp.bfloat16).astype(jnp.float32)
    out_ref[:, :width] = tokens_ref[...]
    out_ref[:, width:] = jnp.where(lane < half, high, dense - high).astype(jnp.bfloat16)


def extend(tokens, ids, weights, half):
    rows, width = tokens.shape
    return pl.pallas_call(
        extend_kernel,
        out_shape=jax.ShapeDtypeStruct((rows, width + 2 * half), tokens.dtype),
        in_specs=[pl.BlockSpec(memory_space=pl.ANY)] * 3,
        out_specs=pl.BlockSpec(memory_space=pltpu.VMEM),
        scratch_shapes=[pltpu.VMEM(v.shape, v.dtype) for v in (tokens, ids, weights)]
        + [pltpu.SemaphoreType.DMA((3,))],
        compiler_params=pltpu.CompilerParams(vmem_limit_bytes=VMEM_LIMIT),
        name="extend",
    )(*(pltpu.with_memory_space_constraint(v, pltpu.HBM) for v in (tokens, ids, weights)))


def stack_kernel(*refs):
    pieces, out_ref = refs[:-1], refs[-1]
    values = [p[...].astype(jnp.float32) for p in pieces]
    out_ref[...] = jnp.concatenate(values, axis=0).astype(out_ref.dtype)


def stack(*pieces):
    rows = sum(p.shape[0] for p in pieces)
    out = jax.ShapeDtypeStruct((rows, pieces[0].shape[1]), pieces[0].dtype)
    return vmem_call(stack_kernel, out, "stack", *pieces)


def gather_rows(block, w_up):
    line, weights, token = block, [], block
    rounds = list(zip(*rounds_of()))
    experts = w_up.shape[0]
    for number, masks in enumerate(rounds):
        arrived = swap(line, masks)
        expert = number - len(rounds) + experts
        if expert >= 0:
            weight, token = fetch(w_up, expert, token)
            weights.append(weight)
            arrived, token = lax.optimization_barrier((arrived, token))
        line = stack(line, arrived)
    return [line, swap_core(line)], weights, token


def down_copy(expert, block, down_hbm, target_ref, sems):
    hidden = down_hbm.shape[1]
    span = pl.ds(pl.multiple_of(block * hidden, hidden), hidden)
    return pltpu.make_async_copy(
        down_hbm.at[expert, :, span], target_ref.at[expert, span], sems.at[expert, block]
    )


def expert_kernel(counts, width, token_ref, *refs):
    pieces, up_refs = refs[:counts[0]], refs[counts[0]:sum(counts)]
    (gate_hbm, down_hbm, keep_ref, send_ref,
     rows_ref, up_ref, hidden_ref, gate_ref, gate_sems, sems) = refs[sum(counts):]
    experts, _, hidden = gate_ref.shape
    place = lax.axis_index("sect") * lax.axis_size("grp") + lax.axis_index("grp")
    first = place * experts
    block = min(256, hidden)
    gate_copies = weight_copies(gate_hbm, gate_ref, gate_sems)
    for gate_copy in gate_copies:
        gate_copy.start()

    at = 0
    for piece in pieces:
        rows_ref[pl.ds(at, piece.shape[0])] = piece[...]
        at += piece.shape[0]

    for e in range(experts):

        @pl.loop(0, hidden // block)
        def _(step):
            span = pl.ds(pl.multiple_of(step * block, block), block)
            up_ref[e, :, span] = jnp.dot(
                rows_ref[:, :width], up_refs[e][0, :, span], preferred_element_type=jnp.float32
            )

    extra = rows_ref[:, width:].astype(jnp.float32)
    lane = lax.broadcasted_iota(jnp.int32, extra.shape, 1)
    parts = gate_sems.shape[1]
    for e in range(experts):
        mine = lax.rem(lane, extra.shape[1] // 2) == first + e
        scale = jnp.sum(jnp.where(mine, extra, 0.0), axis=1, keepdims=True)
        for gate_copy in gate_copies[e * parts:(e + 1) * parts]:
            gate_copy.wait()

        @pl.loop(0, hidden // block)
        def _(step):
            span = pl.ds(pl.multiple_of(step * block, block), block)
            gate = jnp.dot(
                rows_ref[:, :width], gate_ref[e, :, span], preferred_element_type=jnp.float32
            )
            value = gate / (1.0 + jnp.exp(-gate)) * up_ref[e, :, span] * scale
            out = pl.ds(pl.multiple_of(e * hidden + step * block, block), block)
            hidden_ref[:, out] = value.astype(jnp.bfloat16)

        for step in range(width // hidden):
            down_copy(e, step, down_hbm, gate_ref, sems).start()

    middle = keep_ref.shape[0]

    @pl.loop(0, width // hidden)
    def _(step):
        for e in range(experts):
            down_copy(e, step, down_hbm, gate_ref, sems).wait()
        span = pl.ds(pl.multiple_of(step * hidden, hidden), hidden)
        weight = gate_ref[:, span, :].reshape(experts * hidden, hidden)
        total = jnp.dot(hidden_ref[...], weight, preferred_element_type=jnp.float32)
        total = total.astype(jnp.bfloat16)
        keep_ref[:, span] = total[:middle]
        send_ref[:, span] = total[middle:]


def fetch_kernel(expert, after_ref, source_ref, target_ref, token_ref, sems):
    copies = weight_copies(source_ref.at[pl.ds(expert, 1)], target_ref, sems)
    for copy in copies:
        copy.start()
    token_ref[...] = jnp.zeros_like(token_ref)
    for copy in copies:
        copy.wait()


def weight_copies(source_ref, target_ref, sems):
    experts, parts = sems.shape
    depth = source_ref.shape[1] // parts
    return [
        pltpu.make_async_copy(
            source_ref.at[e, pl.ds(p * depth, depth)],
            target_ref.at[e, pl.ds(p * depth, depth)],
            sems.at[e, p],
        )
        for e in range(experts)
        for p in range(parts)
    ]


def fetch(weight, expert, after):
    in_hbm = pl.BlockSpec(memory_space=pl.ANY)
    in_vmem = pl.BlockSpec(memory_space=pltpu.VMEM)
    return pl.pallas_call(
        functools.partial(fetch_kernel, expert),
        out_shape=(
            pltpu.VMEM((1, *weight.shape[1:]), weight.dtype),
            jax.ShapeDtypeStruct((8, 128), jnp.float32),
        ),
        in_specs=[in_hbm, in_hbm],
        out_specs=(in_vmem, in_vmem),
        scratch_shapes=[pltpu.SemaphoreType.DMA((1, 8))],
        compiler_params=pltpu.CompilerParams(vmem_limit_bytes=VMEM_LIMIT),
        cost_estimate=pl.CostEstimate(
            flops=0, bytes_accessed=2 * weight.size // weight.shape[0], transcendentals=0
        ),
        name="fetch",
    )(after, pltpu.with_memory_space_constraint(weight, pltpu.HBM))


def expert_call(entries, w_gate, w_ups, w_down, token):
    experts, width, hidden = w_gate.shape
    full = entries[0].shape[1]
    rows = sum(e.shape[0] for e in entries)
    counts = (len(entries), len(w_ups))
    whole = pl.BlockSpec(memory_space=pltpu.VMEM)
    anywhere = pl.BlockSpec(memory_space=pl.ANY)
    out = jax.ShapeDtypeStruct((rows // 2, width), jnp.bfloat16)
    return pl.pallas_call(
        functools.partial(expert_kernel, counts, width),
        out_shape=(out, out),
        in_specs=[anywhere] + [whole] * sum(counts) + [anywhere] * 2,
        out_specs=(whole,) * 2,
        scratch_shapes=[
            pltpu.VMEM((rows, full), jnp.bfloat16),
            pltpu.VMEM((experts, rows, hidden), jnp.float32),
            pltpu.VMEM((rows, experts * hidden), jnp.bfloat16),
            pltpu.VMEM(w_gate.shape, w_gate.dtype),
            pltpu.SemaphoreType.DMA((experts, 4)),
            pltpu.SemaphoreType.DMA((experts, width // hidden)),
        ],
        compiler_params=pltpu.CompilerParams(vmem_limit_bytes=VMEM_LIMIT),
        cost_estimate=pl.CostEstimate(
            flops=6 * rows * experts * width * hidden,
            bytes_accessed=2 * (w_gate.size + w_down.size),
            transcendentals=rows * experts * hidden,
        ),
        name="experts",
    )(
        token,
        *entries,
        *(pltpu.with_memory_space_constraint(w, pltpu.VMEM) for w in w_ups),
        pltpu.with_memory_space_constraint(w_gate, pltpu.HBM),
        pltpu.with_memory_space_constraint(w_down, pltpu.HBM),
    )


def add(*values):
    total = values[0].astype(jnp.float32)
    for value in values[1:]:
        total = total + value.astype(jnp.float32)
    return total.astype(jnp.bfloat16)


def body(tokens, expert_ids, gate_weights, w_gate, w_up, w_down):
    sects, groups, lanes = (lax.axis_size(a) for a in AXES)
    row_count, width = tokens.shape
    experts = w_gate.shape[0]
    expert_count = sects * groups * experts

    half = -(-expert_count // 64) * 64
    block = extend(tokens, expert_ids, gate_weights, half)
    entries, w_ups, token = gather_rows(block, w_up)

    results = []
    keep, send = expert_call(entries, w_gate, w_ups, w_down, token)
    value = add(keep, swap_core(send))
    for masks in list(zip(*rounds_of()))[::-1]:
        middle = value.shape[0] // 2
        value = add(value[:middle], swap(value[middle:], masks))
    return value


def solution(mesh):
    in_specs = (
        P(AXES, None),
        P(AXES, None),
        P(AXES, None),
        P(("sect", "grp"), None, "dev"),
        P(("sect", "grp"), None, "dev"),
        P(("sect", "grp"), "dev", None),
    )
    return jax.shard_map(
        body, mesh=mesh, in_specs=in_specs, out_specs=P(AXES, None), check_vma=False
    )
```

time: 70.4 us -> 71.2 us (1.011)
  starting transfers between devices: 17.7 us -> 19.1 us
    ppermute x16 -> x10, starting transfers between devices: 17.7 us -> 19.1 us  [the longest x8 18.9 us: swap(): return lax.ppermute(value, AXES, pairs)]
    ppermute x16 -> x10, waiting for transfers between devices: 31.1 us -> 30.6 us  [the longest x8 25.8 us: swap(): return lax.ppermute(value, AXES, pairs)]
    pallas_call x2 -> x1, Pallas kernels: 12.6 us -> 12.6 us  [expert_call(): pl.pallas_call(functools.partial(expert_kernel, counts, width), out_shape...]
  transfers between devices with their start and end apart: 16 -> 10, of which waited for: 12 -> 10; matrix products, arithmetic and copies ran while one was open for 1% -> 0% of each run, Pallas kernels for 14% -> 9%
where the time goes in v9:
time: 71.2 us; the launch traced here: 71.1 us
  waiting for transfers between devices  30.6 us (43%)
  Pallas kernels  20.1 us (28%)
  starting transfers between devices  19.1 us (27%)
  other arithmetic  1.07 us (2%)
    ppermute x8, waiting for transfers between devices, swap(): return lax.ppermute(value, AXES, pairs)  25.8 us
    ppermute x8, starting transfers between devices, swap(): return lax.ppermute(value, AXES, pairs)  18.9 us
    pallas_call x1, Pallas kernels, expert_call(): pl.pallas_call(functools.partial(expert_kernel, counts, width), out_shape...  12.6 us
    pallas_call x2, Pallas kernels, fetch(): pl.pallas_call(functools.partial(fetch_kernel, expert), out_shape=(pltpu....  6.33 us
    ppermute x2, waiting for transfers between devices, swap_core(): return lax.ppermute(value, 'sect', [(0, 1), (1, 0)])  4.82 us
  transfers between devices with their start and end apart: 10, of which 10 were waited for; matrix products, arithmetic and copies ran while one was open for 0% of the time, Pallas kernels for 9%

profile of v9, /device:TPU:0, one launch (start us, length us, event | category | flops | bytes accessed | tf_op | source)
XLA Modules:
  0.0 71.1 jit_solution(10330663433263965192)
XLA Ops:
  0.0 1.0 %extend.1.refs_0_.after_ref = bf16[4,7296]{1,0:T(4,128)(2,1)S(1)} custom-call(bf16[4,7168]{1,0:T(4,128)(2,1)} %tokens_hbm.1, s32[4,8]{1,0:T(4,128)} %ids_hbm.1, f32[4,8]{1,0:T(4,128)} %weights_hbm.1), custom_call_target="tpu_custom_call" | custom-call | tf_op jit(solution)/shard_map/extend/pallas_call | solution.py:67
  1.0 4.1 %collective-permute-start = (bf16[4,7296]{1,0:T(4,128)(2,1)S(1)}, bf16[4,7296]{1,0:T(4,128)(2,1)S(1)}, u32[]{:S(2)}, u32[]{:S(2)}) collective-permute-start(bf16[4,7296]{1,0:T(4,128)(2,1)S(1)} %extend.1.refs_0_.after_ref), channel_id=1, source_target_pairs={{0,2},{1,3},{2,0},{3,1},{4,6},{5,7},{6,4},{7,5},{8,10},{9,11},{10,... | collective-permute-start | bytes 175112 | tf_op jit(solution)/shard_map/ppermute | solution.py:27
  5.1 2.2 %collective-permute-done.refs_1_ = bf16[4,7296]{1,0:T(4,128)(2,1)S(1)} collective-permute-done((bf16[4,7296]{1,0:T(4,128)(2,1)S(1)}, bf16[4,7296]{1,0:T(4,128)(2,1)S(1)}, u32[]{:S(2)}, u32[]{:S(2)}) %collective-permute-start) | collective-permute-done | bytes 58400 | tf_op jit(solution)/shard_map/ppermute | solution.py:27
  7.3 2.0 %collective-permute-start.1 = (bf16[8,7296]{1,0:T(8,128)(2,1)S(1)}, bf16[8,7296]{1,0:T(8,128)(2,1)S(1)}, u32[]{:S(2)}, u32[]{:S(2)}) collective-permute-start(bf16[8,7296]{1,0:T(8,128)(2,1)S(1)} %stack.4.refs_0_), channel_id=1, source_target_pairs={{0,1},{1,0},{2,3},{3,2},{4,5},{5,4},{6,7},{7,6},{8,9},{9,8},{10,11... | collective-permute-start | bytes 350216 | tf_op jit(solution)/shard_map/ppermute | solution.py:27
  9.3 3.0 %collective-permute-done.1.refs_1_ = bf16[8,7296]{1,0:T(8,128)(2,1)S(1)} collective-permute-done((bf16[8,7296]{1,0:T(8,128)(2,1)S(1)}, bf16[8,7296]{1,0:T(8,128)(2,1)S(1)}, u32[]{:S(2)}, u32[]{:S(2)}) %collective-permute-start.1) | collective-permute-done | bytes 116768 | tf_op jit(solution)/shard_map/ppermute | solution.py:27
  12.3 2.0 %collective-permute-start.2 = (bf16[16,7296]{1,0:T(8,128)(2,1)S(1)}, bf16[16,7296]{1,0:T(8,128)(2,1)S(1)}, u32[]{:S(2)}, u32[]{:S(2)}) collective-permute-start(bf16[16,7296]{1,0:T(8,128)(2,1)S(1)} %stack.5.refs_0_), channel_id=1, source_target_pairs={{0,8},{1,9},{2,10},{3,11},{4,12},{5,13},{6,14},{7,15},{8,0},{9,1},... | collective-permute-start | bytes 700424 | tf_op jit(solution)/shard_map/ppermute | solution.py:27
  14.2 3.2 %fetch.2 = (bf16[1,7168,512]{2,1,0:T(8,128)(2,1)S(1)}, f32[8,128]{1,0:T(8,128)S(1)}) custom-call(bf16[4,7296]{1,0:T(4,128)(2,1)S(1)} %extend.1.refs_0_.after_ref, bf16[2,7168,512]{2,1,0:T(8,128)(2,1)} %source_ref.3), custom_call_target="tpu_custom_call" | custom-call | bytes 7340032 | tf_op jit(solution)/shard_map/fetch/pallas_call | solution.py:202
  17.4 1.0 %collective-permute-done.2.refs_1_ = bf16[16,7296]{1,0:T(8,128)(2,1)S(1)} collective-permute-done((bf16[16,7296]{1,0:T(8,128)(2,1)S(1)}, bf16[16,7296]{1,0:T(8,128)(2,1)S(1)}, u32[]{:S(2)}, u32[]{:S(2)}) %collective-permute-start.2) | collective-permute-done | bytes 233504 | tf_op jit(solution)/shard_map/ppermute | solution.py:27
  18.4 1.9 %collective-permute-start.3 = (bf16[32,7296]{1,0:T(8,128)(2,1)S(1)}, bf16[32,7296]{1,0:T(8,128)(2,1)S(1)}, u32[]{:S(2)}, u32[]{:S(2)}) collective-permute-start(bf16[32,7296]{1,0:T(8,128)(2,1)S(1)} %stack.6.refs_0_), channel_id=1, source_target_pairs={{0,4},{1,5},{2,6},{3,7},{4,0},{5,1},{6,2},{7,3},{8,12},{9,13},{10,... | collective-permute-start | bytes 1400840 | tf_op jit(solution)/shard_map/ppermute | solution.py:27
  20.4 3.2 %fetch.3 = (bf16[1,7168,512]{2,1,0:T(8,128)(2,1)S(1)}, f32[8,128]{1,0:T(8,128)S(1)}) custom-call(f32[8,128]{1,0:T(8,128)S(1)} %get-tuple-element.17.after_ref, bf16[2,7168,512]{2,1,0:T(8,128)(2,1)} %source_ref.3), custom_call_target="tpu_custom_call" | custom-call | bytes 7340032 | tf_op jit(solution)/shard_map/fetch/pallas_call | solution.py:202
  23.6 3.5 %collective-permute-done.3.refs_1_ = bf16[32,7296]{1,0:T(8,128)(2,1)S(1)} collective-permute-done((bf16[32,7296]{1,0:T(8,128)(2,1)S(1)}, bf16[32,7296]{1,0:T(8,128)(2,1)S(1)}, u32[]{:S(2)}, u32[]{:S(2)}) %collective-permute-start.3) | collective-permute-done | bytes 466976 | tf_op jit(solution)/shard_map/ppermute | solution.py:27
  27.1 0.1 stack.7.refs_0_
  27.1 0.1 collective-permute-start.4
  27.2 2.5 %collective-permute-done.4.refs_1_ = bf16[64,7296]{1,0:T(8,128)(2,1)S(1)} collective-permute-done((bf16[64,7296]{1,0:T(8,128)(2,1)S(1)}, bf16[64,7296]{1,0:T(8,128)(2,1)S(1)}, u32[]{:S(2)}, u32[]{:S(2)}) %collective-permute-start.4) | collective-permute-done | bytes 933920 | tf_op jit(solution)/shard_map/ppermute | solution.py:31
  29.7 12.6 %experts.1 = (bf16[64,7168]{1,0:T(8,128)(2,1)S(1)}, bf16[64,7168]{1,0:T(8,128)(2,1)S(1)}) custom-call(f32[8,128]{1,0:T(8,128)S(1)} %get-tuple-element.19.token_ref, bf16[64,7296]{1,0:T(8,128)(2,1)S(1)} %stack.7.refs_0_, bf16[64,7296]{1,0:T(8,128)(2,1)S(1)} %collective-permute-done.4.refs_1_, bf16[1,7168,512]{2,1,0:T(8,128)(2,1)S(1)} %get-tuple-element.21.refs_2_, ...), custom_call_target="tpu_custom_call" | custom-call | flops 5637144576 | bytes 29360128 | tf_op jit(solution)/shard_map/experts/pallas_call | solution.py:227
  42.3 0.2 collective-permute-start.5
  42.5 2.3 %collective-permute-done.5 = bf16[64,7168]{1,0:T(8,128)(2,1)S(1)} collective-permute-done((bf16[64,7168]{1,0:T(8,128)(2,1)S(1)}, bf16[64,7168]{1,0:T(8,128)(2,1)S(1)}, u32[]{:S(2)}, u32[]{:S(2)}) %collective-permute-start.5) | collective-permute-done | bytes 917536 | tf_op jit(solution)/shard_map/ppermute | solution.py:31
  44.9 0.2 add_convert_fusion
  45.1 1.9 %collective-permute-start.6 = (bf16[32,7168]{1,0:T(8,128)(2,1)S(1)}, bf16[32,7168]{1,0:T(8,128)(2,1)S(1)}, u32[]{:S(2)}, u32[]{:S(2)}) collective-permute-start(bf16[32,7168]{1,0:T(8,128)(2,1)S(1)} %slice.33), channel_id=1, source_target_pairs={{0,4},{1,5},{2,6},{3,7},{4,0},{5,1},{6,2},{7,3},{8,12},{9,13},{10,... | collective-permute-start | bytes 1376264 | tf_op jit(solution)/shard_map/ppermute | solution.py:27
  47.1 6.6 %collective-permute-done.6 = bf16[32,7168]{1,0:T(8,128)(2,1)S(1)} collective-permute-done((bf16[32,7168]{1,0:T(8,128)(2,1)S(1)}, bf16[32,7168]{1,0:T(8,128)(2,1)S(1)}, u32[]{:S(2)}, u32[]{:S(2)}) %collective-permute-start.6) | collective-permute-done | bytes 458784 | tf_op jit(solution)/shard_map/ppermute | solution.py:27
  53.7 0.1 add_convert_fusion.1
  53.8 2.0 %collective-permute-start.7 = (bf16[16,7168]{1,0:T(8,128)(2,1)S(1)}, bf16[16,7168]{1,0:T(8,128)(2,1)S(1)}, u32[]{:S(2)}, u32[]{:S(2)}) collective-permute-start(bf16[16,7168]{1,0:T(8,128)(2,1)S(1)} %slice.35), channel_id=1, source_target_pairs={{0,8},{1,9},{2,10},{3,11},{4,12},{5,13},{6,14},{7,15},{8,0},{9,1},... | collective-permute-start | bytes 688136 | tf_op jit(solution)/shard_map/ppermute | solution.py:27
  55.8 4.1 %collective-permute-done.7 = bf16[16,7168]{1,0:T(8,128)(2,1)S(1)} collective-permute-done((bf16[16,7168]{1,0:T(8,128)(2,1)S(1)}, bf16[16,7168]{1,0:T(8,128)(2,1)S(1)}, u32[]{:S(2)}, u32[]{:S(2)}) %collective-permute-start.7) | collective-permute-done | bytes 229408 | tf_op jit(solution)/shard_map/ppermute | solution.py:27
  59.9 0.1 add_convert_fusion.2
  60.0 2.1 %collective-permute-start.8 = (bf16[8,7168]{1,0:T(8,128)(2,1)S(1)}, bf16[8,7168]{1,0:T(8,128)(2,1)S(1)}, u32[]{:S(2)}, u32[]{:S(2)}) collective-permute-start(bf16[8,7168]{1,0:T(8,128)(2,1)S(1)} %slice.37), channel_id=1, source_target_pairs={{0,1},{1,0},{2,3},{3,2},{4,5},{5,4},{6,7},{7,6},{8,9},{9,8},{10,11... | collective-permute-start | bytes 344072 | tf_op jit(solution)/shard_map/ppermute | solution.py:27
  62.1 3.1 %collective-permute-done.8 = bf16[8,7168]{1,0:T(8,128)(2,1)S(1)} collective-permute-done((bf16[8,7168]{1,0:T(8,128)(2,1)S(1)}, bf16[8,7168]{1,0:T(8,128)(2,1)S(1)}, u32[]{:S(2)}, u32[]{:S(2)}) %collective-permute-start.8) | collective-permute-done | bytes 114720 | tf_op jit(solution)/shard_map/ppermute | solution.py:27
  65.3 2.9 %collective-permute-start.9 = (bf16[4,7168]{1,0:T(4,128)(2,1)S(1)}, bf16[4,7168]{1,0:T(4,128)(2,1)S(1)}, u32[]{:S(2)}, u32[]{:S(2)}) collective-permute-start(bf16[4,7168]{1,0:T(4,128)(2,1)S(1)} %slice.39), channel_id=1, source_target_pairs={{0,2},{1,3},{2,0},{3,1},{4,6},{5,7},{6,4},{7,5},{8,10},{9,11},{10,... | collective-permute-start | bytes 172040 | tf_op jit(solution)/shard_map/ppermute | solution.py:27
  68.2 2.2 %collective-permute-done.9 = bf16[4,7168]{1,0:T(4,128)(2,1)S(1)} collective-permute-done((bf16[4,7168]{1,0:T(4,128)(2,1)S(1)}, bf16[4,7168]{1,0:T(4,128)(2,1)S(1)}, u32[]{:S(2)}, u32[]{:S(2)}) %collective-permute-start.9) | collective-permute-done | bytes 57376 | tf_op jit(solution)/shard_map/ppermute | solution.py:27
  70.4 0.7 add_convert_fusion.4
  (8 shorter events, 0.2 us)
Async XLA Ops:
  1.0 6.3 %collective-permute-start = (bf16[4,7296]{1,0:T(4,128)(2,1)S(1)}, bf16[4,7296]{1,0:T(4,128)(2,1)S(1)}, u32[]{:S(2)}, u32[]{:S(2)}) collective-permute-start(bf16[4,7296]{1,0:T(4,128)(2,1)S(1)} %extend.1.refs_0_.after_ref), channel_id=1, source_target_pairs={{0,2},{1,3},{2,0},{3,1},{4,6},{5,7},{6,4},{7,5},{8,10},{9,11},{10,... | collective-permute-start | bytes 175112 | tf_op jit(solution)/shard_map/ppermute | solution.py:27
  7.3 5.0 %collective-permute-start.1 = (bf16[8,7296]{1,0:T(8,128)(2,1)S(1)}, bf16[8,7296]{1,0:T(8,128)(2,1)S(1)}, u32[]{:S(2)}, u32[]{:S(2)}) collective-permute-start(bf16[8,7296]{1,0:T(8,128)(2,1)S(1)} %stack.4.refs_0_), channel_id=1, source_target_pairs={{0,1},{1,0},{2,3},{3,2},{4,5},{5,4},{6,7},{7,6},{8,9},{9,8},{10,11... | collective-permute-start | bytes 350216 | tf_op jit(solution)/shard_map/ppermute | solution.py:27
  12.3 6.1 %collective-permute-start.2 = (bf16[16,7296]{1,0:T(8,128)(2,1)S(1)}, bf16[16,7296]{1,0:T(8,128)(2,1)S(1)}, u32[]{:S(2)}, u32[]{:S(2)}) collective-permute-start(bf16[16,7296]{1,0:T(8,128)(2,1)S(1)} %stack.5.refs_0_), channel_id=1, source_target_pairs={{0,8},{1,9},{2,10},{3,11},{4,12},{5,13},{6,14},{7,15},{8,0},{9,1},... | collective-permute-start | bytes 700424 | tf_op jit(solution)/shard_map/ppermute | solution.py:27
  18.4 8.6 %collective-permute-start.3 = (bf16[32,7296]{1,0:T(8,128)(2,1)S(1)}, bf16[32,7296]{1,0:T(8,128)(2,1)S(1)}, u32[]{:S(2)}, u32[]{:S(2)}) collective-permute-start(bf16[32,7296]{1,0:T(8,128)(2,1)S(1)} %stack.6.refs_0_), channel_id=1, source_target_pairs={{0,4},{1,5},{2,6},{3,7},{4,0},{5,1},{6,2},{7,3},{8,12},{9,13},{10,... | collective-permute-start | bytes 1400840 | tf_op jit(solution)/shard_map/ppermute | solution.py:27
  27.1 2.6 %collective-permute-start.4 = (bf16[64,7296]{1,0:T(8,128)(2,1)S(1)}, bf16[64,7296]{1,0:T(8,128)(2,1)S(1)}, u32[]{:S(2)}, u32[]{:S(2)}) collective-permute-start(bf16[64,7296]{1,0:T(8,128)(2,1)S(1)} %stack.7.refs_0_), channel_id=1, source_target_pairs={{0,16},{16,0},{1,17},{17,1},{2,18},{18,2},{3,19},{19,3},{4,20},{20... | collective-permute-start | bytes 2801672 | tf_op jit(solution)/shard_map/ppermute | solution.py:31
  42.3 2.5 %collective-permute-start.5 = (bf16[64,7168]{1,0:T(8,128)(2,1)S(1)}, bf16[64,7168]{1,0:T(8,128)(2,1)S(1)}, u32[]{:S(2)}, u32[]{:S(2)}) collective-permute-start(bf16[64,7168]{1,0:T(8,128)(2,1)S(1)} %get-tuple-element.24), channel_id=1, source_target_pairs={{0,16},{16,0},{1,17},{17,1},{2,18},{18,2},{3,19},{19,3},{4,20},{20... | collective-permute-start | bytes 2752520 | tf_op jit(solution)/shard_map/ppermute | solution.py:31
  45.1 8.5 %collective-permute-start.6 = (bf16[32,7168]{1,0:T(8,128)(2,1)S(1)}, bf16[32,7168]{1,0:T(8,128)(2,1)S(1)}, u32[]{:S(2)}, u32[]{:S(2)}) collective-permute-start(bf16[32,7168]{1,0:T(8,128)(2,1)S(1)} %slice.33), channel_id=1, source_target_pairs={{0,4},{1,5},{2,6},{3,7},{4,0},{5,1},{6,2},{7,3},{8,12},{9,13},{10,... | collective-permute-start | bytes 1376264 | tf_op jit(solution)/shard_map/ppermute | solution.py:27
  53.8 6.1 %collective-permute-start.7 = (bf16[16,7168]{1,0:T(8,128)(2,1)S(1)}, bf16[16,7168]{1,0:T(8,128)(2,1)S(1)}, u32[]{:S(2)}, u32[]{:S(2)}) collective-permute-start(bf16[16,7168]{1,0:T(8,128)(2,1)S(1)} %slice.35), channel_id=1, source_target_pairs={{0,8},{1,9},{2,10},{3,11},{4,12},{5,13},{6,14},{7,15},{8,0},{9,1},... | collective-permute-start | bytes 688136 | tf_op jit(solution)/shard_map/ppermute | solution.py:27
  60.0 5.2 %collective-permute-start.8 = (bf16[8,7168]{1,0:T(8,128)(2,1)S(1)}, bf16[8,7168]{1,0:T(8,128)(2,1)S(1)}, u32[]{:S(2)}, u32[]{:S(2)}) collective-permute-start(bf16[8,7168]{1,0:T(8,128)(2,1)S(1)} %slice.37), channel_id=1, source_target_pairs={{0,1},{1,0},{2,3},{3,2},{4,5},{5,4},{6,7},{7,6},{8,9},{9,8},{10,11... | collective-permute-start | bytes 344072 | tf_op jit(solution)/shard_map/ppermute | solution.py:27
  65.3 5.1 %collective-permute-start.9 = (bf16[4,7168]{1,0:T(4,128)(2,1)S(1)}, bf16[4,7168]{1,0:T(4,128)(2,1)S(1)}, u32[]{:S(2)}, u32[]{:S(2)}) collective-permute-start(bf16[4,7168]{1,0:T(4,128)(2,1)S(1)} %slice.39), channel_id=1, source_target_pairs={{0,2},{1,3},{2,0},{3,1},{4,6},{5,7},{6,4},{7,5},{8,10},{9,11},{10,... | collective-permute-start | bytes 172040 | tf_op jit(solution)/shard_map/ppermute | solution.py:27

commit v10 on v9

--- a/solution.py
+++ b/solution.py
@@ -12,19 +12,22 @@
 
 
 def rounds_of():
-    sects, groups, lanes = (lax.axis_size(a) for a in AXES)
-    near = [1 << b for b in range(lanes.bit_length() - 1)][::-1]
-    far = [lanes << b for b in range(groups.bit_length() - 1)][::-1]
-    orders = [near + far, far[-1:] + near + far[:-1]]
-    return [orders[s % 2] for s in range(sects)]
+    sects, groups, _ = (lax.axis_size(a) for a in AXES)
+    bits = [1 << b for b in range(groups.bit_length() - 1)]
+    orders = [bits[::-1], bits]
+    return list(zip(*(orders[s % 2] for s in range(sects))))
 
 
 def swap(value, masks):
-    count = lax.axis_size(("grp", "dev"))
+    count = lax.axis_size("grp")
     pairs = [
         (s * count + i, s * count + (i ^ mask)) for s, mask in enumerate(masks) for i in range(count)
     ]
-    return lax.ppermute(value, AXES, pairs)
+    return lax.ppermute(value, ("sect", "grp"), pairs)
+
+
+def swap_line(value, mask):
+    return lax.ppermute(value, "dev", [(i, i ^ mask) for i in range(lax.axis_size("dev"))])
 
 
 def swap_core(value):
@@ -88,18 +91,25 @@
     return vmem_call(stack_kernel, out, "stack", *pieces)
 
 
-def gather_rows(block, w_up):
-    line, weights, token = block, [], block
-    rounds = list(zip(*rounds_of()))
-    experts = w_up.shape[0]
-    for number, masks in enumerate(rounds):
-        arrived = swap(line, masks)
-        expert = number - len(rounds) + experts
-        if expert >= 0:
-            weight, token = fetch(w_up, expert, token)
+def gather_rows(block, w_up, w_gate):
+    wanted = [(w_up, e) for e in range(w_up.shape[0])] + [(w_gate, 0)]
+    weights, token = [], block
+
+    def meanwhile(arrived, token):
+        if wanted:
+            weight, token = fetch(*wanted.pop(0), token)
             weights.append(weight)
             arrived, token = lax.optimization_barrier((arrived, token))
+        return arrived, token
+
+    arrived = [swap_line(block, m) for m in range(1, lax.axis_size("dev"))]
+    arrived, token = meanwhile(arrived, token)
+    line = stack(block, *arrived)
+    for masks in rounds_of():
+        arrived, token = meanwhile(swap(line, masks), token)
         line = stack(line, arrived)
+    while wanted:
+        _, token = meanwhile(line, token)
     return [line, swap_core(line)], weights, token
 
 
@@ -112,16 +122,17 @@
 
 
 def expert_kernel(counts, width, token_ref, *refs):
-    pieces, up_refs = refs[:counts[0]], refs[counts[0]:sum(counts)]
+    pieces, up_refs = refs[:counts[0]], refs[counts[0]:sum(counts) - 1]
+    first_gate_ref = refs[sum(counts) - 1]
     (gate_hbm, down_hbm, keep_ref, send_ref,
-     rows_ref, up_ref, hidden_ref, gate_ref, gate_sems, sems) = refs[sum(counts):]
-    experts, _, hidden = gate_ref.shape
+     rows_ref, up_ref, hidden_ref, scratch_ref, gate_sems, sems) = refs[sum(counts):]
+    experts, _, hidden = scratch_ref.shape
     place = lax.axis_index("sect") * lax.axis_size("grp") + lax.axis_index("grp")
     first = place * experts
     block = min(256, hidden)
-    gate_copies = weight_copies(gate_hbm, gate_ref, gate_sems)
-    for gate_copy in gate_copies:
-        gate_copy.start()
+    for e in range(1, experts):
+        for copy in weight_copies(gate_hbm, scratch_ref, gate_sems, e):
+            copy.start()
 
     at = 0
     for piece in pieces:
@@ -137,36 +148,42 @@
                 rows_ref[:, :width], up_refs[e][0, :, span], preferred_element_type=jnp.float32
             )
 
+        if e == 0:
+            for step in range(width // hidden):
+                down_copy(0, step, down_hbm, scratch_ref, sems).start()
+
     extra = rows_ref[:, width:].astype(jnp.float32)
     lane = lax.broadcasted_iota(jnp.int32, extra.shape, 1)
-    parts = gate_sems.shape[1]
     for e in range(experts):
         mine = lax.rem(lane, extra.shape[1] // 2) == first + e
         scale = jnp.sum(jnp.where(mine, extra, 0.0), axis=1, keepdims=True)
-        for gate_copy in gate_copies[e * parts:(e + 1) * parts]:
-            gate_copy.wait()
+        if e > 0:
+            for copy in weight_copies(gate_hbm, scratch_ref, gate_sems, e):
+                copy.wait()
+        gate_ref = first_gate_ref.at[0] if e == 0 else scratch_ref.at[e]
 
         @pl.loop(0, hidden // block)
         def _(step):
             span = pl.ds(pl.multiple_of(step * block, block), block)
             gate = jnp.dot(
-                rows_ref[:, :width], gate_ref[e, :, span], preferred_element_type=jnp.float32
+                rows_ref[:, :width], gate_ref[:, span], preferred_element_type=jnp.float32
             )
             value = gate / (1.0 + jnp.exp(-gate)) * up_ref[e, :, span] * scale
             out = pl.ds(pl.multiple_of(e * hidden + step * block, block), block)
             hidden_ref[:, out] = value.astype(jnp.bfloat16)
 
-        for step in range(width // hidden):
-            down_copy(e, step, down_hbm, gate_ref, sems).start()
+        if e > 0:
+            for step in range(width // hidden):
+                down_copy(e, step, down_hbm, scratch_ref, sems).start()
 
     middle = keep_ref.shape[0]
 
     @pl.loop(0, width // hidden)
     def _(step):
         for e in range(experts):
-            down_copy(e, step, down_hbm, gate_ref, sems).wait()
+            down_copy(e, step, down_hbm, scratch_ref, sems).wait()
         span = pl.ds(pl.multiple_of(step * hidden, hidden), hidden)
-        weight = gate_ref[:, span, :].reshape(experts * hidden, hidden)
+        weight = scratch_ref[:, span, :].reshape(experts * hidden, hidden)
         total = jnp.dot(hidden_ref[...], weight, preferred_element_type=jnp.float32)
         total = total.astype(jnp.bfloat16)
         keep_ref[:, span] = total[:middle]
@@ -174,7 +191,7 @@
 
 
 def fetch_kernel(expert, after_ref, source_ref, target_ref, token_ref, sems):
-    copies = weight_copies(source_ref.at[pl.ds(expert, 1)], target_ref, sems)
+    copies = weight_copies(source_ref.at[pl.ds(expert, 1)], target_ref, sems, 0)
     for copy in copies:
         copy.start()
     token_ref[...] = jnp.zeros_like(token_ref)
@@ -182,16 +199,15 @@
         copy.wait()
 
 
-def weight_copies(source_ref, target_ref, sems):
-    experts, parts = sems.shape
+def weight_copies(source_ref, target_ref, sems, expert):
+    parts = sems.shape[1]
     depth = source_ref.shape[1] // parts
     return [
         pltpu.make_async_copy(
-            source_ref.at[e, pl.ds(p * depth, depth)],
-            target_ref.at[e, pl.ds(p * depth, depth)],
-            sems.at[e, p],
+            source_ref.at[expert, pl.ds(p * depth, depth)],
+            target_ref.at[expert, pl.ds(p * depth, depth)],
+            sems.at[expert, p],
         )
-        for e in range(experts)
         for p in range(parts)
     ]
 
@@ -216,11 +232,11 @@
     )(after, pltpu.with_memory_space_constraint(weight, pltpu.HBM))
 
 
-def expert_call(entries, w_gate, w_ups, w_down, token):
+def expert_call(entries, w_gate, held, w_down, token):
     experts, width, hidden = w_gate.shape
     full = entries[0].shape[1]
     rows = sum(e.shape[0] for e in entries)
-    counts = (len(entries), len(w_ups))
+    counts = (len(entries), len(held))
     whole = pl.BlockSpec(memory_space=pltpu.VMEM)
     anywhere = pl.BlockSpec(memory_space=pl.ANY)
     out = jax.ShapeDtypeStruct((rows // 2, width), jnp.bfloat16)
@@ -247,7 +263,7 @@
     )(
         token,
         *entries,
-        *(pltpu.with_memory_space_constraint(w, pltpu.VMEM) for w in w_ups),
+        *(pltpu.with_memory_space_constraint(w, pltpu.VMEM) for w in held),
         pltpu.with_memory_space_constraint(w_gate, pltpu.HBM),
         pltpu.with_memory_space_constraint(w_down, pltpu.HBM),
     )
@@ -268,15 +284,16 @@
 
     half = -(-expert_count // 64) * 64
     block = extend(tokens, expert_ids, gate_weights, half)
-    entries, w_ups, token = gather_rows(block, w_up)
+    entries, held, token = gather_rows(block, w_up, w_gate)
 
     results = []
-    keep, send = expert_call(entries, w_gate, w_ups, w_down, token)
+    keep, send = expert_call(entries, w_gate, held, w_down, token)
     value = add(keep, swap_core(send))
-    for masks in list(zip(*rounds_of()))[::-1]:
+    for masks in rounds_of()[::-1]:
         middle = value.shape[0] // 2
         value = add(value[:middle], swap(value[middle:], masks))
-    return value
+    own = [value[m * row_count:(m + 1) * row_count] for m in range(lanes)]
+    return add(own[0], *(swap_line(own[m], m) for m in range(1, lanes)))
 
 
 def solution(mesh):

time: 71.2 us -> 67.8 us (0.952)
  starting transfers between devices: 19.1 us -> 16.2 us
  waiting for transfers between devices: 30.6 us -> 28 us
  Pallas kernels: 20.1 us -> 22.2 us
    pallas_call x2 -> x3, Pallas kernels: 6.33 us -> 9.5 us  [fetch(): pl.pallas_call(functools.partial(fetch_kernel, expert), out_shape=(pltpu....]
    ppermute x8 -> x10, starting transfers between devices: 18.9 us -> 15.9 us  [the longest x6 9.31 us: swap_line(): lax.ppermute(value, 'dev', [(i, i ^ mask) for i in range(lax.axis_size('d...]
    ppermute x8 -> x10, waiting for transfers between devices: 25.8 us -> 23.1 us  [the longest x4 16.4 us: swap(): return lax.ppermute(value, ('sect', 'grp'), pairs)]
    pallas_call x1, Pallas kernels: 12.6 us -> 11.5 us  [expert_call(): pl.pallas_call(functools.partial(expert_kernel, counts, width), out_shape...]
  transfers between devices with their start and end apart: 10 -> 12, of which waited for: 10 -> 10; matrix products, arithmetic and copies ran while one was open for 0% -> 0% of each run, Pallas kernels for 9% -> 14%
where the time goes in v10:
time: 67.8 us; the launch traced here: 67.6 us
  waiting for transfers between devices  28 us (41%)
  Pallas kernels  22.2 us (33%)
  starting transfers between devices  16.2 us (24%)
  other arithmetic  1.07 us (2%)
    ppermute x4, waiting for transfers between devices, swap(): return lax.ppermute(value, ('sect', 'grp'), pairs)  16.4 us
    pallas_call x1, Pallas kernels, expert_call(): pl.pallas_call(functools.partial(expert_kernel, counts, width), out_shape...  11.5 us
    pallas_call x3, Pallas kernels, fetch(): pl.pallas_call(functools.partial(fetch_kernel, expert), out_shape=(pltpu....  9.5 us
    ppermute x6, starting transfers between devices, swap_line(): lax.ppermute(value, 'dev', [(i, i ^ mask) for i in range(lax.axis_size('d...  9.31 us
    ppermute x6, waiting for transfers between devices, swap_line(): lax.ppermute(value, 'dev', [(i, i ^ mask) for i in range(lax.axis_size('d...  6.72 us
    ppermute x4, starting transfers between devices, swap(): return lax.ppermute(value, ('sect', 'grp'), pairs)  6.62 us
    ppermute x2, waiting for transfers between devices, swap_core(): return lax.ppermute(value, 'sect', [(0, 1), (1, 0)])  4.82 us
  transfers between devices with their start and end apart: 12, of which 10 were waited for; matrix products, arithmetic and copies ran while one was open for 0% of the time, Pallas kernels for 14%

profile of v10, /device:TPU:0, one launch (start us, length us, event | category | flops | bytes accessed | tf_op | source)
XLA Modules:
  0.0 67.6 jit_solution(6678688165676946339)
XLA Ops:
  0.0 1.0 %extend.1.after_ref.refs_0_ = bf16[4,7296]{1,0:T(4,128)(2,1)S(1)} custom-call(bf16[4,7168]{1,0:T(4,128)(2,1)} %tokens_hbm.1, s32[4,8]{1,0:T(4,128)} %ids_hbm.1, f32[4,8]{1,0:T(4,128)} %weights_hbm.1), custom_call_target="tpu_custom_call" | custom-call | tf_op jit(solution)/shard_map/extend/pallas_call | solution.py:70
  1.0 5.1 %collective-permute-start.2 = (bf16[4,7296]{1,0:T(4,128)(2,1)S(1)}, bf16[4,7296]{1,0:T(4,128)(2,1)S(1)}, u32[]{:S(2)}, u32[]{:S(2)}) collective-permute-start(bf16[4,7296]{1,0:T(4,128)(2,1)S(1)} %extend.1.after_ref.refs_0_), channel_id=1, source_target_pairs={{0,3},{1,2},{2,1},{3,0},{4,7},{5,6},{6,5},{7,4},{8,11},{9,10},{10,... | collective-permute-start | bytes 175112 | tf_op jit(solution)/shard_map/ppermute | solution.py:30
  6.1 0.0 collective-permute-start.1
  6.1 0.6 collective-permute-start
  6.7 3.2 %fetch.3 = (bf16[1,7168,512]{2,1,0:T(8,128)(2,1)S(1)}, f32[8,128]{1,0:T(8,128)S(1)}) custom-call(bf16[4,7296]{1,0:T(4,128)(2,1)S(1)} %extend.1.after_ref.refs_0_, bf16[2,7168,512]{2,1,0:T(8,128)(2,1)} %source_ref.4), custom_call_target="tpu_custom_call" | custom-call | bytes 7340032 | tf_op jit(solution)/shard_map/fetch/pallas_call | solution.py:218
  9.9 0.0 collective-permute-done.2.refs_3_
  9.9 1.3 %collective-permute-done.1.refs_2_ = bf16[4,7296]{1,0:T(4,128)(2,1)S(1)} collective-permute-done((bf16[4,7296]{1,0:T(4,128)(2,1)S(1)}, bf16[4,7296]{1,0:T(4,128)(2,1)S(1)}, u32[]{:S(2)}, u32[]{:S(2)}) %collective-permute-start.1) | collective-permute-done | bytes 58400 | tf_op jit(solution)/shard_map/ppermute | solution.py:30
  11.2 0.0 collective-permute-done.refs_1_
  11.2 0.1 stack.3.refs_0_
  11.3 1.7 %collective-permute-start.3 = (bf16[16,7296]{1,0:T(8,128)(2,1)S(1)}, bf16[16,7296]{1,0:T(8,128)(2,1)S(1)}, u32[]{:S(2)}, u32[]{:S(2)}) collective-permute-start(bf16[16,7296]{1,0:T(8,128)(2,1)S(1)} %stack.3.refs_0_), channel_id=1, source_target_pairs={{0,8},{4,12},{8,0},{12,4},{16,20},{20,16},{24,28},{28,24},{1,9},{5... | collective-permute-start | bytes 700424 | tf_op jit(solution)/shard_map/ppermute | solution.py:26
  12.9 3.2 %fetch.4 = (bf16[1,7168,512]{2,1,0:T(8,128)(2,1)S(1)}, f32[8,128]{1,0:T(8,128)S(1)}) custom-call(f32[8,128]{1,0:T(8,128)S(1)} %get-tuple-element.25.after_ref, bf16[2,7168,512]{2,1,0:T(8,128)(2,1)} %source_ref.4), custom_call_target="tpu_custom_call" | custom-call | bytes 7340032 | tf_op jit(solution)/shard_map/fetch/pallas_call | solution.py:218
  16.1 1.3 %collective-permute-done.3.refs_1_ = bf16[16,7296]{1,0:T(8,128)(2,1)S(1)} collective-permute-done((bf16[16,7296]{1,0:T(8,128)(2,1)S(1)}, bf16[16,7296]{1,0:T(8,128)(2,1)S(1)}, u32[]{:S(2)}, u32[]{:S(2)}) %collective-permute-start.3) | collective-permute-done | bytes 233504 | tf_op jit(solution)/shard_map/ppermute | solution.py:26
  17.4 1.6 %collective-permute-start.4 = (bf16[32,7296]{1,0:T(8,128)(2,1)S(1)}, bf16[32,7296]{1,0:T(8,128)(2,1)S(1)}, u32[]{:S(2)}, u32[]{:S(2)}) collective-permute-start(bf16[32,7296]{1,0:T(8,128)(2,1)S(1)} %stack.4.refs_0_), channel_id=1, source_target_pairs={{0,4},{4,0},{8,12},{12,8},{16,24},{20,28},{24,16},{28,20},{1,5},{5... | collective-permute-start | bytes 1400840 | tf_op jit(solution)/shard_map/ppermute | solution.py:26
  19.1 3.2 %fetch.5 = (bf16[1,7168,512]{2,1,0:T(8,128)(2,1)S(1)}, f32[8,128]{1,0:T(8,128)S(1)}) custom-call(f32[8,128]{1,0:T(8,128)S(1)} %get-tuple-element.28.after_ref, bf16[2,7168,512]{2,1,0:T(8,128)(2,1)} %refs_5_.1), custom_call_target="tpu_custom_call" | custom-call | bytes 7340032 | tf_op jit(solution)/shard_map/fetch/pallas_call | solution.py:218
  22.2 3.8 %collective-permute-done.4.refs_1_ = bf16[32,7296]{1,0:T(8,128)(2,1)S(1)} collective-permute-done((bf16[32,7296]{1,0:T(8,128)(2,1)S(1)}, bf16[32,7296]{1,0:T(8,128)(2,1)S(1)}, u32[]{:S(2)}, u32[]{:S(2)}) %collective-permute-start.4) | collective-permute-done | bytes 466976 | tf_op jit(solution)/shard_map/ppermute | solution.py:26
  26.1 0.1 stack.5.refs_0_
  26.1 0.1 collective-permute-start.5
  26.2 2.5 %collective-permute-done.5.refs_1_ = bf16[64,7296]{1,0:T(8,128)(2,1)S(1)} collective-permute-done((bf16[64,7296]{1,0:T(8,128)(2,1)S(1)}, bf16[64,7296]{1,0:T(8,128)(2,1)S(1)}, u32[]{:S(2)}, u32[]{:S(2)}) %collective-permute-start.5) | collective-permute-done | bytes 933920 | tf_op jit(solution)/shard_map/ppermute | solution.py:34
  28.7 11.5 %experts.1 = (bf16[64,7168]{1,0:T(8,128)(2,1)S(1)}, bf16[64,7168]{1,0:T(8,128)(2,1)S(1)}) custom-call(f32[8,128]{1,0:T(8,128)S(1)} %get-tuple-element.30.token_ref, bf16[64,7296]{1,0:T(8,128)(2,1)S(1)} %stack.5.refs_0_, bf16[64,7296]{1,0:T(8,128)(2,1)S(1)} %collective-permute-done.5.refs_1_, bf16[1,7168,512]{2,1,0:T(8,128)(2,1)S(1)} %get-tuple-element.32.refs_2_, ...), custom_call_target="tpu_custom_call" | custom-call | flops 5637144576 | bytes 29360128 | tf_op jit(solution)/shard_map/experts/pallas_call | solution.py:243
  40.2 0.2 collective-permute-start.6
  40.4 2.3 %collective-permute-done.6 = bf16[64,7168]{1,0:T(8,128)(2,1)S(1)} collective-permute-done((bf16[64,7168]{1,0:T(8,128)(2,1)S(1)}, bf16[64,7168]{1,0:T(8,128)(2,1)S(1)}, u32[]{:S(2)}, u32[]{:S(2)}) %collective-permute-start.6) | collective-permute-done | bytes 917536 | tf_op jit(solution)/shard_map/ppermute | solution.py:34
  42.7 0.2 add_convert_fusion
  43.0 1.6 %collective-permute-start.7 = (bf16[32,7168]{1,0:T(8,128)(2,1)S(1)}, bf16[32,7168]{1,0:T(8,128)(2,1)S(1)}, u32[]{:S(2)}, u32[]{:S(2)}) collective-permute-start(bf16[32,7168]{1,0:T(8,128)(2,1)S(1)} %slice.33), channel_id=1, source_target_pairs={{0,4},{4,0},{8,12},{12,8},{16,24},{20,28},{24,16},{28,20},{1,5},{5... | collective-permute-start | bytes 1376264 | tf_op jit(solution)/shard_map/ppermute | solution.py:26
  44.6 6.9 %collective-permute-done.7 = bf16[32,7168]{1,0:T(8,128)(2,1)S(1)} collective-permute-done((bf16[32,7168]{1,0:T(8,128)(2,1)S(1)}, bf16[32,7168]{1,0:T(8,128)(2,1)S(1)}, u32[]{:S(2)}, u32[]{:S(2)}) %collective-permute-start.7) | collective-permute-done | bytes 458784 | tf_op jit(solution)/shard_map/ppermute | solution.py:26
  51.5 0.1 add_convert_fusion.1
  51.7 1.7 %collective-permute-start.8 = (bf16[16,7168]{1,0:T(8,128)(2,1)S(1)}, bf16[16,7168]{1,0:T(8,128)(2,1)S(1)}, u32[]{:S(2)}, u32[]{:S(2)}) collective-permute-start(bf16[16,7168]{1,0:T(8,128)(2,1)S(1)} %slice.35), channel_id=1, source_target_pairs={{0,8},{4,12},{8,0},{12,4},{16,20},{20,16},{24,28},{28,24},{1,9},{5... | collective-permute-start | bytes 688136 | tf_op jit(solution)/shard_map/ppermute | solution.py:26
  53.3 4.4 %collective-permute-done.8 = bf16[16,7168]{1,0:T(8,128)(2,1)S(1)} collective-permute-done((bf16[16,7168]{1,0:T(8,128)(2,1)S(1)}, bf16[16,7168]{1,0:T(8,128)(2,1)S(1)}, u32[]{:S(2)}, u32[]{:S(2)}) %collective-permute-start.8) | collective-permute-done | bytes 229408 | tf_op jit(solution)/shard_map/ppermute | solution.py:26
  57.8 0.1 add_convert_fusion.2
  57.8 0.1 fusion
  57.9 1.2 %collective-permute-start.9 = (bf16[4,7168]{1,0:T(4,128)(2,1)S(1)}, bf16[4,7168]{1,0:T(4,128)(2,1)S(1)}, u32[]{:S(2)}, u32[]{:S(2)}) collective-permute-start(bf16[4,7168]{1,0:T(4,128)(2,1)S(1)} %get-tuple-element.37), channel_id=1, source_target_pairs={{0,1},{1,0},{2,3},{3,2},{4,5},{5,4},{6,7},{7,6},{8,9},{9,8},{10,11... | collective-permute-start | bytes 172040 | tf_op jit(solution)/shard_map/ppermute | solution.py:30
  59.1 2.3 %collective-permute-start.11 = (bf16[4,7168]{1,0:T(4,128)(2,1)S(1)}, bf16[4,7168]{1,0:T(4,128)(2,1)S(1)}, u32[]{:S(2)}, u32[]{:S(2)}) collective-permute-start(bf16[4,7168]{1,0:T(4,128)(2,1)S(1)} %get-tuple-element.38), channel_id=1, source_target_pairs={{0,3},{1,2},{2,1},{3,0},{4,7},{5,6},{6,5},{7,4},{8,11},{9,10},{10,... | collective-permute-start | bytes 172040 | tf_op jit(solution)/shard_map/ppermute | solution.py:30
  61.5 0.0 collective-permute-start.10
  61.5 1.3 %collective-permute-done.9 = bf16[4,7168]{1,0:T(4,128)(2,1)S(1)} collective-permute-done((bf16[4,7168]{1,0:T(4,128)(2,1)S(1)}, bf16[4,7168]{1,0:T(4,128)(2,1)S(1)}, u32[]{:S(2)}, u32[]{:S(2)}) %collective-permute-start.9) | collective-permute-done | bytes 57376 | tf_op jit(solution)/shard_map/ppermute | solution.py:30
  62.8 2.3 %collective-permute-done.11 = bf16[4,7168]{1,0:T(4,128)(2,1)S(1)} collective-permute-done((bf16[4,7168]{1,0:T(4,128)(2,1)S(1)}, bf16[4,7168]{1,0:T(4,128)(2,1)S(1)}, u32[]{:S(2)}, u32[]{:S(2)}) %collective-permute-start.11) | collective-permute-done | bytes 57376 | tf_op jit(solution)/shard_map/ppermute | solution.py:30
  65.1 1.8 %collective-permute-done.10 = bf16[4,7168]{1,0:T(4,128)(2,1)S(1)} collective-permute-done((bf16[4,7168]{1,0:T(4,128)(2,1)S(1)}, bf16[4,7168]{1,0:T(4,128)(2,1)S(1)}, u32[]{:S(2)}, u32[]{:S(2)}) %collective-permute-start.10) | collective-permute-done | bytes 57376 | tf_op jit(solution)/shard_map/ppermute | solution.py:30
  66.9 0.7 %add_convert_fusion.3 = bf16[4,7168]{1,0:T(4,128)(2,1)} fusion(bf16[4,7168]{1,0:T(4,128)(2,1)S(1)} %collective-permute-done.11, bf16[4,7168]{1,0:T(4,128)(2,1)S(1)} %collective-permute-done.10, bf16[4,7168]{1,0:T(4,128)(2,1)S(1)} %collective-permute-done.9, bf16[16,7168]{1,0:T(8,128)(2,1)S(1)} %add_convert_fusion.2), kind=kLoop, calls=%fused_computation.3 | loop fusion | flops 229376 | bytes 286720 | tf_op jit(solution)/shard_map/convert_element_type | solution.py:276
  (3 shorter events, 0.1 us)
Async XLA Ops:
  1.0 8.9 %collective-permute-start.2 = (bf16[4,7296]{1,0:T(4,128)(2,1)S(1)}, bf16[4,7296]{1,0:T(4,128)(2,1)S(1)}, u32[]{:S(2)}, u32[]{:S(2)}) collective-permute-start(bf16[4,7296]{1,0:T(4,128)(2,1)S(1)} %extend.1.after_ref.refs_0_), channel_id=1, source_target_pairs={{0,3},{1,2},{2,1},{3,0},{4,7},{5,6},{6,5},{7,4},{8,11},{9,10},{10,... | collective-permute-start | bytes 175112 | tf_op jit(solution)/shard_map/ppermute | solution.py:30
  6.1 5.1 %collective-permute-start.1 = (bf16[4,7296]{1,0:T(4,128)(2,1)S(1)}, bf16[4,7296]{1,0:T(4,128)(2,1)S(1)}, u32[]{:S(2)}, u32[]{:S(2)}) collective-permute-start(bf16[4,7296]{1,0:T(4,128)(2,1)S(1)} %extend.1.after_ref.refs_0_), channel_id=1, source_target_pairs={{0,2},{1,3},{2,0},{3,1},{4,6},{5,7},{6,4},{7,5},{8,10},{9,11},{10,... | collective-permute-start | bytes 175112 | tf_op jit(solution)/shard_map/ppermute | solution.py:30
  6.1 5.1 %collective-permute-start = (bf16[4,7296]{1,0:T(4,128)(2,1)S(1)}, bf16[4,7296]{1,0:T(4,128)(2,1)S(1)}, u32[]{:S(2)}, u32[]{:S(2)}) collective-permute-start(bf16[4,7296]{1,0:T(4,128)(2,1)S(1)} %extend.1.after_ref.refs_0_), channel_id=1, source_target_pairs={{0,1},{1,0},{2,3},{3,2},{4,5},{5,4},{6,7},{7,6},{8,9},{9,8},{10,11... | collective-permute-start | bytes 175112 | tf_op jit(solution)/shard_map/ppermute | solution.py:30
  11.3 6.1 %collective-permute-start.3 = (bf16[16,7296]{1,0:T(8,128)(2,1)S(1)}, bf16[16,7296]{1,0:T(8,128)(2,1)S(1)}, u32[]{:S(2)}, u32[]{:S(2)}) collective-permute-start(bf16[16,7296]{1,0:T(8,128)(2,1)S(1)} %stack.3.refs_0_), channel_id=1, source_target_pairs={{0,8},{4,12},{8,0},{12,4},{16,20},{20,16},{24,28},{28,24},{1,9},{5... | collective-permute-start | bytes 700424 | tf_op jit(solution)/shard_map/ppermute | solution.py:26
  17.4 8.6 %collective-permute-start.4 = (bf16[32,7296]{1,0:T(8,128)(2,1)S(1)}, bf16[32,7296]{1,0:T(8,128)(2,1)S(1)}, u32[]{:S(2)}, u32[]{:S(2)}) collective-permute-start(bf16[32,7296]{1,0:T(8,128)(2,1)S(1)} %stack.4.refs_0_), channel_id=1, source_target_pairs={{0,4},{4,0},{8,12},{12,8},{16,24},{20,28},{24,16},{28,20},{1,5},{5... | collective-permute-start | bytes 1400840 | tf_op jit(solution)/shard_map/ppermute | solution.py:26
  26.1 2.6 %collective-permute-start.5 = (bf16[64,7296]{1,0:T(8,128)(2,1)S(1)}, bf16[64,7296]{1,0:T(8,128)(2,1)S(1)}, u32[]{:S(2)}, u32[]{:S(2)}) collective-permute-start(bf16[64,7296]{1,0:T(8,128)(2,1)S(1)} %stack.5.refs_0_), channel_id=1, source_target_pairs={{0,16},{16,0},{1,17},{17,1},{2,18},{18,2},{3,19},{19,3},{4,20},{20... | collective-permute-start | bytes 2801672 | tf_op jit(solution)/shard_map/ppermute | solution.py:34
  40.2 2.5 %collective-permute-start.6 = (bf16[64,7168]{1,0:T(8,128)(2,1)S(1)}, bf16[64,7168]{1,0:T(8,128)(2,1)S(1)}, u32[]{:S(2)}, u32[]{:S(2)}) collective-permute-start(bf16[64,7168]{1,0:T(8,128)(2,1)S(1)} %get-tuple-element.36), channel_id=1, source_target_pairs={{0,16},{16,0},{1,17},{17,1},{2,18},{18,2},{3,19},{19,3},{4,20},{20... | collective-permute-start | bytes 2752520 | tf_op jit(solution)/shard_map/ppermute | solution.py:34
  43.0 8.5 %collective-permute-start.7 = (bf16[32,7168]{1,0:T(8,128)(2,1)S(1)}, bf16[32,7168]{1,0:T(8,128)(2,1)S(1)}, u32[]{:S(2)}, u32[]{:S(2)}) collective-permute-start(bf16[32,7168]{1,0:T(8,128)(2,1)S(1)} %slice.33), channel_id=1, source_target_pairs={{0,4},{4,0},{8,12},{12,8},{16,24},{20,28},{24,16},{28,20},{1,5},{5... | collective-permute-start | bytes 1376264 | tf_op jit(solution)/shard_map/ppermute | solution.py:26
  51.7 6.1 %collective-permute-start.8 = (bf16[16,7168]{1,0:T(8,128)(2,1)S(1)}, bf16[16,7168]{1,0:T(8,128)(2,1)S(1)}, u32[]{:S(2)}, u32[]{:S(2)}) collective-permute-start(bf16[16,7168]{1,0:T(8,128)(2,1)S(1)} %slice.35), channel_id=1, source_target_pairs={{0,8},{4,12},{8,0},{12,4},{16,20},{20,16},{24,28},{28,24},{1,9},{5... | collective-permute-start | bytes 688136 | tf_op jit(solution)/shard_map/ppermute | solution.py:26
  57.9 4.9 %collective-permute-start.9 = (bf16[4,7168]{1,0:T(4,128)(2,1)S(1)}, bf16[4,7168]{1,0:T(4,128)(2,1)S(1)}, u32[]{:S(2)}, u32[]{:S(2)}) collective-permute-start(bf16[4,7168]{1,0:T(4,128)(2,1)S(1)} %get-tuple-element.37), channel_id=1, source_target_pairs={{0,1},{1,0},{2,3},{3,2},{4,5},{5,4},{6,7},{7,6},{8,9},{9,8},{10,11... | collective-permute-start | bytes 172040 | tf_op jit(solution)/shard_map/ppermute | solution.py:30
  59.1 6.0 %collective-permute-start.11 = (bf16[4,7168]{1,0:T(4,128)(2,1)S(1)}, bf16[4,7168]{1,0:T(4,128)(2,1)S(1)}, u32[]{:S(2)}, u32[]{:S(2)}) collective-permute-start(bf16[4,7168]{1,0:T(4,128)(2,1)S(1)} %get-tuple-element.38), channel_id=1, source_target_pairs={{0,3},{1,2},{2,1},{3,0},{4,7},{5,6},{6,5},{7,4},{8,11},{9,10},{10,... | collective-permute-start | bytes 172040 | tf_op jit(solution)/shard_map/ppermute | solution.py:30
  61.5 5.5 %collective-permute-start.10 = (bf16[4,7168]{1,0:T(4,128)(2,1)S(1)}, bf16[4,7168]{1,0:T(4,128)(2,1)S(1)}, u32[]{:S(2)}, u32[]{:S(2)}) collective-permute-start(bf16[4,7168]{1,0:T(4,128)(2,1)S(1)} %get-tuple-element.39), channel_id=1, source_target_pairs={{0,2},{1,3},{2,0},{3,1},{4,6},{5,7},{6,4},{7,5},{8,10},{9,11},{10,... | collective-permute-start | bytes 172040 | tf_op jit(solution)/shard_map/ppermute | solution.py:30

commit v11 on v10

--- a/solution.py
+++ b/solution.py
@@ -8,7 +8,7 @@
 from jax.sharding import PartitionSpec as P
 
 AXES = ("sect", "grp", "dev")
-VMEM_LIMIT = 20 * 2**20
+VMEM_LIMIT = 10 * 2**20
 
 
 def rounds_of():
@@ -105,12 +105,16 @@
     arrived = [swap_line(block, m) for m in range(1, lax.axis_size("dev"))]
     arrived, token = meanwhile(arrived, token)
     line = stack(block, *arrived)
-    for masks in rounds_of():
+    rounds = rounds_of()
+    for masks in rounds[:-1]:
         arrived, token = meanwhile(swap(line, masks), token)
         line = stack(line, arrived)
+    last = swap(line, rounds[-1])
+    mine, token = meanwhile(line, token)
+    last, other, token = lax.optimization_barrier((last, swap_core(mine), token))
     while wanted:
         _, token = meanwhile(line, token)
-    return [line, swap_core(line)], weights, token
+    return [line, last, other, swap_core(last)], weights, token
 
 
 def down_copy(expert, block, down_hbm, target_ref, sems):
@@ -121,17 +125,30 @@
     )
 
 
+def down_block(step, hidden_ref, weights_ref, keep_ref, send_ref, first):
+    experts, _, hidden = weights_ref.shape
+    middle = keep_ref.shape[0]
+    rows = pl.ds(pl.multiple_of((first + step) * hidden, hidden), hidden)
+    weight = weights_ref[:, rows, :].reshape(experts * hidden, hidden)
+    total = jnp.dot(hidden_ref[...], weight, preferred_element_type=jnp.float32)
+    total = total.astype(jnp.bfloat16)
+    span = pl.ds(pl.multiple_of(step * hidden, hidden), hidden)
+    keep_ref[:, span] = total[:middle]
+    send_ref[:, span] = total[middle:]
+
+
 def expert_kernel(counts, width, token_ref, *refs):
     pieces, up_refs = refs[:counts[0]], refs[counts[0]:sum(counts) - 1]
     first_gate_ref = refs[sum(counts) - 1]
-    (gate_hbm, down_hbm, keep_ref, send_ref,
-     rows_ref, up_ref, hidden_ref, scratch_ref, gate_sems, sems) = refs[sum(counts):]
-    experts, _, hidden = scratch_ref.shape
+    (gate_hbm, down_hbm, hidden_ref, keep_ref, send_ref, weights_ref,
+     rows_ref, up_ref, gate_sems, sems) = refs[sum(counts):]
+    experts, _, hidden = weights_ref.shape
     place = lax.axis_index("sect") * lax.axis_size("grp") + lax.axis_index("grp")
     first = place * experts
     block = min(256, hidden)
+    blocks = width // hidden
     for e in range(1, experts):
-        for copy in weight_copies(gate_hbm, scratch_ref, gate_sems, e):
+        for copy in weight_copies(gate_hbm, weights_ref, gate_sems, e):
             copy.start()
 
     at = 0
@@ -141,7 +158,7 @@
 
     for e in range(experts):
 
-        @pl.loop(0, hidden // block)
+        @pl.loop(0, hidden // block, unroll=True)
         def _(step):
             span = pl.ds(pl.multiple_of(step * block, block), block)
             up_ref[e, :, span] = jnp.dot(
@@ -149,8 +166,8 @@
             )
 
         if e == 0:
-            for step in range(width // hidden):
-                down_copy(0, step, down_hbm, scratch_ref, sems).start()
+            for step in range(blocks):
+                down_copy(0, step, down_hbm, weights_ref, sems).start()
 
     extra = rows_ref[:, width:].astype(jnp.float32)
     lane = lax.broadcasted_iota(jnp.int32, extra.shape, 1)
@@ -158,11 +175,11 @@
         mine = lax.rem(lane, extra.shape[1] // 2) == first + e
         scale = jnp.sum(jnp.where(mine, extra, 0.0), axis=1, keepdims=True)
         if e > 0:
-            for copy in weight_copies(gate_hbm, scratch_ref, gate_sems, e):
+            for copy in weight_copies(gate_hbm, weights_ref, gate_sems, e):
                 copy.wait()
-        gate_ref = first_gate_ref.at[0] if e == 0 else scratch_ref.at[e]
-
-        @pl.loop(0, hidden // block)
+        gate_ref = first_gate_ref.at[0] if e == 0 else weights_ref.at[e]
+
+        @pl.loop(0, hidden // block, unroll=True)
         def _(step):
             span = pl.ds(pl.multiple_of(step * block, block), block)
             gate = jnp.dot(
@@ -173,21 +190,24 @@
             hidden_ref[:, out] = value.astype(jnp.bfloat16)
 
         if e > 0:
-            for step in range(width // hidden):
-                down_copy(e, step, down_hbm, scratch_ref, sems).start()
-
-    middle = keep_ref.shape[0]
-
-    @pl.loop(0, width // hidden)
+            for step in range(blocks):
+                down_copy(e, step, down_hbm, weights_ref, sems).start()
+
+    @pl.loop(0, blocks // 2)
     def _(step):
         for e in range(experts):
-            down_copy(e, step, down_hbm, scratch_ref, sems).wait()
-        span = pl.ds(pl.multiple_of(step * hidden, hidden), hidden)
-        weight = scratch_ref[:, span, :].reshape(experts * hidden, hidden)
-        total = jnp.dot(hidden_ref[...], weight, preferred_element_type=jnp.float32)
-        total = total.astype(jnp.bfloat16)
-        keep_ref[:, span] = total[:middle]
-        send_ref[:, span] = total[middle:]
+            down_copy(e, step, down_hbm, weights_ref, sems).wait()
+        down_block(step, hidden_ref, weights_ref, keep_ref, send_ref, 0)
+
+    for step in range(blocks // 2, blocks):
+        for e in range(experts):
+            down_copy(e, step, down_hbm, weights_ref, sems).wait()
+
+
+def down_kernel(first, hidden_ref, weights_ref, keep_ref, send_ref):
+    @pl.loop(0, keep_ref.shape[1] // weights_ref.shape[2], unroll=True)
+    def _(step):
+        down_block(step, hidden_ref, weights_ref, keep_ref, send_ref, first)
 
 
 def fetch_kernel(expert, after_ref, source_ref, target_ref, token_ref, sems):
@@ -237,25 +257,30 @@
     full = entries[0].shape[1]
     rows = sum(e.shape[0] for e in entries)
     counts = (len(entries), len(held))
+    blocks = width // hidden
     whole = pl.BlockSpec(memory_space=pltpu.VMEM)
     anywhere = pl.BlockSpec(memory_space=pl.ANY)
-    out = jax.ShapeDtypeStruct((rows // 2, width), jnp.bfloat16)
-    return pl.pallas_call(
+    columns = (blocks // 2 * hidden, (blocks - blocks // 2) * hidden)
+    outs = [jax.ShapeDtypeStruct((rows // 2, c), jnp.bfloat16) for c in columns]
+    hiddens, keep, send, weights = pl.pallas_call(
         functools.partial(expert_kernel, counts, width),
-        out_shape=(out, out),
+        out_shape=(
+            jax.ShapeDtypeStruct((rows, experts * hidden), jnp.bfloat16),
+            outs[0],
+            outs[0],
+            pltpu.VMEM(w_gate.shape, w_gate.dtype),
+        ),
         in_specs=[anywhere] + [whole] * sum(counts) + [anywhere] * 2,
-        out_specs=(whole,) * 2,
+        out_specs=(whole,) * 4,
         scratch_shapes=[
             pltpu.VMEM((rows, full), jnp.bfloat16),
             pltpu.VMEM((experts, rows, hidden), jnp.float32),
-            pltpu.VMEM((rows, experts * hidden), jnp.bfloat16),
-            pltpu.VMEM(w_gate.shape, w_gate.dtype),
             pltpu.SemaphoreType.DMA((experts, 4)),
-            pltpu.SemaphoreType.DMA((experts, width // hidden)),
+            pltpu.SemaphoreType.DMA((experts, blocks)),
         ],
         compiler_params=pltpu.CompilerParams(vmem_limit_bytes=VMEM_LIMIT),
         cost_estimate=pl.CostEstimate(
-            flops=6 * rows * experts * width * hidden,
+            flops=5 * rows * experts * width * hidden,
             bytes_accessed=2 * (w_gate.size + w_down.size),
             transcendentals=rows * experts * hidden,
         ),
@@ -267,6 +292,20 @@
         pltpu.with_memory_space_constraint(w_gate, pltpu.HBM),
         pltpu.with_memory_space_constraint(w_down, pltpu.HBM),
     )
+    later = pl.pallas_call(
+        functools.partial(down_kernel, blocks // 2),
+        out_shape=(outs[1], outs[1]),
+        in_specs=[whole, whole],
+        out_specs=(whole, whole),
+        compiler_params=pltpu.CompilerParams(vmem_limit_bytes=VMEM_LIMIT),
+        cost_estimate=pl.CostEstimate(
+            flops=rows * experts * width * hidden,
+            bytes_accessed=2 * rows * columns[1],
+            transcendentals=0,
+        ),
+        name="down",
+    )(hiddens, pltpu.with_memory_space_constraint(weights, pltpu.VMEM))
+    return (keep, send), later
 
 
 def add(*values):
@@ -287,11 +326,14 @@
     entries, held, token = gather_rows(block, w_up, w_gate)
 
     results = []
-    keep, send = expert_call(entries, w_gate, held, w_down, token)
-    value = add(keep, swap_core(send))
-    for masks in rounds_of()[::-1]:
-        middle = value.shape[0] // 2
-        value = add(value[:middle], swap(value[middle:], masks))
+    halves = []
+    for keep, send in expert_call(entries, w_gate, held, w_down, token):
+        value = add(keep, swap_core(send))
+        for masks in rounds_of()[::-1]:
+            middle = value.shape[0] // 2
+            value = add(value[:middle], swap(value[middle:], masks))
+        halves.append(value)
+    value = jnp.concatenate(halves, axis=1)
     own = [value[m * row_count:(m + 1) * row_count] for m in range(lanes)]
     return add(own[0], *(swap_line(own[m], m) for m in range(1, lanes)))
 

time: 67.8 us -> 64.8 us (0.956)
  waiting for transfers between devices: 28 us -> 21 us
  starting transfers between devices: 16.2 us -> 19.5 us
    ppermute x4 -> x6, waiting for transfers between devices: 16.4 us -> 12.4 us  [swap(): return lax.ppermute(value, ('sect', 'grp'), pairs)]
    ppermute x4 -> x6, starting transfers between devices: 6.62 us -> 9.5 us  [swap(): return lax.ppermute(value, ('sect', 'grp'), pairs)]
    ppermute x2 -> x4, waiting for transfers between devices: 4.82 us -> 1.94 us  [swap_core(): return lax.ppermute(value, 'sect', [(0, 1), (1, 0)])]
    pallas_call x0 -> x1, Pallas kernels: none -> 1.12 us  [expert_call(): pl.pallas_call(functools.partial(down_kernel, blocks // 2), out_shape=(ou...]
  transfers between devices with their start and end apart: 12 -> 16, of which waited for: 10 -> 12; matrix products, arithmetic and copies ran while one was open for 0% -> 1% of each run, Pallas kernels for 14% -> 16%
where the time goes in v11:
time: 64.8 us; the launch traced here: 64.6 us
  Pallas kernels  22.7 us (35%)
  waiting for transfers between devices  21 us (32%)
  starting transfers between devices  19.5 us (30%)
  other arithmetic  1.15 us (2%)
    ppermute x6, waiting for transfers between devices, swap(): return lax.ppermute(value, ('sect', 'grp'), pairs)  12.4 us
    pallas_call x1, Pallas kernels, expert_call(): pl.pallas_call(functools.partial(expert_kernel, counts, width), out_shape...  11 us
    pallas_call x3, Pallas kernels, fetch(): pl.pallas_call(functools.partial(fetch_kernel, expert), out_shape=(pltpu....  9.5 us
    ppermute x6, starting transfers between devices, swap(): return lax.ppermute(value, ('sect', 'grp'), pairs)  9.5 us
    ppermute x6, starting transfers between devices, swap_line(): lax.ppermute(value, 'dev', [(i, i ^ mask) for i in range(lax.axis_size('d...  9.31 us
    ppermute x6, waiting for transfers between devices, swap_line(): lax.ppermute(value, 'dev', [(i, i ^ mask) for i in range(lax.axis_size('d...  6.72 us
    ppermute x4, waiting for transfers between devices, swap_core(): return lax.ppermute(value, 'sect', [(0, 1), (1, 0)])  1.94 us
  transfers between devices with their start and end apart: 16, of which 12 were waited for; matrix products, arithmetic and copies ran while one was open for 1% of the time, Pallas kernels for 16%

profile of v11, /device:TPU:0, one launch (start us, length us, event | category | flops | bytes accessed | tf_op | source)
XLA Modules:
  0.0 64.6 jit_solution(10473494793715220786)
XLA Ops:
  0.0 1.0 %extend.1.after_ref.refs_0_ = bf16[4,7296]{1,0:T(4,128)(2,1)S(1)} custom-call(bf16[4,7168]{1,0:T(4,128)(2,1)} %tokens_hbm.1, s32[4,8]{1,0:T(4,128)} %ids_hbm.1, f32[4,8]{1,0:T(4,128)} %weights_hbm.1), custom_call_target="tpu_custom_call" | custom-call | tf_op jit(solution)/shard_map/extend/pallas_call | solution.py:70
  1.0 5.1 %collective-permute-start.2 = (bf16[4,7296]{1,0:T(4,128)(2,1)S(1)}, bf16[4,7296]{1,0:T(4,128)(2,1)S(1)}, u32[]{:S(2)}, u32[]{:S(2)}) collective-permute-start(bf16[4,7296]{1,0:T(4,128)(2,1)S(1)} %extend.1.after_ref.refs_0_), channel_id=1, source_target_pairs={{0,3},{1,2},{2,1},{3,0},{4,7},{5,6},{6,5},{7,4},{8,11},{9,10},{10,... | collective-permute-start | bytes 175112 | tf_op jit(solution)/shard_map/ppermute | solution.py:30
  6.1 0.0 collective-permute-start.1
  6.1 0.6 collective-permute-start
  6.7 3.2 %fetch.3 = (bf16[1,7168,512]{2,1,0:T(8,128)(2,1)S(1)}, f32[8,128]{1,0:T(8,128)S(1)}) custom-call(bf16[4,7296]{1,0:T(4,128)(2,1)S(1)} %extend.1.after_ref.refs_0_, bf16[2,7168,512]{2,1,0:T(8,128)(2,1)} %source_ref.4), custom_call_target="tpu_custom_call" | custom-call | bytes 7340032 | tf_op jit(solution)/shard_map/fetch/pallas_call | solution.py:238
  9.9 0.0 collective-permute-done.2.refs_3_
  9.9 1.3 %collective-permute-done.1.refs_2_ = bf16[4,7296]{1,0:T(4,128)(2,1)S(1)} collective-permute-done((bf16[4,7296]{1,0:T(4,128)(2,1)S(1)}, bf16[4,7296]{1,0:T(4,128)(2,1)S(1)}, u32[]{:S(2)}, u32[]{:S(2)}) %collective-permute-start.1) | collective-permute-done | bytes 58400 | tf_op jit(solution)/shard_map/ppermute | solution.py:30
  11.2 0.0 collective-permute-done.refs_1_
  11.2 0.1 stack.2.refs_0_
  11.3 1.7 %collective-permute-start.3 = (bf16[16,7296]{1,0:T(8,128)(2,1)S(1)}, bf16[16,7296]{1,0:T(8,128)(2,1)S(1)}, u32[]{:S(2)}, u32[]{:S(2)}) collective-permute-start(bf16[16,7296]{1,0:T(8,128)(2,1)S(1)} %stack.2.refs_0_), channel_id=1, source_target_pairs={{0,8},{4,12},{8,0},{12,4},{16,20},{20,16},{24,28},{28,24},{1,9},{5... | collective-permute-start | bytes 700424 | tf_op jit(solution)/shard_map/ppermute | solution.py:26
  12.9 3.2 %fetch.4 = (bf16[1,7168,512]{2,1,0:T(8,128)(2,1)S(1)}, f32[8,128]{1,0:T(8,128)S(1)}) custom-call(f32[8,128]{1,0:T(8,128)S(1)} %get-tuple-element.32.after_ref, bf16[2,7168,512]{2,1,0:T(8,128)(2,1)} %source_ref.4), custom_call_target="tpu_custom_call" | custom-call | bytes 7340032 | tf_op jit(solution)/shard_map/fetch/pallas_call | solution.py:238
  16.1 1.3 %collective-permute-done.3.refs_1_ = bf16[16,7296]{1,0:T(8,128)(2,1)S(1)} collective-permute-done((bf16[16,7296]{1,0:T(8,128)(2,1)S(1)}, bf16[16,7296]{1,0:T(8,128)(2,1)S(1)}, u32[]{:S(2)}, u32[]{:S(2)}) %collective-permute-start.3) | collective-permute-done | bytes 233504 | tf_op jit(solution)/shard_map/ppermute | solution.py:26
  17.4 1.6 %collective-permute-start.4 = (bf16[32,7296]{1,0:T(8,128)(2,1)S(1)}, bf16[32,7296]{1,0:T(8,128)(2,1)S(1)}, u32[]{:S(2)}, u32[]{:S(2)}) collective-permute-start(bf16[32,7296]{1,0:T(8,128)(2,1)S(1)} %stack.3.refs_0_), channel_id=1, source_target_pairs={{0,4},{4,0},{8,12},{12,8},{16,24},{20,28},{24,16},{28,20},{1,5},{5... | collective-permute-start | bytes 1400840 | tf_op jit(solution)/shard_map/ppermute | solution.py:26
  19.1 3.2 %fetch.5 = (bf16[1,7168,512]{2,1,0:T(8,128)(2,1)S(1)}, f32[8,128]{1,0:T(8,128)S(1)}) custom-call(f32[8,128]{1,0:T(8,128)S(1)} %get-tuple-element.35.after_ref, bf16[2,7168,512]{2,1,0:T(8,128)(2,1)} %refs_7_.1), custom_call_target="tpu_custom_call" | custom-call | bytes 7340032 | tf_op jit(solution)/shard_map/fetch/pallas_call | solution.py:238
  22.2 0.1 collective-permute-start.5
  22.3 3.7 %collective-permute-done.4.refs_1_ = bf16[32,7296]{1,0:T(8,128)(2,1)S(1)} collective-permute-done((bf16[32,7296]{1,0:T(8,128)(2,1)S(1)}, bf16[32,7296]{1,0:T(8,128)(2,1)S(1)}, u32[]{:S(2)}, u32[]{:S(2)}) %collective-permute-start.4) | collective-permute-done | bytes 466976 | tf_op jit(solution)/shard_map/ppermute | solution.py:26
  26.1 0.0 collective-permute-done.5.refs_2_
  26.1 0.0 collective-permute-start.6
  26.1 1.8 %collective-permute-done.6.refs_3_ = bf16[32,7296]{1,0:T(8,128)(2,1)S(1)} collective-permute-done((bf16[32,7296]{1,0:T(8,128)(2,1)S(1)}, bf16[32,7296]{1,0:T(8,128)(2,1)S(1)}, u32[]{:S(2)}, u32[]{:S(2)}) %collective-permute-start.6) | collective-permute-done | bytes 466976 | tf_op jit(solution)/shard_map/ppermute | solution.py:34
  27.9 11.0 %experts.1 = (bf16[128,1024]{1,0:T(8,128)(2,1)S(1)}, bf16[64,3584]{1,0:T(8,128)(2,1)S(1)}, bf16[64,3584]{1,0:T(8,128)(2,1)S(1)}, bf16[2,7168,512]{2,1,0:T(8,128)(2,1)S(1)}) custom-call(f32[8,128]{1,0:T(8,128)S(1)} %get-tuple-element.39.token_ref, bf16[32,7296]{1,0:T(8,128)(2,1)S(1)} %stack.3.refs_0_, bf16[32,7296]{1,0:T(8,128)(2,1)S(1)} %collective-permute-done.4.refs_1_, ...), custom_call_target="tpu_custom_call" | custom-call | flops 4697620480 | bytes 29360128 | tf_op jit(solution)/shard_map/experts/pallas_call | solution.py:265
  38.9 0.2 collective-permute-start.7
  39.1 1.1 %down.1 = (bf16[64,3584]{1,0:T(8,128)(2,1)S(1)}, bf16[64,3584]{1,0:T(8,128)(2,1)S(1)}) custom-call(bf16[128,1024]{1,0:T(8,128)(2,1)S(1)} %get-tuple-element.47.hidden_ref, bf16[2,7168,512]{2,1,0:T(8,128)(2,1)S(1)} %get-tuple-element.48.weights_ref), custom_call_target="tpu_custom_call" | custom-call | flops 939524096 | bytes 917504 | tf_op jit(solution)/shard_map/down/pallas_call | solution.py:295
  40.2 0.4 collective-permute-start.10
  40.7 0.1 collective-permute-done.7
  40.8 0.1 add_convert_fusion.1
  40.9 1.6 %collective-permute-start.8 = (bf16[32,3584]{1,0:T(8,128)(2,1)S(1)}, bf16[32,3584]{1,0:T(8,128)(2,1)S(1)}, u32[]{:S(2)}, u32[]{:S(2)}) collective-permute-start(bf16[32,3584]{1,0:T(8,128)(2,1)S(1)} %slice.49), channel_id=1, source_target_pairs={{0,4},{4,0},{8,12},{12,8},{16,24},{20,28},{24,16},{28,20},{1,5},{5... | collective-permute-start | bytes 688136 | tf_op jit(solution)/shard_map/ppermute | solution.py:26
  42.6 0.0 collective-permute-done.10
  42.6 0.1 add_convert_fusion
  42.7 1.2 %collective-permute-start.11 = (bf16[32,3584]{1,0:T(8,128)(2,1)S(1)}, bf16[32,3584]{1,0:T(8,128)(2,1)S(1)}, u32[]{:S(2)}, u32[]{:S(2)}) collective-permute-start(bf16[32,3584]{1,0:T(8,128)(2,1)S(1)} %slice.53), channel_id=1, source_target_pairs={{0,4},{4,0},{8,12},{12,8},{16,24},{20,28},{24,16},{28,20},{1,5},{5... | collective-permute-start | bytes 688136 | tf_op jit(solution)/shard_map/ppermute | solution.py:26
  43.9 3.1 %collective-permute-done.8 = bf16[32,3584]{1,0:T(8,128)(2,1)S(1)} collective-permute-done((bf16[32,3584]{1,0:T(8,128)(2,1)S(1)}, bf16[32,3584]{1,0:T(8,128)(2,1)S(1)}, u32[]{:S(2)}, u32[]{:S(2)}) %collective-permute-start.8) | collective-permute-done | bytes 229408 | tf_op jit(solution)/shard_map/ppermute | solution.py:26
  47.0 0.1 add_convert_fusion.3
  47.1 1.7 %collective-permute-start.9 = (bf16[16,3584]{1,0:T(8,128)(2,1)S(1)}, bf16[16,3584]{1,0:T(8,128)(2,1)S(1)}, u32[]{:S(2)}, u32[]{:S(2)}) collective-permute-start(bf16[16,3584]{1,0:T(8,128)(2,1)S(1)} %slice.51), channel_id=1, source_target_pairs={{0,8},{4,12},{8,0},{12,4},{16,20},{20,16},{24,28},{28,24},{1,9},{5... | collective-permute-start | bytes 344072 | tf_op jit(solution)/shard_map/ppermute | solution.py:26
  48.8 1.1 %collective-permute-done.11 = bf16[32,3584]{1,0:T(8,128)(2,1)S(1)} collective-permute-done((bf16[32,3584]{1,0:T(8,128)(2,1)S(1)}, bf16[32,3584]{1,0:T(8,128)(2,1)S(1)}, u32[]{:S(2)}, u32[]{:S(2)}) %collective-permute-start.11) | collective-permute-done | bytes 229408 | tf_op jit(solution)/shard_map/ppermute | solution.py:26
  49.8 0.1 add_convert_fusion.2
  49.9 1.7 %collective-permute-start.12 = (bf16[16,3584]{1,0:T(8,128)(2,1)S(1)}, bf16[16,3584]{1,0:T(8,128)(2,1)S(1)}, u32[]{:S(2)}, u32[]{:S(2)}) collective-permute-start(bf16[16,3584]{1,0:T(8,128)(2,1)S(1)} %slice.55), channel_id=1, source_target_pairs={{0,8},{4,12},{8,0},{12,4},{16,20},{20,16},{24,28},{28,24},{1,9},{5... | collective-permute-start | bytes 344072 | tf_op jit(solution)/shard_map/ppermute | solution.py:26
  51.6 0.4 collective-permute-done.9
  52.0 2.8 %collective-permute-done.12 = bf16[16,3584]{1,0:T(8,128)(2,1)S(1)} collective-permute-done((bf16[16,3584]{1,0:T(8,128)(2,1)S(1)}, bf16[16,3584]{1,0:T(8,128)(2,1)S(1)}, u32[]{:S(2)}, u32[]{:S(2)}) %collective-permute-start.12) | collective-permute-done | bytes 114720 | tf_op jit(solution)/shard_map/ppermute | solution.py:26
  54.8 0.1 fusion.2
  54.9 1.2 %collective-permute-start.13 = (bf16[4,7168]{1,0:T(4,128)(2,1)S(1)}, bf16[4,7168]{1,0:T(4,128)(2,1)S(1)}, u32[]{:S(2)}, u32[]{:S(2)}) collective-permute-start(bf16[4,7168]{1,0:T(4,128)(2,1)S(1)} %get-tuple-element.51), channel_id=1, source_target_pairs={{0,1},{1,0},{2,3},{3,2},{4,5},{5,4},{6,7},{7,6},{8,9},{9,8},{10,11... | collective-permute-start | bytes 172040 | tf_op jit(solution)/shard_map/ppermute | solution.py:30
  56.1 2.3 %collective-permute-start.15 = (bf16[4,7168]{1,0:T(4,128)(2,1)S(1)}, bf16[4,7168]{1,0:T(4,128)(2,1)S(1)}, u32[]{:S(2)}, u32[]{:S(2)}) collective-permute-start(bf16[4,7168]{1,0:T(4,128)(2,1)S(1)} %get-tuple-element.52), channel_id=1, source_target_pairs={{0,3},{1,2},{2,1},{3,0},{4,7},{5,6},{6,5},{7,4},{8,11},{9,10},{10,... | collective-permute-start | bytes 172040 | tf_op jit(solution)/shard_map/ppermute | solution.py:30
  58.4 0.0 collective-permute-start.14
  58.5 0.8 %collective-permute-done.13 = bf16[4,7168]{1,0:T(4,128)(2,1)S(1)} collective-permute-done((bf16[4,7168]{1,0:T(4,128)(2,1)S(1)}, bf16[4,7168]{1,0:T(4,128)(2,1)S(1)}, u32[]{:S(2)}, u32[]{:S(2)}) %collective-permute-start.13) | collective-permute-done | bytes 57376 | tf_op jit(solution)/shard_map/ppermute | solution.py:30
  59.2 2.9 %collective-permute-done.15 = bf16[4,7168]{1,0:T(4,128)(2,1)S(1)} collective-permute-done((bf16[4,7168]{1,0:T(4,128)(2,1)S(1)}, bf16[4,7168]{1,0:T(4,128)(2,1)S(1)}, u32[]{:S(2)}, u32[]{:S(2)}) %collective-permute-start.15) | collective-permute-done | bytes 57376 | tf_op jit(solution)/shard_map/ppermute | solution.py:30
  62.1 1.8 %collective-permute-done.14 = bf16[4,7168]{1,0:T(4,128)(2,1)S(1)} collective-permute-done((bf16[4,7168]{1,0:T(4,128)(2,1)S(1)}, bf16[4,7168]{1,0:T(4,128)(2,1)S(1)}, u32[]{:S(2)}, u32[]{:S(2)}) %collective-permute-start.14) | collective-permute-done | bytes 57376 | tf_op jit(solution)/shard_map/ppermute | solution.py:30
  63.9 0.7 %add_convert_fusion.6 = bf16[4,7168]{1,0:T(4,128)(2,1)} fusion(bf16[4,7168]{1,0:T(4,128)(2,1)S(1)} %collective-permute-done.15, bf16[4,7168]{1,0:T(4,128)(2,1)S(1)} %collective-permute-done.14, bf16[4,7168]{1,0:T(4,128)(2,1)S(1)} %collective-permute-done.13, bf16[16,3584]{1,0:T(8,128)(2,1)S(1)} %add_convert_fusion.5, bf16[16,3584]{1,0:T(8,128)(2,1)S(1)} %add_convert_fusion.4), kind=kLoop, calls=%fused_computation.12 | loop fusion | flops 315392 | bytes 458752 | tf_op jit(solution)/shard_map/convert_element_type | solution.py:315
  (7 shorter events, 0.1 us)
Async XLA Ops:
  1.0 8.9 %collective-permute-start.2 = (bf16[4,7296]{1,0:T(4,128)(2,1)S(1)}, bf16[4,7296]{1,0:T(4,128)(2,1)S(1)}, u32[]{:S(2)}, u32[]{:S(2)}) collective-permute-start(bf16[4,7296]{1,0:T(4,128)(2,1)S(1)} %extend.1.after_ref.refs_0_), channel_id=1, source_target_pairs={{0,3},{1,2},{2,1},{3,0},{4,7},{5,6},{6,5},{7,4},{8,11},{9,10},{10,... | collective-permute-start | bytes 175112 | tf_op jit(solution)/shard_map/ppermute | solution.py:30
  6.1 5.1 %collective-permute-start.1 = (bf16[4,7296]{1,0:T(4,128)(2,1)S(1)}, bf16[4,7296]{1,0:T(4,128)(2,1)S(1)}, u32[]{:S(2)}, u32[]{:S(2)}) collective-permute-start(bf16[4,7296]{1,0:T(4,128)(2,1)S(1)} %extend.1.after_ref.refs_0_), channel_id=1, source_target_pairs={{0,2},{1,3},{2,0},{3,1},{4,6},{5,7},{6,4},{7,5},{8,10},{9,11},{10,... | collective-permute-start | bytes 175112 | tf_op jit(solution)/shard_map/ppermute | solution.py:30
  6.1 5.1 %collective-permute-start = (bf16[4,7296]{1,0:T(4,128)(2,1)S(1)}, bf16[4,7296]{1,0:T(4,128)(2,1)S(1)}, u32[]{:S(2)}, u32[]{:S(2)}) collective-permute-start(bf16[4,7296]{1,0:T(4,128)(2,1)S(1)} %extend.1.after_ref.refs_0_), channel_id=1, source_target_pairs={{0,1},{1,0},{2,3},{3,2},{4,5},{5,4},{6,7},{7,6},{8,9},{9,8},{10,11... | collective-permute-start | bytes 175112 | tf_op jit(solution)/shard_map/ppermute | solution.py:30
  11.3 6.1 %collective-permute-start.3 = (bf16[16,7296]{1,0:T(8,128)(2,1)S(1)}, bf16[16,7296]{1,0:T(8,128)(2,1)S(1)}, u32[]{:S(2)}, u32[]{:S(2)}) collective-permute-start(bf16[16,7296]{1,0:T(8,128)(2,1)S(1)} %stack.2.refs_0_), channel_id=1, source_target_pairs={{0,8},{4,12},{8,0},{12,4},{16,20},{20,16},{24,28},{28,24},{1,9},{5... | collective-permute-start | bytes 700424 | tf_op jit(solution)/shard_map/ppermute | solution.py:26
  17.4 8.6 %collective-permute-start.4 = (bf16[32,7296]{1,0:T(8,128)(2,1)S(1)}, bf16[32,7296]{1,0:T(8,128)(2,1)S(1)}, u32[]{:S(2)}, u32[]{:S(2)}) collective-permute-start(bf16[32,7296]{1,0:T(8,128)(2,1)S(1)} %stack.3.refs_0_), channel_id=1, source_target_pairs={{0,4},{4,0},{8,12},{12,8},{16,24},{20,28},{24,16},{28,20},{1,5},{5... | collective-permute-start | bytes 1400840 | tf_op jit(solution)/shard_map/ppermute | solution.py:26
  22.2 3.8 %collective-permute-start.5 = (bf16[32,7296]{1,0:T(8,128)(2,1)S(1)}, bf16[32,7296]{1,0:T(8,128)(2,1)S(1)}, u32[]{:S(2)}, u32[]{:S(2)}) collective-permute-start(bf16[32,7296]{1,0:T(8,128)(2,1)S(1)} %stack.3.refs_0_), channel_id=1, source_target_pairs={{0,16},{16,0},{1,17},{17,1},{2,18},{18,2},{3,19},{19,3},{4,20},{20... | collective-permute-start | bytes 1400840 | tf_op jit(solution)/shard_map/ppermute | solution.py:34
  26.1 1.8 %collective-permute-start.6 = (bf16[32,7296]{1,0:T(8,128)(2,1)S(1)}, bf16[32,7296]{1,0:T(8,128)(2,1)S(1)}, u32[]{:S(2)}, u32[]{:S(2)}) collective-permute-start(bf16[32,7296]{1,0:T(8,128)(2,1)S(1)} %collective-permute-done.4.refs_1_), channel_id=1, source_target_pairs={{0,16},{16,0},{1,17},{17,1},{2,18},{18,2},{3,19},{19,3},{4,20},{20... | collective-permute-start | bytes 1400840 | tf_op jit(solution)/shard_map/ppermute | solution.py:34
  38.9 1.9 %collective-permute-start.7 = (bf16[64,3584]{1,0:T(8,128)(2,1)S(1)}, bf16[64,3584]{1,0:T(8,128)(2,1)S(1)}, u32[]{:S(2)}, u32[]{:S(2)}) collective-permute-start(bf16[64,3584]{1,0:T(8,128)(2,1)S(1)} %get-tuple-element.46), channel_id=1, source_target_pairs={{0,16},{16,0},{1,17},{17,1},{2,18},{18,2},{3,19},{19,3},{4,20},{20... | collective-permute-start | bytes 1376264 | tf_op jit(solution)/shard_map/ppermute | solution.py:34
  40.2 2.3 %collective-permute-start.10 = (bf16[64,3584]{1,0:T(8,128)(2,1)S(1)}, bf16[64,3584]{1,0:T(8,128)(2,1)S(1)}, u32[]{:S(2)}, u32[]{:S(2)}) collective-permute-start(bf16[64,3584]{1,0:T(8,128)(2,1)S(1)} %get-tuple-element.50), channel_id=1, source_target_pairs={{0,16},{16,0},{1,17},{17,1},{2,18},{18,2},{3,19},{19,3},{4,20},{20... | collective-permute-start | bytes 1376264 | tf_op jit(solution)/shard_map/ppermute | solution.py:34
  40.9 6.1 %collective-permute-start.8 = (bf16[32,3584]{1,0:T(8,128)(2,1)S(1)}, bf16[32,3584]{1,0:T(8,128)(2,1)S(1)}, u32[]{:S(2)}, u32[]{:S(2)}) collective-permute-start(bf16[32,3584]{1,0:T(8,128)(2,1)S(1)} %slice.49), channel_id=1, source_target_pairs={{0,4},{4,0},{8,12},{12,8},{16,24},{20,28},{24,16},{28,20},{1,5},{5... | collective-permute-start | bytes 688136 | tf_op jit(solution)/shard_map/ppermute | solution.py:26
  42.7 7.1 %collective-permute-start.11 = (bf16[32,3584]{1,0:T(8,128)(2,1)S(1)}, bf16[32,3584]{1,0:T(8,128)(2,1)S(1)}, u32[]{:S(2)}, u32[]{:S(2)}) collective-permute-start(bf16[32,3584]{1,0:T(8,128)(2,1)S(1)} %slice.53), channel_id=1, source_target_pairs={{0,4},{4,0},{8,12},{12,8},{16,24},{20,28},{24,16},{28,20},{1,5},{5... | collective-permute-start | bytes 688136 | tf_op jit(solution)/shard_map/ppermute | solution.py:26
  47.1 4.9 %collective-permute-start.9 = (bf16[16,3584]{1,0:T(8,128)(2,1)S(1)}, bf16[16,3584]{1,0:T(8,128)(2,1)S(1)}, u32[]{:S(2)}, u32[]{:S(2)}) collective-permute-start(bf16[16,3584]{1,0:T(8,128)(2,1)S(1)} %slice.51), channel_id=1, source_target_pairs={{0,8},{4,12},{8,0},{12,4},{16,20},{20,16},{24,28},{28,24},{1,9},{5... | collective-permute-start | bytes 344072 | tf_op jit(solution)/shard_map/ppermute | solution.py:26
  49.9 4.9 %collective-permute-start.12 = (bf16[16,3584]{1,0:T(8,128)(2,1)S(1)}, bf16[16,3584]{1,0:T(8,128)(2,1)S(1)}, u32[]{:S(2)}, u32[]{:S(2)}) collective-permute-start(bf16[16,3584]{1,0:T(8,128)(2,1)S(1)} %slice.55), channel_id=1, source_target_pairs={{0,8},{4,12},{8,0},{12,4},{16,20},{20,16},{24,28},{28,24},{1,9},{5... | collective-permute-start | bytes 344072 | tf_op jit(solution)/shard_map/ppermute | solution.py:26
  54.9 4.3 %collective-permute-start.13 = (bf16[4,7168]{1,0:T(4,128)(2,1)S(1)}, bf16[4,7168]{1,0:T(4,128)(2,1)S(1)}, u32[]{:S(2)}, u32[]{:S(2)}) collective-permute-start(bf16[4,7168]{1,0:T(4,128)(2,1)S(1)} %get-tuple-element.51), channel_id=1, source_target_pairs={{0,1},{1,0},{2,3},{3,2},{4,5},{5,4},{6,7},{7,6},{8,9},{9,8},{10,11... | collective-permute-start | bytes 172040 | tf_op jit(solution)/shard_map/ppermute | solution.py:30
  56.1 6.0 %collective-permute-start.15 = (bf16[4,7168]{1,0:T(4,128)(2,1)S(1)}, bf16[4,7168]{1,0:T(4,128)(2,1)S(1)}, u32[]{:S(2)}, u32[]{:S(2)}) collective-permute-start(bf16[4,7168]{1,0:T(4,128)(2,1)S(1)} %get-tuple-element.52), channel_id=1, source_target_pairs={{0,3},{1,2},{2,1},{3,0},{4,7},{5,6},{6,5},{7,4},{8,11},{9,10},{10,... | collective-permute-start | bytes 172040 | tf_op jit(solution)/shard_map/ppermute | solution.py:30
  58.4 5.5 %collective-permute-start.14 = (bf16[4,7168]{1,0:T(4,128)(2,1)S(1)}, bf16[4,7168]{1,0:T(4,128)(2,1)S(1)}, u32[]{:S(2)}, u32[]{:S(2)}) collective-permute-start(bf16[4,7168]{1,0:T(4,128)(2,1)S(1)} %get-tuple-element.53), channel_id=1, source_target_pairs={{0,2},{1,3},{2,0},{3,1},{4,6},{5,7},{6,4},{7,5},{8,10},{9,11},{10,... | collective-permute-start | bytes 172040 | tf_op jit(solution)/shard_map/ppermute | solution.py:30

commit v12 on v11

--- a/solution.py
+++ b/solution.py
@@ -8,7 +8,7 @@
 from jax.sharding import PartitionSpec as P
 
 AXES = ("sect", "grp", "dev")
-VMEM_LIMIT = 10 * 2**20
+VMEM_LIMIT = 12 * 2**20
 
 
 def rounds_of():
@@ -92,7 +92,7 @@
 
 
 def gather_rows(block, w_up, w_gate):
-    wanted = [(w_up, e) for e in range(w_up.shape[0])] + [(w_gate, 0)]
+    wanted = [(w, e) for w in (w_gate, w_up) for e in range(w.shape[0])]
     weights, token = [], block
 
     def meanwhile(arrived, token):
@@ -111,45 +111,44 @@
         line = stack(line, arrived)
     last = swap(line, rounds[-1])
     mine, token = meanwhile(line, token)
-    last, other, token = lax.optimization_barrier((last, swap_core(mine), token))
+    other = swap_core(mine)
     while wanted:
-        _, token = meanwhile(line, token)
+        weight, token = fetch(*wanted.pop(0), token)
+        weights.append(weight)
+    last, other, token = lax.optimization_barrier((last, other, token))
     return [line, last, other, swap_core(last)], weights, token
 
 
 def down_copy(expert, block, down_hbm, target_ref, sems):
     hidden = down_hbm.shape[1]
-    span = pl.ds(pl.multiple_of(block * hidden, hidden), hidden)
+    span = pl.ds(block * hidden, hidden)
     return pltpu.make_async_copy(
-        down_hbm.at[expert, :, span], target_ref.at[expert, span], sems.at[expert, block]
+        down_hbm.at[expert, :, span], target_ref.at[0, span], sems.at[expert, block]
     )
 
 
-def down_block(step, hidden_ref, weights_ref, keep_ref, send_ref, first):
-    experts, _, hidden = weights_ref.shape
+def down_block(block, at, hidden_ref, down_refs, keep_ref, send_ref):
+    hidden = down_refs[0].shape[2]
     middle = keep_ref.shape[0]
-    rows = pl.ds(pl.multiple_of((first + step) * hidden, hidden), hidden)
-    weight = weights_ref[:, rows, :].reshape(experts * hidden, hidden)
+    rows = pl.ds(block * hidden, hidden)
+    weight = jnp.concatenate([ref[0, rows, :] for ref in down_refs], axis=0)
     total = jnp.dot(hidden_ref[...], weight, preferred_element_type=jnp.float32)
     total = total.astype(jnp.bfloat16)
-    span = pl.ds(pl.multiple_of(step * hidden, hidden), hidden)
+    span = pl.ds(at * hidden, hidden)
     keep_ref[:, span] = total[:middle]
     send_ref[:, span] = total[middle:]
 
 
-def expert_kernel(counts, width, token_ref, *refs):
-    pieces, up_refs = refs[:counts[0]], refs[counts[0]:sum(counts) - 1]
-    first_gate_ref = refs[sum(counts) - 1]
-    (gate_hbm, down_hbm, hidden_ref, keep_ref, send_ref, weights_ref,
-     rows_ref, up_ref, gate_sems, sems) = refs[sum(counts):]
-    experts, _, hidden = weights_ref.shape
+def expert_kernel(entry_count, experts, width, token_ref, *refs):
+    pieces, refs = refs[:entry_count], refs[entry_count:]
+    gate_refs, up_refs, refs = refs[:experts], refs[experts:2 * experts], refs[2 * experts:]
+    down_hbm, hidden_ref, keep_ref, send_ref = refs[:4]
+    down_refs, (rows_ref, value_ref, sems) = refs[4:4 + experts], refs[4 + experts:]
+    hidden = gate_refs[0].shape[2]
     place = lax.axis_index("sect") * lax.axis_size("grp") + lax.axis_index("grp")
     first = place * experts
     block = min(256, hidden)
     blocks = width // hidden
-    for e in range(1, experts):
-        for copy in weight_copies(gate_hbm, weights_ref, gate_sems, e):
-            copy.start()
 
     at = 0
     for piece in pieces:
@@ -157,57 +156,46 @@
         at += piece.shape[0]
 
     for e in range(experts):
-
-        @pl.loop(0, hidden // block, unroll=True)
-        def _(step):
-            span = pl.ds(pl.multiple_of(step * block, block), block)
-            up_ref[e, :, span] = jnp.dot(
-                rows_ref[:, :width], up_refs[e][0, :, span], preferred_element_type=jnp.float32
+        for step in range(hidden // block):
+            span = pl.ds(step * block, block)
+            gate = jnp.dot(
+                rows_ref[:, :width], gate_refs[e][0, :, span], preferred_element_type=jnp.float32
             )
-
-        if e == 0:
-            for step in range(blocks):
-                down_copy(0, step, down_hbm, weights_ref, sems).start()
+            value_ref[e, :, span] = gate / (1.0 + jnp.exp(-gate))
+        for step in range(blocks // 2):
+            down_copy(e, step, down_hbm, down_refs[e], sems).start()
+
+    for step in range(blocks // 2, blocks):
+        for e in range(experts):
+            down_copy(e, step, down_hbm, down_refs[e], sems).start()
 
     extra = rows_ref[:, width:].astype(jnp.float32)
     lane = lax.broadcasted_iota(jnp.int32, extra.shape, 1)
     for e in range(experts):
         mine = lax.rem(lane, extra.shape[1] // 2) == first + e
         scale = jnp.sum(jnp.where(mine, extra, 0.0), axis=1, keepdims=True)
-        if e > 0:
-            for copy in weight_copies(gate_hbm, weights_ref, gate_sems, e):
-                copy.wait()
-        gate_ref = first_gate_ref.at[0] if e == 0 else weights_ref.at[e]
-
-        @pl.loop(0, hidden // block, unroll=True)
-        def _(step):
-            span = pl.ds(pl.multiple_of(step * block, block), block)
-            gate = jnp.dot(
-                rows_ref[:, :width], gate_ref[:, span], preferred_element_type=jnp.float32
+        for step in range(hidden // block):
+            span = pl.ds(step * block, block)
+            up = jnp.dot(
+                rows_ref[:, :width], up_refs[e][0, :, span], preferred_element_type=jnp.float32
             )
-            value = gate / (1.0 + jnp.exp(-gate)) * up_ref[e, :, span] * scale
-            out = pl.ds(pl.multiple_of(e * hidden + step * block, block), block)
-            hidden_ref[:, out] = value.astype(jnp.bfloat16)
-
-        if e > 0:
-            for step in range(blocks):
-                down_copy(e, step, down_hbm, weights_ref, sems).start()
-
-    @pl.loop(0, blocks // 2)
-    def _(step):
+            value = value_ref[e, :, span] * up * scale
+            hidden_ref[:, pl.ds(e * hidden + step * block, block)] = value.astype(jnp.bfloat16)
+
+    for step in range(blocks // 2):
         for e in range(experts):
-            down_copy(e, step, down_hbm, weights_ref, sems).wait()
-        down_block(step, hidden_ref, weights_ref, keep_ref, send_ref, 0)
+            down_copy(e, step, down_hbm, down_refs[e], sems).wait()
+        down_block(step, step, hidden_ref, down_refs, keep_ref, send_ref)
 
     for step in range(blocks // 2, blocks):
         for e in range(experts):
-            down_copy(e, step, down_hbm, weights_ref, sems).wait()
-
-
-def down_kernel(first, hidden_ref, weights_ref, keep_ref, send_ref):
-    @pl.loop(0, keep_ref.shape[1] // weights_ref.shape[2], unroll=True)
-    def _(step):
-        down_block(step, hidden_ref, weights_ref, keep_ref, send_ref, first)
+            down_copy(e, step, down_hbm, down_refs[e], sems).wait()
+
+
+def down_kernel(first, hidden_ref, *refs):
+    *down_refs, keep_ref, send_ref = refs
+    for step in range(keep_ref.shape[1] // down_refs[0].shape[2]):
+        down_block(first + step, step, hidden_ref, down_refs, keep_ref, send_ref)
 
 
 def fetch_kernel(expert, after_ref, source_ref, target_ref, token_ref, sems):
@@ -252,59 +240,61 @@
     )(after, pltpu.with_memory_space_constraint(weight, pltpu.HBM))
 
 
-def expert_call(entries, w_gate, held, w_down, token):
-    experts, width, hidden = w_gate.shape
+def in_vmem(values):
+    return [pltpu.with_memory_space_constraint(v, pltpu.VMEM) for v in values]
+
+
+def expert_call(entries, held, w_down, token):
+    experts, hidden, width = w_down.shape
     full = entries[0].shape[1]
     rows = sum(e.shape[0] for e in entries)
-    counts = (len(entries), len(held))
     blocks = width // hidden
     whole = pl.BlockSpec(memory_space=pltpu.VMEM)
     anywhere = pl.BlockSpec(memory_space=pl.ANY)
     columns = (blocks // 2 * hidden, (blocks - blocks // 2) * hidden)
     outs = [jax.ShapeDtypeStruct((rows // 2, c), jnp.bfloat16) for c in columns]
-    hiddens, keep, send, weights = pl.pallas_call(
-        functools.partial(expert_kernel, counts, width),
+    hiddens, keep, send, *down = pl.pallas_call(
+        functools.partial(expert_kernel, len(entries), experts, width),
         out_shape=(
             jax.ShapeDtypeStruct((rows, experts * hidden), jnp.bfloat16),
             outs[0],
             outs[0],
-            pltpu.VMEM(w_gate.shape, w_gate.dtype),
-        ),
-        in_specs=[anywhere] + [whole] * sum(counts) + [anywhere] * 2,
-        out_specs=(whole,) * 4,
+            *(pltpu.VMEM(w.shape, w.dtype) for w in held[:experts]),
+        ),
+        in_specs=[anywhere] + [whole] * (len(entries) + len(held)) + [anywhere],
+        out_specs=(whole,) * (3 + experts),
+        input_output_aliases={1 + len(entries) + e: 3 + e for e in range(experts)},
         scratch_shapes=[
             pltpu.VMEM((rows, full), jnp.bfloat16),
             pltpu.VMEM((experts, rows, hidden), jnp.float32),
-            pltpu.SemaphoreType.DMA((experts, 4)),
             pltpu.SemaphoreType.DMA((experts, blocks)),
         ],
         compiler_params=pltpu.CompilerParams(vmem_limit_bytes=VMEM_LIMIT),
         cost_estimate=pl.CostEstimate(
-            flops=5 * rows * experts * width * hidden,
-            bytes_accessed=2 * (w_gate.size + w_down.size),
+            flops=5 * rows * w_down.size,
+            bytes_accessed=2 * w_down.size,
             transcendentals=rows * experts * hidden,
         ),
         name="experts",
     )(
         token,
         *entries,
-        *(pltpu.with_memory_space_constraint(w, pltpu.VMEM) for w in held),
-        pltpu.with_memory_space_constraint(w_gate, pltpu.HBM),
+        *in_vmem(held),
         pltpu.with_memory_space_constraint(w_down, pltpu.HBM),
     )
     later = pl.pallas_call(
         functools.partial(down_kernel, blocks // 2),
         out_shape=(outs[1], outs[1]),
-        in_specs=[whole, whole],
+        in_specs=[whole] * (1 + experts),
         out_specs=(whole, whole),
         compiler_params=pltpu.CompilerParams(vmem_limit_bytes=VMEM_LIMIT),
         cost_estimate=pl.CostEstimate(
-            flops=rows * experts * width * hidden,
+            flops=rows * w_down.size,
             bytes_accessed=2 * rows * columns[1],
             transcendentals=0,
         ),
         name="down",
-    )(hiddens, pltpu.with_memory_space_constraint(weights, pltpu.VMEM))
+    )(hiddens, *in_vmem(down))
     return (keep, send), later
 
 
@@ -327,7 +317,7 @@
 
     results = []
     halves = []
-    for keep, send in expert_call(entries, w_gate, held, w_down, token):
+    for keep, send in expert_call(entries, held, w_down, token):
         value = add(keep, swap_core(send))
         for masks in rounds_of()[::-1]:
             middle = value.shape[0] // 2

time: 64.8 us -> 62.2 us (0.960)
  waiting for transfers between devices: 21 us -> 17.8 us
    ppermute x6, waiting for transfers between devices: 12.4 us -> 9.17 us  [swap(): return lax.ppermute(value, ('sect', 'grp'), pairs)]
    pallas_call x3 -> x4, Pallas kernels: 9.5 us -> 12.7 us  [fetch(): pl.pallas_call(functools.partial(fetch_kernel, expert), out_shape=(pltpu....]
    pallas_call x1, Pallas kernels: 11 us -> 8.46 us  [expert_call(): pl.pallas_call(functools.partial(expert_kernel, len(entries), experts, wi...]
  transfers between devices with their start and end apart: 16 -> 16, of which waited for: 12 -> 12; matrix products, arithmetic and copies ran while one was open for 1% -> 1% of each run, Pallas kernels for 16% -> 22%
where the time goes in v12:
time: 62.2 us; the launch traced here: 62 us
  Pallas kernels  23.3 us (37%)
  starting transfers between devices  19.5 us (31%)
  waiting for transfers between devices  17.8 us (29%)
  other arithmetic  1.14 us (2%)
    pallas_call x4, Pallas kernels, fetch(): pl.pallas_call(functools.partial(fetch_kernel, expert), out_shape=(pltpu....  12.7 us
    ppermute x6, starting transfers between devices, swap(): return lax.ppermute(value, ('sect', 'grp'), pairs)  9.5 us
    ppermute x6, starting transfers between devices, swap_line(): lax.ppermute(value, 'dev', [(i, i ^ mask) for i in range(lax.axis_size('d...  9.31 us
    ppermute x6, waiting for transfers between devices, swap(): return lax.ppermute(value, ('sect', 'grp'), pairs)  9.17 us
    pallas_call x1, Pallas kernels, expert_call(): pl.pallas_call(functools.partial(expert_kernel, len(entries), experts, wi...  8.46 us
    ppermute x6, waiting for transfers between devices, swap_line(): lax.ppermute(value, 'dev', [(i, i ^ mask) for i in range(lax.axis_size('d...  6.72 us
    ppermute x4, waiting for transfers between devices, swap_core(): return lax.ppermute(value, 'sect', [(0, 1), (1, 0)])  1.92 us
  transfers between devices with their start and end apart: 16, of which 12 were waited for; matrix products, arithmetic and copies ran while one was open for 1% of the time, Pallas kernels for 22%

profile of v12, /device:TPU:0, one launch (start us, length us, event | category | flops | bytes accessed | tf_op | source)
XLA Modules:
  0.0 62.0 jit_solution(5186714931600383898)
XLA Ops:
  0.0 1.0 %extend.1.after_ref.refs_0_ = bf16[4,7296]{1,0:T(4,128)(2,1)S(1)} custom-call(bf16[4,7168]{1,0:T(4,128)(2,1)} %tokens_hbm.1, s32[4,8]{1,0:T(4,128)} %ids_hbm.1, f32[4,8]{1,0:T(4,128)} %weights_hbm.1), custom_call_target="tpu_custom_call" | custom-call | tf_op jit(solution)/shard_map/extend/pallas_call | solution.py:70
  1.0 5.1 %collective-permute-start.2 = (bf16[4,7296]{1,0:T(4,128)(2,1)S(1)}, bf16[4,7296]{1,0:T(4,128)(2,1)S(1)}, u32[]{:S(2)}, u32[]{:S(2)}) collective-permute-start(bf16[4,7296]{1,0:T(4,128)(2,1)S(1)} %extend.1.after_ref.refs_0_), channel_id=1, source_target_pairs={{0,3},{1,2},{2,1},{3,0},{4,7},{5,6},{6,5},{7,4},{8,11},{9,10},{10,... | collective-permute-start | bytes 175112 | tf_op jit(solution)/shard_map/ppermute | solution.py:30
  6.1 0.0 collective-permute-start.1
  6.1 0.6 %collective-permute-start = (bf16[4,7296]{1,0:T(4,128)(2,1)S(1)}, bf16[4,7296]{1,0:T(4,128)(2,1)S(1)}, u32[]{:S(2)}, u32[]{:S(2)}) collective-permute-start(bf16[4,7296]{1,0:T(4,128)(2,1)S(1)} %extend.1.after_ref.refs_0_), channel_id=1, source_target_pairs={{0,1},{1,0},{2,3},{3,2},{4,5},{5,4},{6,7},{7,6},{8,9},{9,8},{10,11... | collective-permute-start | bytes 175112 | tf_op jit(solution)/shard_map/ppermute | solution.py:30
  6.7 3.2 %fetch.4 = (bf16[1,7168,512]{2,1,0:T(8,128)(2,1)S(1)}, f32[8,128]{1,0:T(8,128)S(1)}) custom-call(bf16[4,7296]{1,0:T(4,128)(2,1)S(1)} %extend.1.after_ref.refs_0_, bf16[2,7168,512]{2,1,0:T(8,128)(2,1)} %source_ref.5), custom_call_target="tpu_custom_call" | custom-call | bytes 7340032 | tf_op jit(solution)/shard_map/fetch/pallas_call | solution.py:226
  9.9 0.0 collective-permute-done.2.refs_3_
  9.9 1.3 %collective-permute-done.1.refs_2_ = bf16[4,7296]{1,0:T(4,128)(2,1)S(1)} collective-permute-done((bf16[4,7296]{1,0:T(4,128)(2,1)S(1)}, bf16[4,7296]{1,0:T(4,128)(2,1)S(1)}, u32[]{:S(2)}, u32[]{:S(2)}) %collective-permute-start.1) | collective-permute-done | bytes 58400 | tf_op jit(solution)/shard_map/ppermute | solution.py:30
  11.2 0.0 collective-permute-done.refs_1_
  11.2 0.1 stack.2.refs_0_
  11.3 1.7 %collective-permute-start.3 = (bf16[16,7296]{1,0:T(8,128)(2,1)S(1)}, bf16[16,7296]{1,0:T(8,128)(2,1)S(1)}, u32[]{:S(2)}, u32[]{:S(2)}) collective-permute-start(bf16[16,7296]{1,0:T(8,128)(2,1)S(1)} %stack.2.refs_0_), channel_id=1, source_target_pairs={{0,8},{4,12},{8,0},{12,4},{16,20},{20,16},{24,28},{28,24},{1,9},{5... | collective-permute-start | bytes 700424 | tf_op jit(solution)/shard_map/ppermute | solution.py:26
  12.9 3.2 %fetch.5 = (bf16[1,7168,512]{2,1,0:T(8,128)(2,1)S(1)}, f32[8,128]{1,0:T(8,128)S(1)}) custom-call(f32[8,128]{1,0:T(8,128)S(1)} %get-tuple-element.35.after_ref, bf16[2,7168,512]{2,1,0:T(8,128)(2,1)} %source_ref.5), custom_call_target="tpu_custom_call" | custom-call | bytes 7340032 | tf_op jit(solution)/shard_map/fetch/pallas_call | solution.py:226
  16.1 1.3 %collective-permute-done.3.refs_1_ = bf16[16,7296]{1,0:T(8,128)(2,1)S(1)} collective-permute-done((bf16[16,7296]{1,0:T(8,128)(2,1)S(1)}, bf16[16,7296]{1,0:T(8,128)(2,1)S(1)}, u32[]{:S(2)}, u32[]{:S(2)}) %collective-permute-start.3) | collective-permute-done | bytes 233504 | tf_op jit(solution)/shard_map/ppermute | solution.py:26
  17.4 1.6 %collective-permute-start.4 = (bf16[32,7296]{1,0:T(8,128)(2,1)S(1)}, bf16[32,7296]{1,0:T(8,128)(2,1)S(1)}, u32[]{:S(2)}, u32[]{:S(2)}) collective-permute-start(bf16[32,7296]{1,0:T(8,128)(2,1)S(1)} %stack.3.refs_0_), channel_id=1, source_target_pairs={{0,4},{4,0},{8,12},{12,8},{16,24},{20,28},{24,16},{28,20},{1,5},{5... | collective-permute-start | bytes 1400840 | tf_op jit(solution)/shard_map/ppermute | solution.py:26
  19.1 3.2 %fetch.6 = (bf16[1,7168,512]{2,1,0:T(8,128)(2,1)S(1)}, f32[8,128]{1,0:T(8,128)S(1)}) custom-call(f32[8,128]{1,0:T(8,128)S(1)} %get-tuple-element.38.after_ref, bf16[2,7168,512]{2,1,0:T(8,128)(2,1)} %source_ref.7), custom_call_target="tpu_custom_call" | custom-call | bytes 7340032 | tf_op jit(solution)/shard_map/fetch/pallas_call | solution.py:226
  22.2 0.1 collective-permute-start.5
  22.3 3.2 %fetch.7 = (bf16[1,7168,512]{2,1,0:T(8,128)(2,1)S(1)}, f32[8,128]{1,0:T(8,128)S(1)}) custom-call(f32[8,128]{1,0:T(8,128)S(1)} %get-tuple-element.41.after_ref, bf16[2,7168,512]{2,1,0:T(8,128)(2,1)} %source_ref.7), custom_call_target="tpu_custom_call" | custom-call | bytes 7340032 | tf_op jit(solution)/shard_map/fetch/pallas_call | solution.py:226
  25.5 0.6 collective-permute-done.4.refs_1_
  26.1 0.0 collective-permute-done.5.refs_2_
  26.1 0.0 collective-permute-start.6
  26.1 1.8 %collective-permute-done.6.refs_3_ = bf16[32,7296]{1,0:T(8,128)(2,1)S(1)} collective-permute-done((bf16[32,7296]{1,0:T(8,128)(2,1)S(1)}, bf16[32,7296]{1,0:T(8,128)(2,1)S(1)}, u32[]{:S(2)}, u32[]{:S(2)}) %collective-permute-start.6) | collective-permute-done | bytes 466976 | tf_op jit(solution)/shard_map/ppermute | solution.py:34
  27.9 8.5 %experts.1 = (bf16[128,1024]{1,0:T(8,128)(2,1)S(1)}, bf16[64,3584]{1,0:T(8,128)(2,1)S(1)}, bf16[64,3584]{1,0:T(8,128)(2,1)S(1)}, bf16[1,7168,512]{2,1,0:T(8,128)(2,1)S(1)}, bf16[1,7168,512]{2,1,0:T(8,128)(2,1)S(1)}) custom-call(f32[8,128]{1,0:T(8,128)S(1)} %get-tuple-element.43.token_ref, ...), custom_call_target="tpu_custom_call", output_to_operand_aliasing={{3}: (5, {}), {4}: (6, {})} | custom-call | flops 4697620480 | bytes 14680064 | tf_op jit(solution)/shard_map/experts/pallas_call | solution.py:256
  36.4 0.2 collective-permute-start.7
  36.6 1.1 %down.1 = (bf16[64,3584]{1,0:T(8,128)(2,1)S(1)}, bf16[64,3584]{1,0:T(8,128)(2,1)S(1)}) custom-call(bf16[128,1024]{1,0:T(8,128)(2,1)S(1)} %get-tuple-element.52.hidden_ref, bf16[1,7168,512]{2,1,0:T(8,128)(2,1)S(1)} %get-tuple-element.53.refs_0_, bf16[1,7168,512]{2,1,0:T(8,128)(2,1)S(1)} %get-tuple-element.54.refs_1_), custom_call_target="tpu_custom_call" | custom-call | flops 939524096 | bytes 917504 | tf_op jit(solution)/shard_map/down/pallas_call | solution.py:285
  37.7 0.4 collective-permute-start.10
  38.1 0.1 collective-permute-done.7
  38.2 0.1 add_convert_fusion.1
  38.4 1.6 %collective-permute-start.8 = (bf16[32,3584]{1,0:T(8,128)(2,1)S(1)}, bf16[32,3584]{1,0:T(8,128)(2,1)S(1)}, u32[]{:S(2)}, u32[]{:S(2)}) collective-permute-start(bf16[32,3584]{1,0:T(8,128)(2,1)S(1)} %slice.49), channel_id=1, source_target_pairs={{0,4},{4,0},{8,12},{12,8},{16,24},{20,28},{24,16},{28,20},{1,5},{5... | collective-permute-start | bytes 688136 | tf_op jit(solution)/shard_map/ppermute | solution.py:26
  40.0 0.0 collective-permute-done.10
  40.0 0.1 add_convert_fusion
  40.2 1.2 %collective-permute-start.11 = (bf16[32,3584]{1,0:T(8,128)(2,1)S(1)}, bf16[32,3584]{1,0:T(8,128)(2,1)S(1)}, u32[]{:S(2)}, u32[]{:S(2)}) collective-permute-start(bf16[32,3584]{1,0:T(8,128)(2,1)S(1)} %slice.53), channel_id=1, source_target_pairs={{0,4},{4,0},{8,12},{12,8},{16,24},{20,28},{24,16},{28,20},{1,5},{5... | collective-permute-start | bytes 688136 | tf_op jit(solution)/shard_map/ppermute | solution.py:26
  41.4 3.1 %collective-permute-done.8 = bf16[32,3584]{1,0:T(8,128)(2,1)S(1)} collective-permute-done((bf16[32,3584]{1,0:T(8,128)(2,1)S(1)}, bf16[32,3584]{1,0:T(8,128)(2,1)S(1)}, u32[]{:S(2)}, u32[]{:S(2)}) %collective-permute-start.8) | collective-permute-done | bytes 229408 | tf_op jit(solution)/shard_map/ppermute | solution.py:26
  44.5 0.1 add_convert_fusion.3
  44.5 1.7 %collective-permute-start.9 = (bf16[16,3584]{1,0:T(8,128)(2,1)S(1)}, bf16[16,3584]{1,0:T(8,128)(2,1)S(1)}, u32[]{:S(2)}, u32[]{:S(2)}) collective-permute-start(bf16[16,3584]{1,0:T(8,128)(2,1)S(1)} %slice.51), channel_id=1, source_target_pairs={{0,8},{4,12},{8,0},{12,4},{16,20},{20,16},{24,28},{28,24},{1,9},{5... | collective-permute-start | bytes 344072 | tf_op jit(solution)/shard_map/ppermute | solution.py:26
  46.2 1.1 %collective-permute-done.11 = bf16[32,3584]{1,0:T(8,128)(2,1)S(1)} collective-permute-done((bf16[32,3584]{1,0:T(8,128)(2,1)S(1)}, bf16[32,3584]{1,0:T(8,128)(2,1)S(1)}, u32[]{:S(2)}, u32[]{:S(2)}) %collective-permute-start.11) | collective-permute-done | bytes 229408 | tf_op jit(solution)/shard_map/ppermute | solution.py:26
  47.3 0.1 add_convert_fusion.2
  47.4 1.7 %collective-permute-start.12 = (bf16[16,3584]{1,0:T(8,128)(2,1)S(1)}, bf16[16,3584]{1,0:T(8,128)(2,1)S(1)}, u32[]{:S(2)}, u32[]{:S(2)}) collective-permute-start(bf16[16,3584]{1,0:T(8,128)(2,1)S(1)} %slice.55), channel_id=1, source_target_pairs={{0,8},{4,12},{8,0},{12,4},{16,20},{20,16},{24,28},{28,24},{1,9},{5... | collective-permute-start | bytes 344072 | tf_op jit(solution)/shard_map/ppermute | solution.py:26
  49.0 0.4 collective-permute-done.9
  49.4 2.8 %collective-permute-done.12 = bf16[16,3584]{1,0:T(8,128)(2,1)S(1)} collective-permute-done((bf16[16,3584]{1,0:T(8,128)(2,1)S(1)}, bf16[16,3584]{1,0:T(8,128)(2,1)S(1)}, u32[]{:S(2)}, u32[]{:S(2)}) %collective-permute-start.12) | collective-permute-done | bytes 114720 | tf_op jit(solution)/shard_map/ppermute | solution.py:26
  52.3 0.1 fusion.2
  52.3 1.2 %collective-permute-start.13 = (bf16[4,7168]{1,0:T(4,128)(2,1)S(1)}, bf16[4,7168]{1,0:T(4,128)(2,1)S(1)}, u32[]{:S(2)}, u32[]{:S(2)}) collective-permute-start(bf16[4,7168]{1,0:T(4,128)(2,1)S(1)} %get-tuple-element.57), channel_id=1, source_target_pairs={{0,1},{1,0},{2,3},{3,2},{4,5},{5,4},{6,7},{7,6},{8,9},{9,8},{10,11... | collective-permute-start | bytes 172040 | tf_op jit(solution)/shard_map/ppermute | solution.py:30
  53.5 2.3 %collective-permute-start.15 = (bf16[4,7168]{1,0:T(4,128)(2,1)S(1)}, bf16[4,7168]{1,0:T(4,128)(2,1)S(1)}, u32[]{:S(2)}, u32[]{:S(2)}) collective-permute-start(bf16[4,7168]{1,0:T(4,128)(2,1)S(1)} %get-tuple-element.58), channel_id=1, source_target_pairs={{0,3},{1,2},{2,1},{3,0},{4,7},{5,6},{6,5},{7,4},{8,11},{9,10},{10,... | collective-permute-start | bytes 172040 | tf_op jit(solution)/shard_map/ppermute | solution.py:30
  55.9 0.0 collective-permute-start.14
  55.9 0.7 %collective-permute-done.13 = bf16[4,7168]{1,0:T(4,128)(2,1)S(1)} collective-permute-done((bf16[4,7168]{1,0:T(4,128)(2,1)S(1)}, bf16[4,7168]{1,0:T(4,128)(2,1)S(1)}, u32[]{:S(2)}, u32[]{:S(2)}) %collective-permute-start.13) | collective-permute-done | bytes 57376 | tf_op jit(solution)/shard_map/ppermute | solution.py:30
  56.6 2.9 %collective-permute-done.15 = bf16[4,7168]{1,0:T(4,128)(2,1)S(1)} collective-permute-done((bf16[4,7168]{1,0:T(4,128)(2,1)S(1)}, bf16[4,7168]{1,0:T(4,128)(2,1)S(1)}, u32[]{:S(2)}, u32[]{:S(2)}) %collective-permute-start.15) | collective-permute-done | bytes 57376 | tf_op jit(solution)/shard_map/ppermute | solution.py:30
  59.5 1.8 %collective-permute-done.14 = bf16[4,7168]{1,0:T(4,128)(2,1)S(1)} collective-permute-done((bf16[4,7168]{1,0:T(4,128)(2,1)S(1)}, bf16[4,7168]{1,0:T(4,128)(2,1)S(1)}, u32[]{:S(2)}, u32[]{:S(2)}) %collective-permute-start.14) | collective-permute-done | bytes 57376 | tf_op jit(solution)/shard_map/ppermute | solution.py:30
  61.4 0.7 %add_convert_fusion.6 = bf16[4,7168]{1,0:T(4,128)(2,1)} fusion(bf16[4,7168]{1,0:T(4,128)(2,1)S(1)} %collective-permute-done.15, bf16[4,7168]{1,0:T(4,128)(2,1)S(1)} %collective-permute-done.14, bf16[4,7168]{1,0:T(4,128)(2,1)S(1)} %collective-permute-done.13, bf16[16,3584]{1,0:T(8,128)(2,1)S(1)} %add_convert_fusion.5, bf16[16,3584]{1,0:T(8,128)(2,1)S(1)} %add_convert_fusion.4), kind=kLoop, calls=%fused_computation.12 | loop fusion | flops 315392 | bytes 458752 | tf_op jit(solution)/shard_map/convert_element_type | solution.py:305
  (7 shorter events, 0.1 us)
Async XLA Ops:
  1.0 8.9 %collective-permute-start.2 = (bf16[4,7296]{1,0:T(4,128)(2,1)S(1)}, bf16[4,7296]{1,0:T(4,128)(2,1)S(1)}, u32[]{:S(2)}, u32[]{:S(2)}) collective-permute-start(bf16[4,7296]{1,0:T(4,128)(2,1)S(1)} %extend.1.after_ref.refs_0_), channel_id=1, source_target_pairs={{0,3},{1,2},{2,1},{3,0},{4,7},{5,6},{6,5},{7,4},{8,11},{9,10},{10,... | collective-permute-start | bytes 175112 | tf_op jit(solution)/shard_map/ppermute | solution.py:30
  6.1 5.1 %collective-permute-start.1 = (bf16[4,7296]{1,0:T(4,128)(2,1)S(1)}, bf16[4,7296]{1,0:T(4,128)(2,1)S(1)}, u32[]{:S(2)}, u32[]{:S(2)}) collective-permute-start(bf16[4,7296]{1,0:T(4,128)(2,1)S(1)} %extend.1.after_ref.refs_0_), channel_id=1, source_target_pairs={{0,2},{1,3},{2,0},{3,1},{4,6},{5,7},{6,4},{7,5},{8,10},{9,11},{10,... | collective-permute-start | bytes 175112 | tf_op jit(solution)/shard_map/ppermute | solution.py:30
  6.1 5.1 %collective-permute-start = (bf16[4,7296]{1,0:T(4,128)(2,1)S(1)}, bf16[4,7296]{1,0:T(4,128)(2,1)S(1)}, u32[]{:S(2)}, u32[]{:S(2)}) collective-permute-start(bf16[4,7296]{1,0:T(4,128)(2,1)S(1)} %extend.1.after_ref.refs_0_), channel_id=1, source_target_pairs={{0,1},{1,0},{2,3},{3,2},{4,5},{5,4},{6,7},{7,6},{8,9},{9,8},{10,11... | collective-permute-start | bytes 175112 | tf_op jit(solution)/shard_map/ppermute | solution.py:30
  11.3 6.1 %collective-permute-start.3 = (bf16[16,7296]{1,0:T(8,128)(2,1)S(1)}, bf16[16,7296]{1,0:T(8,128)(2,1)S(1)}, u32[]{:S(2)}, u32[]{:S(2)}) collective-permute-start(bf16[16,7296]{1,0:T(8,128)(2,1)S(1)} %stack.2.refs_0_), channel_id=1, source_target_pairs={{0,8},{4,12},{8,0},{12,4},{16,20},{20,16},{24,28},{28,24},{1,9},{5... | collective-permute-start | bytes 700424 | tf_op jit(solution)/shard_map/ppermute | solution.py:26
  17.4 8.6 %collective-permute-start.4 = (bf16[32,7296]{1,0:T(8,128)(2,1)S(1)}, bf16[32,7296]{1,0:T(8,128)(2,1)S(1)}, u32[]{:S(2)}, u32[]{:S(2)}) collective-permute-start(bf16[32,7296]{1,0:T(8,128)(2,1)S(1)} %stack.3.refs_0_), channel_id=1, source_target_pairs={{0,4},{4,0},{8,12},{12,8},{16,24},{20,28},{24,16},{28,20},{1,5},{5... | collective-permute-start | bytes 1400840 | tf_op jit(solution)/shard_map/ppermute | solution.py:26
  22.2 3.8 %collective-permute-start.5 = (bf16[32,7296]{1,0:T(8,128)(2,1)S(1)}, bf16[32,7296]{1,0:T(8,128)(2,1)S(1)}, u32[]{:S(2)}, u32[]{:S(2)}) collective-permute-start(bf16[32,7296]{1,0:T(8,128)(2,1)S(1)} %stack.3.refs_0_), channel_id=1, source_target_pairs={{0,16},{16,0},{1,17},{17,1},{2,18},{18,2},{3,19},{19,3},{4,20},{20... | collective-permute-start | bytes 1400840 | tf_op jit(solution)/shard_map/ppermute | solution.py:34
  26.1 1.8 %collective-permute-start.6 = (bf16[32,7296]{1,0:T(8,128)(2,1)S(1)}, bf16[32,7296]{1,0:T(8,128)(2,1)S(1)}, u32[]{:S(2)}, u32[]{:S(2)}) collective-permute-start(bf16[32,7296]{1,0:T(8,128)(2,1)S(1)} %collective-permute-done.4.refs_1_), channel_id=1, source_target_pairs={{0,16},{16,0},{1,17},{17,1},{2,18},{18,2},{3,19},{19,3},{4,20},{20... | collective-permute-start | bytes 1400840 | tf_op jit(solution)/shard_map/ppermute | solution.py:34
  36.4 1.9 %collective-permute-start.7 = (bf16[64,3584]{1,0:T(8,128)(2,1)S(1)}, bf16[64,3584]{1,0:T(8,128)(2,1)S(1)}, u32[]{:S(2)}, u32[]{:S(2)}) collective-permute-start(bf16[64,3584]{1,0:T(8,128)(2,1)S(1)} %get-tuple-element.51), channel_id=1, source_target_pairs={{0,16},{16,0},{1,17},{17,1},{2,18},{18,2},{3,19},{19,3},{4,20},{20... | collective-permute-start | bytes 1376264 | tf_op jit(solution)/shard_map/ppermute | solution.py:34
  37.7 2.3 %collective-permute-start.10 = (bf16[64,3584]{1,0:T(8,128)(2,1)S(1)}, bf16[64,3584]{1,0:T(8,128)(2,1)S(1)}, u32[]{:S(2)}, u32[]{:S(2)}) collective-permute-start(bf16[64,3584]{1,0:T(8,128)(2,1)S(1)} %get-tuple-element.56), channel_id=1, source_target_pairs={{0,16},{16,0},{1,17},{17,1},{2,18},{18,2},{3,19},{19,3},{4,20},{20... | collective-permute-start | bytes 1376264 | tf_op jit(solution)/shard_map/ppermute | solution.py:34
  38.4 6.1 %collective-permute-start.8 = (bf16[32,3584]{1,0:T(8,128)(2,1)S(1)}, bf16[32,3584]{1,0:T(8,128)(2,1)S(1)}, u32[]{:S(2)}, u32[]{:S(2)}) collective-permute-start(bf16[32,3584]{1,0:T(8,128)(2,1)S(1)} %slice.49), channel_id=1, source_target_pairs={{0,4},{4,0},{8,12},{12,8},{16,24},{20,28},{24,16},{28,20},{1,5},{5... | collective-permute-start | bytes 688136 | tf_op jit(solution)/shard_map/ppermute | solution.py:26
  40.2 7.1 %collective-permute-start.11 = (bf16[32,3584]{1,0:T(8,128)(2,1)S(1)}, bf16[32,3584]{1,0:T(8,128)(2,1)S(1)}, u32[]{:S(2)}, u32[]{:S(2)}) collective-permute-start(bf16[32,3584]{1,0:T(8,128)(2,1)S(1)} %slice.53), channel_id=1, source_target_pairs={{0,4},{4,0},{8,12},{12,8},{16,24},{20,28},{24,16},{28,20},{1,5},{5... | collective-permute-start | bytes 688136 | tf_op jit(solution)/shard_map/ppermute | solution.py:26
  44.5 4.9 %collective-permute-start.9 = (bf16[16,3584]{1,0:T(8,128)(2,1)S(1)}, bf16[16,3584]{1,0:T(8,128)(2,1)S(1)}, u32[]{:S(2)}, u32[]{:S(2)}) collective-permute-start(bf16[16,3584]{1,0:T(8,128)(2,1)S(1)} %slice.51), channel_id=1, source_target_pairs={{0,8},{4,12},{8,0},{12,4},{16,20},{20,16},{24,28},{28,24},{1,9},{5... | collective-permute-start | bytes 344072 | tf_op jit(solution)/shard_map/ppermute | solution.py:26
  47.4 4.9 %collective-permute-start.12 = (bf16[16,3584]{1,0:T(8,128)(2,1)S(1)}, bf16[16,3584]{1,0:T(8,128)(2,1)S(1)}, u32[]{:S(2)}, u32[]{:S(2)}) collective-permute-start(bf16[16,3584]{1,0:T(8,128)(2,1)S(1)} %slice.55), channel_id=1, source_target_pairs={{0,8},{4,12},{8,0},{12,4},{16,20},{20,16},{24,28},{28,24},{1,9},{5... | collective-permute-start | bytes 344072 | tf_op jit(solution)/shard_map/ppermute | solution.py:26
  52.3 4.3 %collective-permute-start.13 = (bf16[4,7168]{1,0:T(4,128)(2,1)S(1)}, bf16[4,7168]{1,0:T(4,128)(2,1)S(1)}, u32[]{:S(2)}, u32[]{:S(2)}) collective-permute-start(bf16[4,7168]{1,0:T(4,128)(2,1)S(1)} %get-tuple-element.57), channel_id=1, source_target_pairs={{0,1},{1,0},{2,3},{3,2},{4,5},{5,4},{6,7},{7,6},{8,9},{9,8},{10,11... | collective-permute-start | bytes 172040 | tf_op jit(solution)/shard_map/ppermute | solution.py:30
  53.5 6.0 %collective-permute-start.15 = (bf16[4,7168]{1,0:T(4,128)(2,1)S(1)}, bf16[4,7168]{1,0:T(4,128)(2,1)S(1)}, u32[]{:S(2)}, u32[]{:S(2)}) collective-permute-start(bf16[4,7168]{1,0:T(4,128)(2,1)S(1)} %get-tuple-element.58), channel_id=1, source_target_pairs={{0,3},{1,2},{2,1},{3,0},{4,7},{5,6},{6,5},{7,4},{8,11},{9,10},{10,... | collective-permute-start | bytes 172040 | tf_op jit(solution)/shard_map/ppermute | solution.py:30
  55.9 5.5 %collective-permute-start.14 = (bf16[4,7168]{1,0:T(4,128)(2,1)S(1)}, bf16[4,7168]{1,0:T(4,128)(2,1)S(1)}, u32[]{:S(2)}, u32[]{:S(2)}) collective-permute-start(bf16[4,7168]{1,0:T(4,128)(2,1)S(1)} %get-tuple-element.59), channel_id=1, source_target_pairs={{0,2},{1,3},{2,0},{3,1},{4,6},{5,7},{6,4},{7,5},{8,10},{9,11},{10,... | collective-permute-start | bytes 172040 | tf_op jit(solution)/shard_map/ppermute | solution.py:30

commit v13 on v12

--- a/solution.py
+++ b/solution.py
@@ -8,7 +8,7 @@
 from jax.sharding import PartitionSpec as P
 
 AXES = ("sect", "grp", "dev")
-VMEM_LIMIT = 12 * 2**20
+VMEM_LIMIT = 16 * 2**20
 
 
 def rounds_of():
@@ -26,8 +26,19 @@
     return lax.ppermute(value, ("sect", "grp"), pairs)
 
 
-def swap_line(value, mask):
-    return lax.ppermute(value, "dev", [(i, i ^ mask) for i in range(lax.axis_size("dev"))])
+def line_masks():
+    sects, _, lanes = (lax.axis_size(a) for a in AXES)
+    near = list(range(1, lanes))
+    orders = [near[-1:] + near[:-1], near]
+    return list(zip(*(orders[s % 2] for s in range(sects))))
+
+
+def swap_line(value, masks):
+    lanes = lax.axis_size("dev")
+    pairs = [
+        (s * lanes + i, s * lanes + (i ^ mask)) for s, mask in enumerate(masks) for i in range(lanes)
+    ]
+    return lax.ppermute(value, ("sect", "dev"), pairs)
 
 
 def swap_core(value):
@@ -102,7 +113,7 @@
             arrived, token = lax.optimization_barrier((arrived, token))
         return arrived, token
 
-    arrived = [swap_line(block, m) for m in range(1, lax.axis_size("dev"))]
+    arrived = [swap_line(block, masks) for masks in line_masks()]
     arrived, token = meanwhile(arrived, token)
     line = stack(block, *arrived)
     rounds = rounds_of()
@@ -119,19 +130,19 @@
     return [line, last, other, swap_core(last)], weights, token
 
 
-def down_copy(expert, block, down_hbm, target_ref, sems):
+def down_copy(expert, block, at, down_hbm, target_ref, sems):
     hidden = down_hbm.shape[1]
-    span = pl.ds(block * hidden, hidden)
     return pltpu.make_async_copy(
-        down_hbm.at[expert, :, span], target_ref.at[0, span], sems.at[expert, block]
+        down_hbm.at[expert, :, pl.ds(block * hidden, hidden)],
+        target_ref.at[pl.ds(at * hidden, hidden)],
+        sems.at[expert, block],
     )
 
 
-def down_block(block, at, hidden_ref, down_refs, keep_ref, send_ref):
-    hidden = down_refs[0].shape[2]
+def down_block(at, hidden_ref, down_refs, keep_ref, send_ref):
+    hidden = down_refs[0].shape[1]
     middle = keep_ref.shape[0]
-    rows = pl.ds(block * hidden, hidden)
-    weight = jnp.concatenate([ref[0, rows, :] for ref in down_refs], axis=0)
+    weight = jnp.concatenate([ref[pl.ds(at * hidden, hidden), :] for ref in down_refs], axis=0)
     total = jnp.dot(hidden_ref[...], weight, preferred_element_type=jnp.float32)
     total = total.astype(jnp.bfloat16)
     span = pl.ds(at * hidden, hidden)
@@ -143,12 +154,27 @@
     pieces, refs = refs[:entry_count], refs[entry_count:]
     gate_refs, up_refs, refs = refs[:experts], refs[experts:2 * experts], refs[2 * experts:]
     down_hbm, hidden_ref, keep_ref, send_ref = refs[:4]
-    down_refs, (rows_ref, value_ref, sems) = refs[4:4 + experts], refs[4 + experts:]
+    down_refs, (rows_ref, value_ref, early_ref, sems) = refs[4:4 + experts], refs[4 + experts:]
     hidden = gate_refs[0].shape[2]
     place = lax.axis_index("sect") * lax.axis_size("grp") + lax.axis_index("grp")
     first = place * experts
     block = min(256, hidden)
     blocks = width // hidden
+
+    early = [
+        down_copy(e, step, step, down_hbm, early_ref.at[e], sems)
+        for step in range(blocks // 2)
+        for e in range(experts)
+    ]
+    late = [
+        [
+            down_copy(e, step, step - blocks // 2, down_hbm, down_refs[e].at[0], sems)
+            for step in range(blocks // 2, blocks)
+        ]
+        for e in range(experts)
+    ]
+    for copy in early:
+        copy.start()
 
     at = 0
     for piece in pieces:
@@ -162,12 +188,8 @@
                 rows_ref[:, :width], gate_refs[e][0, :, span], preferred_element_type=jnp.float32
             )
             value_ref[e, :, span] = gate / (1.0 + jnp.exp(-gate))
-        for step in range(blocks // 2):
-            down_copy(e, step, down_hbm, down_refs[e], sems).start()
-
-    for step in range(blocks // 2, blocks):
-        for e in range(experts):
-            down_copy(e, step, down_hbm, down_refs[e], sems).start()
+        for copy in late[e]:
+            copy.start()
 
     extra = rows_ref[:, width:].astype(jnp.float32)
     lane = lax.broadcasted_iota(jnp.int32, extra.shape, 1)
@@ -183,19 +205,19 @@
             hidden_ref[:, pl.ds(e * hidden + step * block, block)] = value.astype(jnp.bfloat16)
 
     for step in range(blocks // 2):
-        for e in range(experts):
-            down_copy(e, step, down_hbm, down_refs[e], sems).wait()
-        down_block(step, step, hidden_ref, down_refs, keep_ref, send_ref)
-
-    for step in range(blocks // 2, blocks):
-        for e in range(experts):
-            down_copy(e, step, down_hbm, down_refs[e], sems).wait()
-
-
-def down_kernel(first, hidden_ref, *refs):
+        for copy in early[step * experts:(step + 1) * experts]:
+            copy.wait()
+        down_block(step, hidden_ref, [early_ref.at[e] for e in range(experts)], keep_ref, send_ref)
+
+    for copies in late:
+        for copy in copies:
+            copy.wait()
+
+
+def down_kernel(hidden_ref, *refs):
     *down_refs, keep_ref, send_ref = refs
     for step in range(keep_ref.shape[1] // down_refs[0].shape[2]):
-        down_block(first + step, step, hidden_ref, down_refs, keep_ref, send_ref)
+        down_block(step, hidden_ref, [ref.at[0] for ref in down_refs], keep_ref, send_ref)
 
 
 def fetch_kernel(expert, after_ref, source_ref, target_ref, token_ref, sems):
@@ -267,6 +289,7 @@
         scratch_shapes=[
             pltpu.VMEM((rows, full), jnp.bfloat16),
             pltpu.VMEM((experts, rows, hidden), jnp.float32),
+            pltpu.VMEM((experts, columns[0], hidden), w_down.dtype),
             pltpu.SemaphoreType.DMA((experts, blocks)),
         ],
         compiler_params=pltpu.CompilerParams(vmem_limit_bytes=VMEM_LIMIT),
@@ -283,7 +306,7 @@
         pltpu.with_memory_space_constraint(w_down, pltpu.HBM),
     )
     later = pl.pallas_call(
-        functools.partial(down_kernel, blocks // 2),
+        down_kernel,
         out_shape=(outs[1], outs[1]),
         in_specs=[whole] * (1 + experts),
         out_specs=(whole, whole),
@@ -325,7 +348,7 @@
         halves.append(value)
     value = jnp.concatenate(halves, axis=1)
     own = [value[m * row_count:(m + 1) * row_count] for m in range(lanes)]
-    return add(own[0], *(swap_line(own[m], m) for m in range(1, lanes)))
+    return add(own[0], *(swap_line(o, masks) for o, masks in zip(own[1:], line_masks())))
 
 
 def solution(mesh):

time: 62.2 us -> 63.5 us (1.021)
  Pallas kernels: 23.3 us -> 24.3 us
    ppermute x6, waiting for transfers between devices: 9.17 us -> 11 us  [swap(): return lax.ppermute(value, ('sect', 'grp'), pairs)]
    ppermute x6, waiting for transfers between devices: 6.72 us -> 5 us  [swap_line(): return lax.ppermute(value, ('sect', 'dev'), pairs)]
    pallas_call x1, Pallas kernels: 8.46 us -> 9.46 us  [expert_call(): pl.pallas_call(functools.partial(expert_kernel, len(entries), experts, wi...]
    ppermute x6, starting transfers between devices: 9.31 us -> 10.1 us  [swap_line(): return lax.ppermute(value, ('sect', 'dev'), pairs)]
where the time goes in v13:
time: 63.5 us; the launch traced here: 63.4 us
  Pallas kernels  24.3 us (38%)
  starting transfers between devices  19.8 us (31%)
  waiting for transfers between devices  17.9 us (28%)
  other arithmetic  1.14 us (2%)
    pallas_call x4, Pallas kernels, fetch(): pl.pallas_call(functools.partial(fetch_kernel, expert), out_shape=(pltpu....  12.7 us
    ppermute x6, waiting for transfers between devices, swap(): return lax.ppermute(value, ('sect', 'grp'), pairs)  11 us
    ppermute x6, starting transfers between devices, swap_line(): return lax.ppermute(value, ('sect', 'dev'), pairs)  10.1 us
    pallas_call x1, Pallas kernels, expert_call(): pl.pallas_call(functools.partial(expert_kernel, len(entries), experts, wi...  9.46 us
    ppermute x6, starting transfers between devices, swap(): return lax.ppermute(value, ('sect', 'grp'), pairs)  8.97 us
    ppermute x6, waiting for transfers between devices, swap_line(): return lax.ppermute(value, ('sect', 'dev'), pairs)  5 us
    ppermute x4, waiting for transfers between devices, swap_core(): return lax.ppermute(value, 'sect', [(0, 1), (1, 0)])  1.94 us
  transfers between devices with their start and end apart: 16, of which 12 were waited for; matrix products, arithmetic and copies ran while one was open for 1% of the time, Pallas kernels for 22%

profile of v13, /device:TPU:0, one launch (start us, length us, event | category | flops | bytes accessed | tf_op | source)
XLA Modules:
  0.0 63.4 jit_solution(18354127686432565329)
XLA Ops:
  0.0 1.0 %extend.1.after_ref.refs_0_ = bf16[4,7296]{1,0:T(4,128)(2,1)S(1)} custom-call(bf16[4,7168]{1,0:T(4,128)(2,1)} %tokens_hbm.1, s32[4,8]{1,0:T(4,128)} %ids_hbm.1, f32[4,8]{1,0:T(4,128)} %weights_hbm.1), custom_call_target="tpu_custom_call" | custom-call | tf_op jit(solution)/shard_map/extend/pallas_call | solution.py:81
  1.0 4.1 %collective-permute-start.2 = (bf16[4,7296]{1,0:T(4,128)(2,1)S(1)}, bf16[4,7296]{1,0:T(4,128)(2,1)S(1)}, u32[]{:S(2)}, u32[]{:S(2)}) collective-permute-start(bf16[4,7296]{1,0:T(4,128)(2,1)S(1)} %extend.1.after_ref.refs_0_), channel_id=1, source_target_pairs={{0,2},{1,3},{2,0},{3,1},{16,19},{17,18},{18,17},{19,16},{4,6},{5,7... | collective-permute-start | bytes 175112 | tf_op jit(solution)/shard_map/ppermute | solution.py:41
  5.1 1.6 %collective-permute-start.1 = (bf16[4,7296]{1,0:T(4,128)(2,1)S(1)}, bf16[4,7296]{1,0:T(4,128)(2,1)S(1)}, u32[]{:S(2)}, u32[]{:S(2)}) collective-permute-start(bf16[4,7296]{1,0:T(4,128)(2,1)S(1)} %extend.1.after_ref.refs_0_), channel_id=1, source_target_pairs={{0,1},{1,0},{2,3},{3,2},{16,18},{17,19},{18,16},{19,17},{4,5},{5,4... | collective-permute-start | bytes 175112 | tf_op jit(solution)/shard_map/ppermute | solution.py:41
  6.7 0.0 collective-permute-start
  6.7 3.2 %fetch.4 = (bf16[1,7168,512]{2,1,0:T(8,128)(2,1)S(1)}, f32[8,128]{1,0:T(8,128)S(1)}) custom-call(bf16[4,7296]{1,0:T(4,128)(2,1)S(1)} %extend.1.after_ref.refs_0_, bf16[2,7168,512]{2,1,0:T(8,128)(2,1)} %source_ref.5), custom_call_target="tpu_custom_call" | custom-call | bytes 7340032 | tf_op jit(solution)/shard_map/fetch/pallas_call | solution.py:248
  9.8 0.0 collective-permute-done.2.refs_3_
  9.9 0.3 collective-permute-done.1.refs_2_
  10.1 2.5 %collective-permute-done.refs_1_ = bf16[4,7296]{1,0:T(4,128)(2,1)S(1)} collective-permute-done((bf16[4,7296]{1,0:T(4,128)(2,1)S(1)}, bf16[4,7296]{1,0:T(4,128)(2,1)S(1)}, u32[]{:S(2)}, u32[]{:S(2)}) %collective-permute-start) | collective-permute-done | bytes 58400 | tf_op jit(solution)/shard_map/ppermute | solution.py:41
  12.7 0.1 stack.2.refs_0_
  12.7 1.6 %collective-permute-start.3 = (bf16[16,7296]{1,0:T(8,128)(2,1)S(1)}, bf16[16,7296]{1,0:T(8,128)(2,1)S(1)}, u32[]{:S(2)}, u32[]{:S(2)}) collective-permute-start(bf16[16,7296]{1,0:T(8,128)(2,1)S(1)} %stack.2.refs_0_), channel_id=1, source_target_pairs={{0,8},{4,12},{8,0},{12,4},{16,20},{20,16},{24,28},{28,24},{1,9},{5... | collective-permute-start | bytes 700424 | tf_op jit(solution)/shard_map/ppermute | solution.py:26
  14.3 3.2 %fetch.5 = (bf16[1,7168,512]{2,1,0:T(8,128)(2,1)S(1)}, f32[8,128]{1,0:T(8,128)S(1)}) custom-call(f32[8,128]{1,0:T(8,128)S(1)} %get-tuple-element.35.after_ref, bf16[2,7168,512]{2,1,0:T(8,128)(2,1)} %source_ref.5), custom_call_target="tpu_custom_call" | custom-call | bytes 7340032 | tf_op jit(solution)/shard_map/fetch/pallas_call | solution.py:248
  17.5 2.6 %collective-permute-done.3.refs_1_ = bf16[16,7296]{1,0:T(8,128)(2,1)S(1)} collective-permute-done((bf16[16,7296]{1,0:T(8,128)(2,1)S(1)}, bf16[16,7296]{1,0:T(8,128)(2,1)S(1)}, u32[]{:S(2)}, u32[]{:S(2)}) %collective-permute-start.3) | collective-permute-done | bytes 233504 | tf_op jit(solution)/shard_map/ppermute | solution.py:26
  20.1 1.5 %collective-permute-start.4 = (bf16[32,7296]{1,0:T(8,128)(2,1)S(1)}, bf16[32,7296]{1,0:T(8,128)(2,1)S(1)}, u32[]{:S(2)}, u32[]{:S(2)}) collective-permute-start(bf16[32,7296]{1,0:T(8,128)(2,1)S(1)} %stack.3.refs_0_), channel_id=1, source_target_pairs={{0,4},{4,0},{8,12},{12,8},{16,24},{20,28},{24,16},{28,20},{1,5},{5... | collective-permute-start | bytes 1400840 | tf_op jit(solution)/shard_map/ppermute | solution.py:26
  21.7 3.2 %fetch.6 = (bf16[1,7168,512]{2,1,0:T(8,128)(2,1)S(1)}, f32[8,128]{1,0:T(8,128)S(1)}) custom-call(f32[8,128]{1,0:T(8,128)S(1)} %get-tuple-element.38.after_ref, bf16[2,7168,512]{2,1,0:T(8,128)(2,1)} %source_ref.7), custom_call_target="tpu_custom_call" | custom-call | bytes 7340032 | tf_op jit(solution)/shard_map/fetch/pallas_call | solution.py:248
  24.8 0.1 collective-permute-start.5
  24.9 3.2 %fetch.7 = (bf16[1,7168,512]{2,1,0:T(8,128)(2,1)S(1)}, f32[8,128]{1,0:T(8,128)S(1)}) custom-call(f32[8,128]{1,0:T(8,128)S(1)} %get-tuple-element.41.after_ref, bf16[2,7168,512]{2,1,0:T(8,128)(2,1)} %source_ref.7), custom_call_target="tpu_custom_call" | custom-call | bytes 7340032 | tf_op jit(solution)/shard_map/fetch/pallas_call | solution.py:248
  28.1 0.7 %collective-permute-done.4.refs_1_ = bf16[32,7296]{1,0:T(8,128)(2,1)S(1)} collective-permute-done((bf16[32,7296]{1,0:T(8,128)(2,1)S(1)}, bf16[32,7296]{1,0:T(8,128)(2,1)S(1)}, u32[]{:S(2)}, u32[]{:S(2)}) %collective-permute-start.4) | collective-permute-done | bytes 466976 | tf_op jit(solution)/shard_map/ppermute | solution.py:26
  28.8 0.0 collective-permute-done.5.refs_2_
  28.8 0.0 collective-permute-start.6
  28.8 1.8 %collective-permute-done.6.refs_3_ = bf16[32,7296]{1,0:T(8,128)(2,1)S(1)} collective-permute-done((bf16[32,7296]{1,0:T(8,128)(2,1)S(1)}, bf16[32,7296]{1,0:T(8,128)(2,1)S(1)}, u32[]{:S(2)}, u32[]{:S(2)}) %collective-permute-start.6) | collective-permute-done | bytes 466976 | tf_op jit(solution)/shard_map/ppermute | solution.py:45
  30.6 9.5 %experts.1 = (bf16[128,1024]{1,0:T(8,128)(2,1)S(1)}, bf16[64,3584]{1,0:T(8,128)(2,1)S(1)}, bf16[64,3584]{1,0:T(8,128)(2,1)S(1)}, bf16[1,7168,512]{2,1,0:T(8,128)(2,1)S(1)}, bf16[1,7168,512]{2,1,0:T(8,128)(2,1)S(1)}) custom-call(f32[8,128]{1,0:T(8,128)S(1)} %get-tuple-element.43.token_ref, ...), custom_call_target="tpu_custom_call", output_to_operand_aliasing={{3}: (5, {}), {4}: (6, {})} | custom-call | flops 4697620480 | bytes 14680064 | tf_op jit(solution)/shard_map/experts/pallas_call | solution.py:278
  40.1 0.2 collective-permute-start.7
  40.3 1.1 %down.1 = (bf16[64,3584]{1,0:T(8,128)(2,1)S(1)}, bf16[64,3584]{1,0:T(8,128)(2,1)S(1)}) custom-call(bf16[128,1024]{1,0:T(8,128)(2,1)S(1)} %get-tuple-element.52.hidden_ref, bf16[1,7168,512]{2,1,0:T(8,128)(2,1)S(1)} %get-tuple-element.53.refs_0_, bf16[1,7168,512]{2,1,0:T(8,128)(2,1)S(1)} %get-tuple-element.54.refs_1_), custom_call_target="tpu_custom_call" | custom-call | flops 939524096 | bytes 917504 | tf_op jit(solution)/shard_map/down/pallas_call | solution.py:308
  41.4 0.4 collective-permute-start.10
  41.8 0.1 collective-permute-done.7
  41.9 0.1 add_convert_fusion.1
  42.1 1.5 %collective-permute-start.8 = (bf16[32,3584]{1,0:T(8,128)(2,1)S(1)}, bf16[32,3584]{1,0:T(8,128)(2,1)S(1)}, u32[]{:S(2)}, u32[]{:S(2)}) collective-permute-start(bf16[32,3584]{1,0:T(8,128)(2,1)S(1)} %slice.49), channel_id=1, source_target_pairs={{0,4},{4,0},{8,12},{12,8},{16,24},{20,28},{24,16},{28,20},{1,5},{5... | collective-permute-start | bytes 688136 | tf_op jit(solution)/shard_map/ppermute | solution.py:26
  43.6 0.0 collective-permute-done.10
  43.6 0.1 add_convert_fusion
  43.8 1.2 %collective-permute-start.11 = (bf16[32,3584]{1,0:T(8,128)(2,1)S(1)}, bf16[32,3584]{1,0:T(8,128)(2,1)S(1)}, u32[]{:S(2)}, u32[]{:S(2)}) collective-permute-start(bf16[32,3584]{1,0:T(8,128)(2,1)S(1)} %slice.53), channel_id=1, source_target_pairs={{0,4},{4,0},{8,12},{12,8},{16,24},{20,28},{24,16},{28,20},{1,5},{5... | collective-permute-start | bytes 688136 | tf_op jit(solution)/shard_map/ppermute | solution.py:26
  45.0 3.2 %collective-permute-done.8 = bf16[32,3584]{1,0:T(8,128)(2,1)S(1)} collective-permute-done((bf16[32,3584]{1,0:T(8,128)(2,1)S(1)}, bf16[32,3584]{1,0:T(8,128)(2,1)S(1)}, u32[]{:S(2)}, u32[]{:S(2)}) %collective-permute-start.8) | collective-permute-done | bytes 229408 | tf_op jit(solution)/shard_map/ppermute | solution.py:26
  48.2 0.1 add_convert_fusion.3
  48.2 1.6 %collective-permute-start.9 = (bf16[16,3584]{1,0:T(8,128)(2,1)S(1)}, bf16[16,3584]{1,0:T(8,128)(2,1)S(1)}, u32[]{:S(2)}, u32[]{:S(2)}) collective-permute-start(bf16[16,3584]{1,0:T(8,128)(2,1)S(1)} %slice.51), channel_id=1, source_target_pairs={{0,8},{4,12},{8,0},{12,4},{16,20},{20,16},{24,28},{28,24},{1,9},{5... | collective-permute-start | bytes 344072 | tf_op jit(solution)/shard_map/ppermute | solution.py:26
  49.8 1.2 %collective-permute-done.11 = bf16[32,3584]{1,0:T(8,128)(2,1)S(1)} collective-permute-done((bf16[32,3584]{1,0:T(8,128)(2,1)S(1)}, bf16[32,3584]{1,0:T(8,128)(2,1)S(1)}, u32[]{:S(2)}, u32[]{:S(2)}) %collective-permute-start.11) | collective-permute-done | bytes 229408 | tf_op jit(solution)/shard_map/ppermute | solution.py:26
  51.0 0.1 add_convert_fusion.2
  51.1 1.6 %collective-permute-start.12 = (bf16[16,3584]{1,0:T(8,128)(2,1)S(1)}, bf16[16,3584]{1,0:T(8,128)(2,1)S(1)}, u32[]{:S(2)}, u32[]{:S(2)}) collective-permute-start(bf16[16,3584]{1,0:T(8,128)(2,1)S(1)} %slice.55), channel_id=1, source_target_pairs={{0,8},{4,12},{8,0},{12,4},{16,20},{20,16},{24,28},{28,24},{1,9},{5... | collective-permute-start | bytes 344072 | tf_op jit(solution)/shard_map/ppermute | solution.py:26
  52.6 0.5 collective-permute-done.9
  53.1 2.8 %collective-permute-done.12 = bf16[16,3584]{1,0:T(8,128)(2,1)S(1)} collective-permute-done((bf16[16,3584]{1,0:T(8,128)(2,1)S(1)}, bf16[16,3584]{1,0:T(8,128)(2,1)S(1)}, u32[]{:S(2)}, u32[]{:S(2)}) %collective-permute-start.12) | collective-permute-done | bytes 114720 | tf_op jit(solution)/shard_map/ppermute | solution.py:26
  56.0 0.1 fusion.2
  56.0 0.3 collective-permute-start.13
  56.3 0.0 collective-permute-start.15
  56.3 4.2 %collective-permute-start.14 = (bf16[4,7168]{1,0:T(4,128)(2,1)S(1)}, bf16[4,7168]{1,0:T(4,128)(2,1)S(1)}, u32[]{:S(2)}, u32[]{:S(2)}) collective-permute-start(bf16[4,7168]{1,0:T(4,128)(2,1)S(1)} %get-tuple-element.59), channel_id=1, source_target_pairs={{0,1},{1,0},{2,3},{3,2},{16,18},{17,19},{18,16},{19,17},{4,5},{5,4... | collective-permute-start | bytes 172040 | tf_op jit(solution)/shard_map/ppermute | solution.py:41
  60.5 1.6 %collective-permute-done.13 = bf16[4,7168]{1,0:T(4,128)(2,1)S(1)} collective-permute-done((bf16[4,7168]{1,0:T(4,128)(2,1)S(1)}, bf16[4,7168]{1,0:T(4,128)(2,1)S(1)}, u32[]{:S(2)}, u32[]{:S(2)}) %collective-permute-start.13) | collective-permute-done | bytes 57376 | tf_op jit(solution)/shard_map/ppermute | solution.py:41
  62.1 0.0 collective-permute-done.15
  62.1 0.6 collective-permute-done.14
  62.7 0.7 %add_convert_fusion.6 = bf16[4,7168]{1,0:T(4,128)(2,1)} fusion(bf16[4,7168]{1,0:T(4,128)(2,1)S(1)} %collective-permute-done.15, bf16[4,7168]{1,0:T(4,128)(2,1)S(1)} %collective-permute-done.14, bf16[4,7168]{1,0:T(4,128)(2,1)S(1)} %collective-permute-done.13, bf16[16,3584]{1,0:T(8,128)(2,1)S(1)} %add_convert_fusion.5, bf16[16,3584]{1,0:T(8,128)(2,1)S(1)} %add_convert_fusion.4), kind=kLoop, calls=%fused_computation.12 | loop fusion | flops 315392 | bytes 458752 | tf_op jit(solution)/shard_map/convert_element_type | solution.py:328
  (7 shorter events, 0.1 us)
Async XLA Ops:
  1.0 8.9 %collective-permute-start.2 = (bf16[4,7296]{1,0:T(4,128)(2,1)S(1)}, bf16[4,7296]{1,0:T(4,128)(2,1)S(1)}, u32[]{:S(2)}, u32[]{:S(2)}) collective-permute-start(bf16[4,7296]{1,0:T(4,128)(2,1)S(1)} %extend.1.after_ref.refs_0_), channel_id=1, source_target_pairs={{0,2},{1,3},{2,0},{3,1},{16,19},{17,18},{18,17},{19,16},{4,6},{5,7... | collective-permute-start | bytes 175112 | tf_op jit(solution)/shard_map/ppermute | solution.py:41
  5.1 5.0 %collective-permute-start.1 = (bf16[4,7296]{1,0:T(4,128)(2,1)S(1)}, bf16[4,7296]{1,0:T(4,128)(2,1)S(1)}, u32[]{:S(2)}, u32[]{:S(2)}) collective-permute-start(bf16[4,7296]{1,0:T(4,128)(2,1)S(1)} %extend.1.after_ref.refs_0_), channel_id=1, source_target_pairs={{0,1},{1,0},{2,3},{3,2},{16,18},{17,19},{18,16},{19,17},{4,5},{5,4... | collective-permute-start | bytes 175112 | tf_op jit(solution)/shard_map/ppermute | solution.py:41
  6.7 6.0 %collective-permute-start = (bf16[4,7296]{1,0:T(4,128)(2,1)S(1)}, bf16[4,7296]{1,0:T(4,128)(2,1)S(1)}, u32[]{:S(2)}, u32[]{:S(2)}) collective-permute-start(bf16[4,7296]{1,0:T(4,128)(2,1)S(1)} %extend.1.after_ref.refs_0_), channel_id=1, source_target_pairs={{0,3},{1,2},{2,1},{3,0},{16,17},{17,16},{18,19},{19,18},{4,7},{5,6... | collective-permute-start | bytes 175112 | tf_op jit(solution)/shard_map/ppermute | solution.py:41
  12.7 7.4 %collective-permute-start.3 = (bf16[16,7296]{1,0:T(8,128)(2,1)S(1)}, bf16[16,7296]{1,0:T(8,128)(2,1)S(1)}, u32[]{:S(2)}, u32[]{:S(2)}) collective-permute-start(bf16[16,7296]{1,0:T(8,128)(2,1)S(1)} %stack.2.refs_0_), channel_id=1, source_target_pairs={{0,8},{4,12},{8,0},{12,4},{16,20},{20,16},{24,28},{28,24},{1,9},{5... | collective-permute-start | bytes 700424 | tf_op jit(solution)/shard_map/ppermute | solution.py:26
  20.1 8.6 %collective-permute-start.4 = (bf16[32,7296]{1,0:T(8,128)(2,1)S(1)}, bf16[32,7296]{1,0:T(8,128)(2,1)S(1)}, u32[]{:S(2)}, u32[]{:S(2)}) collective-permute-start(bf16[32,7296]{1,0:T(8,128)(2,1)S(1)} %stack.3.refs_0_), channel_id=1, source_target_pairs={{0,4},{4,0},{8,12},{12,8},{16,24},{20,28},{24,16},{28,20},{1,5},{5... | collective-permute-start | bytes 1400840 | tf_op jit(solution)/shard_map/ppermute | solution.py:26
  24.8 3.9 %collective-permute-start.5 = (bf16[32,7296]{1,0:T(8,128)(2,1)S(1)}, bf16[32,7296]{1,0:T(8,128)(2,1)S(1)}, u32[]{:S(2)}, u32[]{:S(2)}) collective-permute-start(bf16[32,7296]{1,0:T(8,128)(2,1)S(1)} %stack.3.refs_0_), channel_id=1, source_target_pairs={{0,16},{16,0},{1,17},{17,1},{2,18},{18,2},{3,19},{19,3},{4,20},{20... | collective-permute-start | bytes 1400840 | tf_op jit(solution)/shard_map/ppermute | solution.py:45
  28.8 1.8 %collective-permute-start.6 = (bf16[32,7296]{1,0:T(8,128)(2,1)S(1)}, bf16[32,7296]{1,0:T(8,128)(2,1)S(1)}, u32[]{:S(2)}, u32[]{:S(2)}) collective-permute-start(bf16[32,7296]{1,0:T(8,128)(2,1)S(1)} %collective-permute-done.4.refs_1_), channel_id=1, source_target_pairs={{0,16},{16,0},{1,17},{17,1},{2,18},{18,2},{3,19},{19,3},{4,20},{20... | collective-permute-start | bytes 1400840 | tf_op jit(solution)/shard_map/ppermute | solution.py:45
  40.1 1.9 %collective-permute-start.7 = (bf16[64,3584]{1,0:T(8,128)(2,1)S(1)}, bf16[64,3584]{1,0:T(8,128)(2,1)S(1)}, u32[]{:S(2)}, u32[]{:S(2)}) collective-permute-start(bf16[64,3584]{1,0:T(8,128)(2,1)S(1)} %get-tuple-element.51), channel_id=1, source_target_pairs={{0,16},{16,0},{1,17},{17,1},{2,18},{18,2},{3,19},{19,3},{4,20},{20... | collective-permute-start | bytes 1376264 | tf_op jit(solution)/shard_map/ppermute | solution.py:45
  41.4 2.2 %collective-permute-start.10 = (bf16[64,3584]{1,0:T(8,128)(2,1)S(1)}, bf16[64,3584]{1,0:T(8,128)(2,1)S(1)}, u32[]{:S(2)}, u32[]{:S(2)}) collective-permute-start(bf16[64,3584]{1,0:T(8,128)(2,1)S(1)} %get-tuple-element.56), channel_id=1, source_target_pairs={{0,16},{16,0},{1,17},{17,1},{2,18},{18,2},{3,19},{19,3},{4,20},{20... | collective-permute-start | bytes 1376264 | tf_op jit(solution)/shard_map/ppermute | solution.py:45
  42.1 6.1 %collective-permute-start.8 = (bf16[32,3584]{1,0:T(8,128)(2,1)S(1)}, bf16[32,3584]{1,0:T(8,128)(2,1)S(1)}, u32[]{:S(2)}, u32[]{:S(2)}) collective-permute-start(bf16[32,3584]{1,0:T(8,128)(2,1)S(1)} %slice.49), channel_id=1, source_target_pairs={{0,4},{4,0},{8,12},{12,8},{16,24},{20,28},{24,16},{28,20},{1,5},{5... | collective-permute-start | bytes 688136 | tf_op jit(solution)/shard_map/ppermute | solution.py:26
  43.8 7.2 %collective-permute-start.11 = (bf16[32,3584]{1,0:T(8,128)(2,1)S(1)}, bf16[32,3584]{1,0:T(8,128)(2,1)S(1)}, u32[]{:S(2)}, u32[]{:S(2)}) collective-permute-start(bf16[32,3584]{1,0:T(8,128)(2,1)S(1)} %slice.53), channel_id=1, source_target_pairs={{0,4},{4,0},{8,12},{12,8},{16,24},{20,28},{24,16},{28,20},{1,5},{5... | collective-permute-start | bytes 688136 | tf_op jit(solution)/shard_map/ppermute | solution.py:26
  48.2 4.9 %collective-permute-start.9 = (bf16[16,3584]{1,0:T(8,128)(2,1)S(1)}, bf16[16,3584]{1,0:T(8,128)(2,1)S(1)}, u32[]{:S(2)}, u32[]{:S(2)}) collective-permute-start(bf16[16,3584]{1,0:T(8,128)(2,1)S(1)} %slice.51), channel_id=1, source_target_pairs={{0,8},{4,12},{8,0},{12,4},{16,20},{20,16},{24,28},{28,24},{1,9},{5... | collective-permute-start | bytes 344072 | tf_op jit(solution)/shard_map/ppermute | solution.py:26
  51.1 4.9 %collective-permute-start.12 = (bf16[16,3584]{1,0:T(8,128)(2,1)S(1)}, bf16[16,3584]{1,0:T(8,128)(2,1)S(1)}, u32[]{:S(2)}, u32[]{:S(2)}) collective-permute-start(bf16[16,3584]{1,0:T(8,128)(2,1)S(1)} %slice.55), channel_id=1, source_target_pairs={{0,8},{4,12},{8,0},{12,4},{16,20},{20,16},{24,28},{28,24},{1,9},{5... | collective-permute-start | bytes 344072 | tf_op jit(solution)/shard_map/ppermute | solution.py:26
  56.0 6.0 %collective-permute-start.13 = (bf16[4,7168]{1,0:T(4,128)(2,1)S(1)}, bf16[4,7168]{1,0:T(4,128)(2,1)S(1)}, u32[]{:S(2)}, u32[]{:S(2)}) collective-permute-start(bf16[4,7168]{1,0:T(4,128)(2,1)S(1)} %get-tuple-element.57), channel_id=1, source_target_pairs={{0,3},{1,2},{2,1},{3,0},{16,17},{17,16},{18,19},{19,18},{4,7},{5,6... | collective-permute-start | bytes 172040 | tf_op jit(solution)/shard_map/ppermute | solution.py:41
  56.3 5.8 %collective-permute-start.15 = (bf16[4,7168]{1,0:T(4,128)(2,1)S(1)}, bf16[4,7168]{1,0:T(4,128)(2,1)S(1)}, u32[]{:S(2)}, u32[]{:S(2)}) collective-permute-start(bf16[4,7168]{1,0:T(4,128)(2,1)S(1)} %get-tuple-element.58), channel_id=1, source_target_pairs={{0,2},{1,3},{2,0},{3,1},{16,19},{17,18},{18,17},{19,16},{4,6},{5,7... | collective-permute-start | bytes 172040 | tf_op jit(solution)/shard_map/ppermute | solution.py:41
  56.3 6.4 %collective-permute-start.14 = (bf16[4,7168]{1,0:T(4,128)(2,1)S(1)}, bf16[4,7168]{1,0:T(4,128)(2,1)S(1)}, u32[]{:S(2)}, u32[]{:S(2)}) collective-permute-start(bf16[4,7168]{1,0:T(4,128)(2,1)S(1)} %get-tuple-element.59), channel_id=1, source_target_pairs={{0,1},{1,0},{2,3},{3,2},{16,18},{17,19},{18,16},{19,17},{4,5},{5,4... | collective-permute-start | bytes 172040 | tf_op jit(solution)/shard_map/ppermute | solution.py:41

commit v14 on v13

--- a/solution.py
+++ b/solution.py
@@ -8,7 +8,7 @@
 from jax.sharding import PartitionSpec as P
 
 AXES = ("sect", "grp", "dev")
-VMEM_LIMIT = 16 * 2**20
+VMEM_LIMIT = 10 * 2**20
 
 
 def rounds_of():
@@ -26,11 +26,11 @@
     return lax.ppermute(value, ("sect", "grp"), pairs)
 
 
-def line_masks():
-    sects, _, lanes = (lax.axis_size(a) for a in AXES)
+def line_orders():
+    lanes = lax.axis_size("dev")
     near = list(range(1, lanes))
-    orders = [near[-1:] + near[:-1], near]
-    return list(zip(*(orders[s % 2] for s in range(sects))))
+    orders = [[0] + near[-1:] + near[:-1], [0] + near]
+    return [orders[s % 2] for s in range(lax.axis_size("sect"))]
 
 
 def swap_line(value, masks):
@@ -90,44 +90,67 @@
     )(*(pltpu.with_memory_space_constraint(v, pltpu.HBM) for v in (tokens, ids, weights)))
 
 
-def stack_kernel(*refs):
+def stack_kernel(orders, *refs):
     pieces, out_ref = refs[:-1], refs[-1]
-    values = [p[...].astype(jnp.float32) for p in pieces]
-    out_ref[...] = jnp.concatenate(values, axis=0).astype(out_ref.dtype)
-
-
-def stack(*pieces):
+    for core, order in enumerate(orders):
+
+        @pl.when(lax.axis_index("sect") == core)
+        def _():
+            values = [pieces[i][...].astype(jnp.float32) for i in order]
+            out_ref[...] = jnp.concatenate(values, axis=0).astype(out_ref.dtype)
+
+
+def stack(pieces, orders=None):
     rows = sum(p.shape[0] for p in pieces)
     out = jax.ShapeDtypeStruct((rows, pieces[0].shape[1]), pieces[0].dtype)
-    return vmem_call(stack_kernel, out, "stack", *pieces)
-
-
-def gather_rows(block, w_up, w_gate):
-    wanted = [(w, e) for w in (w_gate, w_up) for e in range(w.shape[0])]
-    weights, token = [], block
-
-    def meanwhile(arrived, token):
-        if wanted:
-            weight, token = fetch(*wanted.pop(0), token)
-            weights.append(weight)
-            arrived, token = lax.optimization_barrier((arrived, token))
-        return arrived, token
-
-    arrived = [swap_line(block, masks) for masks in line_masks()]
-    arrived, token = meanwhile(arrived, token)
-    line = stack(block, *arrived)
+    if orders is None:
+        orders = [range(len(pieces))] * lax.axis_size("sect")
+    return vmem_call(functools.partial(stack_kernel, orders), out, "stack", *pieces)
+
+
+def gather_rows(block, w_gate, w_up, w_down):
+    experts, sects, lanes = w_gate.shape[0], lax.axis_size("sect"), lax.axis_size("dev")
+    early = early_columns(w_down)
+    gates, ups, downs = ([(w, e, w.shape[2]) for e in range(experts)] for w in (w_gate, w_up, w_down))
+    downs = [(w, e, early) for w, e, _ in downs]
+    held, token = {}, block
+
+    def fetch_next(wanted, token):
+        weight, expert, columns = wanted.pop(0)
+        held[id(weight), expert], token = fetch(weight, expert, columns, token)
+        return token
+
+    arrived = [swap_line(block, (m,) * sects) for m in range(1, lanes)]
+    token = fetch_next(gates, token)
+    arrived, token = lax.optimization_barrier((arrived, token))
+    line = stack([block, *arrived], line_orders())
     rounds = rounds_of()
-    for masks in rounds[:-1]:
-        arrived, token = meanwhile(swap(line, masks), token)
-        line = stack(line, arrived)
+    for number, masks in enumerate(rounds[:-1]):
+        arrived = swap(line, masks)
+        if gates:
+            token = fetch_next(gates, token)
+            if len(downs) > 1:
+                token = fetch_next(downs, token)
+        arrived, token = lax.optimization_barrier((arrived, token))
+        line = stack([line, arrived])
     last = swap(line, rounds[-1])
-    mine, token = meanwhile(line, token)
+    token = fetch_next(gates if gates else ups, token)
+    mine, token = lax.optimization_barrier((line, token))
     other = swap_core(mine)
-    while wanted:
-        weight, token = fetch(*wanted.pop(0), token)
-        weights.append(weight)
+    while gates or ups:
+        token = fetch_next(gates if gates else ups, token)
     last, other, token = lax.optimization_barrier((last, other, token))
-    return [line, last, other, swap_core(last)], weights, token
+    last_other = swap_core(last)
+    while downs:
+        token = fetch_next(downs, token)
+    last_other, token = lax.optimization_barrier((last_other, token))
+    weights = [held[id(w), e] for w in (w_gate, w_up, w_down) for e in range(experts)]
+    return [line, last, other, last_other], weights, token
+
+
+def early_columns(w_down):
+    _, hidden, width = w_down.shape
+    return width // hidden // 2 * hidden
 
 
 def down_copy(expert, block, at, down_hbm, target_ref, sems):
@@ -139,10 +162,10 @@
     )
 
 
-def down_block(at, hidden_ref, down_refs, keep_ref, send_ref):
-    hidden = down_refs[0].shape[1]
+def down_block(at, hidden_ref, weights, keep_ref, send_ref):
+    hidden = weights[0].shape[1]
     middle = keep_ref.shape[0]
-    weight = jnp.concatenate([ref[pl.ds(at * hidden, hidden), :] for ref in down_refs], axis=0)
+    weight = jnp.concatenate(weights, axis=0)
     total = jnp.dot(hidden_ref[...], weight, preferred_element_type=jnp.float32)
     total = total.astype(jnp.bfloat16)
     span = pl.ds(at * hidden, hidden)
@@ -152,20 +175,17 @@
 
 def expert_kernel(entry_count, experts, width, token_ref, *refs):
     pieces, refs = refs[:entry_count], refs[entry_count:]
-    gate_refs, up_refs, refs = refs[:experts], refs[experts:2 * experts], refs[2 * experts:]
+    gate_refs, up_refs, early_refs, refs = (
+        refs[:experts], refs[experts:2 * experts], refs[2 * experts:3 * experts], refs[3 * experts:]
+    )
     down_hbm, hidden_ref, keep_ref, send_ref = refs[:4]
-    down_refs, (rows_ref, value_ref, early_ref, sems) = refs[4:4 + experts], refs[4 + experts:]
+    down_refs, (rows_ref, value_ref, sems) = refs[4:4 + experts], refs[4 + experts:]
     hidden = gate_refs[0].shape[2]
     place = lax.axis_index("sect") * lax.axis_size("grp") + lax.axis_index("grp")
     first = place * experts
     block = min(256, hidden)
     blocks = width // hidden
 
-    early = [
-        down_copy(e, step, step, down_hbm, early_ref.at[e], sems)
-        for step in range(blocks // 2)
-        for e in range(experts)
-    ]
     late = [
         [
             down_copy(e, step, step - blocks // 2, down_hbm, down_refs[e].at[0], sems)
@@ -173,8 +193,6 @@
         ]
         for e in range(experts)
     ]
-    for copy in early:
-        copy.start()
 
     at = 0
     for piece in pieces:
@@ -205,9 +223,8 @@
             hidden_ref[:, pl.ds(e * hidden + step * block, block)] = value.astype(jnp.bfloat16)
 
     for step in range(blocks // 2):
-        for copy in early[step * experts:(step + 1) * experts]:
-            copy.wait()
-        down_block(step, hidden_ref, [early_ref.at[e] for e in range(experts)], keep_ref, send_ref)
+        span = pl.ds(step * hidden, hidden)
+        down_block(step, hidden_ref, [ref[0, :, span] for ref in early_refs], keep_ref, send_ref)
 
     for copies in late:
         for copy in copies:
@@ -216,12 +233,15 @@
 
 def down_kernel(hidden_ref, *refs):
     *down_refs, keep_ref, send_ref = refs
-    for step in range(keep_ref.shape[1] // down_refs[0].shape[2]):
-        down_block(step, hidden_ref, [ref.at[0] for ref in down_refs], keep_ref, send_ref)
+    hidden = down_refs[0].shape[2]
+    for step in range(keep_ref.shape[1] // hidden):
+        span = pl.ds(step * hidden, hidden)
+        down_block(step, hidden_ref, [ref[0, span, :] for ref in down_refs], keep_ref, send_ref)
 
 
 def fetch_kernel(expert, after_ref, source_ref, target_ref, token_ref, sems):
-    copies = weight_copies(source_ref.at[pl.ds(expert, 1)], target_ref, sems, 0)
+    columns = pl.ds(0, target_ref.shape[2])
+    copies = weight_copies(source_ref.at[pl.ds(expert, 1), :, columns], target_ref, sems, 0)
     for copy in copies:
         copy.start()
     token_ref[...] = jnp.zeros_like(token_ref)
@@ -242,13 +262,13 @@
     ]
 
 
-def fetch(weight, expert, after):
+def fetch(weight, expert, columns, after):
     in_hbm = pl.BlockSpec(memory_space=pl.ANY)
     in_vmem = pl.BlockSpec(memory_space=pltpu.VMEM)
     return pl.pallas_call(
         functools.partial(fetch_kernel, expert),
         out_shape=(
-            pltpu.VMEM((1, *weight.shape[1:]), weight.dtype),
+            pltpu.VMEM((1, weight.shape[1], columns), weight.dtype),
             jax.ShapeDtypeStruct((8, 128), jnp.float32),
         ),
         in_specs=[in_hbm, in_hbm],
@@ -256,7 +276,7 @@
         scratch_shapes=[pltpu.SemaphoreType.DMA((1, 8))],
         compiler_params=pltpu.CompilerParams(vmem_limit_bytes=VMEM_LIMIT),
         cost_estimate=pl.CostEstimate(
-            flops=0, bytes_accessed=2 * weight.size // weight.shape[0], transcendentals=0
+            flops=0, bytes_accessed=2 * weight.shape[1] * columns, transcendentals=0
         ),
         name="fetch",
     )(after, pltpu.with_memory_space_constraint(weight, pltpu.HBM))
@@ -273,7 +293,7 @@
     blocks = width // hidden
     whole = pl.BlockSpec(memory_space=pltpu.VMEM)
     anywhere = pl.BlockSpec(memory_space=pl.ANY)
-    columns = (blocks // 2 * hidden, (blocks - blocks // 2) * hidden)
+    columns = (early_columns(w_down), width - early_columns(w_down))
     outs = [jax.ShapeDtypeStruct((rows // 2, c), jnp.bfloat16) for c in columns]
     hiddens, keep, send, *down = pl.pallas_call(
         functools.partial(expert_kernel, len(entries), experts, width),
@@ -289,7 +309,6 @@
         scratch_shapes=[
             pltpu.VMEM((rows, full), jnp.bfloat16),
             pltpu.VMEM((experts, rows, hidden), jnp.float32),
-            pltpu.VMEM((experts, columns[0], hidden), w_down.dtype),
             pltpu.SemaphoreType.DMA((experts, blocks)),
         ],
         compiler_params=pltpu.CompilerParams(vmem_limit_bytes=VMEM_LIMIT),
@@ -336,7 +355,7 @@
 
     half = -(-expert_count // 64) * 64
     block = extend(tokens, expert_ids, gate_weights, half)
-    entries, held, token = gather_rows(block, w_up, w_gate)
+    entries, held, token = gather_rows(block, w_gate, w_up, w_down)
 
     results = []
     halves = []
@@ -348,7 +367,8 @@
         halves.append(value)
     value = jnp.concatenate(halves, axis=1)
     own = [value[m * row_count:(m + 1) * row_count] for m in range(lanes)]
-    return add(own[0], *(swap_line(o, masks) for o, masks in zip(own[1:], line_masks())))
+    masks = list(zip(*line_orders()))
+    return add(own[0], *(swap_line(own[i], masks[i]) for i in range(1, lanes)))
 
 
 def solution(mesh):

time: 63.5 us -> 61.8 us (0.973)
  waiting for transfers between devices: 17.9 us -> 14.1 us
  Pallas kernels: 24.3 us -> 27.3 us
  starting transfers between devices: 19.8 us -> 18.9 us
    pallas_call x4 -> x6, Pallas kernels: 12.7 us -> 16.8 us  [fetch(): pl.pallas_call(functools.partial(fetch_kernel, expert), out_shape=(pltpu....]
    ppermute x6, waiting for transfers between devices: 11 us -> 9.22 us  [swap(): return lax.ppermute(value, ('sect', 'grp'), pairs)]
    ppermute x4, waiting for transfers between devices: 1.94 us -> 0.24 us  [swap_core(): return lax.ppermute(value, 'sect', [(0, 1), (1, 0)])]
    pallas_call x1, Pallas kernels: 9.46 us -> 8.26 us  [expert_call(): pl.pallas_call(functools.partial(expert_kernel, len(entries), experts, wi...]
    ppermute x6, starting transfers between devices: 8.97 us -> 7.94 us  [swap(): return lax.ppermute(value, ('sect', 'grp'), pairs)]
  transfers between devices with their start and end apart: 16 -> 16, of which waited for: 12 -> 9; matrix products, arithmetic and copies ran while one was open for 1% -> 1% of each run, Pallas kernels for 22% -> 29%
where the time goes in v14:
time: 61.8 us; the launch traced here: 61.6 us
  Pallas kernels  27.3 us (44%)
  starting transfers between devices  18.9 us (31%)
  waiting for transfers between devices  14.1 us (23%)
  other arithmetic  1.14 us (2%)
    pallas_call x6, Pallas kernels, fetch(): pl.pallas_call(functools.partial(fetch_kernel, expert), out_shape=(pltpu....  16.8 us
    ppermute x6, starting transfers between devices, swap_line(): return lax.ppermute(value, ('sect', 'dev'), pairs)  10.2 us
    ppermute x6, waiting for transfers between devices, swap(): return lax.ppermute(value, ('sect', 'grp'), pairs)  9.22 us
    pallas_call x1, Pallas kernels, expert_call(): pl.pallas_call(functools.partial(expert_kernel, len(entries), experts, wi...  8.26 us
    ppermute x6, starting transfers between devices, swap(): return lax.ppermute(value, ('sect', 'grp'), pairs)  7.94 us
    ppermute x6, waiting for transfers between devices, swap_line(): return lax.ppermute(value, ('sect', 'dev'), pairs)  4.61 us
  transfers between devices with their start and end apart: 16, of which 9 were waited for; matrix products, arithmetic and copies ran while one was open for 1% of the time, Pallas kernels for 29%

profile of v14, /device:TPU:0, one launch (start us, length us, event | category | flops | bytes accessed | tf_op | source)
XLA Modules:
  0.0 61.6 jit_solution(3966379550492201026)
XLA Ops:
  0.0 1.0 %extend.1.after_ref.refs_0_ = bf16[4,7296]{1,0:T(4,128)(2,1)S(1)} custom-call(bf16[4,7168]{1,0:T(4,128)(2,1)} %tokens_hbm.1, s32[4,8]{1,0:T(4,128)} %ids_hbm.1, f32[4,8]{1,0:T(4,128)} %weights_hbm.1), custom_call_target="tpu_custom_call" | custom-call | tf_op jit(solution)/shard_map/extend/pallas_call | solution.py:81
  1.0 5.1 %collective-permute-start.2 = (bf16[4,7296]{1,0:T(4,128)(2,1)S(1)}, bf16[4,7296]{1,0:T(4,128)(2,1)S(1)}, u32[]{:S(2)}, u32[]{:S(2)}) collective-permute-start(bf16[4,7296]{1,0:T(4,128)(2,1)S(1)} %extend.1.after_ref.refs_0_), channel_id=1, source_target_pairs={{0,3},{1,2},{2,1},{3,0},{16,19},{17,18},{18,17},{19,16},{4,7},{5,6... | collective-permute-start | bytes 175112 | tf_op jit(solution)/shard_map/ppermute | solution.py:41
  6.1 0.0 collective-permute-start.1
  6.1 0.6 %collective-permute-start = (bf16[4,7296]{1,0:T(4,128)(2,1)S(1)}, bf16[4,7296]{1,0:T(4,128)(2,1)S(1)}, u32[]{:S(2)}, u32[]{:S(2)}) collective-permute-start(bf16[4,7296]{1,0:T(4,128)(2,1)S(1)} %extend.1.after_ref.refs_0_), channel_id=1, source_target_pairs={{0,1},{1,0},{2,3},{3,2},{16,17},{17,16},{18,19},{19,18},{4,5},{5,4... | collective-permute-start | bytes 175112 | tf_op jit(solution)/shard_map/ppermute | solution.py:41
  6.7 3.2 %fetch.6 = (bf16[1,7168,512]{2,1,0:T(8,128)(2,1)S(1)}, f32[8,128]{1,0:T(8,128)S(1)}) custom-call(bf16[4,7296]{1,0:T(4,128)(2,1)S(1)} %extend.1.after_ref.refs_0_, bf16[2,7168,512]{2,1,0:T(8,128)(2,1)} %source_ref.7), custom_call_target="tpu_custom_call" | custom-call | bytes 7340032 | tf_op jit(solution)/shard_map/fetch/pallas_call | solution.py:268
  9.9 0.0 collective-permute-done.2.refs_3_
  9.9 1.3 %collective-permute-done.1.refs_2_ = bf16[4,7296]{1,0:T(4,128)(2,1)S(1)} collective-permute-done((bf16[4,7296]{1,0:T(4,128)(2,1)S(1)}, bf16[4,7296]{1,0:T(4,128)(2,1)S(1)}, u32[]{:S(2)}, u32[]{:S(2)}) %collective-permute-start.1) | collective-permute-done | bytes 58400 | tf_op jit(solution)/shard_map/ppermute | solution.py:41
  11.2 0.0 collective-permute-done.refs_1_
  11.2 0.1 stack.2.refs_0_
  11.3 1.7 %collective-permute-start.3 = (bf16[16,7296]{1,0:T(8,128)(2,1)S(1)}, bf16[16,7296]{1,0:T(8,128)(2,1)S(1)}, u32[]{:S(2)}, u32[]{:S(2)}) collective-permute-start(bf16[16,7296]{1,0:T(8,128)(2,1)S(1)} %stack.2.refs_0_), channel_id=1, source_target_pairs={{0,8},{4,12},{8,0},{12,4},{16,20},{20,16},{24,28},{28,24},{1,9},{5... | collective-permute-start | bytes 700424 | tf_op jit(solution)/shard_map/ppermute | solution.py:26
  12.9 3.2 %fetch.7 = (bf16[1,7168,512]{2,1,0:T(8,128)(2,1)S(1)}, f32[8,128]{1,0:T(8,128)S(1)}) custom-call(f32[8,128]{1,0:T(8,128)S(1)} %get-tuple-element.41.after_ref, bf16[2,7168,512]{2,1,0:T(8,128)(2,1)} %source_ref.7), custom_call_target="tpu_custom_call" | custom-call | bytes 7340032 | tf_op jit(solution)/shard_map/fetch/pallas_call | solution.py:268
  16.1 2.1 %fetch.8 = (bf16[1,512,3584]{2,1,0:T(8,128)(2,1)S(1)}, f32[8,128]{1,0:T(8,128)S(1)}) custom-call(f32[8,128]{1,0:T(8,128)S(1)} %get-tuple-element.42.after_ref, bf16[2,512,7168]{2,1,0:T(8,128)(2,1)} %refs_10_.1), custom_call_target="tpu_custom_call" | custom-call | bytes 3670016 | tf_op jit(solution)/shard_map/fetch/pallas_call | solution.py:268
  18.2 0.0 collective-permute-done.3.refs_1_
  18.2 1.6 %collective-permute-start.4 = (bf16[32,7296]{1,0:T(8,128)(2,1)S(1)}, bf16[32,7296]{1,0:T(8,128)(2,1)S(1)}, u32[]{:S(2)}, u32[]{:S(2)}) collective-permute-start(bf16[32,7296]{1,0:T(8,128)(2,1)S(1)} %stack.3.refs_0_), channel_id=1, source_target_pairs={{0,4},{4,0},{8,12},{12,8},{16,24},{20,28},{24,16},{28,20},{1,5},{5... | collective-permute-start | bytes 1400840 | tf_op jit(solution)/shard_map/ppermute | solution.py:26
  19.8 3.2 %fetch.9 = (bf16[1,7168,512]{2,1,0:T(8,128)(2,1)S(1)}, f32[8,128]{1,0:T(8,128)S(1)}) custom-call(f32[8,128]{1,0:T(8,128)S(1)} %get-tuple-element.45.after_ref, bf16[2,7168,512]{2,1,0:T(8,128)(2,1)} %source_ref.10), custom_call_target="tpu_custom_call" | custom-call | bytes 7340032 | tf_op jit(solution)/shard_map/fetch/pallas_call | solution.py:268
  23.0 0.1 collective-permute-start.5
  23.1 3.2 %fetch.10 = (bf16[1,7168,512]{2,1,0:T(8,128)(2,1)S(1)}, f32[8,128]{1,0:T(8,128)S(1)}) custom-call(f32[8,128]{1,0:T(8,128)S(1)} %get-tuple-element.48.after_ref, bf16[2,7168,512]{2,1,0:T(8,128)(2,1)} %source_ref.10), custom_call_target="tpu_custom_call" | custom-call | bytes 7340032 | tf_op jit(solution)/shard_map/fetch/pallas_call | solution.py:268
  26.2 0.6 %collective-permute-done.4.refs_1_ = bf16[32,7296]{1,0:T(8,128)(2,1)S(1)} collective-permute-done((bf16[32,7296]{1,0:T(8,128)(2,1)S(1)}, bf16[32,7296]{1,0:T(8,128)(2,1)S(1)}, u32[]{:S(2)}, u32[]{:S(2)}) %collective-permute-start.4) | collective-permute-done | bytes 466976 | tf_op jit(solution)/shard_map/ppermute | solution.py:26
  26.9 0.0 collective-permute-done.5.refs_2_
  26.9 0.0 collective-permute-start.6
  26.9 2.1 %fetch.11 = (bf16[1,512,3584]{2,1,0:T(8,128)(2,1)S(1)}, f32[8,128]{1,0:T(8,128)S(1)}) custom-call(f32[8,128]{1,0:T(8,128)S(1)} %get-tuple-element.51.after_ref, bf16[2,512,7168]{2,1,0:T(8,128)(2,1)} %refs_10_.1), custom_call_target="tpu_custom_call" | custom-call | bytes 3670016 | tf_op jit(solution)/shard_map/fetch/pallas_call | solution.py:268
  28.9 0.0 collective-permute-done.6.refs_3_
  29.0 8.3 %experts.1 = (bf16[128,1024]{1,0:T(8,128)(2,1)S(1)}, bf16[64,3584]{1,0:T(8,128)(2,1)S(1)}, bf16[64,3584]{1,0:T(8,128)(2,1)S(1)}, bf16[1,7168,512]{2,1,0:T(8,128)(2,1)S(1)}, bf16[1,7168,512]{2,1,0:T(8,128)(2,1)S(1)}) custom-call(f32[8,128]{1,0:T(8,128)S(1)} %get-tuple-element.53.token_ref, ...), custom_call_target="tpu_custom_call", output_to_operand_aliasing={{3}: (5, {}), {4}: (6, {})} | custom-call | flops 4697620480 | bytes 14680064 | tf_op jit(solution)/shard_map/experts/pallas_call | solution.py:298
  37.2 0.6 collective-permute-start.7
  37.8 1.1 %down.1 = (bf16[64,3584]{1,0:T(8,128)(2,1)S(1)}, bf16[64,3584]{1,0:T(8,128)(2,1)S(1)}) custom-call(bf16[128,1024]{1,0:T(8,128)(2,1)S(1)} %get-tuple-element.64.hidden_ref, bf16[1,7168,512]{2,1,0:T(8,128)(2,1)S(1)} %get-tuple-element.65.refs_0_, bf16[1,7168,512]{2,1,0:T(8,128)(2,1)S(1)} %get-tuple-element.66.refs_1_), custom_call_target="tpu_custom_call" | custom-call | flops 939524096 | bytes 917504 | tf_op jit(solution)/shard_map/down/pallas_call | solution.py:327
  38.9 0.1 collective-permute-start.10
  39.0 0.2 collective-permute-done.7
  39.2 0.1 add_convert_fusion.1
  39.4 1.6 %collective-permute-start.8 = (bf16[32,3584]{1,0:T(8,128)(2,1)S(1)}, bf16[32,3584]{1,0:T(8,128)(2,1)S(1)}, u32[]{:S(2)}, u32[]{:S(2)}) collective-permute-start(bf16[32,3584]{1,0:T(8,128)(2,1)S(1)} %slice.49), channel_id=1, source_target_pairs={{0,4},{4,0},{8,12},{12,8},{16,24},{20,28},{24,16},{28,20},{1,5},{5... | collective-permute-start | bytes 688136 | tf_op jit(solution)/shard_map/ppermute | solution.py:26
  40.9 0.0 collective-permute-done.10
  40.9 0.1 add_convert_fusion
  41.1 1.4 %collective-permute-start.11 = (bf16[32,3584]{1,0:T(8,128)(2,1)S(1)}, bf16[32,3584]{1,0:T(8,128)(2,1)S(1)}, u32[]{:S(2)}, u32[]{:S(2)}) collective-permute-start(bf16[32,3584]{1,0:T(8,128)(2,1)S(1)} %slice.53), channel_id=1, source_target_pairs={{0,4},{4,0},{8,12},{12,8},{16,24},{20,28},{24,16},{28,20},{1,5},{5... | collective-permute-start | bytes 688136 | tf_op jit(solution)/shard_map/ppermute | solution.py:26
  42.5 3.0 %collective-permute-done.8 = bf16[32,3584]{1,0:T(8,128)(2,1)S(1)} collective-permute-done((bf16[32,3584]{1,0:T(8,128)(2,1)S(1)}, bf16[32,3584]{1,0:T(8,128)(2,1)S(1)}, u32[]{:S(2)}, u32[]{:S(2)}) %collective-permute-start.8) | collective-permute-done | bytes 229408 | tf_op jit(solution)/shard_map/ppermute | solution.py:26
  45.5 0.1 add_convert_fusion.3
  45.5 0.9 %collective-permute-start.9 = (bf16[16,3584]{1,0:T(8,128)(2,1)S(1)}, bf16[16,3584]{1,0:T(8,128)(2,1)S(1)}, u32[]{:S(2)}, u32[]{:S(2)}) collective-permute-start(bf16[16,3584]{1,0:T(8,128)(2,1)S(1)} %slice.51), channel_id=1, source_target_pairs={{0,8},{4,12},{8,0},{12,4},{16,20},{20,16},{24,28},{28,24},{1,9},{5... | collective-permute-start | bytes 344072 | tf_op jit(solution)/shard_map/ppermute | solution.py:26
  46.4 1.7 %collective-permute-done.11 = bf16[32,3584]{1,0:T(8,128)(2,1)S(1)} collective-permute-done((bf16[32,3584]{1,0:T(8,128)(2,1)S(1)}, bf16[32,3584]{1,0:T(8,128)(2,1)S(1)}, u32[]{:S(2)}, u32[]{:S(2)}) %collective-permute-start.11) | collective-permute-done | bytes 229408 | tf_op jit(solution)/shard_map/ppermute | solution.py:26
  48.1 0.1 add_convert_fusion.2
  48.1 0.9 %collective-permute-start.12 = (bf16[16,3584]{1,0:T(8,128)(2,1)S(1)}, bf16[16,3584]{1,0:T(8,128)(2,1)S(1)}, u32[]{:S(2)}, u32[]{:S(2)}) collective-permute-start(bf16[16,3584]{1,0:T(8,128)(2,1)S(1)} %slice.55), channel_id=1, source_target_pairs={{0,8},{4,12},{8,0},{12,4},{16,20},{20,16},{24,28},{28,24},{1,9},{5... | collective-permute-start | bytes 344072 | tf_op jit(solution)/shard_map/ppermute | solution.py:26
  49.0 1.4 %collective-permute-done.9 = bf16[16,3584]{1,0:T(8,128)(2,1)S(1)} collective-permute-done((bf16[16,3584]{1,0:T(8,128)(2,1)S(1)}, bf16[16,3584]{1,0:T(8,128)(2,1)S(1)}, u32[]{:S(2)}, u32[]{:S(2)}) %collective-permute-start.9) | collective-permute-done | bytes 114720 | tf_op jit(solution)/shard_map/ppermute | solution.py:26
  50.4 2.6 %collective-permute-done.12 = bf16[16,3584]{1,0:T(8,128)(2,1)S(1)} collective-permute-done((bf16[16,3584]{1,0:T(8,128)(2,1)S(1)}, bf16[16,3584]{1,0:T(8,128)(2,1)S(1)}, u32[]{:S(2)}, u32[]{:S(2)}) %collective-permute-start.12) | collective-permute-done | bytes 114720 | tf_op jit(solution)/shard_map/ppermute | solution.py:26
  53.0 0.1 fusion.2
  53.1 2.7 %collective-permute-start.13 = (bf16[4,7168]{1,0:T(4,128)(2,1)S(1)}, bf16[4,7168]{1,0:T(4,128)(2,1)S(1)}, u32[]{:S(2)}, u32[]{:S(2)}) collective-permute-start(bf16[4,7168]{1,0:T(4,128)(2,1)S(1)} %get-tuple-element.69), channel_id=1, source_target_pairs={{0,3},{1,2},{2,1},{3,0},{16,17},{17,16},{18,19},{19,18},{4,7},{5,6... | collective-permute-start | bytes 172040 | tf_op jit(solution)/shard_map/ppermute | solution.py:41
  55.8 0.0 collective-permute-start.15
  55.8 1.8 %collective-permute-start.14 = (bf16[4,7168]{1,0:T(4,128)(2,1)S(1)}, bf16[4,7168]{1,0:T(4,128)(2,1)S(1)}, u32[]{:S(2)}, u32[]{:S(2)}) collective-permute-start(bf16[4,7168]{1,0:T(4,128)(2,1)S(1)} %get-tuple-element.71), channel_id=1, source_target_pairs={{0,1},{1,0},{2,3},{3,2},{16,18},{17,19},{18,16},{19,17},{4,5},{5,4... | collective-permute-start | bytes 172040 | tf_op jit(solution)/shard_map/ppermute | solution.py:41
  57.6 1.6 %collective-permute-done.13 = bf16[4,7168]{1,0:T(4,128)(2,1)S(1)} collective-permute-done((bf16[4,7168]{1,0:T(4,128)(2,1)S(1)}, bf16[4,7168]{1,0:T(4,128)(2,1)S(1)}, u32[]{:S(2)}, u32[]{:S(2)}) %collective-permute-start.13) | collective-permute-done | bytes 57376 | tf_op jit(solution)/shard_map/ppermute | solution.py:41
  59.1 1.8 %collective-permute-done.15 = bf16[4,7168]{1,0:T(4,128)(2,1)S(1)} collective-permute-done((bf16[4,7168]{1,0:T(4,128)(2,1)S(1)}, bf16[4,7168]{1,0:T(4,128)(2,1)S(1)}, u32[]{:S(2)}, u32[]{:S(2)}) %collective-permute-start.15) | collective-permute-done | bytes 57376 | tf_op jit(solution)/shard_map/ppermute | solution.py:41
  60.9 0.0 collective-permute-done.14
  60.9 0.7 %add_convert_fusion.6 = bf16[4,7168]{1,0:T(4,128)(2,1)} fusion(bf16[4,7168]{1,0:T(4,128)(2,1)S(1)} %collective-permute-done.15, bf16[4,7168]{1,0:T(4,128)(2,1)S(1)} %collective-permute-done.14, bf16[4,7168]{1,0:T(4,128)(2,1)S(1)} %collective-permute-done.13, bf16[16,3584]{1,0:T(8,128)(2,1)S(1)} %add_convert_fusion.5, bf16[16,3584]{1,0:T(8,128)(2,1)S(1)} %add_convert_fusion.4), kind=kLoop, calls=%fused_computation.12 | loop fusion | flops 315392 | bytes 458752 | tf_op jit(solution)/shard_map/convert_element_type | solution.py:347
  (7 shorter events, 0.2 us)
Async XLA Ops:
  1.0 8.9 %collective-permute-start.2 = (bf16[4,7296]{1,0:T(4,128)(2,1)S(1)}, bf16[4,7296]{1,0:T(4,128)(2,1)S(1)}, u32[]{:S(2)}, u32[]{:S(2)}) collective-permute-start(bf16[4,7296]{1,0:T(4,128)(2,1)S(1)} %extend.1.after_ref.refs_0_), channel_id=1, source_target_pairs={{0,3},{1,2},{2,1},{3,0},{16,19},{17,18},{18,17},{19,16},{4,7},{5,6... | collective-permute-start | bytes 175112 | tf_op jit(solution)/shard_map/ppermute | solution.py:41
  6.1 5.1 %collective-permute-start.1 = (bf16[4,7296]{1,0:T(4,128)(2,1)S(1)}, bf16[4,7296]{1,0:T(4,128)(2,1)S(1)}, u32[]{:S(2)}, u32[]{:S(2)}) collective-permute-start(bf16[4,7296]{1,0:T(4,128)(2,1)S(1)} %extend.1.after_ref.refs_0_), channel_id=1, source_target_pairs={{0,2},{1,3},{2,0},{3,1},{16,18},{17,19},{18,16},{19,17},{4,6},{5,7... | collective-permute-start | bytes 175112 | tf_op jit(solution)/shard_map/ppermute | solution.py:41
  6.1 5.1 %collective-permute-start = (bf16[4,7296]{1,0:T(4,128)(2,1)S(1)}, bf16[4,7296]{1,0:T(4,128)(2,1)S(1)}, u32[]{:S(2)}, u32[]{:S(2)}) collective-permute-start(bf16[4,7296]{1,0:T(4,128)(2,1)S(1)} %extend.1.after_ref.refs_0_), channel_id=1, source_target_pairs={{0,1},{1,0},{2,3},{3,2},{16,17},{17,16},{18,19},{19,18},{4,5},{5,4... | collective-permute-start | bytes 175112 | tf_op jit(solution)/shard_map/ppermute | solution.py:41
  11.3 6.9 %collective-permute-start.3 = (bf16[16,7296]{1,0:T(8,128)(2,1)S(1)}, bf16[16,7296]{1,0:T(8,128)(2,1)S(1)}, u32[]{:S(2)}, u32[]{:S(2)}) collective-permute-start(bf16[16,7296]{1,0:T(8,128)(2,1)S(1)} %stack.2.refs_0_), channel_id=1, source_target_pairs={{0,8},{4,12},{8,0},{12,4},{16,20},{20,16},{24,28},{28,24},{1,9},{5... | collective-permute-start | bytes 700424 | tf_op jit(solution)/shard_map/ppermute | solution.py:26
  18.2 8.6 %collective-permute-start.4 = (bf16[32,7296]{1,0:T(8,128)(2,1)S(1)}, bf16[32,7296]{1,0:T(8,128)(2,1)S(1)}, u32[]{:S(2)}, u32[]{:S(2)}) collective-permute-start(bf16[32,7296]{1,0:T(8,128)(2,1)S(1)} %stack.3.refs_0_), channel_id=1, source_target_pairs={{0,4},{4,0},{8,12},{12,8},{16,24},{20,28},{24,16},{28,20},{1,5},{5... | collective-permute-start | bytes 1400840 | tf_op jit(solution)/shard_map/ppermute | solution.py:26
  23.0 3.9 %collective-permute-start.5 = (bf16[32,7296]{1,0:T(8,128)(2,1)S(1)}, bf16[32,7296]{1,0:T(8,128)(2,1)S(1)}, u32[]{:S(2)}, u32[]{:S(2)}) collective-permute-start(bf16[32,7296]{1,0:T(8,128)(2,1)S(1)} %stack.3.refs_0_), channel_id=1, source_target_pairs={{0,16},{16,0},{1,17},{17,1},{2,18},{18,2},{3,19},{19,3},{4,20},{20... | collective-permute-start | bytes 1400840 | tf_op jit(solution)/shard_map/ppermute | solution.py:45
  26.9 2.1 %collective-permute-start.6 = (bf16[32,7296]{1,0:T(8,128)(2,1)S(1)}, bf16[32,7296]{1,0:T(8,128)(2,1)S(1)}, u32[]{:S(2)}, u32[]{:S(2)}) collective-permute-start(bf16[32,7296]{1,0:T(8,128)(2,1)S(1)} %collective-permute-done.4.refs_1_), channel_id=1, source_target_pairs={{0,16},{16,0},{1,17},{17,1},{2,18},{18,2},{3,19},{19,3},{4,20},{20... | collective-permute-start | bytes 1400840 | tf_op jit(solution)/shard_map/ppermute | solution.py:45
  37.2 2.0 %collective-permute-start.7 = (bf16[64,3584]{1,0:T(8,128)(2,1)S(1)}, bf16[64,3584]{1,0:T(8,128)(2,1)S(1)}, u32[]{:S(2)}, u32[]{:S(2)}) collective-permute-start(bf16[64,3584]{1,0:T(8,128)(2,1)S(1)} %get-tuple-element.63), channel_id=1, source_target_pairs={{0,16},{16,0},{1,17},{17,1},{2,18},{18,2},{3,19},{19,3},{4,20},{20... | collective-permute-start | bytes 1376264 | tf_op jit(solution)/shard_map/ppermute | solution.py:45
  38.9 2.0 %collective-permute-start.10 = (bf16[64,3584]{1,0:T(8,128)(2,1)S(1)}, bf16[64,3584]{1,0:T(8,128)(2,1)S(1)}, u32[]{:S(2)}, u32[]{:S(2)}) collective-permute-start(bf16[64,3584]{1,0:T(8,128)(2,1)S(1)} %get-tuple-element.68), channel_id=1, source_target_pairs={{0,16},{16,0},{1,17},{17,1},{2,18},{18,2},{3,19},{19,3},{4,20},{20... | collective-permute-start | bytes 1376264 | tf_op jit(solution)/shard_map/ppermute | solution.py:45
  39.4 6.1 %collective-permute-start.8 = (bf16[32,3584]{1,0:T(8,128)(2,1)S(1)}, bf16[32,3584]{1,0:T(8,128)(2,1)S(1)}, u32[]{:S(2)}, u32[]{:S(2)}) collective-permute-start(bf16[32,3584]{1,0:T(8,128)(2,1)S(1)} %slice.49), channel_id=1, source_target_pairs={{0,4},{4,0},{8,12},{12,8},{16,24},{20,28},{24,16},{28,20},{1,5},{5... | collective-permute-start | bytes 688136 | tf_op jit(solution)/shard_map/ppermute | solution.py:26
  41.1 7.0 %collective-permute-start.11 = (bf16[32,3584]{1,0:T(8,128)(2,1)S(1)}, bf16[32,3584]{1,0:T(8,128)(2,1)S(1)}, u32[]{:S(2)}, u32[]{:S(2)}) collective-permute-start(bf16[32,3584]{1,0:T(8,128)(2,1)S(1)} %slice.53), channel_id=1, source_target_pairs={{0,4},{4,0},{8,12},{12,8},{16,24},{20,28},{24,16},{28,20},{1,5},{5... | collective-permute-start | bytes 688136 | tf_op jit(solution)/shard_map/ppermute | solution.py:26
  45.5 4.9 %collective-permute-start.9 = (bf16[16,3584]{1,0:T(8,128)(2,1)S(1)}, bf16[16,3584]{1,0:T(8,128)(2,1)S(1)}, u32[]{:S(2)}, u32[]{:S(2)}) collective-permute-start(bf16[16,3584]{1,0:T(8,128)(2,1)S(1)} %slice.51), channel_id=1, source_target_pairs={{0,8},{4,12},{8,0},{12,4},{16,20},{20,16},{24,28},{28,24},{1,9},{5... | collective-permute-start | bytes 344072 | tf_op jit(solution)/shard_map/ppermute | solution.py:26
  48.1 4.9 %collective-permute-start.12 = (bf16[16,3584]{1,0:T(8,128)(2,1)S(1)}, bf16[16,3584]{1,0:T(8,128)(2,1)S(1)}, u32[]{:S(2)}, u32[]{:S(2)}) collective-permute-start(bf16[16,3584]{1,0:T(8,128)(2,1)S(1)} %slice.55), channel_id=1, source_target_pairs={{0,8},{4,12},{8,0},{12,4},{16,20},{20,16},{24,28},{28,24},{1,9},{5... | collective-permute-start | bytes 344072 | tf_op jit(solution)/shard_map/ppermute | solution.py:26
  53.1 6.0 %collective-permute-start.13 = (bf16[4,7168]{1,0:T(4,128)(2,1)S(1)}, bf16[4,7168]{1,0:T(4,128)(2,1)S(1)}, u32[]{:S(2)}, u32[]{:S(2)}) collective-permute-start(bf16[4,7168]{1,0:T(4,128)(2,1)S(1)} %get-tuple-element.69), channel_id=1, source_target_pairs={{0,3},{1,2},{2,1},{3,0},{16,17},{17,16},{18,19},{19,18},{4,7},{5,6... | collective-permute-start | bytes 172040 | tf_op jit(solution)/shard_map/ppermute | solution.py:41
  55.8 5.1 %collective-permute-start.15 = (bf16[4,7168]{1,0:T(4,128)(2,1)S(1)}, bf16[4,7168]{1,0:T(4,128)(2,1)S(1)}, u32[]{:S(2)}, u32[]{:S(2)}) collective-permute-start(bf16[4,7168]{1,0:T(4,128)(2,1)S(1)} %get-tuple-element.70), channel_id=1, source_target_pairs={{0,2},{1,3},{2,0},{3,1},{16,19},{17,18},{18,17},{19,16},{4,6},{5,7... | collective-permute-start | bytes 172040 | tf_op jit(solution)/shard_map/ppermute | solution.py:41
  55.8 5.1 %collective-permute-start.14 = (bf16[4,7168]{1,0:T(4,128)(2,1)S(1)}, bf16[4,7168]{1,0:T(4,128)(2,1)S(1)}, u32[]{:S(2)}, u32[]{:S(2)}) collective-permute-start(bf16[4,7168]{1,0:T(4,128)(2,1)S(1)} %get-tuple-element.71), channel_id=1, source_target_pairs={{0,1},{1,0},{2,3},{3,2},{16,18},{17,19},{18,16},{19,17},{4,5},{5,4... | collective-permute-start | bytes 172040 | tf_op jit(solution)/shard_map/ppermute | solution.py:41

commit v15 on v14

--- a/solution.py
+++ b/solution.py
@@ -110,41 +110,42 @@
 
 def gather_rows(block, w_gate, w_up, w_down):
     experts, sects, lanes = w_gate.shape[0], lax.axis_size("sect"), lax.axis_size("dev")
-    early = early_columns(w_down)
-    gates, ups, downs = ([(w, e, w.shape[2]) for e in range(experts)] for w in (w_gate, w_up, w_down))
-    downs = [(w, e, early) for w, e, _ in downs]
+    half, early = w_down.shape[1] // 2, early_columns(w_down)
+    whole = [(w, e, 0, w.shape[1], w.shape[2]) for w in (w_gate, w_up) for e in range(experts)]
+    parts = [(w_down, e, r, half, early) for e in range(experts) for r in (0, half)]
     held, token = {}, block
 
-    def fetch_next(wanted, token):
-        weight, expert, columns = wanted.pop(0)
-        held[id(weight), expert], token = fetch(weight, expert, columns, token)
+    def fetch_next(wholes, part, token):
+        wanted = [whole.pop(0) for _ in range(min(wholes, len(whole)))] + parts[:part]
+        del parts[:part]
+        if not wanted:
+            return token
+        *arrays, token = fetch(wanted, token)
+        for (weight, expert, row, _, _), array in zip(wanted, arrays):
+            held[id(weight), expert, row] = array
         return token
 
     arrived = [swap_line(block, (m,) * sects) for m in range(1, lanes)]
-    token = fetch_next(gates, token)
+    token = fetch_next(1, 1, token)
     arrived, token = lax.optimization_barrier((arrived, token))
     line = stack([block, *arrived], line_orders())
     rounds = rounds_of()
-    for number, masks in enumerate(rounds[:-1]):
+    for masks in rounds[:-1]:
         arrived = swap(line, masks)
-        if gates:
-            token = fetch_next(gates, token)
-            if len(downs) > 1:
-                token = fetch_next(downs, token)
+        token = fetch_next(1, 1, token)
         arrived, token = lax.optimization_barrier((arrived, token))
         line = stack([line, arrived])
     last = swap(line, rounds[-1])
-    token = fetch_next(gates if gates else ups, token)
+    token = fetch_next(1, 1, token)
     mine, token = lax.optimization_barrier((line, token))
     other = swap_core(mine)
-    while gates or ups:
-        token = fetch_next(gates if gates else ups, token)
+    token = fetch_next(len(whole), 0, token)
     last, other, token = lax.optimization_barrier((last, other, token))
     last_other = swap_core(last)
-    while downs:
-        token = fetch_next(downs, token)
+    token = fetch_next(0, len(parts), token)
     last_other, token = lax.optimization_barrier((last_other, token))
-    weights = [held[id(w), e] for w in (w_gate, w_up, w_down) for e in range(experts)]
+    weights = [held[id(w), e, 0] for w in (w_gate, w_up) for e in range(experts)]
+    weights += [held[id(w_down), e, r] for e in range(experts) for r in (0, half)]
     return [line, last, other, last_other], weights, token
 
 
@@ -176,14 +177,14 @@
 def expert_kernel(entry_count, experts, width, token_ref, *refs):
     pieces, refs = refs[:entry_count], refs[entry_count:]
     gate_refs, up_refs, early_refs, refs = (
-        refs[:experts], refs[experts:2 * experts], refs[2 * experts:3 * experts], refs[3 * experts:]
+        refs[:experts], refs[experts:2 * experts], refs[2 * experts:4 * experts], refs[4 * experts:]
     )
     down_hbm, hidden_ref, keep_ref, send_ref = refs[:4]
     down_refs, (rows_ref, value_ref, sems) = refs[4:4 + experts], refs[4 + experts:]
     hidden = gate_refs[0].shape[2]
     place = lax.axis_index("sect") * lax.axis_size("grp") + lax.axis_index("grp")
     first = place * experts
-    block = min(256, hidden)
+    block = min(512, hidden)
     blocks = width // hidden
 
     late = [
@@ -239,9 +240,20 @@
         down_block(step, hidden_ref, [ref[0, span, :] for ref in down_refs], keep_ref, send_ref)
 
 
-def fetch_kernel(expert, after_ref, source_ref, target_ref, token_ref, sems):
-    columns = pl.ds(0, target_ref.shape[2])
-    copies = weight_copies(source_ref.at[pl.ds(expert, 1), :, columns], target_ref, sems, 0)
+def fetch_kernel(wanted, after_ref, *refs):
+    count = len(wanted)
+    sources, targets, (token_ref, sems) = refs[:count], refs[count:2 * count], refs[2 * count:]
+    copies = []
+    for i, (_, expert, first, rows, columns) in enumerate(wanted):
+        depth = rows // sems.shape[1]
+        copies += [
+            pltpu.make_async_copy(
+                sources[i].at[expert, pl.ds(first + p * depth, depth), pl.ds(0, columns)],
+                targets[i].at[0, pl.ds(p * depth, depth)],
+                sems.at[i, p],
+            )
+            for p in range(sems.shape[1])
+        ]
     for copy in copies:
         copy.start()
     token_ref[...] = jnp.zeros_like(token_ref)
@@ -249,37 +261,26 @@
         copy.wait()
 
 
-def weight_copies(source_ref, target_ref, sems, expert):
-    parts = sems.shape[1]
-    depth = source_ref.shape[1] // parts
-    return [
-        pltpu.make_async_copy(
-            source_ref.at[expert, pl.ds(p * depth, depth)],
-            target_ref.at[expert, pl.ds(p * depth, depth)],
-            sems.at[expert, p],
-        )
-        for p in range(parts)
-    ]
-
-
-def fetch(weight, expert, columns, after):
+def fetch(wanted, after):
     in_hbm = pl.BlockSpec(memory_space=pl.ANY)
-    in_vmem = pl.BlockSpec(memory_space=pltpu.VMEM)
+    whole = pl.BlockSpec(memory_space=pltpu.VMEM)
     return pl.pallas_call(
-        functools.partial(fetch_kernel, expert),
+        functools.partial(fetch_kernel, [(None, *w[1:]) for w in wanted]),
         out_shape=(
-            pltpu.VMEM((1, weight.shape[1], columns), weight.dtype),
+            *(pltpu.VMEM((1, rows, columns), w.dtype) for w, _, _, rows, columns in wanted),
             jax.ShapeDtypeStruct((8, 128), jnp.float32),
         ),
-        in_specs=[in_hbm, in_hbm],
-        out_specs=(in_vmem, in_vmem),
-        scratch_shapes=[pltpu.SemaphoreType.DMA((1, 8))],
+        in_specs=[in_hbm] * (1 + len(wanted)),
+        out_specs=(whole,) * (1 + len(wanted)),
+        scratch_shapes=[pltpu.SemaphoreType.DMA((len(wanted), 8))],
         compiler_params=pltpu.CompilerParams(vmem_limit_bytes=VMEM_LIMIT),
         cost_estimate=pl.CostEstimate(
-            flops=0, bytes_accessed=2 * weight.shape[1] * columns, transcendentals=0
+            flops=0,
+            bytes_accessed=2 * sum(rows * columns for _, _, _, rows, columns in wanted),
+            transcendentals=0,
         ),
         name="fetch",
-    )(after, pltpu.with_memory_space_constraint(weight, pltpu.HBM))
+    )(after, *(pltpu.with_memory_space_constraint(w[0], pltpu.HBM) for w in wanted))
 
 
 def in_vmem(values):

time: 61.8 us -> 61.6 us (level)
  starting transfers between devices: 18.9 us -> 20.5 us
  waiting for transfers between devices: 14.1 us -> 13 us
  Pallas kernels: 27.3 us -> 26.5 us
    ppermute x6, starting transfers between devices: 7.94 us -> 9.01 us  [swap(): return lax.ppermute(value, ('sect', 'grp'), pairs)]
    pallas_call x6 -> x5, Pallas kernels: 16.8 us -> 16 us  [fetch(): pl.pallas_call(functools.partial(fetch_kernel, [(None, *w[1:]) for w in w...]
    ppermute x6, waiting for transfers between devices: 9.22 us -> 8.48 us  [swap(): return lax.ppermute(value, ('sect', 'grp'), pairs)]
  transfers between devices with their start and end apart: 16 -> 16, of which waited for: 9 -> 10; matrix products, arithmetic and copies ran while one was open for 1% -> 1% of each run, Pallas kernels for 29% -> 28%
where the time goes in v15:
time: 61.6 us; the launch traced here: 61.4 us
  Pallas kernels  26.5 us (43%)
  starting transfers between devices  20.5 us (33%)
  waiting for transfers between devices  13 us (21%)
  other arithmetic  1.14 us (2%)
    pallas_call x5, Pallas kernels, fetch(): pl.pallas_call(functools.partial(fetch_kernel, [(None, *w[1:]) for w in w...  16 us
    ppermute x6, starting transfers between devices, swap_line(): return lax.ppermute(value, ('sect', 'dev'), pairs)  10.2 us
    ppermute x6, starting transfers between devices, swap(): return lax.ppermute(value, ('sect', 'grp'), pairs)  9.01 us
    ppermute x6, waiting for transfers between devices, swap(): return lax.ppermute(value, ('sect', 'grp'), pairs)  8.48 us
    pallas_call x1, Pallas kernels, expert_call(): pl.pallas_call(functools.partial(expert_kernel, len(entries), experts, wi...  8.27 us
    ppermute x6, waiting for transfers between devices, swap_line(): return lax.ppermute(value, ('sect', 'dev'), pairs)  4.39 us
    ppermute x4, starting transfers between devices, swap_core(): return lax.ppermute(value, 'sect', [(0, 1), (1, 0)])  1.27 us
  transfers between devices with their start and end apart: 16, of which 10 were waited for; matrix products, arithmetic and copies ran while one was open for 1% of the time, Pallas kernels for 28%

profile of v15, /device:TPU:0, one launch (start us, length us, event | category | flops | bytes accessed | tf_op | source)
XLA Modules:
  0.0 61.4 jit_solution(6031947172971816390)
XLA Ops:
  0.0 1.0 %extend.1.after_ref.refs_0_ = bf16[4,7296]{1,0:T(4,128)(2,1)S(1)} custom-call(bf16[4,7168]{1,0:T(4,128)(2,1)} %tokens_hbm.1, s32[4,8]{1,0:T(4,128)} %ids_hbm.1, f32[4,8]{1,0:T(4,128)} %weights_hbm.1), custom_call_target="tpu_custom_call" | custom-call | tf_op jit(solution)/shard_map/extend/pallas_call | solution.py:81
  1.0 5.1 %collective-permute-start.2 = (bf16[4,7296]{1,0:T(4,128)(2,1)S(1)}, bf16[4,7296]{1,0:T(4,128)(2,1)S(1)}, u32[]{:S(2)}, u32[]{:S(2)}) collective-permute-start(bf16[4,7296]{1,0:T(4,128)(2,1)S(1)} %extend.1.after_ref.refs_0_), channel_id=1, source_target_pairs={{0,3},{1,2},{2,1},{3,0},{16,19},{17,18},{18,17},{19,16},{4,7},{5,6... | collective-permute-start | bytes 175112 | tf_op jit(solution)/shard_map/ppermute | solution.py:41
  6.1 0.0 collective-permute-start.1
  6.1 0.6 %collective-permute-start = (bf16[4,7296]{1,0:T(4,128)(2,1)S(1)}, bf16[4,7296]{1,0:T(4,128)(2,1)S(1)}, u32[]{:S(2)}, u32[]{:S(2)}) collective-permute-start(bf16[4,7296]{1,0:T(4,128)(2,1)S(1)} %extend.1.after_ref.refs_0_), channel_id=1, source_target_pairs={{0,1},{1,0},{2,3},{3,2},{16,17},{17,16},{18,19},{19,18},{4,5},{5,4... | collective-permute-start | bytes 175112 | tf_op jit(solution)/shard_map/ppermute | solution.py:41
  6.7 3.7 %fetch.5 = (bf16[1,7168,512]{2,1,0:T(8,128)(2,1)S(1)}, bf16[1,256,3584]{2,1,0:T(8,128)(2,1)S(1)}, f32[8,128]{1,0:T(8,128)S(1)}) custom-call(bf16[4,7296]{1,0:T(4,128)(2,1)S(1)} %extend.1.after_ref.refs_0_, bf16[2,7168,512]{2,1,0:T(8,128)(2,1)} %refs_0_.6, bf16[2,512,7168]{2,1,0:T(8,128)(2,1)} %refs_12_.1), custom_call_target="tpu_custom_call" | custom-call | bytes 9175040 | tf_op jit(solution)/shard_map/fetch/pallas_call | solution.py:267
  10.5 0.0 collective-permute-done.2.refs_3_
  10.5 0.7 %collective-permute-done.1.refs_2_ = bf16[4,7296]{1,0:T(4,128)(2,1)S(1)} collective-permute-done((bf16[4,7296]{1,0:T(4,128)(2,1)S(1)}, bf16[4,7296]{1,0:T(4,128)(2,1)S(1)}, u32[]{:S(2)}, u32[]{:S(2)}) %collective-permute-start.1) | collective-permute-done | bytes 58400 | tf_op jit(solution)/shard_map/ppermute | solution.py:41
  11.2 0.0 collective-permute-done.refs_1_
  11.2 0.1 stack.2.refs_0_
  11.3 1.7 %collective-permute-start.3 = (bf16[16,7296]{1,0:T(8,128)(2,1)S(1)}, bf16[16,7296]{1,0:T(8,128)(2,1)S(1)}, u32[]{:S(2)}, u32[]{:S(2)}) collective-permute-start(bf16[16,7296]{1,0:T(8,128)(2,1)S(1)} %stack.2.refs_0_), channel_id=1, source_target_pairs={{0,8},{4,12},{8,0},{12,4},{16,20},{20,16},{24,28},{28,24},{1,9},{5... | collective-permute-start | bytes 700424 | tf_op jit(solution)/shard_map/ppermute | solution.py:26
  12.9 3.7 %fetch.6 = (bf16[1,7168,512]{2,1,0:T(8,128)(2,1)S(1)}, bf16[1,256,3584]{2,1,0:T(8,128)(2,1)S(1)}, f32[8,128]{1,0:T(8,128)S(1)}) custom-call(f32[8,128]{1,0:T(8,128)S(1)} %get-tuple-element.42.after_ref, bf16[2,7168,512]{2,1,0:T(8,128)(2,1)} %refs_0_.6, bf16[2,512,7168]{2,1,0:T(8,128)(2,1)} %refs_12_.1), custom_call_target="tpu_custom_call" | custom-call | bytes 9175040 | tf_op jit(solution)/shard_map/fetch/pallas_call | solution.py:267
  16.6 0.7 %collective-permute-done.3.refs_1_ = bf16[16,7296]{1,0:T(8,128)(2,1)S(1)} collective-permute-done((bf16[16,7296]{1,0:T(8,128)(2,1)S(1)}, bf16[16,7296]{1,0:T(8,128)(2,1)S(1)}, u32[]{:S(2)}, u32[]{:S(2)}) %collective-permute-start.3) | collective-permute-done | bytes 233504 | tf_op jit(solution)/shard_map/ppermute | solution.py:26
  17.4 1.6 %collective-permute-start.4 = (bf16[32,7296]{1,0:T(8,128)(2,1)S(1)}, bf16[32,7296]{1,0:T(8,128)(2,1)S(1)}, u32[]{:S(2)}, u32[]{:S(2)}) collective-permute-start(bf16[32,7296]{1,0:T(8,128)(2,1)S(1)} %stack.3.refs_0_), channel_id=1, source_target_pairs={{0,4},{4,0},{8,12},{12,8},{16,24},{20,28},{24,16},{28,20},{1,5},{5... | collective-permute-start | bytes 1400840 | tf_op jit(solution)/shard_map/ppermute | solution.py:26
  19.1 3.8 %fetch.7 = (bf16[1,7168,512]{2,1,0:T(8,128)(2,1)S(1)}, bf16[1,256,3584]{2,1,0:T(8,128)(2,1)S(1)}, f32[8,128]{1,0:T(8,128)S(1)}) custom-call(f32[8,128]{1,0:T(8,128)S(1)} %get-tuple-element.45.after_ref, bf16[2,7168,512]{2,1,0:T(8,128)(2,1)} %refs_0_.8, bf16[2,512,7168]{2,1,0:T(8,128)(2,1)} %refs_12_.1), custom_call_target="tpu_custom_call" | custom-call | bytes 9175040 | tf_op jit(solution)/shard_map/fetch/pallas_call | solution.py:267
  22.9 0.1 collective-permute-start.5
  22.9 3.2 %fetch.8 = (bf16[1,7168,512]{2,1,0:T(8,128)(2,1)S(1)}, f32[8,128]{1,0:T(8,128)S(1)}) custom-call(f32[8,128]{1,0:T(8,128)S(1)} %get-tuple-element.48.after_ref, bf16[2,7168,512]{2,1,0:T(8,128)(2,1)} %refs_0_.8), custom_call_target="tpu_custom_call" | custom-call | bytes 7340032 | tf_op jit(solution)/shard_map/fetch/pallas_call | solution.py:267
  26.1 0.0 collective-permute-done.4.refs_1_
  26.1 0.0 collective-permute-done.5.refs_2_
  26.1 0.6 collective-permute-start.6
  26.7 1.6 %fetch.9 = (bf16[1,256,3584]{2,1,0:T(8,128)(2,1)S(1)}, f32[8,128]{1,0:T(8,128)S(1)}) custom-call(f32[8,128]{1,0:T(8,128)S(1)} %get-tuple-element.51.after_ref, bf16[2,512,7168]{2,1,0:T(8,128)(2,1)} %refs_12_.1), custom_call_target="tpu_custom_call" | custom-call | bytes 1835008 | tf_op jit(solution)/shard_map/fetch/pallas_call | solution.py:267
  28.3 0.0 collective-permute-done.6.refs_3_
  28.3 8.3 %experts.1 = (bf16[128,1024]{1,0:T(8,128)(2,1)S(1)}, bf16[64,3584]{1,0:T(8,128)(2,1)S(1)}, bf16[64,3584]{1,0:T(8,128)(2,1)S(1)}, bf16[1,7168,512]{2,1,0:T(8,128)(2,1)S(1)}, bf16[1,7168,512]{2,1,0:T(8,128)(2,1)S(1)}) custom-call(f32[8,128]{1,0:T(8,128)S(1)} %get-tuple-element.53.token_ref, ...), custom_call_target="tpu_custom_call", output_to_operand_aliasing={{3}: (5, {}), {4}: (6, {})} | custom-call | flops 4697620480 | bytes 14680064 | tf_op jit(solution)/shard_map/experts/pallas_call | solution.py:299
  36.6 0.2 collective-permute-start.7
  36.9 1.1 %down.1 = (bf16[64,3584]{1,0:T(8,128)(2,1)S(1)}, bf16[64,3584]{1,0:T(8,128)(2,1)S(1)}) custom-call(bf16[128,1024]{1,0:T(8,128)(2,1)S(1)} %get-tuple-element.66.hidden_ref, bf16[1,7168,512]{2,1,0:T(8,128)(2,1)S(1)} %get-tuple-element.67.refs_0_, bf16[1,7168,512]{2,1,0:T(8,128)(2,1)S(1)} %get-tuple-element.68.refs_1_), custom_call_target="tpu_custom_call" | custom-call | flops 939524096 | bytes 917504 | tf_op jit(solution)/shard_map/down/pallas_call | solution.py:328
  38.0 0.4 collective-permute-start.10
  38.4 0.1 collective-permute-done.7
  38.5 0.1 add_convert_fusion.1
  38.6 1.2 %collective-permute-start.8 = (bf16[32,3584]{1,0:T(8,128)(2,1)S(1)}, bf16[32,3584]{1,0:T(8,128)(2,1)S(1)}, u32[]{:S(2)}, u32[]{:S(2)}) collective-permute-start(bf16[32,3584]{1,0:T(8,128)(2,1)S(1)} %slice.49), channel_id=1, source_target_pairs={{0,4},{4,0},{8,12},{12,8},{16,24},{20,28},{24,16},{28,20},{1,5},{5... | collective-permute-start | bytes 688136 | tf_op jit(solution)/shard_map/ppermute | solution.py:26
  39.8 0.1 collective-permute-done.10
  39.9 0.1 add_convert_fusion
  40.0 1.3 %collective-permute-start.11 = (bf16[32,3584]{1,0:T(8,128)(2,1)S(1)}, bf16[32,3584]{1,0:T(8,128)(2,1)S(1)}, u32[]{:S(2)}, u32[]{:S(2)}) collective-permute-start(bf16[32,3584]{1,0:T(8,128)(2,1)S(1)} %slice.53), channel_id=1, source_target_pairs={{0,4},{4,0},{8,12},{12,8},{16,24},{20,28},{24,16},{28,20},{1,5},{5... | collective-permute-start | bytes 688136 | tf_op jit(solution)/shard_map/ppermute | solution.py:26
  41.4 3.4 %collective-permute-done.8 = bf16[32,3584]{1,0:T(8,128)(2,1)S(1)} collective-permute-done((bf16[32,3584]{1,0:T(8,128)(2,1)S(1)}, bf16[32,3584]{1,0:T(8,128)(2,1)S(1)}, u32[]{:S(2)}, u32[]{:S(2)}) %collective-permute-start.8) | collective-permute-done | bytes 229408 | tf_op jit(solution)/shard_map/ppermute | solution.py:26
  44.7 0.1 add_convert_fusion.3
  44.8 1.6 %collective-permute-start.9 = (bf16[16,3584]{1,0:T(8,128)(2,1)S(1)}, bf16[16,3584]{1,0:T(8,128)(2,1)S(1)}, u32[]{:S(2)}, u32[]{:S(2)}) collective-permute-start(bf16[16,3584]{1,0:T(8,128)(2,1)S(1)} %slice.51), channel_id=1, source_target_pairs={{0,8},{4,12},{8,0},{12,4},{16,20},{20,16},{24,28},{28,24},{1,9},{5... | collective-permute-start | bytes 344072 | tf_op jit(solution)/shard_map/ppermute | solution.py:26
  46.4 1.1 %collective-permute-done.11 = bf16[32,3584]{1,0:T(8,128)(2,1)S(1)} collective-permute-done((bf16[32,3584]{1,0:T(8,128)(2,1)S(1)}, bf16[32,3584]{1,0:T(8,128)(2,1)S(1)}, u32[]{:S(2)}, u32[]{:S(2)}) %collective-permute-start.11) | collective-permute-done | bytes 229408 | tf_op jit(solution)/shard_map/ppermute | solution.py:26
  47.5 0.1 add_convert_fusion.2
  47.6 1.6 %collective-permute-start.12 = (bf16[16,3584]{1,0:T(8,128)(2,1)S(1)}, bf16[16,3584]{1,0:T(8,128)(2,1)S(1)}, u32[]{:S(2)}, u32[]{:S(2)}) collective-permute-start(bf16[16,3584]{1,0:T(8,128)(2,1)S(1)} %slice.55), channel_id=1, source_target_pairs={{0,8},{4,12},{8,0},{12,4},{16,20},{20,16},{24,28},{28,24},{1,9},{5... | collective-permute-start | bytes 344072 | tf_op jit(solution)/shard_map/ppermute | solution.py:26
  49.2 0.5 collective-permute-done.9
  49.7 2.8 %collective-permute-done.12 = bf16[16,3584]{1,0:T(8,128)(2,1)S(1)} collective-permute-done((bf16[16,3584]{1,0:T(8,128)(2,1)S(1)}, bf16[16,3584]{1,0:T(8,128)(2,1)S(1)}, u32[]{:S(2)}, u32[]{:S(2)}) %collective-permute-start.12) | collective-permute-done | bytes 114720 | tf_op jit(solution)/shard_map/ppermute | solution.py:26
  52.5 0.1 fusion.2
  52.6 3.0 %collective-permute-start.13 = (bf16[4,7168]{1,0:T(4,128)(2,1)S(1)}, bf16[4,7168]{1,0:T(4,128)(2,1)S(1)}, u32[]{:S(2)}, u32[]{:S(2)}) collective-permute-start(bf16[4,7168]{1,0:T(4,128)(2,1)S(1)} %get-tuple-element.71), channel_id=1, source_target_pairs={{0,3},{1,2},{2,1},{3,0},{16,17},{17,16},{18,19},{19,18},{4,7},{5,6... | collective-permute-start | bytes 172040 | tf_op jit(solution)/shard_map/ppermute | solution.py:41
  55.6 0.0 collective-permute-start.15
  55.6 1.4 %collective-permute-start.14 = (bf16[4,7168]{1,0:T(4,128)(2,1)S(1)}, bf16[4,7168]{1,0:T(4,128)(2,1)S(1)}, u32[]{:S(2)}, u32[]{:S(2)}) collective-permute-start(bf16[4,7168]{1,0:T(4,128)(2,1)S(1)} %get-tuple-element.73), channel_id=1, source_target_pairs={{0,1},{1,0},{2,3},{3,2},{16,18},{17,19},{18,16},{19,17},{4,5},{5,4... | collective-permute-start | bytes 172040 | tf_op jit(solution)/shard_map/ppermute | solution.py:41
  57.0 1.6 %collective-permute-done.13 = bf16[4,7168]{1,0:T(4,128)(2,1)S(1)} collective-permute-done((bf16[4,7168]{1,0:T(4,128)(2,1)S(1)}, bf16[4,7168]{1,0:T(4,128)(2,1)S(1)}, u32[]{:S(2)}, u32[]{:S(2)}) %collective-permute-start.13) | collective-permute-done | bytes 57376 | tf_op jit(solution)/shard_map/ppermute | solution.py:41
  58.6 2.1 %collective-permute-done.15 = bf16[4,7168]{1,0:T(4,128)(2,1)S(1)} collective-permute-done((bf16[4,7168]{1,0:T(4,128)(2,1)S(1)}, bf16[4,7168]{1,0:T(4,128)(2,1)S(1)}, u32[]{:S(2)}, u32[]{:S(2)}) %collective-permute-start.15) | collective-permute-done | bytes 57376 | tf_op jit(solution)/shard_map/ppermute | solution.py:41
  60.7 0.0 collective-permute-done.14
  60.7 0.7 %add_convert_fusion.6 = bf16[4,7168]{1,0:T(4,128)(2,1)} fusion(bf16[4,7168]{1,0:T(4,128)(2,1)S(1)} %collective-permute-done.15, bf16[4,7168]{1,0:T(4,128)(2,1)S(1)} %collective-permute-done.14, bf16[4,7168]{1,0:T(4,128)(2,1)S(1)} %collective-permute-done.13, bf16[16,3584]{1,0:T(8,128)(2,1)S(1)} %add_convert_fusion.5, bf16[16,3584]{1,0:T(8,128)(2,1)S(1)} %add_convert_fusion.4), kind=kLoop, calls=%fused_computation.12 | loop fusion | flops 315392 | bytes 458752 | tf_op jit(solution)/shard_map/convert_element_type | solution.py:348
  (7 shorter events, 0.1 us)
Async XLA Ops:
  1.0 9.5 %collective-permute-start.2 = (bf16[4,7296]{1,0:T(4,128)(2,1)S(1)}, bf16[4,7296]{1,0:T(4,128)(2,1)S(1)}, u32[]{:S(2)}, u32[]{:S(2)}) collective-permute-start(bf16[4,7296]{1,0:T(4,128)(2,1)S(1)} %extend.1.after_ref.refs_0_), channel_id=1, source_target_pairs={{0,3},{1,2},{2,1},{3,0},{16,19},{17,18},{18,17},{19,16},{4,7},{5,6... | collective-permute-start | bytes 175112 | tf_op jit(solution)/shard_map/ppermute | solution.py:41
  6.1 5.1 %collective-permute-start.1 = (bf16[4,7296]{1,0:T(4,128)(2,1)S(1)}, bf16[4,7296]{1,0:T(4,128)(2,1)S(1)}, u32[]{:S(2)}, u32[]{:S(2)}) collective-permute-start(bf16[4,7296]{1,0:T(4,128)(2,1)S(1)} %extend.1.after_ref.refs_0_), channel_id=1, source_target_pairs={{0,2},{1,3},{2,0},{3,1},{16,18},{17,19},{18,16},{19,17},{4,6},{5,7... | collective-permute-start | bytes 175112 | tf_op jit(solution)/shard_map/ppermute | solution.py:41
  6.1 5.1 %collective-permute-start = (bf16[4,7296]{1,0:T(4,128)(2,1)S(1)}, bf16[4,7296]{1,0:T(4,128)(2,1)S(1)}, u32[]{:S(2)}, u32[]{:S(2)}) collective-permute-start(bf16[4,7296]{1,0:T(4,128)(2,1)S(1)} %extend.1.after_ref.refs_0_), channel_id=1, source_target_pairs={{0,1},{1,0},{2,3},{3,2},{16,17},{17,16},{18,19},{19,18},{4,5},{5,4... | collective-permute-start | bytes 175112 | tf_op jit(solution)/shard_map/ppermute | solution.py:41
  11.3 6.1 %collective-permute-start.3 = (bf16[16,7296]{1,0:T(8,128)(2,1)S(1)}, bf16[16,7296]{1,0:T(8,128)(2,1)S(1)}, u32[]{:S(2)}, u32[]{:S(2)}) collective-permute-start(bf16[16,7296]{1,0:T(8,128)(2,1)S(1)} %stack.2.refs_0_), channel_id=1, source_target_pairs={{0,8},{4,12},{8,0},{12,4},{16,20},{20,16},{24,28},{28,24},{1,9},{5... | collective-permute-start | bytes 700424 | tf_op jit(solution)/shard_map/ppermute | solution.py:26
  17.4 8.7 %collective-permute-start.4 = (bf16[32,7296]{1,0:T(8,128)(2,1)S(1)}, bf16[32,7296]{1,0:T(8,128)(2,1)S(1)}, u32[]{:S(2)}, u32[]{:S(2)}) collective-permute-start(bf16[32,7296]{1,0:T(8,128)(2,1)S(1)} %stack.3.refs_0_), channel_id=1, source_target_pairs={{0,4},{4,0},{8,12},{12,8},{16,24},{20,28},{24,16},{28,20},{1,5},{5... | collective-permute-start | bytes 1400840 | tf_op jit(solution)/shard_map/ppermute | solution.py:26
  22.9 3.3 %collective-permute-start.5 = (bf16[32,7296]{1,0:T(8,128)(2,1)S(1)}, bf16[32,7296]{1,0:T(8,128)(2,1)S(1)}, u32[]{:S(2)}, u32[]{:S(2)}) collective-permute-start(bf16[32,7296]{1,0:T(8,128)(2,1)S(1)} %stack.3.refs_0_), channel_id=1, source_target_pairs={{0,16},{16,0},{1,17},{17,1},{2,18},{18,2},{3,19},{19,3},{4,20},{20... | collective-permute-start | bytes 1400840 | tf_op jit(solution)/shard_map/ppermute | solution.py:45
  26.1 2.2 %collective-permute-start.6 = (bf16[32,7296]{1,0:T(8,128)(2,1)S(1)}, bf16[32,7296]{1,0:T(8,128)(2,1)S(1)}, u32[]{:S(2)}, u32[]{:S(2)}) collective-permute-start(bf16[32,7296]{1,0:T(8,128)(2,1)S(1)} %collective-permute-done.4.refs_1_), channel_id=1, source_target_pairs={{0,16},{16,0},{1,17},{17,1},{2,18},{18,2},{3,19},{19,3},{4,20},{20... | collective-permute-start | bytes 1400840 | tf_op jit(solution)/shard_map/ppermute | solution.py:45
  36.6 1.9 %collective-permute-start.7 = (bf16[64,3584]{1,0:T(8,128)(2,1)S(1)}, bf16[64,3584]{1,0:T(8,128)(2,1)S(1)}, u32[]{:S(2)}, u32[]{:S(2)}) collective-permute-start(bf16[64,3584]{1,0:T(8,128)(2,1)S(1)} %get-tuple-element.65), channel_id=1, source_target_pairs={{0,16},{16,0},{1,17},{17,1},{2,18},{18,2},{3,19},{19,3},{4,20},{20... | collective-permute-start | bytes 1376264 | tf_op jit(solution)/shard_map/ppermute | solution.py:45
  38.0 1.9 %collective-permute-start.10 = (bf16[64,3584]{1,0:T(8,128)(2,1)S(1)}, bf16[64,3584]{1,0:T(8,128)(2,1)S(1)}, u32[]{:S(2)}, u32[]{:S(2)}) collective-permute-start(bf16[64,3584]{1,0:T(8,128)(2,1)S(1)} %get-tuple-element.70), channel_id=1, source_target_pairs={{0,16},{16,0},{1,17},{17,1},{2,18},{18,2},{3,19},{19,3},{4,20},{20... | collective-permute-start | bytes 1376264 | tf_op jit(solution)/shard_map/ppermute | solution.py:45
  38.6 6.1 %collective-permute-start.8 = (bf16[32,3584]{1,0:T(8,128)(2,1)S(1)}, bf16[32,3584]{1,0:T(8,128)(2,1)S(1)}, u32[]{:S(2)}, u32[]{:S(2)}) collective-permute-start(bf16[32,3584]{1,0:T(8,128)(2,1)S(1)} %slice.49), channel_id=1, source_target_pairs={{0,4},{4,0},{8,12},{12,8},{16,24},{20,28},{24,16},{28,20},{1,5},{5... | collective-permute-start | bytes 688136 | tf_op jit(solution)/shard_map/ppermute | solution.py:26
  40.0 7.5 %collective-permute-start.11 = (bf16[32,3584]{1,0:T(8,128)(2,1)S(1)}, bf16[32,3584]{1,0:T(8,128)(2,1)S(1)}, u32[]{:S(2)}, u32[]{:S(2)}) collective-permute-start(bf16[32,3584]{1,0:T(8,128)(2,1)S(1)} %slice.53), channel_id=1, source_target_pairs={{0,4},{4,0},{8,12},{12,8},{16,24},{20,28},{24,16},{28,20},{1,5},{5... | collective-permute-start | bytes 688136 | tf_op jit(solution)/shard_map/ppermute | solution.py:26
  44.8 4.9 %collective-permute-start.9 = (bf16[16,3584]{1,0:T(8,128)(2,1)S(1)}, bf16[16,3584]{1,0:T(8,128)(2,1)S(1)}, u32[]{:S(2)}, u32[]{:S(2)}) collective-permute-start(bf16[16,3584]{1,0:T(8,128)(2,1)S(1)} %slice.51), channel_id=1, source_target_pairs={{0,8},{4,12},{8,0},{12,4},{16,20},{20,16},{24,28},{28,24},{1,9},{5... | collective-permute-start | bytes 344072 | tf_op jit(solution)/shard_map/ppermute | solution.py:26
  47.6 4.9 %collective-permute-start.12 = (bf16[16,3584]{1,0:T(8,128)(2,1)S(1)}, bf16[16,3584]{1,0:T(8,128)(2,1)S(1)}, u32[]{:S(2)}, u32[]{:S(2)}) collective-permute-start(bf16[16,3584]{1,0:T(8,128)(2,1)S(1)} %slice.55), channel_id=1, source_target_pairs={{0,8},{4,12},{8,0},{12,4},{16,20},{20,16},{24,28},{28,24},{1,9},{5... | collective-permute-start | bytes 344072 | tf_op jit(solution)/shard_map/ppermute | solution.py:26
  52.6 6.0 %collective-permute-start.13 = (bf16[4,7168]{1,0:T(4,128)(2,1)S(1)}, bf16[4,7168]{1,0:T(4,128)(2,1)S(1)}, u32[]{:S(2)}, u32[]{:S(2)}) collective-permute-start(bf16[4,7168]{1,0:T(4,128)(2,1)S(1)} %get-tuple-element.71), channel_id=1, source_target_pairs={{0,3},{1,2},{2,1},{3,0},{16,17},{17,16},{18,19},{19,18},{4,7},{5,6... | collective-permute-start | bytes 172040 | tf_op jit(solution)/shard_map/ppermute | solution.py:41
  55.6 5.1 %collective-permute-start.15 = (bf16[4,7168]{1,0:T(4,128)(2,1)S(1)}, bf16[4,7168]{1,0:T(4,128)(2,1)S(1)}, u32[]{:S(2)}, u32[]{:S(2)}) collective-permute-start(bf16[4,7168]{1,0:T(4,128)(2,1)S(1)} %get-tuple-element.72), channel_id=1, source_target_pairs={{0,2},{1,3},{2,0},{3,1},{16,19},{17,18},{18,17},{19,16},{4,6},{5,7... | collective-permute-start | bytes 172040 | tf_op jit(solution)/shard_map/ppermute | solution.py:41
  55.6 5.1 %collective-permute-start.14 = (bf16[4,7168]{1,0:T(4,128)(2,1)S(1)}, bf16[4,7168]{1,0:T(4,128)(2,1)S(1)}, u32[]{:S(2)}, u32[]{:S(2)}) collective-permute-start(bf16[4,7168]{1,0:T(4,128)(2,1)S(1)} %get-tuple-element.73), channel_id=1, source_target_pairs={{0,1},{1,0},{2,3},{3,2},{16,18},{17,19},{18,16},{19,17},{4,5},{5,4... | collective-permute-start | bytes 172040 | tf_op jit(solution)/shard_map/ppermute | solution.py:41

commit v16 on v15

--- a/solution.py
+++ b/solution.py
@@ -184,7 +184,7 @@
     hidden = gate_refs[0].shape[2]
     place = lax.axis_index("sect") * lax.axis_size("grp") + lax.axis_index("grp")
     first = place * experts
-    block = min(512, hidden)
+    block = min(256, hidden)
     blocks = width // hidden
 
     late = [
@@ -201,12 +201,15 @@
         at += piece.shape[0]
 
     for e in range(experts):
-        for step in range(hidden // block):
-            span = pl.ds(step * block, block)
+
+        @pl.loop(0, hidden // block)
+        def _(step):
+            span = pl.ds(pl.multiple_of(step * block, block), block)
             gate = jnp.dot(
                 rows_ref[:, :width], gate_refs[e][0, :, span], preferred_element_type=jnp.float32
             )
             value_ref[e, :, span] = gate / (1.0 + jnp.exp(-gate))
+
         for copy in late[e]:
             copy.start()
 
@@ -215,13 +218,16 @@
     for e in range(experts):
         mine = lax.rem(lane, extra.shape[1] // 2) == first + e
         scale = jnp.sum(jnp.where(mine, extra, 0.0), axis=1, keepdims=True)
-        for step in range(hidden // block):
-            span = pl.ds(step * block, block)
+
+        @pl.loop(0, hidden // block)
+        def _(step):
+            span = pl.ds(pl.multiple_of(step * block, block), block)
             up = jnp.dot(
                 rows_ref[:, :width], up_refs[e][0, :, span], preferred_element_type=jnp.float32
             )
             value = value_ref[e, :, span] * up * scale
-            hidden_ref[:, pl.ds(e * hidden + step * block, block)] = value.astype(jnp.bfloat16)
+            out = pl.ds(pl.multiple_of(e * hidden + step * block, block), block)
+            hidden_ref[:, out] = value.astype(jnp.bfloat16)
 
     for step in range(blocks // 2):
         span = pl.ds(step * hidden, hidden)

time: 61.6 us -> 60.6 us (0.984)
  Pallas kernels: 26.5 us -> 25.5 us
    pallas_call x1, Pallas kernels: 8.27 us -> 7.33 us  [expert_call(): pl.pallas_call(functools.partial(expert_kernel, len(entries), experts, wi...]
where the time goes in v16:
time: 60.6 us; the launch traced here: 60.4 us
  Pallas kernels  25.5 us (42%)
  starting transfers between devices  20.5 us (34%)
  waiting for transfers between devices  13 us (21%)
  other arithmetic  1.14 us (2%)
    pallas_call x5, Pallas kernels, fetch(): pl.pallas_call(functools.partial(fetch_kernel, [(None, *w[1:]) for w in w...  16 us
    ppermute x6, starting transfers between devices, swap_line(): return lax.ppermute(value, ('sect', 'dev'), pairs)  10.2 us
    ppermute x6, starting transfers between devices, swap(): return lax.ppermute(value, ('sect', 'grp'), pairs)  9 us
    ppermute x6, waiting for transfers between devices, swap(): return lax.ppermute(value, ('sect', 'grp'), pairs)  8.48 us
    pallas_call x1, Pallas kernels, expert_call(): pl.pallas_call(functools.partial(expert_kernel, len(entries), experts, wi...  7.33 us
    ppermute x6, waiting for transfers between devices, swap_line(): return lax.ppermute(value, ('sect', 'dev'), pairs)  4.38 us
    ppermute x4, starting transfers between devices, swap_core(): return lax.ppermute(value, 'sect', [(0, 1), (1, 0)])  1.26 us
  transfers between devices with their start and end apart: 16, of which 10 were waited for; matrix products, arithmetic and copies ran while one was open for 1% of the time, Pallas kernels for 28%

profile of v16, /device:TPU:0, one launch (start us, length us, event | category | flops | bytes accessed | tf_op | source)
XLA Modules:
  0.0 60.4 jit_solution(13552804445430049423)
XLA Ops:
  0.0 1.0 %extend.1.after_ref.refs_0_ = bf16[4,7296]{1,0:T(4,128)(2,1)S(1)} custom-call(bf16[4,7168]{1,0:T(4,128)(2,1)} %tokens_hbm.1, s32[4,8]{1,0:T(4,128)} %ids_hbm.1, f32[4,8]{1,0:T(4,128)} %weights_hbm.1), custom_call_target="tpu_custom_call" | custom-call | tf_op jit(solution)/shard_map/extend/pallas_call | solution.py:81
  1.0 5.1 %collective-permute-start.2 = (bf16[4,7296]{1,0:T(4,128)(2,1)S(1)}, bf16[4,7296]{1,0:T(4,128)(2,1)S(1)}, u32[]{:S(2)}, u32[]{:S(2)}) collective-permute-start(bf16[4,7296]{1,0:T(4,128)(2,1)S(1)} %extend.1.after_ref.refs_0_), channel_id=1, source_target_pairs={{0,3},{1,2},{2,1},{3,0},{16,19},{17,18},{18,17},{19,16},{4,7},{5,6... | collective-permute-start | bytes 175112 | tf_op jit(solution)/shard_map/ppermute | solution.py:41
  6.1 0.0 collective-permute-start.1
  6.1 0.6 %collective-permute-start = (bf16[4,7296]{1,0:T(4,128)(2,1)S(1)}, bf16[4,7296]{1,0:T(4,128)(2,1)S(1)}, u32[]{:S(2)}, u32[]{:S(2)}) collective-permute-start(bf16[4,7296]{1,0:T(4,128)(2,1)S(1)} %extend.1.after_ref.refs_0_), channel_id=1, source_target_pairs={{0,1},{1,0},{2,3},{3,2},{16,17},{17,16},{18,19},{19,18},{4,5},{5,4... | collective-permute-start | bytes 175112 | tf_op jit(solution)/shard_map/ppermute | solution.py:41
  6.7 3.7 %fetch.5 = (bf16[1,7168,512]{2,1,0:T(8,128)(2,1)S(1)}, bf16[1,256,3584]{2,1,0:T(8,128)(2,1)S(1)}, f32[8,128]{1,0:T(8,128)S(1)}) custom-call(bf16[4,7296]{1,0:T(4,128)(2,1)S(1)} %extend.1.after_ref.refs_0_, bf16[2,7168,512]{2,1,0:T(8,128)(2,1)} %refs_0_.6, bf16[2,512,7168]{2,1,0:T(8,128)(2,1)} %refs_12_.1), custom_call_target="tpu_custom_call" | custom-call | bytes 9175040 | tf_op jit(solution)/shard_map/fetch/pallas_call | solution.py:273
  10.5 0.0 collective-permute-done.2.refs_3_
  10.5 0.7 %collective-permute-done.1.refs_2_ = bf16[4,7296]{1,0:T(4,128)(2,1)S(1)} collective-permute-done((bf16[4,7296]{1,0:T(4,128)(2,1)S(1)}, bf16[4,7296]{1,0:T(4,128)(2,1)S(1)}, u32[]{:S(2)}, u32[]{:S(2)}) %collective-permute-start.1) | collective-permute-done | bytes 58400 | tf_op jit(solution)/shard_map/ppermute | solution.py:41
  11.2 0.0 collective-permute-done.refs_1_
  11.2 0.1 stack.2.refs_0_
  11.3 1.7 %collective-permute-start.3 = (bf16[16,7296]{1,0:T(8,128)(2,1)S(1)}, bf16[16,7296]{1,0:T(8,128)(2,1)S(1)}, u32[]{:S(2)}, u32[]{:S(2)}) collective-permute-start(bf16[16,7296]{1,0:T(8,128)(2,1)S(1)} %stack.2.refs_0_), channel_id=1, source_target_pairs={{0,8},{4,12},{8,0},{12,4},{16,20},{20,16},{24,28},{28,24},{1,9},{5... | collective-permute-start | bytes 700424 | tf_op jit(solution)/shard_map/ppermute | solution.py:26
  12.9 3.7 %fetch.6 = (bf16[1,7168,512]{2,1,0:T(8,128)(2,1)S(1)}, bf16[1,256,3584]{2,1,0:T(8,128)(2,1)S(1)}, f32[8,128]{1,0:T(8,128)S(1)}) custom-call(f32[8,128]{1,0:T(8,128)S(1)} %get-tuple-element.42.after_ref, bf16[2,7168,512]{2,1,0:T(8,128)(2,1)} %refs_0_.6, bf16[2,512,7168]{2,1,0:T(8,128)(2,1)} %refs_12_.1), custom_call_target="tpu_custom_call" | custom-call | bytes 9175040 | tf_op jit(solution)/shard_map/fetch/pallas_call | solution.py:273
  16.6 0.7 %collective-permute-done.3.refs_1_ = bf16[16,7296]{1,0:T(8,128)(2,1)S(1)} collective-permute-done((bf16[16,7296]{1,0:T(8,128)(2,1)S(1)}, bf16[16,7296]{1,0:T(8,128)(2,1)S(1)}, u32[]{:S(2)}, u32[]{:S(2)}) %collective-permute-start.3) | collective-permute-done | bytes 233504 | tf_op jit(solution)/shard_map/ppermute | solution.py:26
  17.4 1.6 %collective-permute-start.4 = (bf16[32,7296]{1,0:T(8,128)(2,1)S(1)}, bf16[32,7296]{1,0:T(8,128)(2,1)S(1)}, u32[]{:S(2)}, u32[]{:S(2)}) collective-permute-start(bf16[32,7296]{1,0:T(8,128)(2,1)S(1)} %stack.3.refs_0_), channel_id=1, source_target_pairs={{0,4},{4,0},{8,12},{12,8},{16,24},{20,28},{24,16},{28,20},{1,5},{5... | collective-permute-start | bytes 1400840 | tf_op jit(solution)/shard_map/ppermute | solution.py:26
  19.1 3.8 %fetch.7 = (bf16[1,7168,512]{2,1,0:T(8,128)(2,1)S(1)}, bf16[1,256,3584]{2,1,0:T(8,128)(2,1)S(1)}, f32[8,128]{1,0:T(8,128)S(1)}) custom-call(f32[8,128]{1,0:T(8,128)S(1)} %get-tuple-element.45.after_ref, bf16[2,7168,512]{2,1,0:T(8,128)(2,1)} %refs_0_.8, bf16[2,512,7168]{2,1,0:T(8,128)(2,1)} %refs_12_.1), custom_call_target="tpu_custom_call" | custom-call | bytes 9175040 | tf_op jit(solution)/shard_map/fetch/pallas_call | solution.py:273
  22.9 0.1 collective-permute-start.5
  22.9 3.2 %fetch.8 = (bf16[1,7168,512]{2,1,0:T(8,128)(2,1)S(1)}, f32[8,128]{1,0:T(8,128)S(1)}) custom-call(f32[8,128]{1,0:T(8,128)S(1)} %get-tuple-element.48.after_ref, bf16[2,7168,512]{2,1,0:T(8,128)(2,1)} %refs_0_.8), custom_call_target="tpu_custom_call" | custom-call | bytes 7340032 | tf_op jit(solution)/shard_map/fetch/pallas_call | solution.py:273
  26.1 0.0 collective-permute-done.4.refs_1_
  26.1 0.0 collective-permute-done.5.refs_2_
  26.1 0.6 collective-permute-start.6
  26.7 1.6 %fetch.9 = (bf16[1,256,3584]{2,1,0:T(8,128)(2,1)S(1)}, f32[8,128]{1,0:T(8,128)S(1)}) custom-call(f32[8,128]{1,0:T(8,128)S(1)} %get-tuple-element.51.after_ref, bf16[2,512,7168]{2,1,0:T(8,128)(2,1)} %refs_12_.1), custom_call_target="tpu_custom_call" | custom-call | bytes 1835008 | tf_op jit(solution)/shard_map/fetch/pallas_call | solution.py:273
  28.3 0.0 collective-permute-done.6.refs_3_
  28.3 7.3 %experts.1 = (bf16[128,1024]{1,0:T(8,128)(2,1)S(1)}, bf16[64,3584]{1,0:T(8,128)(2,1)S(1)}, bf16[64,3584]{1,0:T(8,128)(2,1)S(1)}, bf16[1,7168,512]{2,1,0:T(8,128)(2,1)S(1)}, bf16[1,7168,512]{2,1,0:T(8,128)(2,1)S(1)}) custom-call(f32[8,128]{1,0:T(8,128)S(1)} %get-tuple-element.53.token_ref, ...), custom_call_target="tpu_custom_call", output_to_operand_aliasing={{3}: (5, {}), {4}: (6, {})} | custom-call | flops 4697620480 | bytes 14680064 | tf_op jit(solution)/shard_map/experts/pallas_call | solution.py:305
  35.7 0.2 collective-permute-start.7
  35.9 1.1 %down.1 = (bf16[64,3584]{1,0:T(8,128)(2,1)S(1)}, bf16[64,3584]{1,0:T(8,128)(2,1)S(1)}) custom-call(bf16[128,1024]{1,0:T(8,128)(2,1)S(1)} %get-tuple-element.66.hidden_ref, bf16[1,7168,512]{2,1,0:T(8,128)(2,1)S(1)} %get-tuple-element.67.refs_0_, bf16[1,7168,512]{2,1,0:T(8,128)(2,1)S(1)} %get-tuple-element.68.refs_1_), custom_call_target="tpu_custom_call" | custom-call | flops 939524096 | bytes 917504 | tf_op jit(solution)/shard_map/down/pallas_call | solution.py:334
  37.1 0.4 collective-permute-start.10
  37.5 0.1 collective-permute-done.7
  37.6 0.1 add_convert_fusion.1
  37.7 1.2 %collective-permute-start.8 = (bf16[32,3584]{1,0:T(8,128)(2,1)S(1)}, bf16[32,3584]{1,0:T(8,128)(2,1)S(1)}, u32[]{:S(2)}, u32[]{:S(2)}) collective-permute-start(bf16[32,3584]{1,0:T(8,128)(2,1)S(1)} %slice.49), channel_id=1, source_target_pairs={{0,4},{4,0},{8,12},{12,8},{16,24},{20,28},{24,16},{28,20},{1,5},{5... | collective-permute-start | bytes 688136 | tf_op jit(solution)/shard_map/ppermute | solution.py:26
  38.9 0.1 collective-permute-done.10
  38.9 0.1 add_convert_fusion
  39.1 1.3 %collective-permute-start.11 = (bf16[32,3584]{1,0:T(8,128)(2,1)S(1)}, bf16[32,3584]{1,0:T(8,128)(2,1)S(1)}, u32[]{:S(2)}, u32[]{:S(2)}) collective-permute-start(bf16[32,3584]{1,0:T(8,128)(2,1)S(1)} %slice.53), channel_id=1, source_target_pairs={{0,4},{4,0},{8,12},{12,8},{16,24},{20,28},{24,16},{28,20},{1,5},{5... | collective-permute-start | bytes 688136 | tf_op jit(solution)/shard_map/ppermute | solution.py:26
  40.4 3.4 %collective-permute-done.8 = bf16[32,3584]{1,0:T(8,128)(2,1)S(1)} collective-permute-done((bf16[32,3584]{1,0:T(8,128)(2,1)S(1)}, bf16[32,3584]{1,0:T(8,128)(2,1)S(1)}, u32[]{:S(2)}, u32[]{:S(2)}) %collective-permute-start.8) | collective-permute-done | bytes 229408 | tf_op jit(solution)/shard_map/ppermute | solution.py:26
  43.8 0.1 add_convert_fusion.3
  43.9 1.6 %collective-permute-start.9 = (bf16[16,3584]{1,0:T(8,128)(2,1)S(1)}, bf16[16,3584]{1,0:T(8,128)(2,1)S(1)}, u32[]{:S(2)}, u32[]{:S(2)}) collective-permute-start(bf16[16,3584]{1,0:T(8,128)(2,1)S(1)} %slice.51), channel_id=1, source_target_pairs={{0,8},{4,12},{8,0},{12,4},{16,20},{20,16},{24,28},{28,24},{1,9},{5... | collective-permute-start | bytes 344072 | tf_op jit(solution)/shard_map/ppermute | solution.py:26
  45.5 1.1 %collective-permute-done.11 = bf16[32,3584]{1,0:T(8,128)(2,1)S(1)} collective-permute-done((bf16[32,3584]{1,0:T(8,128)(2,1)S(1)}, bf16[32,3584]{1,0:T(8,128)(2,1)S(1)}, u32[]{:S(2)}, u32[]{:S(2)}) %collective-permute-start.11) | collective-permute-done | bytes 229408 | tf_op jit(solution)/shard_map/ppermute | solution.py:26
  46.6 0.1 add_convert_fusion.2
  46.7 1.6 %collective-permute-start.12 = (bf16[16,3584]{1,0:T(8,128)(2,1)S(1)}, bf16[16,3584]{1,0:T(8,128)(2,1)S(1)}, u32[]{:S(2)}, u32[]{:S(2)}) collective-permute-start(bf16[16,3584]{1,0:T(8,128)(2,1)S(1)} %slice.55), channel_id=1, source_target_pairs={{0,8},{4,12},{8,0},{12,4},{16,20},{20,16},{24,28},{28,24},{1,9},{5... | collective-permute-start | bytes 344072 | tf_op jit(solution)/shard_map/ppermute | solution.py:26
  48.2 0.5 collective-permute-done.9
  48.8 2.8 %collective-permute-done.12 = bf16[16,3584]{1,0:T(8,128)(2,1)S(1)} collective-permute-done((bf16[16,3584]{1,0:T(8,128)(2,1)S(1)}, bf16[16,3584]{1,0:T(8,128)(2,1)S(1)}, u32[]{:S(2)}, u32[]{:S(2)}) %collective-permute-start.12) | collective-permute-done | bytes 114720 | tf_op jit(solution)/shard_map/ppermute | solution.py:26
  51.6 0.1 fusion.2
  51.6 3.0 %collective-permute-start.13 = (bf16[4,7168]{1,0:T(4,128)(2,1)S(1)}, bf16[4,7168]{1,0:T(4,128)(2,1)S(1)}, u32[]{:S(2)}, u32[]{:S(2)}) collective-permute-start(bf16[4,7168]{1,0:T(4,128)(2,1)S(1)} %get-tuple-element.71), channel_id=1, source_target_pairs={{0,3},{1,2},{2,1},{3,0},{16,17},{17,16},{18,19},{19,18},{4,7},{5,6... | collective-permute-start | bytes 172040 | tf_op jit(solution)/shard_map/ppermute | solution.py:41
  54.7 0.0 collective-permute-start.15
  54.7 1.4 %collective-permute-start.14 = (bf16[4,7168]{1,0:T(4,128)(2,1)S(1)}, bf16[4,7168]{1,0:T(4,128)(2,1)S(1)}, u32[]{:S(2)}, u32[]{:S(2)}) collective-permute-start(bf16[4,7168]{1,0:T(4,128)(2,1)S(1)} %get-tuple-element.73), channel_id=1, source_target_pairs={{0,1},{1,0},{2,3},{3,2},{16,18},{17,19},{18,16},{19,17},{4,5},{5,4... | collective-permute-start | bytes 172040 | tf_op jit(solution)/shard_map/ppermute | solution.py:41
  56.1 1.6 %collective-permute-done.13 = bf16[4,7168]{1,0:T(4,128)(2,1)S(1)} collective-permute-done((bf16[4,7168]{1,0:T(4,128)(2,1)S(1)}, bf16[4,7168]{1,0:T(4,128)(2,1)S(1)}, u32[]{:S(2)}, u32[]{:S(2)}) %collective-permute-start.13) | collective-permute-done | bytes 57376 | tf_op jit(solution)/shard_map/ppermute | solution.py:41
  57.7 2.1 %collective-permute-done.15 = bf16[4,7168]{1,0:T(4,128)(2,1)S(1)} collective-permute-done((bf16[4,7168]{1,0:T(4,128)(2,1)S(1)}, bf16[4,7168]{1,0:T(4,128)(2,1)S(1)}, u32[]{:S(2)}, u32[]{:S(2)}) %collective-permute-start.15) | collective-permute-done | bytes 57376 | tf_op jit(solution)/shard_map/ppermute | solution.py:41
  59.7 0.0 collective-permute-done.14
  59.7 0.7 %add_convert_fusion.6 = bf16[4,7168]{1,0:T(4,128)(2,1)} fusion(bf16[4,7168]{1,0:T(4,128)(2,1)S(1)} %collective-permute-done.15, bf16[4,7168]{1,0:T(4,128)(2,1)S(1)} %collective-permute-done.14, bf16[4,7168]{1,0:T(4,128)(2,1)S(1)} %collective-permute-done.13, bf16[16,3584]{1,0:T(8,128)(2,1)S(1)} %add_convert_fusion.5, bf16[16,3584]{1,0:T(8,128)(2,1)S(1)} %add_convert_fusion.4), kind=kLoop, calls=%fused_computation.12 | loop fusion | flops 315392 | bytes 458752 | tf_op jit(solution)/shard_map/convert_element_type | solution.py:354
  (7 shorter events, 0.1 us)
Async XLA Ops:
  1.0 9.5 %collective-permute-start.2 = (bf16[4,7296]{1,0:T(4,128)(2,1)S(1)}, bf16[4,7296]{1,0:T(4,128)(2,1)S(1)}, u32[]{:S(2)}, u32[]{:S(2)}) collective-permute-start(bf16[4,7296]{1,0:T(4,128)(2,1)S(1)} %extend.1.after_ref.refs_0_), channel_id=1, source_target_pairs={{0,3},{1,2},{2,1},{3,0},{16,19},{17,18},{18,17},{19,16},{4,7},{5,6... | collective-permute-start | bytes 175112 | tf_op jit(solution)/shard_map/ppermute | solution.py:41
  6.1 5.1 %collective-permute-start.1 = (bf16[4,7296]{1,0:T(4,128)(2,1)S(1)}, bf16[4,7296]{1,0:T(4,128)(2,1)S(1)}, u32[]{:S(2)}, u32[]{:S(2)}) collective-permute-start(bf16[4,7296]{1,0:T(4,128)(2,1)S(1)} %extend.1.after_ref.refs_0_), channel_id=1, source_target_pairs={{0,2},{1,3},{2,0},{3,1},{16,18},{17,19},{18,16},{19,17},{4,6},{5,7... | collective-permute-start | bytes 175112 | tf_op jit(solution)/shard_map/ppermute | solution.py:41
  6.1 5.1 %collective-permute-start = (bf16[4,7296]{1,0:T(4,128)(2,1)S(1)}, bf16[4,7296]{1,0:T(4,128)(2,1)S(1)}, u32[]{:S(2)}, u32[]{:S(2)}) collective-permute-start(bf16[4,7296]{1,0:T(4,128)(2,1)S(1)} %extend.1.after_ref.refs_0_), channel_id=1, source_target_pairs={{0,1},{1,0},{2,3},{3,2},{16,17},{17,16},{18,19},{19,18},{4,5},{5,4... | collective-permute-start | bytes 175112 | tf_op jit(solution)/shard_map/ppermute | solution.py:41
  11.3 6.1 %collective-permute-start.3 = (bf16[16,7296]{1,0:T(8,128)(2,1)S(1)}, bf16[16,7296]{1,0:T(8,128)(2,1)S(1)}, u32[]{:S(2)}, u32[]{:S(2)}) collective-permute-start(bf16[16,7296]{1,0:T(8,128)(2,1)S(1)} %stack.2.refs_0_), channel_id=1, source_target_pairs={{0,8},{4,12},{8,0},{12,4},{16,20},{20,16},{24,28},{28,24},{1,9},{5... | collective-permute-start | bytes 700424 | tf_op jit(solution)/shard_map/ppermute | solution.py:26
  17.4 8.7 %collective-permute-start.4 = (bf16[32,7296]{1,0:T(8,128)(2,1)S(1)}, bf16[32,7296]{1,0:T(8,128)(2,1)S(1)}, u32[]{:S(2)}, u32[]{:S(2)}) collective-permute-start(bf16[32,7296]{1,0:T(8,128)(2,1)S(1)} %stack.3.refs_0_), channel_id=1, source_target_pairs={{0,4},{4,0},{8,12},{12,8},{16,24},{20,28},{24,16},{28,20},{1,5},{5... | collective-permute-start | bytes 1400840 | tf_op jit(solution)/shard_map/ppermute | solution.py:26
  22.9 3.3 %collective-permute-start.5 = (bf16[32,7296]{1,0:T(8,128)(2,1)S(1)}, bf16[32,7296]{1,0:T(8,128)(2,1)S(1)}, u32[]{:S(2)}, u32[]{:S(2)}) collective-permute-start(bf16[32,7296]{1,0:T(8,128)(2,1)S(1)} %stack.3.refs_0_), channel_id=1, source_target_pairs={{0,16},{16,0},{1,17},{17,1},{2,18},{18,2},{3,19},{19,3},{4,20},{20... | collective-permute-start | bytes 1400840 | tf_op jit(solution)/shard_map/ppermute | solution.py:45
  26.1 2.2 %collective-permute-start.6 = (bf16[32,7296]{1,0:T(8,128)(2,1)S(1)}, bf16[32,7296]{1,0:T(8,128)(2,1)S(1)}, u32[]{:S(2)}, u32[]{:S(2)}) collective-permute-start(bf16[32,7296]{1,0:T(8,128)(2,1)S(1)} %collective-permute-done.4.refs_1_), channel_id=1, source_target_pairs={{0,16},{16,0},{1,17},{17,1},{2,18},{18,2},{3,19},{19,3},{4,20},{20... | collective-permute-start | bytes 1400840 | tf_op jit(solution)/shard_map/ppermute | solution.py:45
  35.7 1.9 %collective-permute-start.7 = (bf16[64,3584]{1,0:T(8,128)(2,1)S(1)}, bf16[64,3584]{1,0:T(8,128)(2,1)S(1)}, u32[]{:S(2)}, u32[]{:S(2)}) collective-permute-start(bf16[64,3584]{1,0:T(8,128)(2,1)S(1)} %get-tuple-element.65), channel_id=1, source_target_pairs={{0,16},{16,0},{1,17},{17,1},{2,18},{18,2},{3,19},{19,3},{4,20},{20... | collective-permute-start | bytes 1376264 | tf_op jit(solution)/shard_map/ppermute | solution.py:45
  37.1 1.9 %collective-permute-start.10 = (bf16[64,3584]{1,0:T(8,128)(2,1)S(1)}, bf16[64,3584]{1,0:T(8,128)(2,1)S(1)}, u32[]{:S(2)}, u32[]{:S(2)}) collective-permute-start(bf16[64,3584]{1,0:T(8,128)(2,1)S(1)} %get-tuple-element.70), channel_id=1, source_target_pairs={{0,16},{16,0},{1,17},{17,1},{2,18},{18,2},{3,19},{19,3},{4,20},{20... | collective-permute-start | bytes 1376264 | tf_op jit(solution)/shard_map/ppermute | solution.py:45
  37.7 6.1 %collective-permute-start.8 = (bf16[32,3584]{1,0:T(8,128)(2,1)S(1)}, bf16[32,3584]{1,0:T(8,128)(2,1)S(1)}, u32[]{:S(2)}, u32[]{:S(2)}) collective-permute-start(bf16[32,3584]{1,0:T(8,128)(2,1)S(1)} %slice.49), channel_id=1, source_target_pairs={{0,4},{4,0},{8,12},{12,8},{16,24},{20,28},{24,16},{28,20},{1,5},{5... | collective-permute-start | bytes 688136 | tf_op jit(solution)/shard_map/ppermute | solution.py:26
  39.1 7.5 %collective-permute-start.11 = (bf16[32,3584]{1,0:T(8,128)(2,1)S(1)}, bf16[32,3584]{1,0:T(8,128)(2,1)S(1)}, u32[]{:S(2)}, u32[]{:S(2)}) collective-permute-start(bf16[32,3584]{1,0:T(8,128)(2,1)S(1)} %slice.53), channel_id=1, source_target_pairs={{0,4},{4,0},{8,12},{12,8},{16,24},{20,28},{24,16},{28,20},{1,5},{5... | collective-permute-start | bytes 688136 | tf_op jit(solution)/shard_map/ppermute | solution.py:26
  43.9 4.9 %collective-permute-start.9 = (bf16[16,3584]{1,0:T(8,128)(2,1)S(1)}, bf16[16,3584]{1,0:T(8,128)(2,1)S(1)}, u32[]{:S(2)}, u32[]{:S(2)}) collective-permute-start(bf16[16,3584]{1,0:T(8,128)(2,1)S(1)} %slice.51), channel_id=1, source_target_pairs={{0,8},{4,12},{8,0},{12,4},{16,20},{20,16},{24,28},{28,24},{1,9},{5... | collective-permute-start | bytes 344072 | tf_op jit(solution)/shard_map/ppermute | solution.py:26
  46.7 4.9 %collective-permute-start.12 = (bf16[16,3584]{1,0:T(8,128)(2,1)S(1)}, bf16[16,3584]{1,0:T(8,128)(2,1)S(1)}, u32[]{:S(2)}, u32[]{:S(2)}) collective-permute-start(bf16[16,3584]{1,0:T(8,128)(2,1)S(1)} %slice.55), channel_id=1, source_target_pairs={{0,8},{4,12},{8,0},{12,4},{16,20},{20,16},{24,28},{28,24},{1,9},{5... | collective-permute-start | bytes 344072 | tf_op jit(solution)/shard_map/ppermute | solution.py:26
  51.6 6.0 %collective-permute-start.13 = (bf16[4,7168]{1,0:T(4,128)(2,1)S(1)}, bf16[4,7168]{1,0:T(4,128)(2,1)S(1)}, u32[]{:S(2)}, u32[]{:S(2)}) collective-permute-start(bf16[4,7168]{1,0:T(4,128)(2,1)S(1)} %get-tuple-element.71), channel_id=1, source_target_pairs={{0,3},{1,2},{2,1},{3,0},{16,17},{17,16},{18,19},{19,18},{4,7},{5,6... | collective-permute-start | bytes 172040 | tf_op jit(solution)/shard_map/ppermute | solution.py:41
  54.7 5.1 %collective-permute-start.15 = (bf16[4,7168]{1,0:T(4,128)(2,1)S(1)}, bf16[4,7168]{1,0:T(4,128)(2,1)S(1)}, u32[]{:S(2)}, u32[]{:S(2)}) collective-permute-start(bf16[4,7168]{1,0:T(4,128)(2,1)S(1)} %get-tuple-element.72), channel_id=1, source_target_pairs={{0,2},{1,3},{2,0},{3,1},{16,19},{17,18},{18,17},{19,16},{4,6},{5,7... | collective-permute-start | bytes 172040 | tf_op jit(solution)/shard_map/ppermute | solution.py:41
  54.7 5.1 %collective-permute-start.14 = (bf16[4,7168]{1,0:T(4,128)(2,1)S(1)}, bf16[4,7168]{1,0:T(4,128)(2,1)S(1)}, u32[]{:S(2)}, u32[]{:S(2)}) collective-permute-start(bf16[4,7168]{1,0:T(4,128)(2,1)S(1)} %get-tuple-element.73), channel_id=1, source_target_pairs={{0,1},{1,0},{2,3},{3,2},{16,18},{17,19},{18,16},{19,17},{4,5},{5,4... | collective-permute-start | bytes 172040 | tf_op jit(solution)/shard_map/ppermute | solution.py:41

commit v17 on v16

--- a/solution.py
+++ b/solution.py
@@ -8,7 +8,7 @@
 from jax.sharding import PartitionSpec as P
 
 AXES = ("sect", "grp", "dev")
-VMEM_LIMIT = 10 * 2**20
+VMEM_LIMIT = 14 * 2**20
 
 
 def rounds_of():
@@ -112,6 +112,7 @@
     experts, sects, lanes = w_gate.shape[0], lax.axis_size("sect"), lax.axis_size("dev")
     half, early = w_down.shape[1] // 2, early_columns(w_down)
     whole = [(w, e, 0, w.shape[1], w.shape[2]) for w in (w_gate, w_up) for e in range(experts)]
+    whole = whole[:-1]
     parts = [(w_down, e, r, half, early) for e in range(experts) for r in (0, half)]
     held, token = {}, block
 
@@ -126,7 +127,7 @@
         return token
 
     arrived = [swap_line(block, (m,) * sects) for m in range(1, lanes)]
-    token = fetch_next(1, 1, token)
+    token = fetch_next(0, 2, token)
     arrived, token = lax.optimization_barrier((arrived, token))
     line = stack([block, *arrived], line_orders())
     rounds = rounds_of()
@@ -136,7 +137,7 @@
         arrived, token = lax.optimization_barrier((arrived, token))
         line = stack([line, arrived])
     last = swap(line, rounds[-1])
-    token = fetch_next(1, 1, token)
+    token = fetch_next(1, 0, token)
     mine, token = lax.optimization_barrier((line, token))
     other = swap_core(mine)
     token = fetch_next(len(whole), 0, token)
@@ -144,7 +145,8 @@
     last_other = swap_core(last)
     token = fetch_next(0, len(parts), token)
     last_other, token = lax.optimization_barrier((last_other, token))
-    weights = [held[id(w), e, 0] for w in (w_gate, w_up) for e in range(experts)]
+    weights = [held[id(w_gate), e, 0] for e in range(experts)]
+    weights += [held[id(w_up), e, 0] for e in range(experts - 1)]
     weights += [held[id(w_down), e, r] for e in range(experts) for r in (0, half)]
     return [line, last, other, last_other], weights, token
 
@@ -163,24 +165,22 @@
     )
 
 
-def down_block(at, hidden_ref, weights, keep_ref, send_ref):
-    hidden = weights[0].shape[1]
+def down_block(span, hidden_ref, weights, keep_ref, send_ref):
     middle = keep_ref.shape[0]
     weight = jnp.concatenate(weights, axis=0)
     total = jnp.dot(hidden_ref[...], weight, preferred_element_type=jnp.float32)
     total = total.astype(jnp.bfloat16)
-    span = pl.ds(at * hidden, hidden)
     keep_ref[:, span] = total[:middle]
     send_ref[:, span] = total[middle:]
 
 
 def expert_kernel(entry_count, experts, width, token_ref, *refs):
     pieces, refs = refs[:entry_count], refs[entry_count:]
-    gate_refs, up_refs, early_refs, refs = (
-        refs[:experts], refs[experts:2 * experts], refs[2 * experts:4 * experts], refs[4 * experts:]
-    )
-    down_hbm, hidden_ref, keep_ref, send_ref = refs[:4]
-    down_refs, (rows_ref, value_ref, sems) = refs[4:4 + experts], refs[4 + experts:]
+    gate_refs, up_refs, refs = refs[:experts], refs[experts:2 * experts - 1], refs[2 * experts - 1:]
+    early_refs, refs = refs[:2 * experts], refs[2 * experts:]
+    up_hbm, down_hbm, hidden_ref, keep_ref, send_ref = refs[:5]
+    down_refs, (rows_ref, value_ref, last_up_ref, up_sems, sems) = refs[5:5 + experts], refs[5 + experts:]
+    up_refs = [*up_refs, last_up_ref]
     hidden = gate_refs[0].shape[2]
     place = lax.axis_index("sect") * lax.axis_size("grp") + lax.axis_index("grp")
     first = place * experts
@@ -195,6 +195,18 @@
         for e in range(experts)
     ]
 
+    depth = width // up_sems.shape[0]
+    up_copies = [
+        pltpu.make_async_copy(
+            up_hbm.at[experts - 1, pl.ds(p * depth, depth)],
+            last_up_ref.at[0, pl.ds(p * depth, depth)],
+            up_sems.at[p],
+        )
+        for p in range(up_sems.shape[0])
+    ]
+    for copy in up_copies:
+        copy.start()
+
     at = 0
     for piece in pieces:
         rows_ref[pl.ds(at, piece.shape[0])] = piece[...]
@@ -218,6 +230,9 @@
     for e in range(experts):
         mine = lax.rem(lane, extra.shape[1] // 2) == first + e
         scale = jnp.sum(jnp.where(mine, extra, 0.0), axis=1, keepdims=True)
+        if e == experts - 1:
+            for copy in up_copies:
+                copy.wait()
 
         @pl.loop(0, hidden // block)
         def _(step):
@@ -229,9 +244,12 @@
             out = pl.ds(pl.multiple_of(e * hidden + step * block, block), block)
             hidden_ref[:, out] = value.astype(jnp.bfloat16)
 
-    for step in range(blocks // 2):
-        span = pl.ds(step * hidden, hidden)
-        down_block(step, hidden_ref, [ref[0, :, span] for ref in early_refs], keep_ref, send_ref)
+    part = keep_ref.shape[1] // 2
+
+    @pl.loop(0, 2)
+    def _(step):
+        span = pl.ds(pl.multiple_of(step * part, 128), part)
+        down_block(span, hidden_ref, [ref[0, :, span] for ref in early_refs], keep_ref, send_ref)
 
     for copies in late:
         for copy in copies:
@@ -243,7 +261,7 @@
     hidden = down_refs[0].shape[2]
     for step in range(keep_ref.shape[1] // hidden):
         span = pl.ds(step * hidden, hidden)
-        down_block(step, hidden_ref, [ref[0, span, :] for ref in down_refs], keep_ref, send_ref)
+        down_block(span, hidden_ref, [ref[0, span, :] for ref in down_refs], keep_ref, send_ref)
 
 
 def fetch_kernel(wanted, after_ref, *refs):
@@ -293,7 +311,7 @@
     return [pltpu.with_memory_space_constraint(v, pltpu.VMEM) for v in values]
 
 
-def expert_call(entries, held, w_down, token):
+def expert_call(entries, held, w_up, w_down, token):
     experts, hidden, width = w_down.shape
     full = entries[0].shape[1]
     rows = sum(e.shape[0] for e in entries)
@@ -310,12 +328,14 @@
             outs[0],
             *(pltpu.VMEM(w.shape, w.dtype) for w in held[:experts]),
         ),
-        in_specs=[anywhere] + [whole] * (len(entries) + len(held)) + [anywhere],
+        in_specs=[anywhere] + [whole] * (len(entries) + len(held)) + [anywhere] * 2,
         out_specs=(whole,) * (3 + experts),
         input_output_aliases={1 + len(entries) + e: 3 + e for e in range(experts)},
         scratch_shapes=[
             pltpu.VMEM((rows, full), jnp.bfloat16),
             pltpu.VMEM((experts, rows, hidden), jnp.float32),
+            pltpu.VMEM((1, *w_up.shape[1:]), w_up.dtype),
+            pltpu.SemaphoreType.DMA((8,)),
             pltpu.SemaphoreType.DMA((experts, blocks)),
         ],
         compiler_params=pltpu.CompilerParams(vmem_limit_bytes=VMEM_LIMIT),
@@ -329,6 +349,7 @@
         token,
         *entries,
         *in_vmem(held),
+        pltpu.with_memory_space_constraint(w_up, pltpu.HBM),
         pltpu.with_memory_space_constraint(w_down, pltpu.HBM),
     )
     later = pl.pallas_call(
@@ -366,7 +387,7 @@
 
     results = []
     halves = []
-    for keep, send in expert_call(entries, held, w_down, token):
+    for keep, send in expert_call(entries, held, w_up, w_down, token):
         value = add(keep, swap_core(send))
         for masks in rounds_of()[::-1]:
             middle = value.shape[0] // 2

time: 60.6 us -> 60 us (0.990)
  Pallas kernels: 25.5 us -> 23.6 us
  waiting for transfers between devices: 13 us -> 14.2 us
    pallas_call x5, Pallas kernels: 16 us -> 13.9 us  [fetch(): pl.pallas_call(functools.partial(fetch_kernel, [(None, *w[1:]) for w in w...]
    ppermute x6, waiting for transfers between devices: 4.38 us -> 5.57 us  [swap_line(): return lax.ppermute(value, ('sect', 'dev'), pairs)]
    ppermute x6, starting transfers between devices: 9 us -> 9.64 us  [swap(): return lax.ppermute(value, ('sect', 'grp'), pairs)]
  transfers between devices with their start and end apart: 16 -> 16, of which waited for: 10 -> 11; matrix products, arithmetic and copies ran while one was open for 1% -> 1% of each run, Pallas kernels for 28% -> 25%
where the time goes in v17:
time: 60 us; the launch traced here: 59.8 us
  Pallas kernels  23.6 us (39%)
  starting transfers between devices  20.6 us (34%)
  waiting for transfers between devices  14.2 us (24%)
  other arithmetic  1.14 us (2%)
    pallas_call x5, Pallas kernels, fetch(): pl.pallas_call(functools.partial(fetch_kernel, [(None, *w[1:]) for w in w...  13.9 us
    ppermute x6, starting transfers between devices, swap_line(): return lax.ppermute(value, ('sect', 'dev'), pairs)  10.2 us
    ppermute x6, starting transfers between devices, swap(): return lax.ppermute(value, ('sect', 'grp'), pairs)  9.64 us
    ppermute x6, waiting for transfers between devices, swap(): return lax.ppermute(value, ('sect', 'grp'), pairs)  8.32 us
    pallas_call x1, Pallas kernels, expert_call(): pl.pallas_call(functools.partial(expert_kernel, len(entries), experts, wi...  7.53 us
    ppermute x6, waiting for transfers between devices, swap_line(): return lax.ppermute(value, ('sect', 'dev'), pairs)  5.57 us
  transfers between devices with their start and end apart: 16, of which 11 were waited for; matrix products, arithmetic and copies ran while one was open for 1% of the time, Pallas kernels for 25%

profile of v17, /device:TPU:0, one launch (start us, length us, event | category | flops | bytes accessed | tf_op | source)
XLA Modules:
  0.0 59.8 jit_solution(10256866191720189844)
XLA Ops:
  0.0 1.0 %extend.1.after_ref.refs_0_ = bf16[4,7296]{1,0:T(4,128)(2,1)S(1)} custom-call(bf16[4,7168]{1,0:T(4,128)(2,1)} %tokens_hbm.1, s32[4,8]{1,0:T(4,128)} %ids_hbm.1, f32[4,8]{1,0:T(4,128)} %weights_hbm.1), custom_call_target="tpu_custom_call" | custom-call | tf_op jit(solution)/shard_map/extend/pallas_call | solution.py:81
  1.0 5.1 %collective-permute-start.2 = (bf16[4,7296]{1,0:T(4,128)(2,1)S(1)}, bf16[4,7296]{1,0:T(4,128)(2,1)S(1)}, u32[]{:S(2)}, u32[]{:S(2)}) collective-permute-start(bf16[4,7296]{1,0:T(4,128)(2,1)S(1)} %extend.1.after_ref.refs_0_), channel_id=1, source_target_pairs={{0,3},{1,2},{2,1},{3,0},{16,19},{17,18},{18,17},{19,16},{4,7},{5,6... | collective-permute-start | bytes 175112 | tf_op jit(solution)/shard_map/ppermute | solution.py:41
  6.1 0.0 collective-permute-start.1
  6.1 0.6 %collective-permute-start = (bf16[4,7296]{1,0:T(4,128)(2,1)S(1)}, bf16[4,7296]{1,0:T(4,128)(2,1)S(1)}, u32[]{:S(2)}, u32[]{:S(2)}) collective-permute-start(bf16[4,7296]{1,0:T(4,128)(2,1)S(1)} %extend.1.after_ref.refs_0_), channel_id=1, source_target_pairs={{0,1},{1,0},{2,3},{3,2},{16,17},{17,16},{18,19},{19,18},{4,5},{5,4... | collective-permute-start | bytes 175112 | tf_op jit(solution)/shard_map/ppermute | solution.py:41
  6.7 2.2 %fetch.5 = (bf16[1,256,3584]{2,1,0:T(8,128)(2,1)S(1)}, bf16[1,256,3584]{2,1,0:T(8,128)(2,1)S(1)}, f32[8,128]{1,0:T(8,128)S(1)}) custom-call(bf16[4,7296]{1,0:T(4,128)(2,1)S(1)} %extend.1.after_ref.refs_0_, bf16[2,512,7168]{2,1,0:T(8,128)(2,1)} %refs_12_.1, bf16[2,512,7168]{2,1,0:T(8,128)(2,1)} %refs_12_.1), custom_call_target="tpu_custom_call" | custom-call | bytes 3670016 | tf_op jit(solution)/shard_map/fetch/pallas_call | solution.py:291
  9.0 0.0 collective-permute-done.2.refs_3_
  9.0 2.2 %collective-permute-done.1.refs_2_ = bf16[4,7296]{1,0:T(4,128)(2,1)S(1)} collective-permute-done((bf16[4,7296]{1,0:T(4,128)(2,1)S(1)}, bf16[4,7296]{1,0:T(4,128)(2,1)S(1)}, u32[]{:S(2)}, u32[]{:S(2)}) %collective-permute-start.1) | collective-permute-done | bytes 58400 | tf_op jit(solution)/shard_map/ppermute | solution.py:41
  11.2 0.0 collective-permute-done.refs_1_
  11.2 0.1 stack.2.refs_0_
  11.3 1.7 %collective-permute-start.3 = (bf16[16,7296]{1,0:T(8,128)(2,1)S(1)}, bf16[16,7296]{1,0:T(8,128)(2,1)S(1)}, u32[]{:S(2)}, u32[]{:S(2)}) collective-permute-start(bf16[16,7296]{1,0:T(8,128)(2,1)S(1)} %stack.2.refs_0_), channel_id=1, source_target_pairs={{0,8},{4,12},{8,0},{12,4},{16,20},{20,16},{24,28},{28,24},{1,9},{5... | collective-permute-start | bytes 700424 | tf_op jit(solution)/shard_map/ppermute | solution.py:26
  12.9 3.7 %fetch.6 = (bf16[1,7168,512]{2,1,0:T(8,128)(2,1)S(1)}, bf16[1,256,3584]{2,1,0:T(8,128)(2,1)S(1)}, f32[8,128]{1,0:T(8,128)S(1)}) custom-call(f32[8,128]{1,0:T(8,128)S(1)} %get-tuple-element.41.after_ref, bf16[2,7168,512]{2,1,0:T(8,128)(2,1)} %refs_0_.7, bf16[2,512,7168]{2,1,0:T(8,128)(2,1)} %refs_12_.1), custom_call_target="tpu_custom_call" | custom-call | bytes 9175040 | tf_op jit(solution)/shard_map/fetch/pallas_call | solution.py:291
  16.6 0.7 %collective-permute-done.3.refs_1_ = bf16[16,7296]{1,0:T(8,128)(2,1)S(1)} collective-permute-done((bf16[16,7296]{1,0:T(8,128)(2,1)S(1)}, bf16[16,7296]{1,0:T(8,128)(2,1)S(1)}, u32[]{:S(2)}, u32[]{:S(2)}) %collective-permute-start.3) | collective-permute-done | bytes 233504 | tf_op jit(solution)/shard_map/ppermute | solution.py:26
  17.4 1.6 %collective-permute-start.4 = (bf16[32,7296]{1,0:T(8,128)(2,1)S(1)}, bf16[32,7296]{1,0:T(8,128)(2,1)S(1)}, u32[]{:S(2)}, u32[]{:S(2)}) collective-permute-start(bf16[32,7296]{1,0:T(8,128)(2,1)S(1)} %stack.3.refs_0_), channel_id=1, source_target_pairs={{0,4},{4,0},{8,12},{12,8},{16,24},{20,28},{24,16},{28,20},{1,5},{5... | collective-permute-start | bytes 1400840 | tf_op jit(solution)/shard_map/ppermute | solution.py:26
  19.1 3.2 %fetch.7 = (bf16[1,7168,512]{2,1,0:T(8,128)(2,1)S(1)}, f32[8,128]{1,0:T(8,128)S(1)}) custom-call(f32[8,128]{1,0:T(8,128)S(1)} %get-tuple-element.44.after_ref, bf16[2,7168,512]{2,1,0:T(8,128)(2,1)} %refs_0_.7), custom_call_target="tpu_custom_call" | custom-call | bytes 7340032 | tf_op jit(solution)/shard_map/fetch/pallas_call | solution.py:291
  22.2 0.1 collective-permute-start.5
  22.3 3.2 %fetch.8 = (bf16[1,7168,512]{2,1,0:T(8,128)(2,1)S(1)}, f32[8,128]{1,0:T(8,128)S(1)}) custom-call(f32[8,128]{1,0:T(8,128)S(1)} %get-tuple-element.47.after_ref, bf16[2,7168,512]{2,1,0:T(8,128)(2,1)} %refs_11_.1), custom_call_target="tpu_custom_call" | custom-call | bytes 7340032 | tf_op jit(solution)/shard_map/fetch/pallas_call | solution.py:291
  25.5 0.6 collective-permute-done.4.refs_1_
  26.1 0.0 collective-permute-done.5.refs_2_
  26.1 0.0 collective-permute-start.6
  26.1 1.6 %fetch.9 = (bf16[1,256,3584]{2,1,0:T(8,128)(2,1)S(1)}, f32[8,128]{1,0:T(8,128)S(1)}) custom-call(f32[8,128]{1,0:T(8,128)S(1)} %get-tuple-element.50.after_ref, bf16[2,512,7168]{2,1,0:T(8,128)(2,1)} %refs_12_.1), custom_call_target="tpu_custom_call" | custom-call | bytes 1835008 | tf_op jit(solution)/shard_map/fetch/pallas_call | solution.py:291
  27.7 0.2 collective-permute-done.6.refs_3_
  27.9 7.5 %experts.1 = (bf16[128,1024]{1,0:T(8,128)(2,1)S(1)}, bf16[64,3584]{1,0:T(8,128)(2,1)S(1)}, bf16[64,3584]{1,0:T(8,128)(2,1)S(1)}, bf16[1,7168,512]{2,1,0:T(8,128)(2,1)S(1)}, bf16[1,7168,512]{2,1,0:T(8,128)(2,1)S(1)}) custom-call(f32[8,128]{1,0:T(8,128)S(1)} %get-tuple-element.52.token_ref, ...), custom_call_target="tpu_custom_call", output_to_operand_aliasing={{3}: (5, {}), {4}: (6, {})} | custom-call | flops 4697620480 | bytes 14680064 | tf_op jit(solution)/shard_map/experts/pallas_call | solution.py:323
  35.4 0.4 collective-permute-start.7
  35.8 1.1 %down.1 = (bf16[64,3584]{1,0:T(8,128)(2,1)S(1)}, bf16[64,3584]{1,0:T(8,128)(2,1)S(1)}) custom-call(bf16[128,1024]{1,0:T(8,128)(2,1)S(1)} %get-tuple-element.64.hidden_ref, bf16[1,7168,512]{2,1,0:T(8,128)(2,1)S(1)} %get-tuple-element.65.refs_0_, bf16[1,7168,512]{2,1,0:T(8,128)(2,1)S(1)} %get-tuple-element.66.refs_1_), custom_call_target="tpu_custom_call" | custom-call | flops 939524096 | bytes 917504 | tf_op jit(solution)/shard_map/down/pallas_call | solution.py:355
  36.9 0.3 collective-permute-start.10
  37.2 0.1 collective-permute-done.7
  37.3 0.1 add_convert_fusion.1
  37.5 1.6 %collective-permute-start.8 = (bf16[32,3584]{1,0:T(8,128)(2,1)S(1)}, bf16[32,3584]{1,0:T(8,128)(2,1)S(1)}, u32[]{:S(2)}, u32[]{:S(2)}) collective-permute-start(bf16[32,3584]{1,0:T(8,128)(2,1)S(1)} %slice.49), channel_id=1, source_target_pairs={{0,4},{4,0},{8,12},{12,8},{16,24},{20,28},{24,16},{28,20},{1,5},{5... | collective-permute-start | bytes 688136 | tf_op jit(solution)/shard_map/ppermute | solution.py:26
  39.1 0.0 collective-permute-done.10
  39.1 0.1 add_convert_fusion
  39.2 1.4 %collective-permute-start.11 = (bf16[32,3584]{1,0:T(8,128)(2,1)S(1)}, bf16[32,3584]{1,0:T(8,128)(2,1)S(1)}, u32[]{:S(2)}, u32[]{:S(2)}) collective-permute-start(bf16[32,3584]{1,0:T(8,128)(2,1)S(1)} %slice.53), channel_id=1, source_target_pairs={{0,4},{4,0},{8,12},{12,8},{16,24},{20,28},{24,16},{28,20},{1,5},{5... | collective-permute-start | bytes 688136 | tf_op jit(solution)/shard_map/ppermute | solution.py:26
  40.6 2.9 %collective-permute-done.8 = bf16[32,3584]{1,0:T(8,128)(2,1)S(1)} collective-permute-done((bf16[32,3584]{1,0:T(8,128)(2,1)S(1)}, bf16[32,3584]{1,0:T(8,128)(2,1)S(1)}, u32[]{:S(2)}, u32[]{:S(2)}) %collective-permute-start.8) | collective-permute-done | bytes 229408 | tf_op jit(solution)/shard_map/ppermute | solution.py:26
  43.5 0.1 add_convert_fusion.3
  43.6 1.7 %collective-permute-start.9 = (bf16[16,3584]{1,0:T(8,128)(2,1)S(1)}, bf16[16,3584]{1,0:T(8,128)(2,1)S(1)}, u32[]{:S(2)}, u32[]{:S(2)}) collective-permute-start(bf16[16,3584]{1,0:T(8,128)(2,1)S(1)} %slice.51), channel_id=1, source_target_pairs={{0,8},{4,12},{8,0},{12,4},{16,20},{20,16},{24,28},{28,24},{1,9},{5... | collective-permute-start | bytes 344072 | tf_op jit(solution)/shard_map/ppermute | solution.py:26
  45.3 0.9 %collective-permute-done.11 = bf16[32,3584]{1,0:T(8,128)(2,1)S(1)} collective-permute-done((bf16[32,3584]{1,0:T(8,128)(2,1)S(1)}, bf16[32,3584]{1,0:T(8,128)(2,1)S(1)}, u32[]{:S(2)}, u32[]{:S(2)}) %collective-permute-start.11) | collective-permute-done | bytes 229408 | tf_op jit(solution)/shard_map/ppermute | solution.py:26
  46.2 0.1 add_convert_fusion.2
  46.3 1.6 %collective-permute-start.12 = (bf16[16,3584]{1,0:T(8,128)(2,1)S(1)}, bf16[16,3584]{1,0:T(8,128)(2,1)S(1)}, u32[]{:S(2)}, u32[]{:S(2)}) collective-permute-start(bf16[16,3584]{1,0:T(8,128)(2,1)S(1)} %slice.55), channel_id=1, source_target_pairs={{0,8},{4,12},{8,0},{12,4},{16,20},{20,16},{24,28},{28,24},{1,9},{5... | collective-permute-start | bytes 344072 | tf_op jit(solution)/shard_map/ppermute | solution.py:26
  47.9 0.6 collective-permute-done.9
  48.5 2.6 %collective-permute-done.12 = bf16[16,3584]{1,0:T(8,128)(2,1)S(1)} collective-permute-done((bf16[16,3584]{1,0:T(8,128)(2,1)S(1)}, bf16[16,3584]{1,0:T(8,128)(2,1)S(1)}, u32[]{:S(2)}, u32[]{:S(2)}) %collective-permute-start.12) | collective-permute-done | bytes 114720 | tf_op jit(solution)/shard_map/ppermute | solution.py:26
  51.2 0.1 fusion.2
  51.2 2.8 %collective-permute-start.13 = (bf16[4,7168]{1,0:T(4,128)(2,1)S(1)}, bf16[4,7168]{1,0:T(4,128)(2,1)S(1)}, u32[]{:S(2)}, u32[]{:S(2)}) collective-permute-start(bf16[4,7168]{1,0:T(4,128)(2,1)S(1)} %get-tuple-element.69), channel_id=1, source_target_pairs={{0,3},{1,2},{2,1},{3,0},{16,17},{17,16},{18,19},{19,18},{4,7},{5,6... | collective-permute-start | bytes 172040 | tf_op jit(solution)/shard_map/ppermute | solution.py:41
  54.0 0.0 collective-permute-start.15
  54.0 1.7 %collective-permute-start.14 = (bf16[4,7168]{1,0:T(4,128)(2,1)S(1)}, bf16[4,7168]{1,0:T(4,128)(2,1)S(1)}, u32[]{:S(2)}, u32[]{:S(2)}) collective-permute-start(bf16[4,7168]{1,0:T(4,128)(2,1)S(1)} %get-tuple-element.71), channel_id=1, source_target_pairs={{0,1},{1,0},{2,3},{3,2},{16,18},{17,19},{18,16},{19,17},{4,5},{5,4... | collective-permute-start | bytes 172040 | tf_op jit(solution)/shard_map/ppermute | solution.py:41
  55.7 1.6 %collective-permute-done.13 = bf16[4,7168]{1,0:T(4,128)(2,1)S(1)} collective-permute-done((bf16[4,7168]{1,0:T(4,128)(2,1)S(1)}, bf16[4,7168]{1,0:T(4,128)(2,1)S(1)}, u32[]{:S(2)}, u32[]{:S(2)}) %collective-permute-start.13) | collective-permute-done | bytes 57376 | tf_op jit(solution)/shard_map/ppermute | solution.py:41
  57.3 1.8 %collective-permute-done.15 = bf16[4,7168]{1,0:T(4,128)(2,1)S(1)} collective-permute-done((bf16[4,7168]{1,0:T(4,128)(2,1)S(1)}, bf16[4,7168]{1,0:T(4,128)(2,1)S(1)}, u32[]{:S(2)}, u32[]{:S(2)}) %collective-permute-start.15) | collective-permute-done | bytes 57376 | tf_op jit(solution)/shard_map/ppermute | solution.py:41
  59.1 0.0 collective-permute-done.14
  59.1 0.7 %add_convert_fusion.6 = bf16[4,7168]{1,0:T(4,128)(2,1)} fusion(bf16[4,7168]{1,0:T(4,128)(2,1)S(1)} %collective-permute-done.15, bf16[4,7168]{1,0:T(4,128)(2,1)S(1)} %collective-permute-done.14, bf16[4,7168]{1,0:T(4,128)(2,1)S(1)} %collective-permute-done.13, bf16[16,3584]{1,0:T(8,128)(2,1)S(1)} %add_convert_fusion.5, bf16[16,3584]{1,0:T(8,128)(2,1)S(1)} %add_convert_fusion.4), kind=kLoop, calls=%fused_computation.12 | loop fusion | flops 315392 | bytes 458752 | tf_op jit(solution)/shard_map/convert_element_type | solution.py:375
  (7 shorter events, 0.1 us)
Async XLA Ops:
  1.0 8.0 %collective-permute-start.2 = (bf16[4,7296]{1,0:T(4,128)(2,1)S(1)}, bf16[4,7296]{1,0:T(4,128)(2,1)S(1)}, u32[]{:S(2)}, u32[]{:S(2)}) collective-permute-start(bf16[4,7296]{1,0:T(4,128)(2,1)S(1)} %extend.1.after_ref.refs_0_), channel_id=1, source_target_pairs={{0,3},{1,2},{2,1},{3,0},{16,19},{17,18},{18,17},{19,16},{4,7},{5,6... | collective-permute-start | bytes 175112 | tf_op jit(solution)/shard_map/ppermute | solution.py:41
  6.1 5.1 %collective-permute-start.1 = (bf16[4,7296]{1,0:T(4,128)(2,1)S(1)}, bf16[4,7296]{1,0:T(4,128)(2,1)S(1)}, u32[]{:S(2)}, u32[]{:S(2)}) collective-permute-start(bf16[4,7296]{1,0:T(4,128)(2,1)S(1)} %extend.1.after_ref.refs_0_), channel_id=1, source_target_pairs={{0,2},{1,3},{2,0},{3,1},{16,18},{17,19},{18,16},{19,17},{4,6},{5,7... | collective-permute-start | bytes 175112 | tf_op jit(solution)/shard_map/ppermute | solution.py:41
  6.1 5.1 %collective-permute-start = (bf16[4,7296]{1,0:T(4,128)(2,1)S(1)}, bf16[4,7296]{1,0:T(4,128)(2,1)S(1)}, u32[]{:S(2)}, u32[]{:S(2)}) collective-permute-start(bf16[4,7296]{1,0:T(4,128)(2,1)S(1)} %extend.1.after_ref.refs_0_), channel_id=1, source_target_pairs={{0,1},{1,0},{2,3},{3,2},{16,17},{17,16},{18,19},{19,18},{4,5},{5,4... | collective-permute-start | bytes 175112 | tf_op jit(solution)/shard_map/ppermute | solution.py:41
  11.3 6.1 %collective-permute-start.3 = (bf16[16,7296]{1,0:T(8,128)(2,1)S(1)}, bf16[16,7296]{1,0:T(8,128)(2,1)S(1)}, u32[]{:S(2)}, u32[]{:S(2)}) collective-permute-start(bf16[16,7296]{1,0:T(8,128)(2,1)S(1)} %stack.2.refs_0_), channel_id=1, source_target_pairs={{0,8},{4,12},{8,0},{12,4},{16,20},{20,16},{24,28},{28,24},{1,9},{5... | collective-permute-start | bytes 700424 | tf_op jit(solution)/shard_map/ppermute | solution.py:26
  17.4 8.6 %collective-permute-start.4 = (bf16[32,7296]{1,0:T(8,128)(2,1)S(1)}, bf16[32,7296]{1,0:T(8,128)(2,1)S(1)}, u32[]{:S(2)}, u32[]{:S(2)}) collective-permute-start(bf16[32,7296]{1,0:T(8,128)(2,1)S(1)} %stack.3.refs_0_), channel_id=1, source_target_pairs={{0,4},{4,0},{8,12},{12,8},{16,24},{20,28},{24,16},{28,20},{1,5},{5... | collective-permute-start | bytes 1400840 | tf_op jit(solution)/shard_map/ppermute | solution.py:26
  22.2 3.8 %collective-permute-start.5 = (bf16[32,7296]{1,0:T(8,128)(2,1)S(1)}, bf16[32,7296]{1,0:T(8,128)(2,1)S(1)}, u32[]{:S(2)}, u32[]{:S(2)}) collective-permute-start(bf16[32,7296]{1,0:T(8,128)(2,1)S(1)} %stack.3.refs_0_), channel_id=1, source_target_pairs={{0,16},{16,0},{1,17},{17,1},{2,18},{18,2},{3,19},{19,3},{4,20},{20... | collective-permute-start | bytes 1400840 | tf_op jit(solution)/shard_map/ppermute | solution.py:45
  26.1 1.8 %collective-permute-start.6 = (bf16[32,7296]{1,0:T(8,128)(2,1)S(1)}, bf16[32,7296]{1,0:T(8,128)(2,1)S(1)}, u32[]{:S(2)}, u32[]{:S(2)}) collective-permute-start(bf16[32,7296]{1,0:T(8,128)(2,1)S(1)} %collective-permute-done.4.refs_1_), channel_id=1, source_target_pairs={{0,16},{16,0},{1,17},{17,1},{2,18},{18,2},{3,19},{19,3},{4,20},{20... | collective-permute-start | bytes 1400840 | tf_op jit(solution)/shard_map/ppermute | solution.py:45
  35.4 1.9 %collective-permute-start.7 = (bf16[64,3584]{1,0:T(8,128)(2,1)S(1)}, bf16[64,3584]{1,0:T(8,128)(2,1)S(1)}, u32[]{:S(2)}, u32[]{:S(2)}) collective-permute-start(bf16[64,3584]{1,0:T(8,128)(2,1)S(1)} %get-tuple-element.63), channel_id=1, source_target_pairs={{0,16},{16,0},{1,17},{17,1},{2,18},{18,2},{3,19},{19,3},{4,20},{20... | collective-permute-start | bytes 1376264 | tf_op jit(solution)/shard_map/ppermute | solution.py:45
  36.9 2.1 %collective-permute-start.10 = (bf16[64,3584]{1,0:T(8,128)(2,1)S(1)}, bf16[64,3584]{1,0:T(8,128)(2,1)S(1)}, u32[]{:S(2)}, u32[]{:S(2)}) collective-permute-start(bf16[64,3584]{1,0:T(8,128)(2,1)S(1)} %get-tuple-element.68), channel_id=1, source_target_pairs={{0,16},{16,0},{1,17},{17,1},{2,18},{18,2},{3,19},{19,3},{4,20},{20... | collective-permute-start | bytes 1376264 | tf_op jit(solution)/shard_map/ppermute | solution.py:45
  37.5 6.1 %collective-permute-start.8 = (bf16[32,3584]{1,0:T(8,128)(2,1)S(1)}, bf16[32,3584]{1,0:T(8,128)(2,1)S(1)}, u32[]{:S(2)}, u32[]{:S(2)}) collective-permute-start(bf16[32,3584]{1,0:T(8,128)(2,1)S(1)} %slice.49), channel_id=1, source_target_pairs={{0,4},{4,0},{8,12},{12,8},{16,24},{20,28},{24,16},{28,20},{1,5},{5... | collective-permute-start | bytes 688136 | tf_op jit(solution)/shard_map/ppermute | solution.py:26
  39.2 7.0 %collective-permute-start.11 = (bf16[32,3584]{1,0:T(8,128)(2,1)S(1)}, bf16[32,3584]{1,0:T(8,128)(2,1)S(1)}, u32[]{:S(2)}, u32[]{:S(2)}) collective-permute-start(bf16[32,3584]{1,0:T(8,128)(2,1)S(1)} %slice.53), channel_id=1, source_target_pairs={{0,4},{4,0},{8,12},{12,8},{16,24},{20,28},{24,16},{28,20},{1,5},{5... | collective-permute-start | bytes 688136 | tf_op jit(solution)/shard_map/ppermute | solution.py:26
  43.6 4.9 %collective-permute-start.9 = (bf16[16,3584]{1,0:T(8,128)(2,1)S(1)}, bf16[16,3584]{1,0:T(8,128)(2,1)S(1)}, u32[]{:S(2)}, u32[]{:S(2)}) collective-permute-start(bf16[16,3584]{1,0:T(8,128)(2,1)S(1)} %slice.51), channel_id=1, source_target_pairs={{0,8},{4,12},{8,0},{12,4},{16,20},{20,16},{24,28},{28,24},{1,9},{5... | collective-permute-start | bytes 344072 | tf_op jit(solution)/shard_map/ppermute | solution.py:26
  46.3 4.9 %collective-permute-start.12 = (bf16[16,3584]{1,0:T(8,128)(2,1)S(1)}, bf16[16,3584]{1,0:T(8,128)(2,1)S(1)}, u32[]{:S(2)}, u32[]{:S(2)}) collective-permute-start(bf16[16,3584]{1,0:T(8,128)(2,1)S(1)} %slice.55), channel_id=1, source_target_pairs={{0,8},{4,12},{8,0},{12,4},{16,20},{20,16},{24,28},{28,24},{1,9},{5... | collective-permute-start | bytes 344072 | tf_op jit(solution)/shard_map/ppermute | solution.py:26
  51.2 6.0 %collective-permute-start.13 = (bf16[4,7168]{1,0:T(4,128)(2,1)S(1)}, bf16[4,7168]{1,0:T(4,128)(2,1)S(1)}, u32[]{:S(2)}, u32[]{:S(2)}) collective-permute-start(bf16[4,7168]{1,0:T(4,128)(2,1)S(1)} %get-tuple-element.69), channel_id=1, source_target_pairs={{0,3},{1,2},{2,1},{3,0},{16,17},{17,16},{18,19},{19,18},{4,7},{5,6... | collective-permute-start | bytes 172040 | tf_op jit(solution)/shard_map/ppermute | solution.py:41
  54.0 5.1 %collective-permute-start.15 = (bf16[4,7168]{1,0:T(4,128)(2,1)S(1)}, bf16[4,7168]{1,0:T(4,128)(2,1)S(1)}, u32[]{:S(2)}, u32[]{:S(2)}) collective-permute-start(bf16[4,7168]{1,0:T(4,128)(2,1)S(1)} %get-tuple-element.70), channel_id=1, source_target_pairs={{0,2},{1,3},{2,0},{3,1},{16,19},{17,18},{18,17},{19,16},{4,6},{5,7... | collective-permute-start | bytes 172040 | tf_op jit(solution)/shard_map/ppermute | solution.py:41
  54.0 5.1 %collective-permute-start.14 = (bf16[4,7168]{1,0:T(4,128)(2,1)S(1)}, bf16[4,7168]{1,0:T(4,128)(2,1)S(1)}, u32[]{:S(2)}, u32[]{:S(2)}) collective-permute-start(bf16[4,7168]{1,0:T(4,128)(2,1)S(1)} %get-tuple-element.71), channel_id=1, source_target_pairs={{0,1},{1,0},{2,3},{3,2},{16,18},{17,19},{18,16},{19,17},{4,5},{5,4... | collective-permute-start | bytes 172040 | tf_op jit(solution)/shard_map/ppermute | solution.py:41

commit v18 on v17

--- a/solution.py
+++ b/solution.py
@@ -28,9 +28,14 @@
 
 def line_orders():
     lanes = lax.axis_size("dev")
-    near = list(range(1, lanes))
-    orders = [[0] + near[-1:] + near[:-1], [0] + near]
+    near = list(range(lanes))
+    orders = [[0, 2, 1, 3] if lanes == 4 else near, near]
     return [orders[s % 2] for s in range(lax.axis_size("sect"))]
+
+
+def line_masks():
+    lanes = lax.axis_size("dev")
+    return (1, 3, 2) if lanes == 4 else range(1, lanes)
 
 
 def swap_line(value, masks):
@@ -126,7 +131,8 @@
             held[id(weight), expert, row] = array
         return token
 
-    arrived = [swap_line(block, (m,) * sects) for m in range(1, lanes)]
+    by_mask = {m: swap_line(block, (m,) * sects) for m in line_masks()}
+    arrived = [by_mask[m] for m in range(1, lanes)]
     token = fetch_next(0, 2, token)
     arrived, token = lax.optimization_barrier((arrived, token))
     line = stack([block, *arrived], line_orders())

time: 60 us -> 60.5 us (level)
  waiting for transfers between devices: 14.2 us -> 15.5 us
  starting transfers between devices: 20.6 us -> 19.8 us
    ppermute x6, waiting for transfers between devices: 5.57 us -> 6.97 us  [swap_line(): return lax.ppermute(value, ('sect', 'dev'), pairs)]
    ppermute x6, starting transfers between devices: 10.2 us -> 9.35 us  [swap_line(): return lax.ppermute(value, ('sect', 'dev'), pairs)]
  transfers between devices with their start and end apart: 16 -> 16, of which waited for: 11 -> 12; matrix products, arithmetic and copies ran while one was open for 1% -> 1% of each run, Pallas kernels for 25% -> 25%
where the time goes in v18:
time: 60.5 us; the launch traced here: 60.3 us
  Pallas kernels  23.6 us (39%)
  starting transfers between devices  19.8 us (33%)
  waiting for transfers between devices  15.5 us (26%)
  other arithmetic  1.14 us (2%)
    pallas_call x5, Pallas kernels, fetch(): pl.pallas_call(functools.partial(fetch_kernel, [(None, *w[1:]) for w in w...  13.9 us
    ppermute x6, starting transfers between devices, swap(): return lax.ppermute(value, ('sect', 'grp'), pairs)  9.68 us
    ppermute x6, starting transfers between devices, swap_line(): return lax.ppermute(value, ('sect', 'dev'), pairs)  9.35 us
    ppermute x6, waiting for transfers between devices, swap(): return lax.ppermute(value, ('sect', 'grp'), pairs)  8.24 us
    pallas_call x1, Pallas kernels, expert_call(): pl.pallas_call(functools.partial(expert_kernel, len(entries), experts, wi...  7.52 us
    ppermute x6, waiting for transfers between devices, swap_line(): return lax.ppermute(value, ('sect', 'dev'), pairs)  6.97 us
  transfers between devices with their start and end apart: 16, of which 12 were waited for; matrix products, arithmetic and copies ran while one was open for 1% of the time, Pallas kernels for 25%

profile of v18, /device:TPU:0, one launch (start us, length us, event | category | flops | bytes accessed | tf_op | source)
XLA Modules:
  0.0 60.3 jit_solution(15182716445771356560)
XLA Ops:
  0.0 1.0 %extend.1.after_ref.refs_0_ = bf16[4,7296]{1,0:T(4,128)(2,1)S(1)} custom-call(bf16[4,7168]{1,0:T(4,128)(2,1)} %tokens_hbm.1, s32[4,8]{1,0:T(4,128)} %ids_hbm.1, f32[4,8]{1,0:T(4,128)} %weights_hbm.1), custom_call_target="tpu_custom_call" | custom-call | tf_op jit(solution)/shard_map/extend/pallas_call | solution.py:86
  1.0 5.1 %collective-permute-start.2 = (bf16[4,7296]{1,0:T(4,128)(2,1)S(1)}, bf16[4,7296]{1,0:T(4,128)(2,1)S(1)}, u32[]{:S(2)}, u32[]{:S(2)}) collective-permute-start(bf16[4,7296]{1,0:T(4,128)(2,1)S(1)} %extend.1.after_ref.refs_0_), channel_id=1, source_target_pairs={{0,3},{1,2},{2,1},{3,0},{16,19},{17,18},{18,17},{19,16},{4,7},{5,6... | collective-permute-start | bytes 175112 | tf_op jit(solution)/shard_map/ppermute | solution.py:46
  6.1 0.0 collective-permute-start.1
  6.1 0.6 %collective-permute-start = (bf16[4,7296]{1,0:T(4,128)(2,1)S(1)}, bf16[4,7296]{1,0:T(4,128)(2,1)S(1)}, u32[]{:S(2)}, u32[]{:S(2)}) collective-permute-start(bf16[4,7296]{1,0:T(4,128)(2,1)S(1)} %extend.1.after_ref.refs_0_), channel_id=1, source_target_pairs={{0,1},{1,0},{2,3},{3,2},{16,17},{17,16},{18,19},{19,18},{4,5},{5,4... | collective-permute-start | bytes 175112 | tf_op jit(solution)/shard_map/ppermute | solution.py:46
  6.7 2.2 %fetch.5 = (bf16[1,256,3584]{2,1,0:T(8,128)(2,1)S(1)}, bf16[1,256,3584]{2,1,0:T(8,128)(2,1)S(1)}, f32[8,128]{1,0:T(8,128)S(1)}) custom-call(bf16[4,7296]{1,0:T(4,128)(2,1)S(1)} %extend.1.after_ref.refs_0_, bf16[2,512,7168]{2,1,0:T(8,128)(2,1)} %refs_12_.1, bf16[2,512,7168]{2,1,0:T(8,128)(2,1)} %refs_12_.1), custom_call_target="tpu_custom_call" | custom-call | bytes 3670016 | tf_op jit(solution)/shard_map/fetch/pallas_call | solution.py:297
  9.0 0.0 collective-permute-done.2.refs_3_
  9.0 2.2 %collective-permute-done.1.refs_2_ = bf16[4,7296]{1,0:T(4,128)(2,1)S(1)} collective-permute-done((bf16[4,7296]{1,0:T(4,128)(2,1)S(1)}, bf16[4,7296]{1,0:T(4,128)(2,1)S(1)}, u32[]{:S(2)}, u32[]{:S(2)}) %collective-permute-start.1) | collective-permute-done | bytes 58400 | tf_op jit(solution)/shard_map/ppermute | solution.py:46
  11.2 0.0 collective-permute-done.refs_1_
  11.2 0.1 stack.2.refs_0_
  11.3 1.7 %collective-permute-start.3 = (bf16[16,7296]{1,0:T(8,128)(2,1)S(1)}, bf16[16,7296]{1,0:T(8,128)(2,1)S(1)}, u32[]{:S(2)}, u32[]{:S(2)}) collective-permute-start(bf16[16,7296]{1,0:T(8,128)(2,1)S(1)} %stack.2.refs_0_), channel_id=1, source_target_pairs={{0,8},{4,12},{8,0},{12,4},{16,20},{20,16},{24,28},{28,24},{1,9},{5... | collective-permute-start | bytes 700424 | tf_op jit(solution)/shard_map/ppermute | solution.py:26
  12.9 3.7 %fetch.6 = (bf16[1,7168,512]{2,1,0:T(8,128)(2,1)S(1)}, bf16[1,256,3584]{2,1,0:T(8,128)(2,1)S(1)}, f32[8,128]{1,0:T(8,128)S(1)}) custom-call(f32[8,128]{1,0:T(8,128)S(1)} %get-tuple-element.41.after_ref, bf16[2,7168,512]{2,1,0:T(8,128)(2,1)} %refs_0_.7, bf16[2,512,7168]{2,1,0:T(8,128)(2,1)} %refs_12_.1), custom_call_target="tpu_custom_call" | custom-call | bytes 9175040 | tf_op jit(solution)/shard_map/fetch/pallas_call | solution.py:297
  16.6 0.7 %collective-permute-done.3.refs_1_ = bf16[16,7296]{1,0:T(8,128)(2,1)S(1)} collective-permute-done((bf16[16,7296]{1,0:T(8,128)(2,1)S(1)}, bf16[16,7296]{1,0:T(8,128)(2,1)S(1)}, u32[]{:S(2)}, u32[]{:S(2)}) %collective-permute-start.3) | collective-permute-done | bytes 233504 | tf_op jit(solution)/shard_map/ppermute | solution.py:26
  17.4 1.6 %collective-permute-start.4 = (bf16[32,7296]{1,0:T(8,128)(2,1)S(1)}, bf16[32,7296]{1,0:T(8,128)(2,1)S(1)}, u32[]{:S(2)}, u32[]{:S(2)}) collective-permute-start(bf16[32,7296]{1,0:T(8,128)(2,1)S(1)} %stack.3.refs_0_), channel_id=1, source_target_pairs={{0,4},{4,0},{8,12},{12,8},{16,24},{20,28},{24,16},{28,20},{1,5},{5... | collective-permute-start | bytes 1400840 | tf_op jit(solution)/shard_map/ppermute | solution.py:26
  19.1 3.2 %fetch.7 = (bf16[1,7168,512]{2,1,0:T(8,128)(2,1)S(1)}, f32[8,128]{1,0:T(8,128)S(1)}) custom-call(f32[8,128]{1,0:T(8,128)S(1)} %get-tuple-element.44.after_ref, bf16[2,7168,512]{2,1,0:T(8,128)(2,1)} %refs_0_.7), custom_call_target="tpu_custom_call" | custom-call | bytes 7340032 | tf_op jit(solution)/shard_map/fetch/pallas_call | solution.py:297
  22.3 0.1 collective-permute-start.5
  22.3 3.2 %fetch.8 = (bf16[1,7168,512]{2,1,0:T(8,128)(2,1)S(1)}, f32[8,128]{1,0:T(8,128)S(1)}) custom-call(f32[8,128]{1,0:T(8,128)S(1)} %get-tuple-element.47.after_ref, bf16[2,7168,512]{2,1,0:T(8,128)(2,1)} %refs_11_.1), custom_call_target="tpu_custom_call" | custom-call | bytes 7340032 | tf_op jit(solution)/shard_map/fetch/pallas_call | solution.py:297
  25.5 0.6 collective-permute-done.4.refs_1_
  26.1 0.0 collective-permute-done.5.refs_2_
  26.1 0.0 collective-permute-start.6
  26.1 1.6 %fetch.9 = (bf16[1,256,3584]{2,1,0:T(8,128)(2,1)S(1)}, f32[8,128]{1,0:T(8,128)S(1)}) custom-call(f32[8,128]{1,0:T(8,128)S(1)} %get-tuple-element.50.after_ref, bf16[2,512,7168]{2,1,0:T(8,128)(2,1)} %refs_12_.1), custom_call_target="tpu_custom_call" | custom-call | bytes 1835008 | tf_op jit(solution)/shard_map/fetch/pallas_call | solution.py:297
  27.7 0.2 collective-permute-done.6.refs_3_
  27.9 7.5 %experts.1 = (bf16[128,1024]{1,0:T(8,128)(2,1)S(1)}, bf16[64,3584]{1,0:T(8,128)(2,1)S(1)}, bf16[64,3584]{1,0:T(8,128)(2,1)S(1)}, bf16[1,7168,512]{2,1,0:T(8,128)(2,1)S(1)}, bf16[1,7168,512]{2,1,0:T(8,128)(2,1)S(1)}) custom-call(f32[8,128]{1,0:T(8,128)S(1)} %get-tuple-element.52.token_ref, ...), custom_call_target="tpu_custom_call", output_to_operand_aliasing={{3}: (5, {}), {4}: (6, {})} | custom-call | flops 4697620480 | bytes 14680064 | tf_op jit(solution)/shard_map/experts/pallas_call | solution.py:329
  35.4 0.4 collective-permute-start.7
  35.8 1.1 %down.1 = (bf16[64,3584]{1,0:T(8,128)(2,1)S(1)}, bf16[64,3584]{1,0:T(8,128)(2,1)S(1)}) custom-call(bf16[128,1024]{1,0:T(8,128)(2,1)S(1)} %get-tuple-element.64.hidden_ref, bf16[1,7168,512]{2,1,0:T(8,128)(2,1)S(1)} %get-tuple-element.65.refs_0_, bf16[1,7168,512]{2,1,0:T(8,128)(2,1)S(1)} %get-tuple-element.66.refs_1_), custom_call_target="tpu_custom_call" | custom-call | flops 939524096 | bytes 917504 | tf_op jit(solution)/shard_map/down/pallas_call | solution.py:361
  37.0 0.2 collective-permute-start.10
  37.2 0.1 collective-permute-done.7
  37.3 0.1 add_convert_fusion.1
  37.4 1.7 %collective-permute-start.8 = (bf16[32,3584]{1,0:T(8,128)(2,1)S(1)}, bf16[32,3584]{1,0:T(8,128)(2,1)S(1)}, u32[]{:S(2)}, u32[]{:S(2)}) collective-permute-start(bf16[32,3584]{1,0:T(8,128)(2,1)S(1)} %slice.49), channel_id=1, source_target_pairs={{0,4},{4,0},{8,12},{12,8},{16,24},{20,28},{24,16},{28,20},{1,5},{5... | collective-permute-start | bytes 688136 | tf_op jit(solution)/shard_map/ppermute | solution.py:26
  39.1 0.0 collective-permute-done.10
  39.1 0.1 add_convert_fusion
  39.2 1.4 %collective-permute-start.11 = (bf16[32,3584]{1,0:T(8,128)(2,1)S(1)}, bf16[32,3584]{1,0:T(8,128)(2,1)S(1)}, u32[]{:S(2)}, u32[]{:S(2)}) collective-permute-start(bf16[32,3584]{1,0:T(8,128)(2,1)S(1)} %slice.53), channel_id=1, source_target_pairs={{0,4},{4,0},{8,12},{12,8},{16,24},{20,28},{24,16},{28,20},{1,5},{5... | collective-permute-start | bytes 688136 | tf_op jit(solution)/shard_map/ppermute | solution.py:26
  40.6 2.9 %collective-permute-done.8 = bf16[32,3584]{1,0:T(8,128)(2,1)S(1)} collective-permute-done((bf16[32,3584]{1,0:T(8,128)(2,1)S(1)}, bf16[32,3584]{1,0:T(8,128)(2,1)S(1)}, u32[]{:S(2)}, u32[]{:S(2)}) %collective-permute-start.8) | collective-permute-done | bytes 229408 | tf_op jit(solution)/shard_map/ppermute | solution.py:26
  43.5 0.1 add_convert_fusion.3
  43.6 1.7 %collective-permute-start.9 = (bf16[16,3584]{1,0:T(8,128)(2,1)S(1)}, bf16[16,3584]{1,0:T(8,128)(2,1)S(1)}, u32[]{:S(2)}, u32[]{:S(2)}) collective-permute-start(bf16[16,3584]{1,0:T(8,128)(2,1)S(1)} %slice.51), channel_id=1, source_target_pairs={{0,8},{4,12},{8,0},{12,4},{16,20},{20,16},{24,28},{28,24},{1,9},{5... | collective-permute-start | bytes 344072 | tf_op jit(solution)/shard_map/ppermute | solution.py:26
  45.3 0.9 %collective-permute-done.11 = bf16[32,3584]{1,0:T(8,128)(2,1)S(1)} collective-permute-done((bf16[32,3584]{1,0:T(8,128)(2,1)S(1)}, bf16[32,3584]{1,0:T(8,128)(2,1)S(1)}, u32[]{:S(2)}, u32[]{:S(2)}) %collective-permute-start.11) | collective-permute-done | bytes 229408 | tf_op jit(solution)/shard_map/ppermute | solution.py:26
  46.1 0.1 add_convert_fusion.2
  46.2 1.7 %collective-permute-start.12 = (bf16[16,3584]{1,0:T(8,128)(2,1)S(1)}, bf16[16,3584]{1,0:T(8,128)(2,1)S(1)}, u32[]{:S(2)}, u32[]{:S(2)}) collective-permute-start(bf16[16,3584]{1,0:T(8,128)(2,1)S(1)} %slice.55), channel_id=1, source_target_pairs={{0,8},{4,12},{8,0},{12,4},{16,20},{20,16},{24,28},{28,24},{1,9},{5... | collective-permute-start | bytes 344072 | tf_op jit(solution)/shard_map/ppermute | solution.py:26
  47.9 0.6 collective-permute-done.9
  48.5 2.6 %collective-permute-done.12 = bf16[16,3584]{1,0:T(8,128)(2,1)S(1)} collective-permute-done((bf16[16,3584]{1,0:T(8,128)(2,1)S(1)}, bf16[16,3584]{1,0:T(8,128)(2,1)S(1)}, u32[]{:S(2)}, u32[]{:S(2)}) %collective-permute-start.12) | collective-permute-done | bytes 114720 | tf_op jit(solution)/shard_map/ppermute | solution.py:26
  51.1 0.1 fusion.2
  51.2 2.1 %collective-permute-start.13 = (bf16[4,7168]{1,0:T(4,128)(2,1)S(1)}, bf16[4,7168]{1,0:T(4,128)(2,1)S(1)}, u32[]{:S(2)}, u32[]{:S(2)}) collective-permute-start(bf16[4,7168]{1,0:T(4,128)(2,1)S(1)} %get-tuple-element.69), channel_id=1, source_target_pairs={{0,2},{1,3},{2,0},{3,1},{16,17},{17,16},{18,19},{19,18},{4,6},{5,7... | collective-permute-start | bytes 172040 | tf_op jit(solution)/shard_map/ppermute | solution.py:46
  53.3 1.5 %collective-permute-start.15 = (bf16[4,7168]{1,0:T(4,128)(2,1)S(1)}, bf16[4,7168]{1,0:T(4,128)(2,1)S(1)}, u32[]{:S(2)}, u32[]{:S(2)}) collective-permute-start(bf16[4,7168]{1,0:T(4,128)(2,1)S(1)} %get-tuple-element.70), channel_id=1, source_target_pairs={{0,3},{1,2},{2,1},{3,0},{16,19},{17,18},{18,17},{19,16},{4,7},{5,6... | collective-permute-start | bytes 172040 | tf_op jit(solution)/shard_map/ppermute | solution.py:46
  54.8 0.0 collective-permute-start.14
  54.8 3.3 %collective-permute-done.13 = bf16[4,7168]{1,0:T(4,128)(2,1)S(1)} collective-permute-done((bf16[4,7168]{1,0:T(4,128)(2,1)S(1)}, bf16[4,7168]{1,0:T(4,128)(2,1)S(1)}, u32[]{:S(2)}, u32[]{:S(2)}) %collective-permute-start.13) | collective-permute-done | bytes 57376 | tf_op jit(solution)/shard_map/ppermute | solution.py:46
  58.1 1.3 %collective-permute-done.15 = bf16[4,7168]{1,0:T(4,128)(2,1)S(1)} collective-permute-done((bf16[4,7168]{1,0:T(4,128)(2,1)S(1)}, bf16[4,7168]{1,0:T(4,128)(2,1)S(1)}, u32[]{:S(2)}, u32[]{:S(2)}) %collective-permute-start.15) | collective-permute-done | bytes 57376 | tf_op jit(solution)/shard_map/ppermute | solution.py:46
  59.4 0.2 collective-permute-done.14
  59.6 0.7 %add_convert_fusion.6 = bf16[4,7168]{1,0:T(4,128)(2,1)} fusion(bf16[4,7168]{1,0:T(4,128)(2,1)S(1)} %collective-permute-done.15, bf16[4,7168]{1,0:T(4,128)(2,1)S(1)} %collective-permute-done.14, bf16[4,7168]{1,0:T(4,128)(2,1)S(1)} %collective-permute-done.13, bf16[16,3584]{1,0:T(8,128)(2,1)S(1)} %add_convert_fusion.5, bf16[16,3584]{1,0:T(8,128)(2,1)S(1)} %add_convert_fusion.4), kind=kLoop, calls=%fused_computation.12 | loop fusion | flops 315392 | bytes 458752 | tf_op jit(solution)/shard_map/convert_element_type | solution.py:381
  (7 shorter events, 0.1 us)
Async XLA Ops:
  1.0 8.0 %collective-permute-start.2 = (bf16[4,7296]{1,0:T(4,128)(2,1)S(1)}, bf16[4,7296]{1,0:T(4,128)(2,1)S(1)}, u32[]{:S(2)}, u32[]{:S(2)}) collective-permute-start(bf16[4,7296]{1,0:T(4,128)(2,1)S(1)} %extend.1.after_ref.refs_0_), channel_id=1, source_target_pairs={{0,3},{1,2},{2,1},{3,0},{16,19},{17,18},{18,17},{19,16},{4,7},{5,6... | collective-permute-start | bytes 175112 | tf_op jit(solution)/shard_map/ppermute | solution.py:46
  6.1 5.1 %collective-permute-start.1 = (bf16[4,7296]{1,0:T(4,128)(2,1)S(1)}, bf16[4,7296]{1,0:T(4,128)(2,1)S(1)}, u32[]{:S(2)}, u32[]{:S(2)}) collective-permute-start(bf16[4,7296]{1,0:T(4,128)(2,1)S(1)} %extend.1.after_ref.refs_0_), channel_id=1, source_target_pairs={{0,2},{1,3},{2,0},{3,1},{16,18},{17,19},{18,16},{19,17},{4,6},{5,7... | collective-permute-start | bytes 175112 | tf_op jit(solution)/shard_map/ppermute | solution.py:46
  6.1 5.1 %collective-permute-start = (bf16[4,7296]{1,0:T(4,128)(2,1)S(1)}, bf16[4,7296]{1,0:T(4,128)(2,1)S(1)}, u32[]{:S(2)}, u32[]{:S(2)}) collective-permute-start(bf16[4,7296]{1,0:T(4,128)(2,1)S(1)} %extend.1.after_ref.refs_0_), channel_id=1, source_target_pairs={{0,1},{1,0},{2,3},{3,2},{16,17},{17,16},{18,19},{19,18},{4,5},{5,4... | collective-permute-start | bytes 175112 | tf_op jit(solution)/shard_map/ppermute | solution.py:46
  11.3 6.1 %collective-permute-start.3 = (bf16[16,7296]{1,0:T(8,128)(2,1)S(1)}, bf16[16,7296]{1,0:T(8,128)(2,1)S(1)}, u32[]{:S(2)}, u32[]{:S(2)}) collective-permute-start(bf16[16,7296]{1,0:T(8,128)(2,1)S(1)} %stack.2.refs_0_), channel_id=1, source_target_pairs={{0,8},{4,12},{8,0},{12,4},{16,20},{20,16},{24,28},{28,24},{1,9},{5... | collective-permute-start | bytes 700424 | tf_op jit(solution)/shard_map/ppermute | solution.py:26
  17.4 8.6 %collective-permute-start.4 = (bf16[32,7296]{1,0:T(8,128)(2,1)S(1)}, bf16[32,7296]{1,0:T(8,128)(2,1)S(1)}, u32[]{:S(2)}, u32[]{:S(2)}) collective-permute-start(bf16[32,7296]{1,0:T(8,128)(2,1)S(1)} %stack.3.refs_0_), channel_id=1, source_target_pairs={{0,4},{4,0},{8,12},{12,8},{16,24},{20,28},{24,16},{28,20},{1,5},{5... | collective-permute-start | bytes 1400840 | tf_op jit(solution)/shard_map/ppermute | solution.py:26
  22.3 3.8 %collective-permute-start.5 = (bf16[32,7296]{1,0:T(8,128)(2,1)S(1)}, bf16[32,7296]{1,0:T(8,128)(2,1)S(1)}, u32[]{:S(2)}, u32[]{:S(2)}) collective-permute-start(bf16[32,7296]{1,0:T(8,128)(2,1)S(1)} %stack.3.refs_0_), channel_id=1, source_target_pairs={{0,16},{16,0},{1,17},{17,1},{2,18},{18,2},{3,19},{19,3},{4,20},{20... | collective-permute-start | bytes 1400840 | tf_op jit(solution)/shard_map/ppermute | solution.py:50
  26.1 1.8 %collective-permute-start.6 = (bf16[32,7296]{1,0:T(8,128)(2,1)S(1)}, bf16[32,7296]{1,0:T(8,128)(2,1)S(1)}, u32[]{:S(2)}, u32[]{:S(2)}) collective-permute-start(bf16[32,7296]{1,0:T(8,128)(2,1)S(1)} %collective-permute-done.4.refs_1_), channel_id=1, source_target_pairs={{0,16},{16,0},{1,17},{17,1},{2,18},{18,2},{3,19},{19,3},{4,20},{20... | collective-permute-start | bytes 1400840 | tf_op jit(solution)/shard_map/ppermute | solution.py:50
  35.4 1.9 %collective-permute-start.7 = (bf16[64,3584]{1,0:T(8,128)(2,1)S(1)}, bf16[64,3584]{1,0:T(8,128)(2,1)S(1)}, u32[]{:S(2)}, u32[]{:S(2)}) collective-permute-start(bf16[64,3584]{1,0:T(8,128)(2,1)S(1)} %get-tuple-element.63), channel_id=1, source_target_pairs={{0,16},{16,0},{1,17},{17,1},{2,18},{18,2},{3,19},{19,3},{4,20},{20... | collective-permute-start | bytes 1376264 | tf_op jit(solution)/shard_map/ppermute | solution.py:50
  37.0 2.1 %collective-permute-start.10 = (bf16[64,3584]{1,0:T(8,128)(2,1)S(1)}, bf16[64,3584]{1,0:T(8,128)(2,1)S(1)}, u32[]{:S(2)}, u32[]{:S(2)}) collective-permute-start(bf16[64,3584]{1,0:T(8,128)(2,1)S(1)} %get-tuple-element.68), channel_id=1, source_target_pairs={{0,16},{16,0},{1,17},{17,1},{2,18},{18,2},{3,19},{19,3},{4,20},{20... | collective-permute-start | bytes 1376264 | tf_op jit(solution)/shard_map/ppermute | solution.py:50
  37.4 6.1 %collective-permute-start.8 = (bf16[32,3584]{1,0:T(8,128)(2,1)S(1)}, bf16[32,3584]{1,0:T(8,128)(2,1)S(1)}, u32[]{:S(2)}, u32[]{:S(2)}) collective-permute-start(bf16[32,3584]{1,0:T(8,128)(2,1)S(1)} %slice.49), channel_id=1, source_target_pairs={{0,4},{4,0},{8,12},{12,8},{16,24},{20,28},{24,16},{28,20},{1,5},{5... | collective-permute-start | bytes 688136 | tf_op jit(solution)/shard_map/ppermute | solution.py:26
  39.2 6.9 %collective-permute-start.11 = (bf16[32,3584]{1,0:T(8,128)(2,1)S(1)}, bf16[32,3584]{1,0:T(8,128)(2,1)S(1)}, u32[]{:S(2)}, u32[]{:S(2)}) collective-permute-start(bf16[32,3584]{1,0:T(8,128)(2,1)S(1)} %slice.53), channel_id=1, source_target_pairs={{0,4},{4,0},{8,12},{12,8},{16,24},{20,28},{24,16},{28,20},{1,5},{5... | collective-permute-start | bytes 688136 | tf_op jit(solution)/shard_map/ppermute | solution.py:26
  43.6 4.9 %collective-permute-start.9 = (bf16[16,3584]{1,0:T(8,128)(2,1)S(1)}, bf16[16,3584]{1,0:T(8,128)(2,1)S(1)}, u32[]{:S(2)}, u32[]{:S(2)}) collective-permute-start(bf16[16,3584]{1,0:T(8,128)(2,1)S(1)} %slice.51), channel_id=1, source_target_pairs={{0,8},{4,12},{8,0},{12,4},{16,20},{20,16},{24,28},{28,24},{1,9},{5... | collective-permute-start | bytes 344072 | tf_op jit(solution)/shard_map/ppermute | solution.py:26
  46.2 4.9 %collective-permute-start.12 = (bf16[16,3584]{1,0:T(8,128)(2,1)S(1)}, bf16[16,3584]{1,0:T(8,128)(2,1)S(1)}, u32[]{:S(2)}, u32[]{:S(2)}) collective-permute-start(bf16[16,3584]{1,0:T(8,128)(2,1)S(1)} %slice.55), channel_id=1, source_target_pairs={{0,8},{4,12},{8,0},{12,4},{16,20},{20,16},{24,28},{28,24},{1,9},{5... | collective-permute-start | bytes 344072 | tf_op jit(solution)/shard_map/ppermute | solution.py:26
  51.2 6.9 %collective-permute-start.13 = (bf16[4,7168]{1,0:T(4,128)(2,1)S(1)}, bf16[4,7168]{1,0:T(4,128)(2,1)S(1)}, u32[]{:S(2)}, u32[]{:S(2)}) collective-permute-start(bf16[4,7168]{1,0:T(4,128)(2,1)S(1)} %get-tuple-element.69), channel_id=1, source_target_pairs={{0,2},{1,3},{2,0},{3,1},{16,17},{17,16},{18,19},{19,18},{4,6},{5,7... | collective-permute-start | bytes 172040 | tf_op jit(solution)/shard_map/ppermute | solution.py:46
  53.3 6.1 %collective-permute-start.15 = (bf16[4,7168]{1,0:T(4,128)(2,1)S(1)}, bf16[4,7168]{1,0:T(4,128)(2,1)S(1)}, u32[]{:S(2)}, u32[]{:S(2)}) collective-permute-start(bf16[4,7168]{1,0:T(4,128)(2,1)S(1)} %get-tuple-element.70), channel_id=1, source_target_pairs={{0,3},{1,2},{2,1},{3,0},{16,19},{17,18},{18,17},{19,16},{4,7},{5,6... | collective-permute-start | bytes 172040 | tf_op jit(solution)/shard_map/ppermute | solution.py:46
  54.8 4.8 %collective-permute-start.14 = (bf16[4,7168]{1,0:T(4,128)(2,1)S(1)}, bf16[4,7168]{1,0:T(4,128)(2,1)S(1)}, u32[]{:S(2)}, u32[]{:S(2)}) collective-permute-start(bf16[4,7168]{1,0:T(4,128)(2,1)S(1)} %get-tuple-element.71), channel_id=1, source_target_pairs={{0,1},{1,0},{2,3},{3,2},{16,18},{17,19},{18,16},{19,17},{4,5},{5,4... | collective-permute-start | bytes 172040 | tf_op jit(solution)/shard_map/ppermute | solution.py:46

commit v19 on v17

--- a/solution.py
+++ b/solution.py
@@ -126,10 +126,12 @@
             held[id(weight), expert, row] = array
         return token
 
-    arrived = [swap_line(block, (m,) * sects) for m in range(1, lanes)]
+    masks = [1, 3, 2] if lanes == 4 else list(range(1, lanes))
+    arrived = [swap_line(block, (m,) * sects) for m in masks]
     token = fetch_next(0, 2, token)
     arrived, token = lax.optimization_barrier((arrived, token))
-    line = stack([block, *arrived], line_orders())
+    index = {m: i for i, m in enumerate([0] + masks)}
+    line = stack([block, *arrived], [[index[m] for m in order] for order in line_orders()])
     rounds = rounds_of()
     for masks in rounds[:-1]:
         arrived = swap(line, masks)

time: 60 us -> 60.1 us (level)
  transfers between devices with their start and end apart: 16 -> 16, of which waited for: 11 -> 12; matrix products, arithmetic and copies ran while one was open for 1% -> 1% of each run, Pallas kernels for 25% -> 25%
where the time goes in v19:
time: 60.1 us; the launch traced here: 59.9 us
  Pallas kernels  23.6 us (39%)
  starting transfers between devices  20.2 us (34%)
  waiting for transfers between devices  14.6 us (24%)
  other arithmetic  1.14 us (2%)
    pallas_call x5, Pallas kernels, fetch(): pl.pallas_call(functools.partial(fetch_kernel, [(None, *w[1:]) for w in w...  13.9 us
    ppermute x6, starting transfers between devices, swap_line(): return lax.ppermute(value, ('sect', 'dev'), pairs)  10.1 us
    ppermute x6, starting transfers between devices, swap(): return lax.ppermute(value, ('sect', 'grp'), pairs)  9.37 us
    ppermute x6, waiting for transfers between devices, swap(): return lax.ppermute(value, ('sect', 'grp'), pairs)  8.6 us
    pallas_call x1, Pallas kernels, expert_call(): pl.pallas_call(functools.partial(expert_kernel, len(entries), experts, wi...  7.51 us
    ppermute x6, waiting for transfers between devices, swap_line(): return lax.ppermute(value, ('sect', 'dev'), pairs)  5.73 us
  transfers between devices with their start and end apart: 16, of which 12 were waited for; matrix products, arithmetic and copies ran while one was open for 1% of the time, Pallas kernels for 25%

profile of v19, /device:TPU:0, one launch (start us, length us, event | category | flops | bytes accessed | tf_op | source)
XLA Modules:
  0.0 59.9 jit_solution(12028738571291885934)
XLA Ops:
  0.0 1.0 %extend.1.after_ref.refs_0_ = bf16[4,7296]{1,0:T(4,128)(2,1)S(1)} custom-call(bf16[4,7168]{1,0:T(4,128)(2,1)} %tokens_hbm.1, s32[4,8]{1,0:T(4,128)} %ids_hbm.1, f32[4,8]{1,0:T(4,128)} %weights_hbm.1), custom_call_target="tpu_custom_call" | custom-call | tf_op jit(solution)/shard_map/extend/pallas_call | solution.py:81
  1.0 4.1 %collective-permute-start.2 = (bf16[4,7296]{1,0:T(4,128)(2,1)S(1)}, bf16[4,7296]{1,0:T(4,128)(2,1)S(1)}, u32[]{:S(2)}, u32[]{:S(2)}) collective-permute-start(bf16[4,7296]{1,0:T(4,128)(2,1)S(1)} %extend.1.after_ref.refs_0_), channel_id=1, source_target_pairs={{0,2},{1,3},{2,0},{3,1},{16,18},{17,19},{18,16},{19,17},{4,6},{5,7... | collective-permute-start | bytes 175112 | tf_op jit(solution)/shard_map/ppermute | solution.py:41
  5.1 1.3 %collective-permute-start.1 = (bf16[4,7296]{1,0:T(4,128)(2,1)S(1)}, bf16[4,7296]{1,0:T(4,128)(2,1)S(1)}, u32[]{:S(2)}, u32[]{:S(2)}) collective-permute-start(bf16[4,7296]{1,0:T(4,128)(2,1)S(1)} %extend.1.after_ref.refs_0_), channel_id=1, source_target_pairs={{0,3},{1,2},{2,1},{3,0},{16,19},{17,18},{18,17},{19,16},{4,7},{5,6... | collective-permute-start | bytes 175112 | tf_op jit(solution)/shard_map/ppermute | solution.py:41
  6.4 0.2 collective-permute-start
  6.7 2.2 %fetch.5 = (bf16[1,256,3584]{2,1,0:T(8,128)(2,1)S(1)}, bf16[1,256,3584]{2,1,0:T(8,128)(2,1)S(1)}, f32[8,128]{1,0:T(8,128)S(1)}) custom-call(bf16[4,7296]{1,0:T(4,128)(2,1)S(1)} %extend.1.after_ref.refs_0_, bf16[2,512,7168]{2,1,0:T(8,128)(2,1)} %refs_12_.1, bf16[2,512,7168]{2,1,0:T(8,128)(2,1)} %refs_12_.1), custom_call_target="tpu_custom_call" | custom-call | bytes 3670016 | tf_op jit(solution)/shard_map/fetch/pallas_call | solution.py:293
  8.9 0.0 collective-permute-done.2.refs_3_
  8.9 2.2 %collective-permute-done.1.refs_2_ = bf16[4,7296]{1,0:T(4,128)(2,1)S(1)} collective-permute-done((bf16[4,7296]{1,0:T(4,128)(2,1)S(1)}, bf16[4,7296]{1,0:T(4,128)(2,1)S(1)}, u32[]{:S(2)}, u32[]{:S(2)}) %collective-permute-start.1) | collective-permute-done | bytes 58400 | tf_op jit(solution)/shard_map/ppermute | solution.py:41
  11.2 0.1 collective-permute-done.refs_1_
  11.3 0.1 stack.2.refs_0_
  11.3 1.6 %collective-permute-start.3 = (bf16[16,7296]{1,0:T(8,128)(2,1)S(1)}, bf16[16,7296]{1,0:T(8,128)(2,1)S(1)}, u32[]{:S(2)}, u32[]{:S(2)}) collective-permute-start(bf16[16,7296]{1,0:T(8,128)(2,1)S(1)} %stack.2.refs_0_), channel_id=1, source_target_pairs={{0,8},{4,12},{8,0},{12,4},{16,20},{20,16},{24,28},{28,24},{1,9},{5... | collective-permute-start | bytes 700424 | tf_op jit(solution)/shard_map/ppermute | solution.py:26
  12.9 3.7 %fetch.6 = (bf16[1,7168,512]{2,1,0:T(8,128)(2,1)S(1)}, bf16[1,256,3584]{2,1,0:T(8,128)(2,1)S(1)}, f32[8,128]{1,0:T(8,128)S(1)}) custom-call(f32[8,128]{1,0:T(8,128)S(1)} %get-tuple-element.41.after_ref, bf16[2,7168,512]{2,1,0:T(8,128)(2,1)} %refs_0_.7, bf16[2,512,7168]{2,1,0:T(8,128)(2,1)} %refs_12_.1), custom_call_target="tpu_custom_call" | custom-call | bytes 9175040 | tf_op jit(solution)/shard_map/fetch/pallas_call | solution.py:293
  16.6 0.9 %collective-permute-done.3.refs_1_ = bf16[16,7296]{1,0:T(8,128)(2,1)S(1)} collective-permute-done((bf16[16,7296]{1,0:T(8,128)(2,1)S(1)}, bf16[16,7296]{1,0:T(8,128)(2,1)S(1)}, u32[]{:S(2)}, u32[]{:S(2)}) %collective-permute-start.3) | collective-permute-done | bytes 233504 | tf_op jit(solution)/shard_map/ppermute | solution.py:26
  17.6 1.6 %collective-permute-start.4 = (bf16[32,7296]{1,0:T(8,128)(2,1)S(1)}, bf16[32,7296]{1,0:T(8,128)(2,1)S(1)}, u32[]{:S(2)}, u32[]{:S(2)}) collective-permute-start(bf16[32,7296]{1,0:T(8,128)(2,1)S(1)} %stack.3.refs_0_), channel_id=1, source_target_pairs={{0,4},{4,0},{8,12},{12,8},{16,24},{20,28},{24,16},{28,20},{1,5},{5... | collective-permute-start | bytes 1400840 | tf_op jit(solution)/shard_map/ppermute | solution.py:26
  19.1 3.2 %fetch.7 = (bf16[1,7168,512]{2,1,0:T(8,128)(2,1)S(1)}, f32[8,128]{1,0:T(8,128)S(1)}) custom-call(f32[8,128]{1,0:T(8,128)S(1)} %get-tuple-element.44.after_ref, bf16[2,7168,512]{2,1,0:T(8,128)(2,1)} %refs_0_.7), custom_call_target="tpu_custom_call" | custom-call | bytes 7340032 | tf_op jit(solution)/shard_map/fetch/pallas_call | solution.py:293
  22.3 0.1 collective-permute-start.5
  22.4 3.2 %fetch.8 = (bf16[1,7168,512]{2,1,0:T(8,128)(2,1)S(1)}, f32[8,128]{1,0:T(8,128)S(1)}) custom-call(f32[8,128]{1,0:T(8,128)S(1)} %get-tuple-element.47.after_ref, bf16[2,7168,512]{2,1,0:T(8,128)(2,1)} %refs_11_.1), custom_call_target="tpu_custom_call" | custom-call | bytes 7340032 | tf_op jit(solution)/shard_map/fetch/pallas_call | solution.py:293
  25.6 0.6 %collective-permute-done.4.refs_1_ = bf16[32,7296]{1,0:T(8,128)(2,1)S(1)} collective-permute-done((bf16[32,7296]{1,0:T(8,128)(2,1)S(1)}, bf16[32,7296]{1,0:T(8,128)(2,1)S(1)}, u32[]{:S(2)}, u32[]{:S(2)}) %collective-permute-start.4) | collective-permute-done | bytes 466976 | tf_op jit(solution)/shard_map/ppermute | solution.py:26
  26.2 0.0 collective-permute-done.5.refs_2_
  26.2 0.0 collective-permute-start.6
  26.2 1.6 %fetch.9 = (bf16[1,256,3584]{2,1,0:T(8,128)(2,1)S(1)}, f32[8,128]{1,0:T(8,128)S(1)}) custom-call(f32[8,128]{1,0:T(8,128)S(1)} %get-tuple-element.50.after_ref, bf16[2,512,7168]{2,1,0:T(8,128)(2,1)} %refs_12_.1), custom_call_target="tpu_custom_call" | custom-call | bytes 1835008 | tf_op jit(solution)/shard_map/fetch/pallas_call | solution.py:293
  27.8 0.2 collective-permute-done.6.refs_3_
  28.0 7.5 %experts.1 = (bf16[128,1024]{1,0:T(8,128)(2,1)S(1)}, bf16[64,3584]{1,0:T(8,128)(2,1)S(1)}, bf16[64,3584]{1,0:T(8,128)(2,1)S(1)}, bf16[1,7168,512]{2,1,0:T(8,128)(2,1)S(1)}, bf16[1,7168,512]{2,1,0:T(8,128)(2,1)S(1)}) custom-call(f32[8,128]{1,0:T(8,128)S(1)} %get-tuple-element.52.token_ref, ...), custom_call_target="tpu_custom_call", output_to_operand_aliasing={{3}: (5, {}), {4}: (6, {})} | custom-call | flops 4697620480 | bytes 14680064 | tf_op jit(solution)/shard_map/experts/pallas_call | solution.py:325
  35.5 0.4 collective-permute-start.7
  36.0 1.1 %down.1 = (bf16[64,3584]{1,0:T(8,128)(2,1)S(1)}, bf16[64,3584]{1,0:T(8,128)(2,1)S(1)}) custom-call(bf16[128,1024]{1,0:T(8,128)(2,1)S(1)} %get-tuple-element.64.hidden_ref, bf16[1,7168,512]{2,1,0:T(8,128)(2,1)S(1)} %get-tuple-element.65.refs_0_, bf16[1,7168,512]{2,1,0:T(8,128)(2,1)S(1)} %get-tuple-element.66.refs_1_), custom_call_target="tpu_custom_call" | custom-call | flops 939524096 | bytes 917504 | tf_op jit(solution)/shard_map/down/pallas_call | solution.py:357
  37.1 0.2 collective-permute-start.10
  37.3 0.1 collective-permute-done.7
  37.4 0.1 add_convert_fusion.1
  37.6 1.6 %collective-permute-start.8 = (bf16[32,3584]{1,0:T(8,128)(2,1)S(1)}, bf16[32,3584]{1,0:T(8,128)(2,1)S(1)}, u32[]{:S(2)}, u32[]{:S(2)}) collective-permute-start(bf16[32,3584]{1,0:T(8,128)(2,1)S(1)} %slice.49), channel_id=1, source_target_pairs={{0,4},{4,0},{8,12},{12,8},{16,24},{20,28},{24,16},{28,20},{1,5},{5... | collective-permute-start | bytes 688136 | tf_op jit(solution)/shard_map/ppermute | solution.py:26
  39.2 0.0 collective-permute-done.10
  39.2 0.1 add_convert_fusion
  39.3 1.4 %collective-permute-start.11 = (bf16[32,3584]{1,0:T(8,128)(2,1)S(1)}, bf16[32,3584]{1,0:T(8,128)(2,1)S(1)}, u32[]{:S(2)}, u32[]{:S(2)}) collective-permute-start(bf16[32,3584]{1,0:T(8,128)(2,1)S(1)} %slice.53), channel_id=1, source_target_pairs={{0,4},{4,0},{8,12},{12,8},{16,24},{20,28},{24,16},{28,20},{1,5},{5... | collective-permute-start | bytes 688136 | tf_op jit(solution)/shard_map/ppermute | solution.py:26
  40.7 3.0 %collective-permute-done.8 = bf16[32,3584]{1,0:T(8,128)(2,1)S(1)} collective-permute-done((bf16[32,3584]{1,0:T(8,128)(2,1)S(1)}, bf16[32,3584]{1,0:T(8,128)(2,1)S(1)}, u32[]{:S(2)}, u32[]{:S(2)}) %collective-permute-start.8) | collective-permute-done | bytes 229408 | tf_op jit(solution)/shard_map/ppermute | solution.py:26
  43.6 0.1 add_convert_fusion.3
  43.7 1.6 %collective-permute-start.9 = (bf16[16,3584]{1,0:T(8,128)(2,1)S(1)}, bf16[16,3584]{1,0:T(8,128)(2,1)S(1)}, u32[]{:S(2)}, u32[]{:S(2)}) collective-permute-start(bf16[16,3584]{1,0:T(8,128)(2,1)S(1)} %slice.51), channel_id=1, source_target_pairs={{0,8},{4,12},{8,0},{12,4},{16,20},{20,16},{24,28},{28,24},{1,9},{5... | collective-permute-start | bytes 344072 | tf_op jit(solution)/shard_map/ppermute | solution.py:26
  45.3 0.9 %collective-permute-done.11 = bf16[32,3584]{1,0:T(8,128)(2,1)S(1)} collective-permute-done((bf16[32,3584]{1,0:T(8,128)(2,1)S(1)}, bf16[32,3584]{1,0:T(8,128)(2,1)S(1)}, u32[]{:S(2)}, u32[]{:S(2)}) %collective-permute-start.11) | collective-permute-done | bytes 229408 | tf_op jit(solution)/shard_map/ppermute | solution.py:26
  46.2 0.1 add_convert_fusion.2
  46.3 1.6 %collective-permute-start.12 = (bf16[16,3584]{1,0:T(8,128)(2,1)S(1)}, bf16[16,3584]{1,0:T(8,128)(2,1)S(1)}, u32[]{:S(2)}, u32[]{:S(2)}) collective-permute-start(bf16[16,3584]{1,0:T(8,128)(2,1)S(1)} %slice.55), channel_id=1, source_target_pairs={{0,8},{4,12},{8,0},{12,4},{16,20},{20,16},{24,28},{28,24},{1,9},{5... | collective-permute-start | bytes 344072 | tf_op jit(solution)/shard_map/ppermute | solution.py:26
  47.9 0.6 %collective-permute-done.9 = bf16[16,3584]{1,0:T(8,128)(2,1)S(1)} collective-permute-done((bf16[16,3584]{1,0:T(8,128)(2,1)S(1)}, bf16[16,3584]{1,0:T(8,128)(2,1)S(1)}, u32[]{:S(2)}, u32[]{:S(2)}) %collective-permute-start.9) | collective-permute-done | bytes 114720 | tf_op jit(solution)/shard_map/ppermute | solution.py:26
  48.6 2.6 %collective-permute-done.12 = bf16[16,3584]{1,0:T(8,128)(2,1)S(1)} collective-permute-done((bf16[16,3584]{1,0:T(8,128)(2,1)S(1)}, bf16[16,3584]{1,0:T(8,128)(2,1)S(1)}, u32[]{:S(2)}, u32[]{:S(2)}) %collective-permute-start.12) | collective-permute-done | bytes 114720 | tf_op jit(solution)/shard_map/ppermute | solution.py:26
  51.2 0.1 fusion.2
  51.3 2.6 %collective-permute-start.13 = (bf16[4,7168]{1,0:T(4,128)(2,1)S(1)}, bf16[4,7168]{1,0:T(4,128)(2,1)S(1)}, u32[]{:S(2)}, u32[]{:S(2)}) collective-permute-start(bf16[4,7168]{1,0:T(4,128)(2,1)S(1)} %get-tuple-element.69), channel_id=1, source_target_pairs={{0,3},{1,2},{2,1},{3,0},{16,17},{17,16},{18,19},{19,18},{4,7},{5,6... | collective-permute-start | bytes 172040 | tf_op jit(solution)/shard_map/ppermute | solution.py:41
  53.9 0.0 collective-permute-start.15
  53.9 1.8 %collective-permute-start.14 = (bf16[4,7168]{1,0:T(4,128)(2,1)S(1)}, bf16[4,7168]{1,0:T(4,128)(2,1)S(1)}, u32[]{:S(2)}, u32[]{:S(2)}) collective-permute-start(bf16[4,7168]{1,0:T(4,128)(2,1)S(1)} %get-tuple-element.71), channel_id=1, source_target_pairs={{0,1},{1,0},{2,3},{3,2},{16,18},{17,19},{18,16},{19,17},{4,5},{5,4... | collective-permute-start | bytes 172040 | tf_op jit(solution)/shard_map/ppermute | solution.py:41
  55.8 1.7 %collective-permute-done.13 = bf16[4,7168]{1,0:T(4,128)(2,1)S(1)} collective-permute-done((bf16[4,7168]{1,0:T(4,128)(2,1)S(1)}, bf16[4,7168]{1,0:T(4,128)(2,1)S(1)}, u32[]{:S(2)}, u32[]{:S(2)}) %collective-permute-start.13) | collective-permute-done | bytes 57376 | tf_op jit(solution)/shard_map/ppermute | solution.py:41
  57.4 1.7 %collective-permute-done.15 = bf16[4,7168]{1,0:T(4,128)(2,1)S(1)} collective-permute-done((bf16[4,7168]{1,0:T(4,128)(2,1)S(1)}, bf16[4,7168]{1,0:T(4,128)(2,1)S(1)}, u32[]{:S(2)}, u32[]{:S(2)}) %collective-permute-start.15) | collective-permute-done | bytes 57376 | tf_op jit(solution)/shard_map/ppermute | solution.py:41
  59.2 0.0 collective-permute-done.14
  59.2 0.7 %add_convert_fusion.6 = bf16[4,7168]{1,0:T(4,128)(2,1)} fusion(bf16[4,7168]{1,0:T(4,128)(2,1)S(1)} %collective-permute-done.15, bf16[4,7168]{1,0:T(4,128)(2,1)S(1)} %collective-permute-done.14, bf16[4,7168]{1,0:T(4,128)(2,1)S(1)} %collective-permute-done.13, bf16[16,3584]{1,0:T(8,128)(2,1)S(1)} %add_convert_fusion.5, bf16[16,3584]{1,0:T(8,128)(2,1)S(1)} %add_convert_fusion.4), kind=kLoop, calls=%fused_computation.12 | loop fusion | flops 315392 | bytes 458752 | tf_op jit(solution)/shard_map/convert_element_type | solution.py:377
  (7 shorter events, 0.1 us)
Async XLA Ops:
  1.0 7.9 %collective-permute-start.2 = (bf16[4,7296]{1,0:T(4,128)(2,1)S(1)}, bf16[4,7296]{1,0:T(4,128)(2,1)S(1)}, u32[]{:S(2)}, u32[]{:S(2)}) collective-permute-start(bf16[4,7296]{1,0:T(4,128)(2,1)S(1)} %extend.1.after_ref.refs_0_), channel_id=1, source_target_pairs={{0,2},{1,3},{2,0},{3,1},{16,18},{17,19},{18,16},{19,17},{4,6},{5,7... | collective-permute-start | bytes 175112 | tf_op jit(solution)/shard_map/ppermute | solution.py:41
  5.1 6.1 %collective-permute-start.1 = (bf16[4,7296]{1,0:T(4,128)(2,1)S(1)}, bf16[4,7296]{1,0:T(4,128)(2,1)S(1)}, u32[]{:S(2)}, u32[]{:S(2)}) collective-permute-start(bf16[4,7296]{1,0:T(4,128)(2,1)S(1)} %extend.1.after_ref.refs_0_), channel_id=1, source_target_pairs={{0,3},{1,2},{2,1},{3,0},{16,19},{17,18},{18,17},{19,16},{4,7},{5,6... | collective-permute-start | bytes 175112 | tf_op jit(solution)/shard_map/ppermute | solution.py:41
  6.4 4.8 %collective-permute-start = (bf16[4,7296]{1,0:T(4,128)(2,1)S(1)}, bf16[4,7296]{1,0:T(4,128)(2,1)S(1)}, u32[]{:S(2)}, u32[]{:S(2)}) collective-permute-start(bf16[4,7296]{1,0:T(4,128)(2,1)S(1)} %extend.1.after_ref.refs_0_), channel_id=1, source_target_pairs={{0,1},{1,0},{2,3},{3,2},{16,17},{17,16},{18,19},{19,18},{4,5},{5,4... | collective-permute-start | bytes 175112 | tf_op jit(solution)/shard_map/ppermute | solution.py:41
  11.3 6.2 %collective-permute-start.3 = (bf16[16,7296]{1,0:T(8,128)(2,1)S(1)}, bf16[16,7296]{1,0:T(8,128)(2,1)S(1)}, u32[]{:S(2)}, u32[]{:S(2)}) collective-permute-start(bf16[16,7296]{1,0:T(8,128)(2,1)S(1)} %stack.2.refs_0_), channel_id=1, source_target_pairs={{0,8},{4,12},{8,0},{12,4},{16,20},{20,16},{24,28},{28,24},{1,9},{5... | collective-permute-start | bytes 700424 | tf_op jit(solution)/shard_map/ppermute | solution.py:26
  17.6 8.6 %collective-permute-start.4 = (bf16[32,7296]{1,0:T(8,128)(2,1)S(1)}, bf16[32,7296]{1,0:T(8,128)(2,1)S(1)}, u32[]{:S(2)}, u32[]{:S(2)}) collective-permute-start(bf16[32,7296]{1,0:T(8,128)(2,1)S(1)} %stack.3.refs_0_), channel_id=1, source_target_pairs={{0,4},{4,0},{8,12},{12,8},{16,24},{20,28},{24,16},{28,20},{1,5},{5... | collective-permute-start | bytes 1400840 | tf_op jit(solution)/shard_map/ppermute | solution.py:26
  22.3 3.9 %collective-permute-start.5 = (bf16[32,7296]{1,0:T(8,128)(2,1)S(1)}, bf16[32,7296]{1,0:T(8,128)(2,1)S(1)}, u32[]{:S(2)}, u32[]{:S(2)}) collective-permute-start(bf16[32,7296]{1,0:T(8,128)(2,1)S(1)} %stack.3.refs_0_), channel_id=1, source_target_pairs={{0,16},{16,0},{1,17},{17,1},{2,18},{18,2},{3,19},{19,3},{4,20},{20... | collective-permute-start | bytes 1400840 | tf_op jit(solution)/shard_map/ppermute | solution.py:45
  26.2 1.8 %collective-permute-start.6 = (bf16[32,7296]{1,0:T(8,128)(2,1)S(1)}, bf16[32,7296]{1,0:T(8,128)(2,1)S(1)}, u32[]{:S(2)}, u32[]{:S(2)}) collective-permute-start(bf16[32,7296]{1,0:T(8,128)(2,1)S(1)} %collective-permute-done.4.refs_1_), channel_id=1, source_target_pairs={{0,16},{16,0},{1,17},{17,1},{2,18},{18,2},{3,19},{19,3},{4,20},{20... | collective-permute-start | bytes 1400840 | tf_op jit(solution)/shard_map/ppermute | solution.py:45
  35.5 1.9 %collective-permute-start.7 = (bf16[64,3584]{1,0:T(8,128)(2,1)S(1)}, bf16[64,3584]{1,0:T(8,128)(2,1)S(1)}, u32[]{:S(2)}, u32[]{:S(2)}) collective-permute-start(bf16[64,3584]{1,0:T(8,128)(2,1)S(1)} %get-tuple-element.63), channel_id=1, source_target_pairs={{0,16},{16,0},{1,17},{17,1},{2,18},{18,2},{3,19},{19,3},{4,20},{20... | collective-permute-start | bytes 1376264 | tf_op jit(solution)/shard_map/ppermute | solution.py:45
  37.1 2.1 %collective-permute-start.10 = (bf16[64,3584]{1,0:T(8,128)(2,1)S(1)}, bf16[64,3584]{1,0:T(8,128)(2,1)S(1)}, u32[]{:S(2)}, u32[]{:S(2)}) collective-permute-start(bf16[64,3584]{1,0:T(8,128)(2,1)S(1)} %get-tuple-element.68), channel_id=1, source_target_pairs={{0,16},{16,0},{1,17},{17,1},{2,18},{18,2},{3,19},{19,3},{4,20},{20... | collective-permute-start | bytes 1376264 | tf_op jit(solution)/shard_map/ppermute | solution.py:45
  37.6 6.1 %collective-permute-start.8 = (bf16[32,3584]{1,0:T(8,128)(2,1)S(1)}, bf16[32,3584]{1,0:T(8,128)(2,1)S(1)}, u32[]{:S(2)}, u32[]{:S(2)}) collective-permute-start(bf16[32,3584]{1,0:T(8,128)(2,1)S(1)} %slice.49), channel_id=1, source_target_pairs={{0,4},{4,0},{8,12},{12,8},{16,24},{20,28},{24,16},{28,20},{1,5},{5... | collective-permute-start | bytes 688136 | tf_op jit(solution)/shard_map/ppermute | solution.py:26
  39.3 7.0 %collective-permute-start.11 = (bf16[32,3584]{1,0:T(8,128)(2,1)S(1)}, bf16[32,3584]{1,0:T(8,128)(2,1)S(1)}, u32[]{:S(2)}, u32[]{:S(2)}) collective-permute-start(bf16[32,3584]{1,0:T(8,128)(2,1)S(1)} %slice.53), channel_id=1, source_target_pairs={{0,4},{4,0},{8,12},{12,8},{16,24},{20,28},{24,16},{28,20},{1,5},{5... | collective-permute-start | bytes 688136 | tf_op jit(solution)/shard_map/ppermute | solution.py:26
  43.7 4.9 %collective-permute-start.9 = (bf16[16,3584]{1,0:T(8,128)(2,1)S(1)}, bf16[16,3584]{1,0:T(8,128)(2,1)S(1)}, u32[]{:S(2)}, u32[]{:S(2)}) collective-permute-start(bf16[16,3584]{1,0:T(8,128)(2,1)S(1)} %slice.51), channel_id=1, source_target_pairs={{0,8},{4,12},{8,0},{12,4},{16,20},{20,16},{24,28},{28,24},{1,9},{5... | collective-permute-start | bytes 344072 | tf_op jit(solution)/shard_map/ppermute | solution.py:26
  46.3 4.9 %collective-permute-start.12 = (bf16[16,3584]{1,0:T(8,128)(2,1)S(1)}, bf16[16,3584]{1,0:T(8,128)(2,1)S(1)}, u32[]{:S(2)}, u32[]{:S(2)}) collective-permute-start(bf16[16,3584]{1,0:T(8,128)(2,1)S(1)} %slice.55), channel_id=1, source_target_pairs={{0,8},{4,12},{8,0},{12,4},{16,20},{20,16},{24,28},{28,24},{1,9},{5... | collective-permute-start | bytes 344072 | tf_op jit(solution)/shard_map/ppermute | solution.py:26
  51.3 6.1 %collective-permute-start.13 = (bf16[4,7168]{1,0:T(4,128)(2,1)S(1)}, bf16[4,7168]{1,0:T(4,128)(2,1)S(1)}, u32[]{:S(2)}, u32[]{:S(2)}) collective-permute-start(bf16[4,7168]{1,0:T(4,128)(2,1)S(1)} %get-tuple-element.69), channel_id=1, source_target_pairs={{0,3},{1,2},{2,1},{3,0},{16,17},{17,16},{18,19},{19,18},{4,7},{5,6... | collective-permute-start | bytes 172040 | tf_op jit(solution)/shard_map/ppermute | solution.py:41
  53.9 5.2 %collective-permute-start.15 = (bf16[4,7168]{1,0:T(4,128)(2,1)S(1)}, bf16[4,7168]{1,0:T(4,128)(2,1)S(1)}, u32[]{:S(2)}, u32[]{:S(2)}) collective-permute-start(bf16[4,7168]{1,0:T(4,128)(2,1)S(1)} %get-tuple-element.70), channel_id=1, source_target_pairs={{0,2},{1,3},{2,0},{3,1},{16,19},{17,18},{18,17},{19,16},{4,6},{5,7... | collective-permute-start | bytes 172040 | tf_op jit(solution)/shard_map/ppermute | solution.py:41
  53.9 5.2 %collective-permute-start.14 = (bf16[4,7168]{1,0:T(4,128)(2,1)S(1)}, bf16[4,7168]{1,0:T(4,128)(2,1)S(1)}, u32[]{:S(2)}, u32[]{:S(2)}) collective-permute-start(bf16[4,7168]{1,0:T(4,128)(2,1)S(1)} %get-tuple-element.71), channel_id=1, source_target_pairs={{0,1},{1,0},{2,3},{3,2},{16,18},{17,19},{18,16},{19,17},{4,5},{5,4... | collective-permute-start | bytes 172040 | tf_op jit(solution)/shard_map/ppermute | solution.py:41

commit v20 on v19

--- a/solution.py
+++ b/solution.py
@@ -66,12 +66,13 @@
     half = (out_ref.shape[1] - width) // 2
     lane = lax.broadcasted_iota(jnp.int32, (rows, half * 2), 1)
     dense = jnp.zeros((rows, half * 2), jnp.float32)
-    for copy in copies:
+    for copy in copies[:2]:
         copy.wait()
     for k in range(ids_ref.shape[1]):
         mine = lax.rem(lane, half) == ids_ref[:, k:k + 1]
         dense = dense + jnp.where(mine, weights_ref[:, k:k + 1], 0.0)
     high = dense.astype(jnp.bfloat16).astype(jnp.float32)
+    copies[2].wait()
     out_ref[:, :width] = tokens_ref[...]
     out_ref[:, width:] = jnp.where(lane < half, high, dense - high).astype(jnp.bfloat16)
 
@@ -128,7 +129,7 @@
 
     masks = [1, 3, 2] if lanes == 4 else list(range(1, lanes))
     arrived = [swap_line(block, (m,) * sects) for m in masks]
-    token = fetch_next(0, 2, token)
+    token = fetch_next(0, 3, token)
     arrived, token = lax.optimization_barrier((arrived, token))
     index = {m: i for i, m in enumerate([0] + masks)}
     line = stack([block, *arrived], [[index[m] for m in order] for order in line_orders()])

time: 60.1 us -> 60.2 us (level)
  waiting for transfers between devices: 14.6 us -> 15.9 us
  Pallas kernels: 23.6 us -> 22.6 us
    ppermute x4, waiting for transfers between devices: 0.3 us -> 1.84 us  [swap_core(): return lax.ppermute(value, 'sect', [(0, 1), (1, 0)])]
    pallas_call x5 -> x4, Pallas kernels: 13.9 us -> 12.9 us  [fetch(): pl.pallas_call(functools.partial(fetch_kernel, [(None, *w[1:]) for w in w...]
    ppermute x6, waiting for transfers between devices: 5.73 us -> 5.11 us  [swap_line(): return lax.ppermute(value, ('sect', 'dev'), pairs)]
  transfers between devices with their start and end apart: 16 -> 16, of which waited for: 12 -> 11; matrix products, arithmetic and copies ran while one was open for 1% -> 1% of each run, Pallas kernels for 25% -> 24%
where the time goes in v20:
time: 60.2 us; the launch traced here: 60 us
  Pallas kernels  22.6 us (38%)
  starting transfers between devices  20.1 us (33%)
  waiting for transfers between devices  15.9 us (26%)
  other arithmetic  1.14 us (2%)
    pallas_call x4, Pallas kernels, fetch(): pl.pallas_call(functools.partial(fetch_kernel, [(None, *w[1:]) for w in w...  12.9 us
    ppermute x6, starting transfers between devices, swap_line(): return lax.ppermute(value, ('sect', 'dev'), pairs)  10.1 us
    ppermute x6, starting transfers between devices, swap(): return lax.ppermute(value, ('sect', 'grp'), pairs)  9.22 us
    ppermute x6, waiting for transfers between devices, swap(): return lax.ppermute(value, ('sect', 'grp'), pairs)  8.97 us
    pallas_call x1, Pallas kernels, expert_call(): pl.pallas_call(functools.partial(expert_kernel, len(entries), experts, wi...  7.52 us
    ppermute x6, waiting for transfers between devices, swap_line(): return lax.ppermute(value, ('sect', 'dev'), pairs)  5.11 us
    ppermute x4, waiting for transfers between devices, swap_core(): return lax.ppermute(value, 'sect', [(0, 1), (1, 0)])  1.84 us
    pallas_call x1, Pallas kernels, expert_call(): pl.pallas_call(down_kernel, out_shape=(outs[1], outs[1]), in_specs=[whole...  1.22 us
  transfers between devices with their start and end apart: 16, of which 11 were waited for; matrix products, arithmetic and copies ran while one was open for 1% of the time, Pallas kernels for 24%

profile of v20, /device:TPU:0, one launch (start us, length us, event | category | flops | bytes accessed | tf_op | source)
XLA Modules:
  0.0 60.0 jit_solution(11961797115330793295)
XLA Ops:
  0.0 0.9 %extend.1.after_ref.refs_0_ = bf16[4,7296]{1,0:T(4,128)(2,1)S(1)} custom-call(bf16[4,7168]{1,0:T(4,128)(2,1)} %tokens_hbm.1, s32[4,8]{1,0:T(4,128)} %ids_hbm.1, f32[4,8]{1,0:T(4,128)} %weights_hbm.1), custom_call_target="tpu_custom_call" | custom-call | tf_op jit(solution)/shard_map/extend/pallas_call | solution.py:82
  0.9 4.1 %collective-permute-start.2 = (bf16[4,7296]{1,0:T(4,128)(2,1)S(1)}, bf16[4,7296]{1,0:T(4,128)(2,1)S(1)}, u32[]{:S(2)}, u32[]{:S(2)}) collective-permute-start(bf16[4,7296]{1,0:T(4,128)(2,1)S(1)} %extend.1.after_ref.refs_0_), channel_id=1, source_target_pairs={{0,2},{1,3},{2,0},{3,1},{16,18},{17,19},{18,16},{19,17},{4,6},{5,7... | collective-permute-start | bytes 175112 | tf_op jit(solution)/shard_map/ppermute | solution.py:41
  5.0 1.3 %collective-permute-start.1 = (bf16[4,7296]{1,0:T(4,128)(2,1)S(1)}, bf16[4,7296]{1,0:T(4,128)(2,1)S(1)}, u32[]{:S(2)}, u32[]{:S(2)}) collective-permute-start(bf16[4,7296]{1,0:T(4,128)(2,1)S(1)} %extend.1.after_ref.refs_0_), channel_id=1, source_target_pairs={{0,3},{1,2},{2,1},{3,0},{16,19},{17,18},{18,17},{19,16},{4,7},{5,6... | collective-permute-start | bytes 175112 | tf_op jit(solution)/shard_map/ppermute | solution.py:41
  6.3 0.2 collective-permute-start
  6.6 2.9 %fetch.4 = (bf16[1,256,3584]{2,1,0:T(8,128)(2,1)S(1)}, bf16[1,256,3584]{2,1,0:T(8,128)(2,1)S(1)}, bf16[1,256,3584]{2,1,0:T(8,128)(2,1)S(1)}, f32[8,128]{1,0:T(8,128)S(1)}) custom-call(bf16[4,7296]{1,0:T(4,128)(2,1)S(1)} %extend.1.after_ref.refs_0_, bf16[2,512,7168]{2,1,0:T(8,128)(2,1)} %refs_12_.1, bf16[2,512,7168]{2,1,0:T(8,128)(2,1)} %refs_12_.1, ...), custom_call_target="tpu_custom_call" | custom-call | bytes 5505024 | tf_op jit(solution)/shard_map/fetch/pallas_call | solution.py:294
  9.5 0.0 collective-permute-done.2.refs_3_
  9.5 1.6 %collective-permute-done.1.refs_2_ = bf16[4,7296]{1,0:T(4,128)(2,1)S(1)} collective-permute-done((bf16[4,7296]{1,0:T(4,128)(2,1)S(1)}, bf16[4,7296]{1,0:T(4,128)(2,1)S(1)}, u32[]{:S(2)}, u32[]{:S(2)}) %collective-permute-start.1) | collective-permute-done | bytes 58400 | tf_op jit(solution)/shard_map/ppermute | solution.py:41
  11.1 0.1 collective-permute-done.refs_1_
  11.2 0.1 stack.2.refs_0_
  11.2 1.6 %collective-permute-start.3 = (bf16[16,7296]{1,0:T(8,128)(2,1)S(1)}, bf16[16,7296]{1,0:T(8,128)(2,1)S(1)}, u32[]{:S(2)}, u32[]{:S(2)}) collective-permute-start(bf16[16,7296]{1,0:T(8,128)(2,1)S(1)} %stack.2.refs_0_), channel_id=1, source_target_pairs={{0,8},{4,12},{8,0},{12,4},{16,20},{20,16},{24,28},{28,24},{1,9},{5... | collective-permute-start | bytes 700424 | tf_op jit(solution)/shard_map/ppermute | solution.py:26
  12.8 3.7 %fetch.5 = (bf16[1,7168,512]{2,1,0:T(8,128)(2,1)S(1)}, bf16[1,256,3584]{2,1,0:T(8,128)(2,1)S(1)}, f32[8,128]{1,0:T(8,128)S(1)}) custom-call(f32[8,128]{1,0:T(8,128)S(1)} %get-tuple-element.40.after_ref, bf16[2,7168,512]{2,1,0:T(8,128)(2,1)} %refs_0_.6, bf16[2,512,7168]{2,1,0:T(8,128)(2,1)} %refs_12_.1), custom_call_target="tpu_custom_call" | custom-call | bytes 9175040 | tf_op jit(solution)/shard_map/fetch/pallas_call | solution.py:294
  16.5 0.9 %collective-permute-done.3.refs_1_ = bf16[16,7296]{1,0:T(8,128)(2,1)S(1)} collective-permute-done((bf16[16,7296]{1,0:T(8,128)(2,1)S(1)}, bf16[16,7296]{1,0:T(8,128)(2,1)S(1)}, u32[]{:S(2)}, u32[]{:S(2)}) %collective-permute-start.3) | collective-permute-done | bytes 233504 | tf_op jit(solution)/shard_map/ppermute | solution.py:26
  17.5 1.6 %collective-permute-start.4 = (bf16[32,7296]{1,0:T(8,128)(2,1)S(1)}, bf16[32,7296]{1,0:T(8,128)(2,1)S(1)}, u32[]{:S(2)}, u32[]{:S(2)}) collective-permute-start(bf16[32,7296]{1,0:T(8,128)(2,1)S(1)} %stack.3.refs_0_), channel_id=1, source_target_pairs={{0,4},{4,0},{8,12},{12,8},{16,24},{20,28},{24,16},{28,20},{1,5},{5... | collective-permute-start | bytes 1400840 | tf_op jit(solution)/shard_map/ppermute | solution.py:26
  19.0 3.2 %fetch.6 = (bf16[1,7168,512]{2,1,0:T(8,128)(2,1)S(1)}, f32[8,128]{1,0:T(8,128)S(1)}) custom-call(f32[8,128]{1,0:T(8,128)S(1)} %get-tuple-element.43.after_ref, bf16[2,7168,512]{2,1,0:T(8,128)(2,1)} %refs_0_.6), custom_call_target="tpu_custom_call" | custom-call | bytes 7340032 | tf_op jit(solution)/shard_map/fetch/pallas_call | solution.py:294
  22.2 0.1 collective-permute-start.5
  22.3 3.2 %fetch.7 = (bf16[1,7168,512]{2,1,0:T(8,128)(2,1)S(1)}, f32[8,128]{1,0:T(8,128)S(1)}) custom-call(f32[8,128]{1,0:T(8,128)S(1)} %get-tuple-element.46.after_ref, bf16[2,7168,512]{2,1,0:T(8,128)(2,1)} %refs_11_.1), custom_call_target="tpu_custom_call" | custom-call | bytes 7340032 | tf_op jit(solution)/shard_map/fetch/pallas_call | solution.py:294
  25.5 0.6 %collective-permute-done.4.refs_1_ = bf16[32,7296]{1,0:T(8,128)(2,1)S(1)} collective-permute-done((bf16[32,7296]{1,0:T(8,128)(2,1)S(1)}, bf16[32,7296]{1,0:T(8,128)(2,1)S(1)}, u32[]{:S(2)}, u32[]{:S(2)}) %collective-permute-start.4) | collective-permute-done | bytes 466976 | tf_op jit(solution)/shard_map/ppermute | solution.py:26
  26.1 0.0 collective-permute-done.5.refs_2_
  26.1 0.0 collective-permute-start.6
  26.1 1.8 %collective-permute-done.6.refs_3_ = bf16[32,7296]{1,0:T(8,128)(2,1)S(1)} collective-permute-done((bf16[32,7296]{1,0:T(8,128)(2,1)S(1)}, bf16[32,7296]{1,0:T(8,128)(2,1)S(1)}, u32[]{:S(2)}, u32[]{:S(2)}) %collective-permute-start.6) | collective-permute-done | bytes 466976 | tf_op jit(solution)/shard_map/ppermute | solution.py:45
  27.9 7.5 %experts.1 = (bf16[128,1024]{1,0:T(8,128)(2,1)S(1)}, bf16[64,3584]{1,0:T(8,128)(2,1)S(1)}, bf16[64,3584]{1,0:T(8,128)(2,1)S(1)}, bf16[1,7168,512]{2,1,0:T(8,128)(2,1)S(1)}, bf16[1,7168,512]{2,1,0:T(8,128)(2,1)S(1)}) custom-call(f32[8,128]{1,0:T(8,128)S(1)} %get-tuple-element.50.token_ref, ...), custom_call_target="tpu_custom_call", output_to_operand_aliasing={{3}: (5, {}), {4}: (6, {})} | custom-call | flops 4697620480 | bytes 14680064 | tf_op jit(solution)/shard_map/experts/pallas_call | solution.py:326
  35.5 0.2 collective-permute-start.7
  35.6 1.2 %down.1 = (bf16[64,3584]{1,0:T(8,128)(2,1)S(1)}, bf16[64,3584]{1,0:T(8,128)(2,1)S(1)}) custom-call(bf16[128,1024]{1,0:T(8,128)(2,1)S(1)} %get-tuple-element.62.hidden_ref, bf16[1,7168,512]{2,1,0:T(8,128)(2,1)S(1)} %get-tuple-element.63.refs_0_, bf16[1,7168,512]{2,1,0:T(8,128)(2,1)S(1)} %get-tuple-element.64.refs_1_), custom_call_target="tpu_custom_call" | custom-call | flops 939524096 | bytes 917504 | tf_op jit(solution)/shard_map/down/pallas_call | solution.py:358
  36.9 0.4 collective-permute-start.10
  37.3 0.0 collective-permute-done.7
  37.3 0.1 add_convert_fusion.1
  37.5 1.6 %collective-permute-start.8 = (bf16[32,3584]{1,0:T(8,128)(2,1)S(1)}, bf16[32,3584]{1,0:T(8,128)(2,1)S(1)}, u32[]{:S(2)}, u32[]{:S(2)}) collective-permute-start(bf16[32,3584]{1,0:T(8,128)(2,1)S(1)} %slice.49), channel_id=1, source_target_pairs={{0,4},{4,0},{8,12},{12,8},{16,24},{20,28},{24,16},{28,20},{1,5},{5... | collective-permute-start | bytes 688136 | tf_op jit(solution)/shard_map/ppermute | solution.py:26
  39.1 0.0 collective-permute-done.10
  39.1 0.1 add_convert_fusion
  39.2 1.3 %collective-permute-start.11 = (bf16[32,3584]{1,0:T(8,128)(2,1)S(1)}, bf16[32,3584]{1,0:T(8,128)(2,1)S(1)}, u32[]{:S(2)}, u32[]{:S(2)}) collective-permute-start(bf16[32,3584]{1,0:T(8,128)(2,1)S(1)} %slice.53), channel_id=1, source_target_pairs={{0,4},{4,0},{8,12},{12,8},{16,24},{20,28},{24,16},{28,20},{1,5},{5... | collective-permute-start | bytes 688136 | tf_op jit(solution)/shard_map/ppermute | solution.py:26
  40.5 3.1 %collective-permute-done.8 = bf16[32,3584]{1,0:T(8,128)(2,1)S(1)} collective-permute-done((bf16[32,3584]{1,0:T(8,128)(2,1)S(1)}, bf16[32,3584]{1,0:T(8,128)(2,1)S(1)}, u32[]{:S(2)}, u32[]{:S(2)}) %collective-permute-start.8) | collective-permute-done | bytes 229408 | tf_op jit(solution)/shard_map/ppermute | solution.py:26
  43.6 0.1 add_convert_fusion.3
  43.6 1.6 %collective-permute-start.9 = (bf16[16,3584]{1,0:T(8,128)(2,1)S(1)}, bf16[16,3584]{1,0:T(8,128)(2,1)S(1)}, u32[]{:S(2)}, u32[]{:S(2)}) collective-permute-start(bf16[16,3584]{1,0:T(8,128)(2,1)S(1)} %slice.51), channel_id=1, source_target_pairs={{0,8},{4,12},{8,0},{12,4},{16,20},{20,16},{24,28},{28,24},{1,9},{5... | collective-permute-start | bytes 344072 | tf_op jit(solution)/shard_map/ppermute | solution.py:26
  45.2 1.2 %collective-permute-done.11 = bf16[32,3584]{1,0:T(8,128)(2,1)S(1)} collective-permute-done((bf16[32,3584]{1,0:T(8,128)(2,1)S(1)}, bf16[32,3584]{1,0:T(8,128)(2,1)S(1)}, u32[]{:S(2)}, u32[]{:S(2)}) %collective-permute-start.11) | collective-permute-done | bytes 229408 | tf_op jit(solution)/shard_map/ppermute | solution.py:26
  46.4 0.1 add_convert_fusion.2
  46.5 1.6 %collective-permute-start.12 = (bf16[16,3584]{1,0:T(8,128)(2,1)S(1)}, bf16[16,3584]{1,0:T(8,128)(2,1)S(1)}, u32[]{:S(2)}, u32[]{:S(2)}) collective-permute-start(bf16[16,3584]{1,0:T(8,128)(2,1)S(1)} %slice.55), channel_id=1, source_target_pairs={{0,8},{4,12},{8,0},{12,4},{16,20},{20,16},{24,28},{28,24},{1,9},{5... | collective-permute-start | bytes 344072 | tf_op jit(solution)/shard_map/ppermute | solution.py:26
  48.1 0.4 collective-permute-done.9
  48.5 2.8 %collective-permute-done.12 = bf16[16,3584]{1,0:T(8,128)(2,1)S(1)} collective-permute-done((bf16[16,3584]{1,0:T(8,128)(2,1)S(1)}, bf16[16,3584]{1,0:T(8,128)(2,1)S(1)}, u32[]{:S(2)}, u32[]{:S(2)}) %collective-permute-start.12) | collective-permute-done | bytes 114720 | tf_op jit(solution)/shard_map/ppermute | solution.py:26
  51.4 0.1 fusion.2
  51.4 2.6 %collective-permute-start.13 = (bf16[4,7168]{1,0:T(4,128)(2,1)S(1)}, bf16[4,7168]{1,0:T(4,128)(2,1)S(1)}, u32[]{:S(2)}, u32[]{:S(2)}) collective-permute-start(bf16[4,7168]{1,0:T(4,128)(2,1)S(1)} %get-tuple-element.67), channel_id=1, source_target_pairs={{0,3},{1,2},{2,1},{3,0},{16,17},{17,16},{18,19},{19,18},{4,7},{5,6... | collective-permute-start | bytes 172040 | tf_op jit(solution)/shard_map/ppermute | solution.py:41
  54.0 0.0 collective-permute-start.15
  54.0 1.8 %collective-permute-start.14 = (bf16[4,7168]{1,0:T(4,128)(2,1)S(1)}, bf16[4,7168]{1,0:T(4,128)(2,1)S(1)}, u32[]{:S(2)}, u32[]{:S(2)}) collective-permute-start(bf16[4,7168]{1,0:T(4,128)(2,1)S(1)} %get-tuple-element.69), channel_id=1, source_target_pairs={{0,1},{1,0},{2,3},{3,2},{16,18},{17,19},{18,16},{19,17},{4,5},{5,4... | collective-permute-start | bytes 172040 | tf_op jit(solution)/shard_map/ppermute | solution.py:41
  55.9 1.7 %collective-permute-done.13 = bf16[4,7168]{1,0:T(4,128)(2,1)S(1)} collective-permute-done((bf16[4,7168]{1,0:T(4,128)(2,1)S(1)}, bf16[4,7168]{1,0:T(4,128)(2,1)S(1)}, u32[]{:S(2)}, u32[]{:S(2)}) %collective-permute-start.13) | collective-permute-done | bytes 57376 | tf_op jit(solution)/shard_map/ppermute | solution.py:41
  57.6 1.7 %collective-permute-done.15 = bf16[4,7168]{1,0:T(4,128)(2,1)S(1)} collective-permute-done((bf16[4,7168]{1,0:T(4,128)(2,1)S(1)}, bf16[4,7168]{1,0:T(4,128)(2,1)S(1)}, u32[]{:S(2)}, u32[]{:S(2)}) %collective-permute-start.15) | collective-permute-done | bytes 57376 | tf_op jit(solution)/shard_map/ppermute | solution.py:41
  59.3 0.0 collective-permute-done.14
  59.3 0.7 %add_convert_fusion.6 = bf16[4,7168]{1,0:T(4,128)(2,1)} fusion(bf16[4,7168]{1,0:T(4,128)(2,1)S(1)} %collective-permute-done.15, bf16[4,7168]{1,0:T(4,128)(2,1)S(1)} %collective-permute-done.14, bf16[4,7168]{1,0:T(4,128)(2,1)S(1)} %collective-permute-done.13, bf16[16,3584]{1,0:T(8,128)(2,1)S(1)} %add_convert_fusion.5, bf16[16,3584]{1,0:T(8,128)(2,1)S(1)} %add_convert_fusion.4), kind=kLoop, calls=%fused_computation.12 | loop fusion | flops 315392 | bytes 458752 | tf_op jit(solution)/shard_map/convert_element_type | solution.py:378
  (7 shorter events, 0.1 us)
Async XLA Ops:
  0.9 8.6 %collective-permute-start.2 = (bf16[4,7296]{1,0:T(4,128)(2,1)S(1)}, bf16[4,7296]{1,0:T(4,128)(2,1)S(1)}, u32[]{:S(2)}, u32[]{:S(2)}) collective-permute-start(bf16[4,7296]{1,0:T(4,128)(2,1)S(1)} %extend.1.after_ref.refs_0_), channel_id=1, source_target_pairs={{0,2},{1,3},{2,0},{3,1},{16,18},{17,19},{18,16},{19,17},{4,6},{5,7... | collective-permute-start | bytes 175112 | tf_op jit(solution)/shard_map/ppermute | solution.py:41
  5.0 6.1 %collective-permute-start.1 = (bf16[4,7296]{1,0:T(4,128)(2,1)S(1)}, bf16[4,7296]{1,0:T(4,128)(2,1)S(1)}, u32[]{:S(2)}, u32[]{:S(2)}) collective-permute-start(bf16[4,7296]{1,0:T(4,128)(2,1)S(1)} %extend.1.after_ref.refs_0_), channel_id=1, source_target_pairs={{0,3},{1,2},{2,1},{3,0},{16,19},{17,18},{18,17},{19,16},{4,7},{5,6... | collective-permute-start | bytes 175112 | tf_op jit(solution)/shard_map/ppermute | solution.py:41
  6.3 4.8 %collective-permute-start = (bf16[4,7296]{1,0:T(4,128)(2,1)S(1)}, bf16[4,7296]{1,0:T(4,128)(2,1)S(1)}, u32[]{:S(2)}, u32[]{:S(2)}) collective-permute-start(bf16[4,7296]{1,0:T(4,128)(2,1)S(1)} %extend.1.after_ref.refs_0_), channel_id=1, source_target_pairs={{0,1},{1,0},{2,3},{3,2},{16,17},{17,16},{18,19},{19,18},{4,5},{5,4... | collective-permute-start | bytes 175112 | tf_op jit(solution)/shard_map/ppermute | solution.py:41
  11.2 6.2 %collective-permute-start.3 = (bf16[16,7296]{1,0:T(8,128)(2,1)S(1)}, bf16[16,7296]{1,0:T(8,128)(2,1)S(1)}, u32[]{:S(2)}, u32[]{:S(2)}) collective-permute-start(bf16[16,7296]{1,0:T(8,128)(2,1)S(1)} %stack.2.refs_0_), channel_id=1, source_target_pairs={{0,8},{4,12},{8,0},{12,4},{16,20},{20,16},{24,28},{28,24},{1,9},{5... | collective-permute-start | bytes 700424 | tf_op jit(solution)/shard_map/ppermute | solution.py:26
  17.5 8.6 %collective-permute-start.4 = (bf16[32,7296]{1,0:T(8,128)(2,1)S(1)}, bf16[32,7296]{1,0:T(8,128)(2,1)S(1)}, u32[]{:S(2)}, u32[]{:S(2)}) collective-permute-start(bf16[32,7296]{1,0:T(8,128)(2,1)S(1)} %stack.3.refs_0_), channel_id=1, source_target_pairs={{0,4},{4,0},{8,12},{12,8},{16,24},{20,28},{24,16},{28,20},{1,5},{5... | collective-permute-start | bytes 1400840 | tf_op jit(solution)/shard_map/ppermute | solution.py:26
  22.2 3.9 %collective-permute-start.5 = (bf16[32,7296]{1,0:T(8,128)(2,1)S(1)}, bf16[32,7296]{1,0:T(8,128)(2,1)S(1)}, u32[]{:S(2)}, u32[]{:S(2)}) collective-permute-start(bf16[32,7296]{1,0:T(8,128)(2,1)S(1)} %stack.3.refs_0_), channel_id=1, source_target_pairs={{0,16},{16,0},{1,17},{17,1},{2,18},{18,2},{3,19},{19,3},{4,20},{20... | collective-permute-start | bytes 1400840 | tf_op jit(solution)/shard_map/ppermute | solution.py:45
  26.1 1.8 %collective-permute-start.6 = (bf16[32,7296]{1,0:T(8,128)(2,1)S(1)}, bf16[32,7296]{1,0:T(8,128)(2,1)S(1)}, u32[]{:S(2)}, u32[]{:S(2)}) collective-permute-start(bf16[32,7296]{1,0:T(8,128)(2,1)S(1)} %collective-permute-done.4.refs_1_), channel_id=1, source_target_pairs={{0,16},{16,0},{1,17},{17,1},{2,18},{18,2},{3,19},{19,3},{4,20},{20... | collective-permute-start | bytes 1400840 | tf_op jit(solution)/shard_map/ppermute | solution.py:45
  35.5 1.9 %collective-permute-start.7 = (bf16[64,3584]{1,0:T(8,128)(2,1)S(1)}, bf16[64,3584]{1,0:T(8,128)(2,1)S(1)}, u32[]{:S(2)}, u32[]{:S(2)}) collective-permute-start(bf16[64,3584]{1,0:T(8,128)(2,1)S(1)} %get-tuple-element.61), channel_id=1, source_target_pairs={{0,16},{16,0},{1,17},{17,1},{2,18},{18,2},{3,19},{19,3},{4,20},{20... | collective-permute-start | bytes 1376264 | tf_op jit(solution)/shard_map/ppermute | solution.py:45
  36.9 2.2 %collective-permute-start.10 = (bf16[64,3584]{1,0:T(8,128)(2,1)S(1)}, bf16[64,3584]{1,0:T(8,128)(2,1)S(1)}, u32[]{:S(2)}, u32[]{:S(2)}) collective-permute-start(bf16[64,3584]{1,0:T(8,128)(2,1)S(1)} %get-tuple-element.66), channel_id=1, source_target_pairs={{0,16},{16,0},{1,17},{17,1},{2,18},{18,2},{3,19},{19,3},{4,20},{20... | collective-permute-start | bytes 1376264 | tf_op jit(solution)/shard_map/ppermute | solution.py:45
  37.5 6.1 %collective-permute-start.8 = (bf16[32,3584]{1,0:T(8,128)(2,1)S(1)}, bf16[32,3584]{1,0:T(8,128)(2,1)S(1)}, u32[]{:S(2)}, u32[]{:S(2)}) collective-permute-start(bf16[32,3584]{1,0:T(8,128)(2,1)S(1)} %slice.49), channel_id=1, source_target_pairs={{0,4},{4,0},{8,12},{12,8},{16,24},{20,28},{24,16},{28,20},{1,5},{5... | collective-permute-start | bytes 688136 | tf_op jit(solution)/shard_map/ppermute | solution.py:26
  39.2 7.2 %collective-permute-start.11 = (bf16[32,3584]{1,0:T(8,128)(2,1)S(1)}, bf16[32,3584]{1,0:T(8,128)(2,1)S(1)}, u32[]{:S(2)}, u32[]{:S(2)}) collective-permute-start(bf16[32,3584]{1,0:T(8,128)(2,1)S(1)} %slice.53), channel_id=1, source_target_pairs={{0,4},{4,0},{8,12},{12,8},{16,24},{20,28},{24,16},{28,20},{1,5},{5... | collective-permute-start | bytes 688136 | tf_op jit(solution)/shard_map/ppermute | solution.py:26
  43.6 4.9 %collective-permute-start.9 = (bf16[16,3584]{1,0:T(8,128)(2,1)S(1)}, bf16[16,3584]{1,0:T(8,128)(2,1)S(1)}, u32[]{:S(2)}, u32[]{:S(2)}) collective-permute-start(bf16[16,3584]{1,0:T(8,128)(2,1)S(1)} %slice.51), channel_id=1, source_target_pairs={{0,8},{4,12},{8,0},{12,4},{16,20},{20,16},{24,28},{28,24},{1,9},{5... | collective-permute-start | bytes 344072 | tf_op jit(solution)/shard_map/ppermute | solution.py:26
  46.5 4.9 %collective-permute-start.12 = (bf16[16,3584]{1,0:T(8,128)(2,1)S(1)}, bf16[16,3584]{1,0:T(8,128)(2,1)S(1)}, u32[]{:S(2)}, u32[]{:S(2)}) collective-permute-start(bf16[16,3584]{1,0:T(8,128)(2,1)S(1)} %slice.55), channel_id=1, source_target_pairs={{0,8},{4,12},{8,0},{12,4},{16,20},{20,16},{24,28},{28,24},{1,9},{5... | collective-permute-start | bytes 344072 | tf_op jit(solution)/shard_map/ppermute | solution.py:26
  51.4 6.1 %collective-permute-start.13 = (bf16[4,7168]{1,0:T(4,128)(2,1)S(1)}, bf16[4,7168]{1,0:T(4,128)(2,1)S(1)}, u32[]{:S(2)}, u32[]{:S(2)}) collective-permute-start(bf16[4,7168]{1,0:T(4,128)(2,1)S(1)} %get-tuple-element.67), channel_id=1, source_target_pairs={{0,3},{1,2},{2,1},{3,0},{16,17},{17,16},{18,19},{19,18},{4,7},{5,6... | collective-permute-start | bytes 172040 | tf_op jit(solution)/shard_map/ppermute | solution.py:41
  54.0 5.3 %collective-permute-start.15 = (bf16[4,7168]{1,0:T(4,128)(2,1)S(1)}, bf16[4,7168]{1,0:T(4,128)(2,1)S(1)}, u32[]{:S(2)}, u32[]{:S(2)}) collective-permute-start(bf16[4,7168]{1,0:T(4,128)(2,1)S(1)} %get-tuple-element.68), channel_id=1, source_target_pairs={{0,2},{1,3},{2,0},{3,1},{16,19},{17,18},{18,17},{19,16},{4,6},{5,7... | collective-permute-start | bytes 172040 | tf_op jit(solution)/shard_map/ppermute | solution.py:41
  54.0 5.3 %collective-permute-start.14 = (bf16[4,7168]{1,0:T(4,128)(2,1)S(1)}, bf16[4,7168]{1,0:T(4,128)(2,1)S(1)}, u32[]{:S(2)}, u32[]{:S(2)}) collective-permute-start(bf16[4,7168]{1,0:T(4,128)(2,1)S(1)} %get-tuple-element.69), channel_id=1, source_target_pairs={{0,1},{1,0},{2,3},{3,2},{16,18},{17,19},{18,16},{19,17},{4,5},{5,4... | collective-permute-start | bytes 172040 | tf_op jit(solution)/shard_map/ppermute | solution.py:41
